TPU v7x, 32 devices: a whole 2x2x4 slice. The times are simulated.
32 devices in a mesh: ctx: 8 (over y, x, core), wsh: 4 (over z).
Axes of the slice: x: 2, y: 2, z: 4, core: 2. Of those that a mesh axis runs over, the one named last changes fastest.
Arguments:
- tokens: bfloat16 [8, 2048, 1024], P('wsh', 'ctx'), may hold values from -6 to 6
- out_grad: bfloat16 [8, 2048, 1024], P('wsh', 'ctx'), may hold values from -6 to 6
- seg_ids: int32 [8, 2048], P('wsh', 'ctx'), may hold values from 0 to 4, as said below
- positions: int32 [8, 2048], P('wsh', 'ctx'), may hold values from 0 to 1023, as said below
- ln1_gain: bfloat16 [1024], P('wsh'), may hold values from 0.5 to 1.5
- ln1_bias: bfloat16 [1024], P('wsh'), may hold values from -1.5 to 1.5
- w_qkv: bfloat16 [1024, 3072], P('wsh'), may hold values from -0.1875 to 0.1875
- w_out: bfloat16 [1024, 1024], P('wsh'), may hold values from -3 to 3
- ln2_gain: bfloat16 [1024], P('wsh'), may hold values from 0.5 to 1.5
- ln2_bias: bfloat16 [1024], P('wsh'), may hold values from -1.5 to 1.5
- w_up: bfloat16 [1024, 4096], P('wsh'), may hold values from -0.1875 to 0.1875
- w_down: bfloat16 [4096, 1024], P('wsh'), may hold values from -0.09375 to 0.09375
Outputs:
- output: bfloat16 [8, 2048, 1024], P('wsh', 'ctx')
- in_grad: bfloat16 [8, 2048, 1024], P('wsh', 'ctx')
- grad_ln1_gain: float32 [1024], P('wsh')
- grad_ln1_bias: float32 [1024], P('wsh')
- grad_w_qkv: float32 [1024, 3072], P('wsh')
- grad_w_out: float32 [1024, 1024], P('wsh')
- grad_ln2_gain: float32 [1024], P('wsh')
- grad_ln2_bias: float32 [1024], P('wsh')
- grad_w_up: float32 [1024, 4096], P('wsh')
- grad_w_down: float32 [4096, 1024], P('wsh')
Inputs may be any that keep to these rules, and one draw needn't show every extreme that they name: `seg_ids`: in every group of 2048 tokens segment 0 holds 1024 tokens and segments 1 to 4 hold 256 tokens each; within a segment each position from 0 to its length minus one appears once. The tokens come in aligned blocks of 128 tokens of one segment with consecutive positions; the blocks stand in any order. The positions that belong to seg_ids, as described there.
All inputs are finite; a program needn't handle non-finite values.
Results may differ from a plain program's by a relative error of at most 0.02.
Values may be sent and summed in bfloat16 or wider, within the bound.
No kernel may reach another device: no remote copies, remote signals or barrier semaphores. Data moves between devices by JAX's collectives and lax.ppermute only.
A program may use at most 384 MiB of HBM per device.

v0:
```python
import jax
import jax.numpy as jnp
from jax import lax
from jax.sharding import PartitionSpec as P

HEADS = 16


EPSILON = 1e-05
NEG_BIG = -1e30


def for_sending(value):
    return jax.tree.map(lambda a: a.astype(jnp.bfloat16) if a.dtype == jnp.float32 else a, value)


def layer_norm(values, gain, bias):
    average = jnp.mean(values, -1, keepdims=True)
    centred = values - average
    inv_std = lax.rsqrt(jnp.mean(centred * centred, -1, keepdims=True) + EPSILON)
    normed = centred * inv_std
    return (normed * gain + bias, normed, inv_std)


def norm_back(grad_out, normed, inv_std, gain):
    scaled = grad_out * gain
    return inv_std * (
        scaled
        - jnp.mean(scaled, -1, keepdims=True)
        - normed * jnp.mean(scaled * normed, -1, keepdims=True)
    )


def gelu_exact(values):
    return jax.nn.gelu(values, approximate=False)


def outer_sum(left, right):
    return lax.dot_general(
        left, right, (((0,), (0,)), ((), ())), preferred_element_type=jnp.float32
    )


def inner_dot(left, right):
    return lax.dot_general(
        left, right, (((1,), (1,)), ((), ())), preferred_element_type=jnp.float32
    )


def visible(query_seg, query_pos, key_seg, key_pos):
    shared = (key_seg[None, :] == 0) & (query_seg[:, None] != 0)
    within = (query_seg[:, None] == key_seg[None, :]) & (key_pos[None, :] <= query_pos[:, None])
    return shared | within


def score_grads(scores, allowed, log_rows, delta_rows, grad_heads, value_heads):
    powers = jnp.where(allowed, jnp.exp(scores - log_rows[..., None]), 0.0)
    grad_prob = jnp.einsum(
        "qhd,khd->hqk", grad_heads, value_heads, preferred_element_type=jnp.float32
    )
    grad_score = (powers * (grad_prob - delta_rows[..., None])).astype(jnp.bfloat16)
    return (powers, grad_score)


def shards(
    tokens,
    out_grad,
    seg_ids,
    positions,
    ln1_gain,
    ln1_bias,
    w_qkv,
    w_out,
    ln2_gain,
    ln2_bias,
    w_up,
    w_down,
):
    gathered = (
        lax.all_gather(ln1_gain, "wsh", axis=0, tiled=True),
        lax.all_gather(ln1_bias, "wsh", axis=0, tiled=True),
        lax.all_gather(w_qkv, "wsh", axis=0, tiled=True),
        lax.all_gather(w_out, "wsh", axis=0, tiled=True),
        lax.all_gather(ln2_gain, "wsh", axis=0, tiled=True),
        lax.all_gather(ln2_bias, "wsh", axis=0, tiled=True),
        lax.all_gather(w_up, "wsh", axis=0, tiled=True),
        lax.all_gather(w_down, "wsh", axis=0, tiled=True),
    )
    gain_one = gathered[0].astype(jnp.float32)
    bias_one = gathered[1].astype(jnp.float32)
    whole_proj = gathered[2]
    whole_out = gathered[3]
    gain_two = gathered[4].astype(jnp.float32)
    bias_two = gathered[5].astype(jnp.float32)
    whole_up = gathered[6]
    whole_down = gathered[7]
    key_segs, key_places = (
        lax.all_gather(seg_ids, "ctx", axis=1, tiled=True),
        lax.all_gather(positions, "ctx", axis=1, tiled=True),
    )
    tok_rows = tokens.shape[1]
    model_width = whole_out.shape[0]
    head_count = HEADS
    head_dim = model_width // head_count
    score_scale = head_dim ** (-0.5)

    def micro_step(carried, inputs):
        tokens_mb, cotangent_mb, query_seg, query_pos, key_seg, key_pos = inputs
        stream = tokens_mb.astype(jnp.float32)
        attn_full, attn_norm, attn_rstd = layer_norm(stream, gain_one, bias_one)
        attn_in = attn_full.astype(jnp.bfloat16)
        projected = jnp.dot(attn_in, whole_proj, preferred_element_type=jnp.float32).astype(
            jnp.bfloat16
        )
        query_heads = projected[:, :model_width].reshape(tok_rows, head_count, head_dim)
        key_values = projected[:, model_width:]

        def scores_for(block_rows):
            length = block_rows.shape[0]
            key_heads = block_rows[:, :model_width].reshape(length, head_count, head_dim)
            value_heads = block_rows[:, model_width:].reshape(length, head_count, head_dim)
            scores = (
                jnp.einsum(
                    "qhd,khd->hqk", query_heads, key_heads, preferred_element_type=jnp.float32
                )
                * score_scale
            )
            allowed = visible(query_seg, query_pos, key_seg, key_pos)
            return (scores, allowed[None], key_heads, value_heads)

        highest = jnp.full((head_count, tok_rows), NEG_BIG, jnp.float32)
        scores, allowed, key_heads, value_heads = scores_for(
            lax.all_gather(key_values, "ctx", axis=0, tiled=True)
        )
        scores = jnp.where(allowed, scores, NEG_BIG)
        new_high = jnp.maximum(highest, jnp.max(scores, -1))
        powers = jnp.where(allowed, jnp.exp(scores - new_high[..., None]), 0.0)
        summed = jnp.einsum(
            "hqk,khd->hqd",
            powers.astype(jnp.bfloat16),
            value_heads,
            preferred_element_type=jnp.float32,
        )
        highest, totals, summed = (new_high, jnp.sum(powers, -1), summed)
        log_total = highest + jnp.log(totals)
        attn_exact = summed / totals[..., None]
        attn_low = attn_exact.transpose(1, 0, 2).reshape(tok_rows, model_width).astype(jnp.bfloat16)
        residual = stream + jnp.dot(attn_low, whole_out, preferred_element_type=jnp.float32)
        ffn_full, ffn_norm, ffn_rstd = layer_norm(residual, gain_two, bias_two)
        ffn_in = ffn_full.astype(jnp.bfloat16)
        up_proj = jnp.dot(ffn_in, whole_up, preferred_element_type=jnp.float32)
        hidden_full, gelu_pull = jax.vjp(gelu_exact, up_proj)
        hidden = hidden_full.astype(jnp.bfloat16)
        output = (
            residual + jnp.dot(hidden, whole_down, preferred_element_type=jnp.float32)
        ).astype(jnp.bfloat16)
        cotangent = cotangent_mb.astype(jnp.float32)
        grad_down = outer_sum(hidden, cotangent_mb)
        grad_hidden = inner_dot(cotangent_mb, whole_down)
        grad_up_in = gelu_pull(grad_hidden)[0].astype(jnp.bfloat16)
        grad_upper = outer_sum(ffn_in, grad_up_in)
        grad_ffn_in = inner_dot(grad_up_in, whole_up)
        grad_gain_two = jnp.sum(grad_ffn_in * ffn_norm, 0)
        grad_bias_two = jnp.sum(grad_ffn_in, 0)
        grad_resid = cotangent + norm_back(grad_ffn_in, ffn_norm, ffn_rstd, gain_two)
        grad_branch = grad_resid.astype(jnp.bfloat16)
        grad_outer = outer_sum(attn_low, grad_branch)
        grad_attn = inner_dot(grad_branch, whole_out).astype(jnp.bfloat16)
        grad_heads = grad_attn.reshape(tok_rows, head_count, head_dim)
        delta_sum = jnp.einsum("qhd,hqd->hq", grad_heads.astype(jnp.float32), attn_exact)
        block_rows = lax.all_gather(key_values, "ctx", axis=0, tiled=True)
        scores, allowed, key_heads, value_heads = scores_for(block_rows)
        powers, grad_score = score_grads(
            scores, allowed, log_total, delta_sum, grad_heads, value_heads
        )
        grad_value = jnp.einsum(
            "hqk,qhd->khd",
            powers.astype(jnp.bfloat16),
            grad_heads,
            preferred_element_type=jnp.float32,
        )
        grad_query = (
            jnp.einsum("hqk,khd->qhd", grad_score, key_heads, preferred_element_type=jnp.float32)
            * score_scale
        )
        grad_key = (
            jnp.einsum("hqk,qhd->khd", grad_score, query_heads, preferred_element_type=jnp.float32)
            * score_scale
        )
        length = block_rows.shape[0]
        key_terms = jnp.concatenate(
            [grad_key.reshape(length, model_width), grad_value.reshape(length, model_width)], 1
        )
        back_state = (grad_query, key_terms)
        grad_query, key_buffer = back_state
        grad_kv = lax.psum_scatter(
            key_buffer.astype(jnp.bfloat16), "ctx", scatter_dimension=0, tiled=True
        ).astype(jnp.float32)
        grad_proj = jnp.concatenate([grad_query.reshape(tok_rows, model_width), grad_kv], 1).astype(
            jnp.bfloat16
        )
        grad_projw = outer_sum(attn_in, grad_proj)
        grad_attn_in = inner_dot(grad_proj, whole_proj)
        grad_gain_one = jnp.sum(grad_attn_in * attn_norm, 0)
        grad_bias_one = jnp.sum(grad_attn_in, 0)
        in_grad = (grad_resid + norm_back(grad_attn_in, attn_norm, attn_rstd, gain_one)).astype(
            jnp.bfloat16
        )
        fresh_grads = (
            grad_gain_one,
            grad_bias_one,
            grad_projw,
            grad_outer,
            grad_gain_two,
            grad_bias_two,
            grad_upper,
            grad_down,
        )
        carried = jax.tree.map(
            lambda earlier, latest: earlier + latest, carried, tuple(fresh_grads)
        )
        return (carried, (output, in_grad))

    start_grads = tuple((jnp.zeros(whole.shape, jnp.float32) for whole in gathered))
    summed_grads, produced = lax.scan(
        micro_step, start_grads, (tokens, out_grad, seg_ids, positions, key_segs, key_places)
    )
    summed_grads = jax.tree.map(
        lambda part: part.astype(jnp.float32),
        lax.psum_scatter(for_sending(tuple(summed_grads)), "wsh", scatter_dimension=0, tiled=True),
    )
    summed_grads = jax.tree.map(
        lambda part: part.astype(jnp.float32), lax.psum(for_sending(tuple(summed_grads)), "ctx")
    )
    return (produced[0], produced[1]) + tuple(summed_grads)


def solution(mesh):
    in_specs = (
        P("wsh", "ctx", None),
        P("wsh", "ctx", None),
        P("wsh", "ctx"),
        P("wsh", "ctx"),
        P("wsh"),
        P("wsh"),
        P("wsh", None),
        P("wsh", None),
        P("wsh"),
        P("wsh"),
        P("wsh", None),
        P("wsh", None),
    )
    out_specs = (
        P("wsh", "ctx", None),
        P("wsh", "ctx", None),
        P("wsh"),
        P("wsh"),
        P("wsh", None),
        P("wsh", None),
        P("wsh"),
        P("wsh"),
        P("wsh", None),
        P("wsh", None),
    )
    return jax.shard_map(shards, mesh=mesh, in_specs=in_specs, out_specs=out_specs, check_vma=False)
```

profile of v0, /device:TPU:0, one launch (start us, length us, event | category | flops | bytes accessed | tf_op | source)
XLA Modules:
  0.0 1688.3 jit_solution(7204161132179646974)
XLA Ops:
  10.2 12.6 all-gather
  22.8 7.7 all-gather.1
  30.6 10.7 all-gather.2
  41.3 7.7 all-gather.3
  49.0 8.0 all_gather.37
  57.0 8.9 all_gather.38
  65.9 108.3 %all-gather.10.cloned.1.call-done = bf16[1024,3072]{1,0:T(8,128)(2,1)} async-done(((bf16[256,3072]{1,0:T(8,128)(2,1)}), bf16[1024,3072]{1,0:T(8,128)(2,1)}) %all-gather.10.cloned.1.call-update) | async-done | bytes 6291472 | tf_op jit(solution)/shard_map/all_gather | solution.py:82
  174.3 149.5 %all-gather.14.cloned.1.call-done = bf16[1024,4096]{1,0:T(8,128)(2,1)} async-done(((bf16[256,4096]{1,0:T(8,128)(2,1)}), bf16[1024,4096]{1,0:T(8,128)(2,1)}) %all-gather.14.cloned.1.call-update) | async-done | bytes 8388624 | tf_op jit(solution)/shard_map/all_gather | solution.py:86
  323.7 149.3 %all-gather.16.cloned.1.call-done = bf16[4096,1024]{1,0:T(8,128)(2,1)} async-done(((bf16[1024,1024]{1,0:T(8,128)(2,1)}), bf16[4096,1024]{1,0:T(8,128)(2,1)}) %all-gather.16.cloned.1.call-update) | async-done | bytes 8388624 | tf_op jit(solution)/shard_map/all_gather | solution.py:87
  473.1 633.6 %while.29 = (s32[]{:T(128)}, f32[1024]{0:T(1024)}, f32[1024]{0:T(1024)}, f32[1024,3072]{1,0:T(8,128)}, f32[1024,1024]{1,0:T(8,128)}, /*index=5*/f32[1024]{0:T(10...) while((s32[]{:T(128)}, f32[1024]{0:T(1024)}, ...), condition=%wide.region_16.17_spmd.clone, body=%wide.region_0.16_spmd.clone.sunk | while | flops 26125801472 | bytes 666282624 | solution.py:225
  473.9 4.7 convolution_convert_fusion.4
  483.1 50.6 %all-gather.18.cloned.1.call-done = bf16[2048,2048]{1,0:T(8,128)(2,1)} async-done(((bf16[256,2048]{1,0:T(8,128)(2,1)}), bf16[2048,2048]{1,0:T(8,128)(2,1)}) %all-gather.18.cloned.1.call-update) | async-done | bytes 8388624 | tf_op jit(solution)/shard_map/while/body/eval_jaxpr/all_gather | solution.py:171
  533.6 6.1 fusion.165
  539.7 6.5 copy.51
  546.2 16.0 select_reduce_fusion.2
  562.2 6.4 copy.52
  568.6 15.5 fusion.166
  584.2 16.9 %fusion.167 = (bf16[256,16,64]{0,2,1:T(8,128)(2,1)}, f32[16,256,64]{1,2,0:T(8,128)}) fusion(f32[256,16]{0,1:T(8,128)S(1)} %bitcast.227, bf16[2048,16,64]{0,2,1:T(8,128)(2,1)} %bitcast.218, f32[16,256,2048]{2,1,0:T(8,128)} %get-tuple-element.508, f32[16,256]{1,0:T(8,128)S(1)} %broadcast_maximum_fusion.2, pred[256,2048]{1,0:T(8,128)(4,1)S(1)} %and_or_fusion.2), kind=kOutput, calls=%fused_computation.67.clone.1 | convolution fusion | flops 1116209152 | bytes 39878656 | tf_op jit(solution)/shard_map/while/body/eval_jaxpr/hqk,khd->hqd/dot_general | solution.py:138
  604.1 16.5 multiply_convert_fusion.6
  620.6 11.5 add_convert_fusion.7
  640.5 16.3 fusion.169
  656.8 22.9 %multiply_convert_fusion.7 = bf16[16,256,2048]{2,1,0:T(8,128)(2,1)} fusion(f32[16,256,2048]{2,1,0:T(8,128)} %get-tuple-element.508, bf16[256,16,64]{0,2,1:T(8,128)(2,1)} %bitcast.224, bf16[2048,16,64]{0,2,1:T(8,128)(2,1)} %bitcast.219, f32[16,256]{1,0:T(8,128)S(1)} %fusion.170, f32[16,256]{1,0:T(8,128)S(1)} %log_add_fusion.2, ...), kind=kOutput, calls=%fused_computation.clone.1 | convolution fusion | flops 1124073472 | bytes 55607296 | tf_op jit(solution)/shard_map/while/body/eval_jaxpr/qhd,khd->hqk/dot_general | solution.py:58
  679.7 10.8 multiply_convert_fusion.8
  690.5 8.4 pad_maximum_fusion.7
  702.7 6.6 fusion.173
  710.3 8.8 select_add_fusion.19
  719.1 13.3 fusion.171
  732.5 10.2 select_add_fusion.18
  742.7 27.7 %reduce-scatter.14.cloned.1.call-done = bf16[256,2048]{0,1:T(8,128)(2,1)} async-done(((bf16[2048,2048]{0,1:T(8,128)(2,1)}), bf16[256,2048]{0,1:T(8,128)(2,1)}) %reduce-scatter.14.cloned.1.call-update) | async-done | bytes 1048592 | tf_op jit(solution)/shard_map/while/body/eval_jaxpr/reduce_scatter | solution.py:196
  770.4 5.5 fusion.172
  777.5 8.0 select_add_fusion.15
  786.3 4.7 convolution_convert_fusion.4
  795.5 52.3 %all-gather.18.cloned.1.call-done = bf16[2048,2048]{1,0:T(8,128)(2,1)} async-done(((bf16[256,2048]{1,0:T(8,128)(2,1)}), bf16[2048,2048]{1,0:T(8,128)(2,1)}) %all-gather.18.cloned.1.call-update) | async-done | bytes 8388624 | tf_op jit(solution)/shard_map/while/body/eval_jaxpr/all_gather | solution.py:171
  847.8 6.1 fusion.165
  853.9 6.5 copy.51
  860.4 16.0 select_reduce_fusion.2
  876.4 6.4 copy.52
  882.8 15.5 fusion.166
  898.4 16.9 %fusion.167 = (bf16[256,16,64]{0,2,1:T(8,128)(2,1)}, f32[16,256,64]{1,2,0:T(8,128)}) fusion(f32[256,16]{0,1:T(8,128)S(1)} %bitcast.227, bf16[2048,16,64]{0,2,1:T(8,128)(2,1)} %bitcast.218, f32[16,256,2048]{2,1,0:T(8,128)} %get-tuple-element.508, f32[16,256]{1,0:T(8,128)S(1)} %broadcast_maximum_fusion.2, pred[256,2048]{1,0:T(8,128)(4,1)S(1)} %and_or_fusion.2), kind=kOutput, calls=%fused_computation.67.clone.1 | convolution fusion | flops 1116209152 | bytes 39878656 | tf_op jit(solution)/shard_map/while/body/eval_jaxpr/hqk,khd->hqd/dot_general | solution.py:138
  918.3 16.2 multiply_convert_fusion.6
  934.5 11.7 add_convert_fusion.7
  954.6 16.3 fusion.169
  970.9 22.9 %multiply_convert_fusion.7 = bf16[16,256,2048]{2,1,0:T(8,128)(2,1)} fusion(f32[16,256,2048]{2,1,0:T(8,128)} %get-tuple-element.508, bf16[256,16,64]{0,2,1:T(8,128)(2,1)} %bitcast.224, bf16[2048,16,64]{0,2,1:T(8,128)(2,1)} %bitcast.219, f32[16,256]{1,0:T(8,128)S(1)} %fusion.170, f32[16,256]{1,0:T(8,128)S(1)} %log_add_fusion.2, ...), kind=kOutput, calls=%fused_computation.clone.1 | convolution fusion | flops 1124073472 | bytes 55607296 | tf_op jit(solution)/shard_map/while/body/eval_jaxpr/qhd,khd->hqk/dot_general | solution.py:58
  993.8 10.8 multiply_convert_fusion.8
  1004.6 8.4 pad_maximum_fusion.7
  1014.0 5.1 select_add_fusion.16
  1019.2 7.1 fusion.173
  1027.3 15.1 select_add_fusion.19
  1042.4 13.0 fusion.171
  1055.4 15.3 select_add_fusion.18
  1070.7 13.7 reduce-scatter.14.cloned.1.call-done
  1084.5 5.5 fusion.172
  1091.6 11.7 select_add_fusion.15
  1110.6 8.2 convert_element_type.139
  1118.8 9.1 convert_element_type.147
  1128.0 9.2 convert_element_type.149
  1137.3 17.2 %reduce-scatter.8.cloned.1.call-done = bf16[256,1024]{1,0:T(8,128)(2,1)} async-done(((bf16[1024,1024]{1,0:T(8,128)(2,1)}), bf16[256,1024]{1,0:T(8,128)(2,1)}) %reduce-scatter.8.cloned.1.call-update) | async-done | bytes 524304 | tf_op jit(solution)/shard_map/reduce_scatter | solution.py:230
  1154.6 112.4 %reduce-scatter.6.cloned.1.call-done = bf16[256,3072]{1,0:T(8,128)(2,1)} async-done(((bf16[1024,3072]{1,0:T(8,128)(2,1)}), bf16[256,3072]{1,0:T(8,128)(2,1)}) %reduce-scatter.6.cloned.1.call-update) | async-done | bytes 1572880 | tf_op jit(solution)/shard_map/reduce_scatter | solution.py:230
  1266.9 147.5 %reduce-scatter.10.cloned.1.call-done = bf16[256,4096]{1,0:T(8,128)(2,1)} async-done(((bf16[1024,4096]{1,0:T(8,128)(2,1)}), bf16[256,4096]{1,0:T(8,128)(2,1)}) %reduce-scatter.10.cloned.1.call-update) | async-done | bytes 2097168 | tf_op jit(solution)/shard_map/reduce_scatter | solution.py:230
  1414.4 147.6 %reduce-scatter.12.cloned.1.call-done = bf16[1024,1024]{1,0:T(8,128)(2,1)} async-done(((bf16[4096,1024]{1,0:T(8,128)(2,1)}), bf16[1024,1024]{1,0:T(8,128)(2,1)}) %reduce-scatter.12.cloned.1.call-update) | async-done | bytes 2097168 | tf_op jit(solution)/shard_map/reduce_scatter | solution.py:230
  1563.3 11.3 all-reduce.6
  1574.9 12.6 all-reduce.4
  1589.8 81.9 %all-reduce.9.cloned.1.call-done = (bf16[256,3072]{1,0:T(8,128)(2,1)}, bf16[256,1024]{1,0:T(8,128)(2,1)}, bf16[256,4096]{1,0:T(8,128)(2,1)}, bf16[1024,1024]{1,0:T(8,128)(2,1)}) async-done(((bf16[256,3072]{1,0:T(8,128)(2,1)}, bf16[256,1024]{1,0:T(8,128)(2,1)}, bf16[256,4096]{1,0:T(8,128)(2,1)}, bf16[1024,1024]{1,0:T(8,128)(2,1)}), (bf16[256,3072]{1,0:T(8,128)(2,1)}, bf16[256,1024]{1,0:T(8,128)(2,1)}, ...) | async-done | bytes 6291472 | tf_op jit(solution)/shard_map/psum | solution.py:233
  1671.7 4.2 convert_element_type.148
  (303 shorter events, 58.0 us)
Async XLA Ops:
  7.2 15.6 copy-start.44
  7.2 23.4 %copy-start.45 = (bf16[256]{0:T(256)(128)(2,1)S(1)}, bf16[256]{0:T(256)(128)(2,1)}, u32[]{:S(2)}) copy-start(bf16[256]{0:T(256)(128)(2,1)} %param.22) | copy-start | bytes 1540
  7.2 34.1 %copy-start.46 = (bf16[256]{0:T(256)(128)(2,1)S(1)}, bf16[256]{0:T(256)(128)(2,1)}, u32[]{:S(2)}) copy-start(bf16[256]{0:T(256)(128)(2,1)} %param.23) | copy-start | bytes 1540
  7.2 41.8 %copy-start.37 = (s32[2,256]{1,0:T(2,128)S(1)}, s32[2,256]{1,0:T(2,128)}, u32[]{:S(2)}) copy-start(s32[2,256]{1,0:T(2,128)} %param.16) | copy-start | bytes 6148
  7.2 49.8 %copy-start.39 = (s32[2,256]{1,0:T(2,128)S(1)}, s32[2,256]{1,0:T(2,128)}, u32[]{:S(2)}) copy-start(s32[2,256]{1,0:T(2,128)} %param.17) | copy-start | bytes 6148
  7.2 465.8 %copy-start.1 = (bf16[2,256,1024]{2,1,0:T(8,128)(2,1)S(1)}, bf16[2,256,1024]{2,1,0:T(8,128)(2,1)}, u32[]{:S(2)}) copy-start(bf16[2,256,1024]{2,1,0:T(8,128)(2,1)} %param.14) | copy-start | bytes 3145732
  7.3 58.7 %all-gather.12.cloned.1.call-start = ((), (), s32[]{:S(2)}) async-start(), calls=%async_computation.6 | async-start | bytes 2621440 | tf_op jit(solution)/shard_map/all_gather | solution.py:83
  8.0 166.3 %all-gather.10.cloned.1.call-start = ((), (), s32[]{:S(2)}) async-start(), calls=%async_computation.5 | async-start | bytes 7864320 | tf_op jit(solution)/shard_map/all_gather | solution.py:82
  8.7 315.0 %all-gather.14.cloned.1.call-start = ((), (), s32[]{:S(2)}) async-start(), calls=%async_computation.7 | async-start | bytes 10485760 | tf_op jit(solution)/shard_map/all_gather | solution.py:86
  9.5 463.6 %all-gather.16.cloned.1.call-start = ((), (), s32[]{:S(2)}) async-start(), calls=%async_computation.8 | async-start | bytes 10485760 | tf_op jit(solution)/shard_map/all_gather | solution.py:87
  473.4 8.9 copy-start.21
  473.4 9.0 copy-start.23
  473.4 60.3 %all-gather.18.cloned.1.call-start = ((), (), s32[]{:S(2)}) async-start(), calls=%async_computation.14 | async-start | bytes 9437184 | tf_op jit(solution)/shard_map/while/body/eval_jaxpr/all_gather | solution.py:171
  480.9 289.5 %reduce-scatter.14.cloned.1.call-start = ((), (), s32[]{:S(2)}) async-start(), calls=%async_computation.15 | async-start | bytes 9437184 | tf_op jit(solution)/shard_map/while/body/eval_jaxpr/reduce_scatter | solution.py:196
  601.1 31.0 %slice-start = ((s8[8388608]{0:T(1024)(128)(4,1)}), s8[4194304]{0:T(1024)(128)(4,1)S(1)}, s32[]{:S(2)}) async-start(s8[8388608]{0:T(1024)(128)(4,1)} %bitcast.237), calls=%async_computation.16 | async-start | bytes 8388608 | tf_op jit(solution)/shard_map/while
  604.1 16.5 copy-start.7
  604.1 28.0 %slice-start.1 = ((s8[8388608]{0:T(1024)(128)(4,1)}), s8[4194304]{0:T(1024)(128)(4,1)S(1)}, s32[]{:S(2)}) async-start(s8[8388608]{0:T(1024)(128)(4,1)} %bitcast.237), calls=%async_computation.17 | async-start | bytes 8388608 | tf_op jit(solution)/shard_map/while
  702.7 7.6 copy-start.8
  732.5 37.9 %copy-start.17 = (f32[256]{0:T(256)S(1)}, f32[256]{0:T(256)}, u32[]{:S(2)}) copy-start(f32[256]{0:T(256)} %copy-done.16) | copy-start | bytes 3076 | tf_op jit(solution)/shard_map/while
  732.5 37.9 %copy-start.20 = (f32[256]{0:T(256)S(1)}, f32[256]{0:T(256)}, u32[]{:S(2)}) copy-start(f32[256]{0:T(256)} %copy-done.19) | copy-start | bytes 3076 | tf_op jit(solution)/shard_map/while
  770.4 7.0 copy-start.25
  770.4 7.0 copy-start.28
  770.4 7.0 copy-start.9
  770.4 7.0 copy-start.14
  777.4 8.1 copy-start.42
  777.4 8.1 copy-start.26
  777.4 8.1 copy-start.29
  777.5 8.0 copy-start.2
  777.5 8.0 copy-start.22
  777.5 8.0 copy-start.24
  777.5 8.0 copy-start.38
  777.5 8.0 copy-start.40
  785.8 8.9 copy-start.21
  785.8 9.0 copy-start.23
  785.8 62.0 %all-gather.18.cloned.1.call-start = ((), (), s32[]{:S(2)}) async-start(), calls=%async_computation.14 | async-start | bytes 9437184 | tf_op jit(solution)/shard_map/while/body/eval_jaxpr/all_gather | solution.py:171
  793.3 291.2 %reduce-scatter.14.cloned.1.call-start = ((), (), s32[]{:S(2)}) async-start(), calls=%async_computation.15 | async-start | bytes 9437184 | tf_op jit(solution)/shard_map/while/body/eval_jaxpr/reduce_scatter | solution.py:196
  915.3 30.9 %slice-start = ((s8[8388608]{0:T(1024)(128)(4,1)}), s8[4194304]{0:T(1024)(128)(4,1)S(1)}, s32[]{:S(2)}) async-start(s8[8388608]{0:T(1024)(128)(4,1)} %bitcast.237), calls=%async_computation.16 | async-start | bytes 8388608 | tf_op jit(solution)/shard_map/while
  918.3 16.2 copy-start.7
  918.3 27.9 %slice-start.1 = ((s8[8388608]{0:T(1024)(128)(4,1)}), s8[4194304]{0:T(1024)(128)(4,1)S(1)}, s32[]{:S(2)}) async-start(s8[8388608]{0:T(1024)(128)(4,1)} %bitcast.237), calls=%async_computation.17 | async-start | bytes 8388608 | tf_op jit(solution)/shard_map/while
  1019.2 8.1 copy-start.8
  1055.3 29.1 %copy-start.17 = (f32[256]{0:T(256)S(1)}, f32[256]{0:T(256)}, u32[]{:S(2)}) copy-start(f32[256]{0:T(256)} %copy-done.16) | copy-start | bytes 3076 | tf_op jit(solution)/shard_map/while
  1055.3 29.1 %copy-start.20 = (f32[256]{0:T(256)S(1)}, f32[256]{0:T(256)}, u32[]{:S(2)}) copy-start(f32[256]{0:T(256)} %copy-done.19) | copy-start | bytes 3076 | tf_op jit(solution)/shard_map/while
  1084.4 7.0 copy-start.25
  1084.5 7.0 copy-start.28
  1084.5 7.0 copy-start.9
  1084.5 7.0 copy-start.14
  1091.4 11.8 copy-start.42
  1091.5 11.8 copy-start.26
  1091.5 11.8 copy-start.29
  1091.5 11.7 copy-start.2
  1091.5 11.7 copy-start.22
  1091.5 11.7 copy-start.24
  1091.6 11.7 copy-start.38
  1091.6 11.7 copy-start.40
  1106.6 47.9 %reduce-scatter.8.cloned.1.call-start = ((), (), s32[]{:S(2)}) async-start(), calls=%async_computation.10 | async-start | bytes 2621440 | tf_op jit(solution)/shard_map/reduce_scatter | solution.py:230
  1110.5 156.4 %reduce-scatter.6.cloned.1.call-start = ((), (), s32[]{:S(2)}) async-start(), calls=%async_computation.9 | async-start | bytes 7864320 | tf_op jit(solution)/shard_map/reduce_scatter | solution.py:230
  1118.8 295.6 %reduce-scatter.10.cloned.1.call-start = ((), (), s32[]{:S(2)}) async-start(), calls=%async_computation.11 | async-start | bytes 10485760 | tf_op jit(solution)/shard_map/reduce_scatter | solution.py:230
  1127.9 434.0 %reduce-scatter.12.cloned.1.call-start = ((), (), s32[]{:S(2)}) async-start(), calls=%async_computation.12 | async-start | bytes 10485760 | tf_op jit(solution)/shard_map/reduce_scatter | solution.py:230
  1137.2 424.8 %copy-start.49 = (u32[32]{0:T(128)S(1)}, u32[32]{0:T(128)}, u32[]{:S(2)}) copy-start(u32[32]{0:T(128)} %constant.120) | copy-start | bytes 388
  1137.2 426.0 %copy-start.27 = (f32[1024]{0:T(1024)S(1)}, f32[1024]{0:T(1024)}, u32[]{:S(2)}) copy-start(f32[1024]{0:T(1024)} %get-tuple-element.728) | copy-start | bytes 12292
  1137.2 426.0 %copy-start.30 = (f32[1024]{0:T(1024)S(1)}, f32[1024]{0:T(1024)}, u32[]{:S(2)}) copy-start(f32[1024]{0:T(1024)} %get-tuple-element.729) | copy-start | bytes 12292
  1137.2 426.1 %copy-start.33 = (f32[1024]{0:T(1024)S(1)}, f32[1024]{0:T(1024)}, u32[]{:S(2)}) copy-start(f32[1024]{0:T(1024)} %get-tuple-element.732) | copy-start | bytes 12292
  1137.3 426.1 %copy-start.36 = (f32[1024]{0:T(1024)S(1)}, f32[1024]{0:T(1024)}, u32[]{:S(2)}) copy-start(f32[1024]{0:T(1024)} %get-tuple-element.733) | copy-start | bytes 12292
  1137.3 534.5 %all-reduce.9.cloned.1.call-start = ((), (), s32[]{:S(2)}) async-start(), calls=%async_computation.13 | async-start | bytes 12582912 | tf_op jit(solution)/shard_map/psum | solution.py:233
  (38 other events, 131.0 us)
Sparse Core Ops, SparseCore 0:
  9.7 48.7 all-gather.11
  60.0 114.2 all-gather.9
  175.8 147.8 all-gather.13
  325.2 147.8 all-gather.15
  481.0 52.6 all-gather.17
  699.1 71.2 reduce-scatter.13
  793.4 54.3 all-gather.17
  1013.1 71.2 reduce-scatter.13
  1110.7 43.8 reduce-scatter.7
  1156.8 110.0 reduce-scatter.5
  1269.4 144.9 reduce-scatter.9
  1416.8 145.1 reduce-scatter.11
  1566.0 105.6 all-reduce.8
where the time goes:
time: 1690 us
  waiting for transfers between devices  1060 us (63%)
  matrix products  373 us (22%)
  other arithmetic  100 us (6%)
  blocking collectives  79.5 us (5%)
  local copies, waits for them, and re-layouts  54.3 us (3%)
    reduce_scatter x4, waiting for transfers between devices, shards(): lax.psum_scatter(for_sending(tuple(summed_grads)), 'wsh', scatter_dimensi...  425 us
    all_gather x1, waiting for transfers between devices, shards(): lax.all_gather(w_up, 'wsh', axis=0, tiled=True)  149 us
    all_gather x1, waiting for transfers between devices, shards(): lax.all_gather(w_down, 'wsh', axis=0, tiled=True)  149 us
    all_gather x1, waiting for transfers between devices, shards(): lax.all_gather(w_qkv, 'wsh', axis=0, tiled=True)  108 us
    all_gather x2, waiting for transfers between devices, micro_step(): block_rows = lax.all_gather(key_values, 'ctx', axis=0, tiled=True)  103 us
    psum x1, waiting for transfers between devices, shards(): lax.psum(for_sending(tuple(summed_grads)), 'ctx')  81.9 us
    dot_general x8, matrix products, outer_sum(): lax.dot_general(left, right, (((0,), (0,)), ((), ())), preferred_element_...  77 us
    dot_general x2, matrix products, score_grads(): jnp.einsum('qhd,khd->hqk', grad_heads, value_heads, preferred_element_typ...  45.8 us
  transfers between devices with their start and end apart: 13, of which 12 were waited for; matrix products, arithmetic and copies ran while one was open for 8% of the time, Pallas kernels for 0%

commit v1 on v0

v1 whole, which is shorter than its diff:
```python
import functools

import jax
import jax.numpy as jnp
from jax import lax
from jax.experimental import pallas as pl
from jax.experimental.pallas import tpu as pltpu
from jax.sharding import Mesh
from jax.sharding import PartitionSpec as P

HEADS = 16
PROMPT = 1024
CONT = 256
UNIT = 64
TILE = 256
EPSILON = 1e-05
NEG_BIG = -1e30
CTX = ("a", "b", "c")
F32 = jnp.float32
BF16 = jnp.bfloat16


def layer_norm(values, gain, bias):
    average = jnp.mean(values, -1, keepdims=True)
    centred = values - average
    inv_std = lax.rsqrt(jnp.mean(centred * centred, -1, keepdims=True) + EPSILON)
    normed = centred * inv_std
    return (normed * gain + bias, normed, inv_std)


def norm_back(grad_out, normed, inv_std, gain):
    scaled = grad_out * gain
    return inv_std * (
        scaled
        - jnp.mean(scaled, -1, keepdims=True)
        - normed * jnp.mean(scaled * normed, -1, keepdims=True)
    )


def gelu_exact(values):
    return jax.nn.gelu(values, approximate=False)


def nn(left, right):
    return jnp.dot(left, right, preferred_element_type=F32)


def nt(left, right):
    return lax.dot_general(left, right, (((1,), (1,)), ((), ())), preferred_element_type=F32)


def tn(left, right):
    return lax.dot_general(left, right, (((0,), (0,)), ((), ())), preferred_element_type=F32)


def unit_place(index, per_owner):
    owner = index // per_owner
    return owner, pl.multiple_of((index - owner * per_owner) * UNIT, UNIT)


def forward_attention(heads, width, qkv, g, source, target):
    _, owners, rows, _ = qkv.shape
    total = owners * rows
    units, per_owner = total // UNIT, rows // UNIT
    size = width // heads
    scale = size**-0.5

    def kernel(src, dst, qkv_ref, out_ref, exact_ref, log_ref, qs, ks, vs, vt):
        for s in range(units):
            owner, place = unit_place(src[g * units + s], per_owner)
            block = qkv_ref[0, owner, pl.ds(place, UNIT), :]
            here = slice(s * UNIT, (s + 1) * UNIT)
            qs[here, :] = block[:, :width] * scale
            ks[here, :] = block[:, width : 2 * width]
            vs[here, :] = block[:, 2 * width :]
        vt[...] = vs[...].T
        row = lax.broadcasted_iota(jnp.int32, (TILE, TILE), 0)
        col = lax.broadcasted_iota(jnp.int32, (TILE, TILE), 1)
        causal = row <= col
        for i in range(total // TILE):
            here = slice(i * TILE, (i + 1) * TILE)
            before = min(i * TILE, PROMPT)
            outs = []
            for h in range(heads):
                lanes = slice(h * size, (h + 1) * size)
                query = qs[here, lanes]
                own = jnp.where(causal, nt(ks[here, lanes], query), NEG_BIG)
                high = jnp.max(own, 0, keepdims=True)
                if before:
                    past = nt(ks[:before, lanes], query)
                    high = jnp.maximum(high, jnp.max(past, 0, keepdims=True))
                own = jnp.exp(own - high)
                sums = jnp.sum(own, 0, keepdims=True)
                mixed = nn(vt[lanes, here], own.astype(BF16))
                if before:
                    past = jnp.exp(past - high)
                    sums = sums + jnp.sum(past, 0, keepdims=True)
                    mixed = mixed + nn(vt[lanes, :before], past.astype(BF16))
                log_ref[h : h + 1, here] = high + jnp.log(sums)
                outs.append(mixed / sums)
            both = jnp.concatenate(outs, 0) if heads > 1 else outs[0]
            exact_ref[:, here] = both
            low = both.T.astype(BF16)
            for u in range(TILE // UNIT):
                owner, place = unit_place(dst[g * units + i * (TILE // UNIT) + u], per_owner)
                out_ref[owner, pl.ds(place, UNIT), :] = low[u * UNIT : (u + 1) * UNIT, :]

    return pl.pallas_call(
        kernel,
        grid_spec=pltpu.PrefetchScalarGridSpec(
            num_scalar_prefetch=2,
            grid=(1,),
            in_specs=[pl.BlockSpec((1, owners, rows, 3 * width), lambda i, *_: (g, 0, 0, 0))],
            out_specs=[
                pl.BlockSpec((owners, rows, width), lambda i, *_: (0, 0, 0)),
                pl.BlockSpec((width, total), lambda i, *_: (0, 0)),
                pl.BlockSpec((heads, total), lambda i, *_: (0, 0)),
            ],
            scratch_shapes=[pltpu.VMEM((total, width), BF16)] * 3
            + [pltpu.VMEM((width, total), BF16)],
        ),
        out_shape=[
            jax.ShapeDtypeStruct((owners, rows, width), BF16),
            jax.ShapeDtypeStruct((width, total), F32),
            jax.ShapeDtypeStruct((heads, total), F32),
        ],
        compiler_params=pltpu.CompilerParams(vmem_limit_bytes=48 * 1024 * 1024),
        cost_estimate=pl.CostEstimate(
            flops=12 * total * total * width, bytes_accessed=16 * total * width, transcendentals=0
        ),
    )(source, target, qkv)


def backward_attention(heads, width, qkv, g, grad, exact, logs, source, target):
    _, owners, rows, _ = qkv.shape
    total = owners * rows
    units, per_owner = total // UNIT, rows // UNIT
    size = width // heads
    scale = size**-0.5
    wide = 2 * TILE

    def kernel(
        src, dst, qkv_ref, grad_ref, exact_ref, log_ref, out_ref, qs, ks, vs, gs, kt, delta, dqt, dk, dv
    ):
        for s in range(units):
            owner, place = unit_place(src[g * units + s], per_owner)
            block = qkv_ref[0, owner, pl.ds(place, UNIT), :]
            here = slice(s * UNIT, (s + 1) * UNIT)
            qs[here, :] = block[:, :width] * scale
            ks[here, :] = block[:, width : 2 * width]
            vs[here, :] = block[:, 2 * width :]
            owner, place = unit_place(dst[g * units + s], per_owner)
            gs[here, :] = grad_ref[owner, pl.ds(place, UNIT), :]
        kt[...] = ks[...].T
        for i in range(total // TILE):
            here = slice(i * TILE, (i + 1) * TILE)
            both = gs[here, :].astype(F32).T * exact_ref[:, here]
            for h in range(heads):
                delta[h : h + 1, here] = jnp.sum(
                    both[h * size : (h + 1) * size, :], 0, keepdims=True
                )
        dqt[...] = jnp.zeros_like(dqt)
        for j in range(total // TILE):
            here = slice(j * TILE, (j + 1) * TILE)
            if j * TILE < PROMPT:
                starts = [(j * TILE, TILE)]
                at = (j + 1) * TILE
                if (total - at) % wide:
                    starts.append((at, TILE))
                    at += TILE
                while at < total:
                    starts.append((at, wide))
                    at += wide
            else:
                starts = [(j * TILE, TILE)]
            for h in range(heads):
                lanes = slice(h * size, (h + 1) * size)
                key, value, key_t = ks[here, lanes], vs[here, lanes], kt[lanes, here]
                grad_key = grad_value = None
                for at, count in starts:
                    there = slice(at, at + count)
                    query, pull = qs[there, lanes], gs[there, lanes]
                    powers = jnp.exp(nt(key, query) - log_ref[h : h + 1, there])
                    if at == j * TILE:
                        row = lax.broadcasted_iota(jnp.int32, (TILE, TILE), 0)
                        col = lax.broadcasted_iota(jnp.int32, (TILE, TILE), 1)
                        powers = jnp.where(row <= col, powers, 0.0)
                    slope = powers * (nt(value, pull) - delta[h : h + 1, there])
                    powers, slope = powers.astype(BF16), slope.astype(BF16)
                    more_value, more_key = nn(powers, pull), nn(slope, query)
                    grad_value = more_value if grad_value is None else grad_value + more_value
                    grad_key = more_key if grad_key is None else grad_key + more_key
                    dqt[lanes, there] += nn(key_t, slope)
                dk[here, lanes] = grad_key.astype(BF16)
                dv[here, lanes] = grad_value.astype(BF16)
        for i in range(total // TILE):
            here = slice(i * TILE, (i + 1) * TILE)
            low = (dqt[:, here] * scale).T.astype(BF16)
            for u in range(TILE // UNIT):
                s = i * (TILE // UNIT) + u
                owner, place = unit_place(src[g * units + s], per_owner)
                block = jnp.concatenate(
                    [
                        low[u * UNIT : (u + 1) * UNIT, :],
                        dk[s * UNIT : (s + 1) * UNIT, :],
                        dv[s * UNIT : (s + 1) * UNIT, :],
                    ],
                    1,
                )
                out_ref[owner, pl.ds(place, UNIT), :] = block

    whole = lambda *shape: pl.BlockSpec(shape, lambda i, *_: (0,) * len(shape))
    return pl.pallas_call(
        kernel,
        grid_spec=pltpu.PrefetchScalarGridSpec(
            num_scalar_prefetch=2,
            grid=(1,),
            in_specs=[
                pl.BlockSpec((1, owners, rows, 3 * width), lambda i, *_: (g, 0, 0, 0)),
                whole(owners, rows, width),
                whole(width, total),
                whole(heads, total),
            ],
            out_specs=whole(owners, rows, 3 * width),
            scratch_shapes=[pltpu.VMEM((total, width), BF16)] * 4
            + [
                pltpu.VMEM((width, total), BF16),
                pltpu.VMEM((heads, total), F32),
                pltpu.VMEM((width, total), F32),
                pltpu.VMEM((total, width), BF16),
                pltpu.VMEM((total, width), BF16),
            ],
        ),
        out_shape=jax.ShapeDtypeStruct((owners, rows, 3 * width), BF16),
        compiler_params=pltpu.CompilerParams(vmem_limit_bytes=48 * 1024 * 1024),
        cost_estimate=pl.CostEstimate(
            flops=16 * total * total * width, bytes_accessed=16 * total * width, transcendentals=0
        ),
    )(source, target, qkv, grad, exact, logs)


def feed_forward(h2, pull, sums, others, mine, shares):
    tokens, model = h2.shape
    chunks = others + mine
    ff = chunks[0].shape[1] // 2
    parts = model // ff
    part, rows = model // shares, ff // shares
    first = sums is None
    n_other, n_mine, n_all = len(others), len(mine), len(chunks)
    step = min(ff, TILE)

    def kernel(*refs):
        it = iter(refs)
        h2_ref, pull_ref = next(it), next(it)
        starts = None if first else (next(it), next(it))
        chunk_refs = [next(it) for _ in chunks]
        out_ref, grad_ref = next(it), next(it)
        targets = (next(it), next(it)), (next(it), next(it))
        h2_t, held, down_w, sem = next(it), next(it), next(it), next(it)
        t = pl.program_id(0)
        slot = lax.rem(t, 2)

        def fetch(k, into):
            return pltpu.make_async_copy(chunk_refs[k], held.at[into], sem.at[into])

        @pl.when(t == 0)
        def _():
            fetch(0, 0).start()
            h2_t[...] = h2_ref[...].T
            if first:
                out_ref[...] = jnp.zeros_like(out_ref)
                grad_ref[...] = jnp.zeros_like(grad_ref)
            else:
                out_ref[...] = starts[0][...]
                grad_ref[...] = starts[1][...]

        for k in range(n_all):

            @pl.when(t == k)
            def _(k=k):
                fetch(k, k % 2).wait()
                if k + 1 < n_all:
                    fetch(k + 1, (k + 1) % 2).start()

        for z in range(shares):
            for j in range(parts):
                at = z * part + j * rows
                down_w[z * rows : (z + 1) * rows, j * ff : (j + 1) * ff] = held[
                    slot, at : at + rows, ff:
                ]
        hiddens, slopes = [], []
        for at in range(0, ff, step):
            up = nn(h2_ref[...], held[slot, :, at : at + step])
            cdf = 0.5 * (1.0 + lax.erf(up * (0.5**0.5)))
            slope = cdf + up * (jnp.exp(-0.5 * up * up) * 0.3989422804014327)
            hiddens.append((up * cdf).astype(BF16))
            slopes.append((nt(pull_ref[...], down_w[at : at + step, :]) * slope).astype(BF16))
        hidden = jnp.concatenate(hiddens, 1) if len(hiddens) > 1 else hiddens[0]
        grad_up = jnp.concatenate(slopes, 1) if len(slopes) > 1 else slopes[0]
        out_ref[...] += nn(hidden, down_w[...])
        grad_ref[...] += nt(grad_up, held[slot, :, :ff])
        grad_upper = nn(h2_t[...], grad_up).astype(BF16)
        grad_lower = tn(hidden, pull_ref[...]).astype(BF16)

        def put(refs):
            refs[0][0] = grad_upper
            for z in range(shares):
                for j in range(parts):
                    refs[1][z, 0, j * rows : (j + 1) * rows, :] = grad_lower[
                        z * rows : (z + 1) * rows, j * ff : (j + 1) * ff
                    ]

        @pl.when(t < n_other)
        def _():
            put(targets[0])

        @pl.when(t >= n_other)
        def _():
            put(targets[1])

    whole = pl.BlockSpec((tokens, model), lambda t: (0, 0))
    early = lambda t: jnp.minimum(t, n_other - 1)
    late = lambda t: jnp.maximum(t - n_other, 0)
    acc = jax.ShapeDtypeStruct((tokens, model), F32)
    out_specs, out_shape = [whole, whole], [acc, acc]
    for count, at in ((n_other, early), (n_mine, late)):
        out_specs += [
            pl.BlockSpec((1, model, ff), lambda t, at=at: (at(t), 0, 0)),
            pl.BlockSpec((shares, 1, part, ff), lambda t, at=at: (0, at(t), 0, 0)),
        ]
        out_shape += [
            jax.ShapeDtypeStruct((count, model, ff), BF16),
            jax.ShapeDtypeStruct((shares, count, part, ff), BF16),
        ]
    return pl.pallas_call(
        kernel,
        grid=(n_all,),
        in_specs=[whole] * (2 if first else 4) + [pl.BlockSpec(memory_space=pl.ANY)] * n_all,
        out_specs=out_specs,
        out_shape=out_shape,
        scratch_shapes=[
            pltpu.VMEM((model, tokens), BF16),
            pltpu.VMEM((2, model, 2 * ff), BF16),
            pltpu.VMEM((ff, model), BF16),
            pltpu.SemaphoreType.DMA((2,)),
        ],
        compiler_params=pltpu.CompilerParams(vmem_limit_bytes=56 * 1024 * 1024),
        cost_estimate=pl.CostEstimate(
            flops=12 * tokens * model * ff * n_all,
            bytes_accessed=8 * model * ff * n_all,
            transcendentals=0,
        ),
    )(h2, pull, *(() if first else sums), *chunks)


def outer_gradient(left, right, places, shares):
    tokens, model = left.shape
    owners = places.shape[0]
    part = model // shares
    rows, half = part // owners, model // 2
    per = shares // 2

    def kernel(at_ref, left_ref, right_ref, away_ref, mine_ref, held):
        for z in range(shares):
            held[...] = tn(left_ref[:, z * part : (z + 1) * part], right_ref[...])
            h, at = z // per, z % per * rows
            for k in range(owners):
                ref = mine_ref if k < owners // 2 else away_ref
                block = held[pl.ds(pl.multiple_of(at_ref[k] * rows, rows), rows), :].astype(BF16)
                for j in range(2):
                    lanes = slice(j * half, (j + 1) * half)
                    ref[k % (owners // 2), h, j * per * rows + at : j * per * rows + at + rows, :] = (
                        block[:, lanes]
                    )

    shape = (owners // 2, 2, 2 * per * rows, half)
    whole = lambda *dims: pl.BlockSpec(dims, lambda i, _: (0,) * len(dims))
    return pl.pallas_call(
        kernel,
        grid_spec=pltpu.PrefetchScalarGridSpec(
            num_scalar_prefetch=1,
            grid=(1,),
            in_specs=[whole(tokens, model)] * 2,
            out_specs=[whole(*shape)] * 2,
            scratch_shapes=[pltpu.VMEM((part, model), F32)],
        ),
        out_shape=[jax.ShapeDtypeStruct(shape, BF16)] * 2,
        compiler_params=pltpu.CompilerParams(vmem_limit_bytes=48 * 1024 * 1024),
        cost_estimate=pl.CostEstimate(
            flops=2 * tokens * model * model, bytes_accessed=4 * model * model, transcendentals=0
        ),
    )(places, left, right)


def absolute(owner):
    a, b, c = lax.axis_index("a"), lax.axis_index("b"), lax.axis_index("c")
    owner = owner ^ (c * 4 + a * 2 + b)
    return (owner % 4) * 2 + owner // 4


def project(pieces, places, owners, groups, rows, gain, bias, weight, before):
    model, columns = weight.shape
    mine, steps = groups * rows, groups
    count = len(pieces)
    stride = places[1] - places[0] if count == 2 else 1

    def place(t):
        k = t // steps
        if count == 2:
            at = places[0] + stride * k
        else:
            at = k
            for i in range(1, count):
                if places[i] - places[i - 1] > 1:
                    at = at + (k >= i) * (places[i] - places[i - 1] - 1)
        return t % steps * owners + at

    def kernel(*refs):
        piece_refs = refs[:count]
        gain_ref, bias_ref, weight_ref = refs[count : count + 3]
        norm_ref, out_ref, held = refs[-3:]
        t = pl.program_id(0)
        for k in range(count):

            @pl.when(t // steps == k)
            def _(k=k):
                held[...] = piece_refs[k][...]

        values = held[...].astype(F32)
        normed = layer_norm(values, gain_ref[...], bias_ref[...])[0].astype(BF16)
        norm_ref[...] = normed
        out_ref[...] = nn(normed, weight_ref[...]).astype(BF16)

    specs = [
        pl.BlockSpec((rows, model), lambda t, k=k: (jnp.clip(t - k * steps, 0, steps - 1), 0))
        for k in range(count)
    ]
    fixed = lambda shape: pl.BlockSpec(shape, lambda t: (0, 0))
    specs += [fixed((1, model)), fixed((1, model)), fixed((model, columns))]
    extra = () if before is None else before
    return pl.pallas_call(
        kernel,
        grid=(count * steps,),
        in_specs=specs + [pl.BlockSpec(memory_space=pl.ANY)] * len(extra),
        out_specs=[
            pl.BlockSpec((rows, model), lambda t: (place(t), 0)),
            pl.BlockSpec((rows, columns), lambda t: (place(t), 0)),
        ],
        out_shape=[
            jax.ShapeDtypeStruct((owners * mine, model), BF16),
            jax.ShapeDtypeStruct((owners * mine, columns), BF16),
        ],
        scratch_shapes=[pltpu.VMEM((rows, model), BF16)],
        input_output_aliases={count + 3 + i: i for i in range(len(extra))},
        compiler_params=pltpu.CompilerParams(vmem_limit_bytes=48 * 1024 * 1024),
        cost_estimate=pl.CostEstimate(
            flops=2 * count * mine * model * columns,
            bytes_accessed=2 * count * mine * (2 * model + columns),
            transcendentals=0,
        ),
    )(*pieces, gain[None], bias[None], weight, *extra)


def pack(parts, packed, shares):
    model = packed.shape[0]
    part, half = model // shares, model // 2
    low = part // 2
    outer = (parts[0][0].shape[0] - half) // 2
    per = shares // 2
    out_rows = outer // per
    rows = low + out_rows + low
    flat = [each for terms in parts for each in terms]

    def kernel(*refs):
        packed_ref, out_ref = refs[-2], refs[-1]
        it = iter(refs)
        groups = [[next(it) for _ in terms] for terms in parts]

        def total(refs, at, count):
            summed = refs[0][at : at + count, :].astype(F32)
            for ref in refs[1:]:
                summed = summed + ref[at : at + count, :].astype(F32)
            return summed.astype(BF16)

        for z in range(shares):
            terms, side = groups[z // per], z % per
            for j in range(2):
                lanes = slice(j * half, (j + 1) * half)
                out_ref[z, :low, lanes] = total(terms, side * part + j * low, low)
                out_ref[z, low : low + out_rows, lanes] = total(
                    terms, half + j * outer + side * out_rows, out_rows
                )
                at = z * part + j * low
                out_ref[z, low + out_rows :, lanes] = packed_ref[at : at + low, :]

    return pl.pallas_call(
        kernel,
        out_shape=jax.ShapeDtypeStruct((shares, rows, model), BF16),
        compiler_params=pltpu.CompilerParams(vmem_limit_bytes=48 * 1024 * 1024),
    )(*flat, packed)


def unpack_lower(pieces, places, shares):
    owners = len(pieces)
    part, ff = pieces[0].shape
    parts = part * shares // ff
    rows = part // parts

    def kernel(at_ref, *refs):
        for k in range(owners):
            refs[-1][at_ref[k]] = refs[k][...].astype(F32)

    result = pl.pallas_call(
        kernel,
        grid_spec=pltpu.PrefetchScalarGridSpec(
            num_scalar_prefetch=1,
            grid=(parts,),
            in_specs=[pl.BlockSpec((rows, ff), lambda i, _: (i, 0))] * owners,
            out_specs=pl.BlockSpec((owners, rows, ff), lambda i, _: (0, 0, i)),
        ),
        out_shape=jax.ShapeDtypeStruct((owners, rows, parts * ff), F32),
        compiler_params=pltpu.CompilerParams(vmem_limit_bytes=48 * 1024 * 1024),
    )(places, *pieces)
    return result.reshape(owners * rows, parts * ff)


def unpack(pieces, places, shares, part, width):
    owners = len(pieces)
    rows, model = pieces[0].shape
    half, low = model // 2, part // 2
    out_rows = part // owners
    steps = 4
    block = low // steps
    outer_block = 16

    def kernel(at_ref, *refs):
        mains, outers, projs = refs[:owners], refs[owners : 2 * owners], refs[2 * owners : 3 * owners]
        up_ref, outer_ref, proj_ref, vec_ref = refs[3 * owners :]
        for j in range(2):
            at = j * half + 3 * width
            vectors = [proj[:, at : at + 128].astype(F32) for proj in projs]
            vec_ref[j] = functools.reduce(jnp.add, vectors)
        for k in range(owners):
            d = at_ref[k]
            lane = lambda base: pl.ds(pl.multiple_of(base + d * width, width), width)
            outer_ref[d] = outers[k][...].astype(F32)
            for j in range(2):
                for z in range(shares):
                    at = j * half + z * width
                    up_ref[j, :, lane(z * owners * width)] = mains[k][:, at : at + width].astype(F32)
                for t in range(3):
                    at = j * half + t * width
                    proj_ref[j, :, lane(t * model)] = projs[k][:, at : at + width].astype(F32)

    outer_at, proj_at = low // outer_block, (low + out_rows) // block
    outer_steps = out_rows // outer_block
    results = pl.pallas_call(
        kernel,
        grid_spec=pltpu.PrefetchScalarGridSpec(
            num_scalar_prefetch=1,
            grid=(steps,),
            in_specs=[pl.BlockSpec((block, model), lambda i, _: (i, 0))] * owners
            + [
                pl.BlockSpec(
                    (outer_block, model), lambda i, _: (outer_at + i * outer_steps // steps, 0)
                )
            ]
            * owners
            + [pl.BlockSpec((block, model), lambda i, _: (proj_at + i, 0))] * owners,
            out_specs=[
                pl.BlockSpec((2, block, shares * model), lambda i, _: (0, i, 0)),
                pl.BlockSpec(
                    (owners, outer_block, model), lambda i, _: (0, i * outer_steps // steps, 0)
                ),
                pl.BlockSpec((2, block, 3 * model), lambda i, _: (0, i, 0)),
                pl.BlockSpec((2, block, 128), lambda i, _: (0, i, 0)),
            ],
        ),
        out_shape=[
            jax.ShapeDtypeStruct((2, low, shares * model), F32),
            jax.ShapeDtypeStruct((owners, out_rows, model), F32),
            jax.ShapeDtypeStruct((2, low, 3 * model), F32),
            jax.ShapeDtypeStruct((2, low, 128), F32),
        ],
        compiler_params=pltpu.CompilerParams(vmem_limit_bytes=56 * 1024 * 1024),
    )(places, *pieces, *pieces, *pieces)
    upper, outer, proj, vectors = results
    return (
        upper.reshape(part, shares * model),
        outer.reshape(part, model),
        proj.reshape(part, 3 * model),
        vectors.reshape(part, 128),
    )


def flip(value, axis):
    return lax.ppermute(value, axis, [(0, 1), (1, 0)])


def spread(value):
    if lax.axis_size("a") != 2:
        return list(lax.all_gather(value, CTX, axis=0, tiled=False))
    half = value.shape[0] // 2
    from_b, from_a = flip(value, "b"), flip(value, "a")
    far = jnp.concatenate([flip(from_a[:half], "b"), flip(from_b[half:], "a")], 0)
    near = [value, from_b, from_a, far]
    return near + [flip(each, "c") for each in near]


def add(u, v):
    return (u.astype(F32) + v.astype(F32)).astype(BF16)


def converge_first(from_b, from_a, far):
    far_0, far_1 = flip(far[0], "b"), flip(far[1], "a")
    b_0, a_1 = flip(from_b[0], "b"), flip(from_a[1], "a")
    return add(from_b[1], far_1), add(from_a[0], far_0), b_0, a_1


def converge_last(own, first):
    b_1, a_0, b_0, a_1 = first
    return (own[0], b_0, flip(a_0, "a")), (own[1], flip(b_1, "b"), a_1)


def total(terms):
    return sum(each.astype(F32) for each in terms[1:]) + terms[0].astype(F32)


def shards(
    tokens,
    out_grad,
    seg_ids,
    positions,
    ln1_gain,
    ln1_bias,
    w_qkv,
    w_out,
    ln2_gain,
    ln2_bias,
    w_up,
    w_down,
):
    groups, rows, model = tokens.shape
    owners, shares = lax.axis_size(CTX), lax.axis_size("z")
    square = lax.axis_size("a") == 2
    width = model // owners
    heads = HEADS // owners
    mine = groups * rows
    part = model // shares
    full_ff = w_up.shape[1]
    ff = full_ff // owners
    ff_rows = ff // shares
    ff_parts = model // ff
    me = lax.axis_index(CTX)
    core = lax.axis_index("c")

    first_seg, first_pos = seg_ids[:, ::UNIT], positions[:, ::UNIT]
    slot = jnp.where(
        first_seg == 0,
        first_pos // UNIT,
        PROMPT // UNIT + (first_seg - 1) * (CONT // UNIT) + first_pos // UNIT,
    )
    per_group = rows // UNIT
    note = jnp.zeros((32, model), BF16).at[0, : groups * per_group].set(
        slot.reshape(-1).astype(BF16)
    )
    pieces = spread(jnp.concatenate([tokens.reshape(mine, model), note], 0))
    slots = jnp.stack(
        [each[mine, : groups * per_group].reshape(groups, per_group) for each in pieces], 1
    )
    slots = slots.reshape(groups, owners * per_group).astype(jnp.int32)

    columns = [
        lax.dynamic_slice_in_dim(w_qkv, t * model + me * width, width, 1) for t in range(3)
    ]
    norms = jnp.stack([ln1_gain, ln1_bias, ln2_gain, ln2_bias], 1)
    packed = jnp.concatenate(columns + [norms, jnp.zeros((part, 124), BF16)], 1)
    packed = lax.all_gather(packed, "z", axis=0, tiled=True)
    up_part = [
        lax.dynamic_slice_in_dim(w_up, (z * owners + me) * ff_rows, ff_rows, 1)
        for z in range(shares)
    ]
    down_part = lax.dynamic_slice_in_dim(w_down, me * ff_rows, ff_rows, 0)
    down_part = jnp.concatenate([down_part[:, j * ff : (j + 1) * ff] for j in range(ff_parts)], 0)
    chunk = jnp.concatenate(up_part + [down_part], 1)
    chunk, packed, pieces[1], pieces[2] = lax.optimization_barrier(
        (chunk, packed, pieces[1], pieces[2])
    )
    chunk = lax.all_gather(chunk, "z", axis=0, tiled=True)

    units = owners * per_group
    order = jnp.arange(units, dtype=jnp.int32)
    source = jnp.sum(
        jnp.where(slots[:, None, :] == order[None, :, None], order[None, None, :], 0), -1
    ).reshape(-1)
    w_heads = packed[:, : 3 * width]
    vectors = packed[:, 3 * width : 3 * width + 4].astype(F32).T
    gain_one, bias_one, gain_two, bias_two = vectors[0], vectors[1], vectors[2], vectors[3]

    half = w_out.shape[0] // 2
    piece = lax.dynamic_slice_in_dim(w_out, core * half, half, 0)
    piece, pieces[3], pieces[7] = lax.optimization_barrier((piece, pieces[3], pieces[7]))
    whole_out = lax.all_gather(piece, ("z", "c"), axis=0, tiled=True)

    chunk, pieces[3], pieces[7] = lax.optimization_barrier((chunk, pieces[3], pieces[7]))
    chunks = spread(chunk)
    target = source
    if square:
        owner = source // per_group
        target = absolute(owner) * per_group + source - owner * per_group

    if square:
        early, late = [0, 1, 2, 4, 5, 6], [3, 7]
        calls = [early, late]
    else:
        calls = [list(range(owners))]
    projected = None
    for places in calls:
        projected = project(
            [pieces[k] for k in places],
            places,
            owners,
            groups,
            rows,
            gain_one,
            bias_one,
            w_heads,
            projected,
        )
    attn_in, qkv = projected
    chunk, qkv = lax.optimization_barrier((chunk, qkv))
    chunks = spread(chunk)
    qkv = qkv.reshape(groups, owners, rows, 3 * width)
    attended, attn_low = [], []
    for g in range(groups):
        attn_heads, *kept = forward_attention(heads, width, qkv, g, source, target)
        attended.append(kept)
        attn_low.append(
            lax.all_to_all(attn_heads, CTX, split_axis=0, concat_axis=2, tiled=True)[0]
        )
    attn_low = jnp.concatenate(attn_low, 0)

    stream = tokens.reshape(mine, model).astype(F32)
    residual = stream + nn(attn_low, whole_out)
    ffn_full, ffn_norm, ffn_rstd = layer_norm(residual, gain_two, bias_two)
    ffn_in = ffn_full.astype(BF16)
    grad_low = out_grad.reshape(mine, model)
    cotangent = grad_low.astype(F32)

    if square:
        calls = [([4], [0]), ([5, 6], [1, 2]), ([7], [3])]
    else:
        calls = [([i, i + 1], [i + 2, i + 3]) for i in range(0, owners, 4)]
    sums, chunk_grads = None, []
    for away, here in calls:
        out_sum, in_sum, *each = feed_forward(
            ffn_in, grad_low, sums, [chunks[k] for k in away], [chunks[k] for k in here], shares
        )
        sums = (out_sum, in_sum)
        chunk_grads.append(each)
    output = (residual + sums[0]).astype(BF16)
    grad_ffn_in = sums[1]
    grad_gain_two = jnp.sum(grad_ffn_in * ffn_norm, 0)
    grad_bias_two = jnp.sum(grad_ffn_in, 0)
    grad_resid = cotangent + norm_back(grad_ffn_in, ffn_norm, ffn_rstd, gain_two)
    grad_branch = grad_resid.astype(BF16)
    grad_attn = [
        nt(grad_branch[g * rows : (g + 1) * rows], whole_out).astype(BF16) for g in range(groups)
    ]
    out_rows = part // owners

    if square:
        places = absolute(jnp.arange(owners))
        lower = jnp.concatenate([add(low, flip(away, "c")) for _, away, _, low in chunk_grads], 1)
        lower = lax.psum_scatter(
            lower.reshape(shares * 4, part, ff), "z", scatter_dimension=0, tiled=True
        )
        outer_away, outer = outer_gradient(attn_low, grad_branch, places, shares)
        outer = add(outer, flip(outer_away, "c"))
        upper = [add(up, flip(away, "c")) for away, _, up, _ in chunk_grads]
        upper = [upper[0][0], upper[1][0], upper[1][1], upper[2][0]]
        halves = [
            [
                jnp.concatenate([upper[k][h * model // 2 : (h + 1) * model // 2], outer[k, h]], 0)
                for h in range(2)
            ]
            for k in range(4)
        ]
        halves[3][0], halves[3][1], *grad_attn = lax.optimization_barrier((*halves[3], *grad_attn))
        first = converge_first(*halves[1:])
    else:
        lower = jnp.concatenate([low for _, a, _, b in chunk_grads for low in (a, b)], 1)
        lower = lax.psum_scatter(lower, CTX, scatter_dimension=1, tiled=True)
        lower = lower.reshape(shares, part, ff)
        upper = jnp.concatenate([up for a, _, b, _ in chunk_grads for up in (a, b)], 0)
        upper = lax.psum_scatter(upper, CTX, scatter_dimension=0, tiled=True)
        upper = upper.reshape(shares, part, ff)
        outer = tn(attn_low, grad_branch).astype(BF16)
        outer = outer.reshape(shares, owners, out_rows, model).transpose(1, 0, 2, 3)
        outer = lax.psum_scatter(
            outer.reshape(model, model), CTX, scatter_dimension=0, tiled=True
        )
    grad_heads = [
        lax.all_to_all(each, CTX, split_axis=1, concat_axis=0, tiled=True).reshape(
            owners, rows, width
        )
        for each in grad_attn
    ]

    grad_qkv, near_in = [], []
    split = owners // 2 * rows
    for g in range(groups):
        slopes = backward_attention(
            heads, width, qkv, g, grad_heads[g], *attended[g], source, target
        ).reshape(owners * rows, 3 * width)
        grad_qkv.append(slopes)
        if square:
            away = nt(slopes[split:], w_heads).astype(BF16)
            kept = nt(slopes[:split], w_heads) + flip(away, "c").astype(F32)
            near_in.append(kept.astype(BF16).reshape(4, rows, model))
            if g == 0:
                *first, near_in[0], grad_heads[1] = lax.optimization_barrier(
                    (*first, near_in[0], grad_heads[1])
                )
        else:
            away = nt(slopes, w_heads).astype(BF16)
            near_in.append(lax.psum_scatter(away, CTX, scatter_dimension=0, tiled=True).astype(F32))
    if square:
        upper_terms = converge_last(halves[0], first)
        near_in[1], grad_qkv[0], grad_qkv[1] = lax.optimization_barrier((near_in[1], *grad_qkv))
        pairs = [(near_in[0][k], near_in[1][k]) for k in range(4)]
        terms = converge_last(pairs[0], converge_first(*pairs[1:]))
        near_in = [total(each) for each in terms]
    grad_attn_in = jnp.concatenate(near_in, 0)
    attn_in = attn_in.reshape(groups, owners * rows, model)
    grad_columns = sum(tn(attn_in[g], grad_qkv[g]) for g in range(groups))
    w_wide = w_heads.astype(F32)
    summed = sum(jnp.sum(each.astype(F32), 0) for each in grad_qkv)
    grad_bias_one = jnp.sum(w_wide * summed, 1)
    grad_gain_one = (jnp.sum(w_wide * grad_columns, 1) - bias_one * grad_bias_one) / gain_one
    vector_grads = jnp.stack([grad_gain_one, grad_bias_one, grad_gain_two, grad_bias_two], 1)
    packed_grad = jnp.concatenate(
        [grad_columns, vector_grads, jnp.zeros((model, 124), F32)], 1
    ).astype(BF16)

    if square:
        lower = lower[0].astype(F32) + sum(
            flip(lower[k], axis).astype(F32) for k, axis in ((1, "b"), (2, "a"))
        ) + lax.ppermute(lower[3], ("a", "b"), [(0, 3), (3, 0), (1, 2), (2, 1)]).astype(F32)
        grad_down = unpack_lower(spread(lower.astype(BF16)), places, shares)
        everything = pack(upper_terms, packed_grad, shares)
        everything = lax.psum_scatter(
            everything.reshape(-1, model), "z", scatter_dimension=0, tiled=True
        )
        everything, grad_attn_in, grad_down = lax.optimization_barrier(
            (everything, grad_attn_in, grad_down)
        )
        grad_upper, grad_outer, grad_proj, vector_grads = unpack(
            spread(everything), places, shares, part, width
        )
    else:
        span = 2 * ff
        per_part = packed_grad.shape[1] * part // span
        everything = jnp.concatenate(
            [
                jnp.concatenate([upper, lower], 2),
                outer.reshape(shares, -1, span),
                packed_grad.reshape(shares, per_part, span),
            ],
            1,
        )
        everything = lax.psum_scatter(
            everything.reshape(-1, span), "z", scatter_dimension=0, tiled=True
        )
        everything = lax.all_gather(everything, CTX, axis=0, tiled=False)
        grad_upper = (
            everything[:, :part, :ff]
            .reshape(owners, part, shares, ff_rows)
            .transpose(1, 2, 0, 3)
            .reshape(part, full_ff)
            .astype(F32)
        )
        grad_down = (
            everything[:, :part, ff:]
            .reshape(owners, ff_parts, ff_rows, ff)
            .transpose(0, 2, 1, 3)
            .reshape(owners * ff_rows, model)
            .astype(F32)
        )
        at = part + out_rows * model // span
        grad_outer = everything[:, part:at].reshape(part, model).astype(F32)
        packed_grad = everything[:, at:].reshape(owners, part, -1).astype(F32)
        grad_proj = (
            packed_grad[:, :, : 3 * width]
            .reshape(owners, part, 3, width)
            .transpose(1, 2, 0, 3)
            .reshape(part, 3 * model)
        )
        vector_grads = jnp.sum(packed_grad[:, :, 3 * width : 3 * width + 4], 0)

    attn_full, attn_norm, attn_rstd = layer_norm(stream, gain_one, bias_one)
    in_grad = (grad_resid + norm_back(grad_attn_in, attn_norm, attn_rstd, gain_one)).astype(BF16)

    return (
        output.reshape(tokens.shape),
        in_grad.reshape(tokens.shape),
        vector_grads[:, 0],
        vector_grads[:, 1],
        grad_proj,
        grad_outer,
        vector_grads[:, 2],
        vector_grads[:, 3],
        grad_upper,
        grad_down,
    )


def solution(mesh):
    ctx, wsh = mesh.shape["ctx"], mesh.shape["wsh"]
    fine = Mesh(mesh.devices.reshape(ctx // 4, 2, 2, wsh), ("a", "b", "c", "z"))
    toks = P("z", CTX, None)
    ints = P("z", CTX)
    vec, mat = P("z"), P("z", None)
    in_specs = (toks, toks, ints, ints, vec, vec, mat, mat, vec, vec, mat, mat)
    out_specs = (toks, toks, vec, vec, mat, mat, vec, vec, mat, mat)
    return jax.shard_map(shards, mesh=fine, in_specs=in_specs, out_specs=out_specs, check_vma=False)
```

time: 1690 us -> 520 us (0.31)
  waiting for transfers between devices: 1060 us -> 174 us
  matrix products: 373 us -> 22.1 us
  Pallas kernels: 0 us -> 134 us
  blocking collectives: 79.5 us -> 0 us
  other arithmetic: 100 us -> 38.6 us
  starting transfers between devices: 0.54 us -> 57.2 us
  local copies, waits for them, and re-layouts: 54.3 us -> 73.4 us
    all_gather x6 -> x3, waiting for transfers between devices: 510 us -> 1.21 us  [the longest x1 1.21 us: shards(): chunk = lax.all_gather(chunk, 'z', axis=0, tiled=True)]
    reduce_scatter x6 -> x2, waiting for transfers between devices: 466 us -> 0.01 us  [the longest x1 0.01 us: shards(): lax.psum_scatter(lower.reshape(shares * 4, part, ff), 'z', scatter_dimens...]
    dot_general x36 -> x9, matrix products: 373 us -> 22.1 us  [the longest x6 13.2 us: nt(): lax.dot_general(left, right, (((1,), (1,)), ((), ())), preferred_element_...]
    ppermute x0 -> x56, waiting for transfers between devices: none -> 141 us  [the longest x55 127 us: flip(): return lax.ppermute(value, axis, [(0, 1), (1, 0)])]
    pallas_call x0 -> x13, Pallas kernels: none -> 134 us  [the longest x3 52.6 us: feed_forward(): pl.pallas_call(kernel, grid=(n_all,), in_specs=[whole] * (2 if first else...]
    psum x1 -> x0, waiting for transfers between devices: 81.9 us -> none  [shards(): lax.psum(for_sending(tuple(summed_grads)), 'ctx')]
    all_gather x6 -> x0, blocking collectives: 55.7 us -> none  [the longest x1 12.6 us: shards(): lax.all_gather(ln1_gain, 'wsh', axis=0, tiled=True)]
    ppermute x0 -> x56, starting transfers between devices: none -> 41.8 us  [the longest x55 40.2 us: flip(): return lax.ppermute(value, axis, [(0, 1), (1, 0)])]
  transfers between devices with their start and end apart: 13 -> 65, of which waited for: 12 -> 27; matrix products, arithmetic and copies ran while one was open for 8% -> 20% of each run, Pallas kernels for 0% -> 25%
where the time goes in v1:
time: 520 us; the launch traced here: 514 us
  waiting for transfers between devices  174 us (33%)
  Pallas kernels  134 us (26%)
  local copies, waits for them, and re-layouts  73.4 us (14%)
  starting transfers between devices  57.2 us (11%)
  other arithmetic  38.6 us (7%)
  matrix products  22.1 us (4%)
  between operations  15.2 us (3%)
    ppermute x55, waiting for transfers between devices, flip(): return lax.ppermute(value, axis, [(0, 1), (1, 0)])  127 us
    pallas_call x3, Pallas kernels, feed_forward(): pl.pallas_call(kernel, grid=(n_all,), in_specs=[whole] * (2 if first else...  52.6 us
    ppermute x55, starting transfers between devices, flip(): return lax.ppermute(value, axis, [(0, 1), (1, 0)])  40.2 us
    all_to_all x2, waiting for transfers between devices, shards(): lax.all_to_all(attn_heads, CTX, split_axis=0, concat_axis=2, tiled=True)[0]  28.6 us
    pallas_call x2, Pallas kernels, backward_attention(): pl.pallas_call(kernel, grid_spec=pltpu.PrefetchScalarGridSpec(num_scalar_...  27.7 us
    unnamed x153, local copies, waits for them, and re-layouts  27.6 us
    pallas_call x2, Pallas kernels, forward_attention(): pl.pallas_call(kernel, grid_spec=pltpu.PrefetchScalarGridSpec(num_scalar_...  20.9 us
    pallas_call x2, Pallas kernels, project(): pl.pallas_call(kernel, grid=(count * steps,), in_specs=specs + [pl.BlockS...  17.2 us
  transfers between devices with their start and end apart: 65, of which 27 were waited for; matrix products, arithmetic and copies ran while one was open for 20% of the time, Pallas kernels for 25%

profile of v1, /device:TPU:0, one launch (start us, length us, event | category | flops | bytes accessed | tf_op | source)
XLA Modules:
  0.0 514.1 jit_solution(16657590732946567406)
XLA Ops:
  15.1 2.9 collective-permute-start
  24.0 18.9 %collective-permute-done.refs_1_ = bf16[544,1024]{1,0:T(8,128)(2,1)} collective-permute-done((bf16[544,1024]{1,0:T(8,128)(2,1)}, bf16[544,1024]{1,0:T(8,128)(2,1)}, u32[]{:S(2)}, u32[]{:S(2)}) %collective-permute-start) | collective-permute-done | bytes 1114144 | tf_op jit(solution)/shard_map/ppermute | solution.py:597
  45.9 1.7 collective-permute-start.2
  47.6 10.1 %collective-permute-done.6 = bf16[272,1024]{1,0:T(8,128)(2,1)S(1)} collective-permute-done((bf16[272,1024]{1,0:T(8,128)(2,1)S(1)}, bf16[272,1024]{1,0:T(8,128)(2,1)S(1)}, u32[]{:S(2)}, u32[]{:S(2)}) %collective-permute-start.6) | collective-permute-done | bytes 557088 | tf_op jit(solution)/shard_map/ppermute | solution.py:597
  57.8 2.1 collective-permute-done.2
  68.3 1.9 slice_reduce_fusion.10
  75.2 13.6 %shard_map.195 = (bf16[4096,1024]{1,0:T(8,128)(2,1)}, bf16[4096,384]{1,0:T(8,128)(2,1)}) custom-call(bf16[544,1024]{1,0:T(8,128)(2,1)} %fusion.20.refs_0_, bf16[544,1024]{1,0:T(8,128)(2,1)} %collective-permute-done.refs_1_, bf16[544,1024]{1,0:T(8,128)(2,1)S(1)} %copy-done.11, bf16[544,1024]{1,0:T(8,128)(2,1)} %collective-permute-done.3.refs_3_, ...), custom_call_target="tpu_custom_call" | custom-call | flops 2415919104 | bytes 14942208 | tf_op jit(solution)/shard_map/pallas_call | solution.py:441
  90.7 1.9 copy-done.2
  92.6 3.6 shard_map.196
  96.2 1.7 copy-done.3
  100.8 1.9 copy-done.4
  102.7 10.5 %shard_map.197 = (bf16[8,256,128]{2,1,0:T(8,128)(2,1)S(1)}, f32[128,2048]{1,0:T(8,128)S(1)}, f32[2,2048]{1,0:T(2,128)S(1)}) custom-call(s32[64]{0:T(128)S(1)} %reshape.256.src, s32[64]{0:T(128)S(1)} %multiply_subtract_fusion.dst, bf16[2,8,256,384]{3,2,1,0:T(8,128)(2,1)S(1)} %bitcast.141), custom_call_target="tpu_custom_call" | custom-call | flops 6442450944 | bytes 4194304 | tf_op jit(solution)/shard_map/pallas_call | solution.py:108
  114.9 4.3 all-to-all-start
  119.3 10.5 %shard_map.198 = (bf16[8,256,128]{2,1,0:T(8,128)(2,1)S(1)}, f32[128,2048]{1,0:T(8,128)S(1)}, f32[2,2048]{1,0:T(2,128)S(1)}) custom-call(s32[64]{0:T(128)S(1)} %reshape.256.src, s32[64]{0:T(128)S(1)} %multiply_subtract_fusion.dst, bf16[2,8,256,384]{3,2,1,0:T(8,128)(2,1)S(1)} %bitcast.142), custom_call_target="tpu_custom_call" | custom-call | flops 6442450944 | bytes 4194304 | tf_op jit(solution)/shard_map/pallas_call | solution.py:108
  131.5 20.9 %all-to-all-done = bf16[8,256,128]{2,1,0:T(8,128)(2,1)} async-done(((bf16[8,256,128]{2,1,0:T(8,128)(2,1)}), bf16[8,256,128]{2,1,0:T(8,128)(2,1)}, u32[]{:S(2)}, u32[]{:S(2)}) %all-to-all-start) | async-done | bytes 524320 | tf_op jit(solution)/shard_map/all_to_all | solution.py:739
  152.4 3.9 all-to-all-start.1
  158.2 7.8 %all-to-all-done.1 = bf16[8,256,128]{2,1,0:T(8,128)(2,1)S(1)} async-done(((bf16[8,256,128]{2,1,0:T(8,128)(2,1)}), bf16[8,256,128]{2,1,0:T(8,128)(2,1)S(1)}, u32[]{:S(2)}, u32[]{:S(2)}) %all-to-all-start.1) | async-done | bytes 524320 | tf_op jit(solution)/shard_map/all_to_all | solution.py:739
  166.5 2.3 slice.346
  169.3 2.3 slice.347
  172.6 3.2 fusion.42
  176.2 16.8 %collective-permute-done.13 = bf16[512,1024]{1,0:T(8,128)(2,1)} collective-permute-done((bf16[512,1024]{1,0:T(8,128)(2,1)}, bf16[512,1024]{1,0:T(8,128)(2,1)}, u32[]{:S(2)}, u32[]{:S(2)}) %collective-permute-start.13) | collective-permute-done | bytes 1048608 | tf_op jit(solution)/shard_map/ppermute | solution.py:597
  194.3 2.4 collective-permute-done.14
  198.1 1.6 add_convert_fusion.10.refs_0_
  199.7 14.0 %shard_map.199 = (f32[512,1024]{1,0:T(8,128)}, f32[512,1024]{1,0:T(8,128)}, bf16[1,1024,512]{2,1,0:T(8,128)(2,1)}, bf16[4,1,256,512]{3,2,1,0:T(8,128)(2,1)}, bf1...) custom-call(bf16[512,1024]{1,0:T(8,128)(2,1)} %add_convert_fusion.10.refs_0_, bf16[512,1024]{1,0:T(8,128)(2,1)} %bitcast.164, ...), custom_call_target="tpu_custom_call" | custom-call | flops 6442450944 | bytes 8388608 | tf_op jit(solution)/shard_map/pallas_call | solution.py:335
  214.1 23.0 %shard_map.200 = (f32[512,1024]{1,0:T(8,128)}, f32[512,1024]{1,0:T(8,128)}, bf16[2,1024,512]{2,1,0:T(8,128)(2,1)}, bf16[4,2,256,512]{3,2,1,0:T(8,128)(2,1)}, bf1...) custom-call(bf16[512,1024]{1,0:T(8,128)(2,1)} %add_convert_fusion.10.refs_0_, bf16[512,1024]{1,0:T(8,128)(2,1)} %bitcast.165, ...), custom_call_target="tpu_custom_call" | custom-call | flops 12884901888 | bytes 16777216 | tf_op jit(solution)/shard_map/pallas_call | solution.py:335
  237.1 15.6 %shard_map.201 = (f32[512,1024]{1,0:T(8,128)}, f32[512,1024]{1,0:T(8,128)}, bf16[1,1024,512]{2,1,0:T(8,128)(2,1)}, bf16[4,1,256,512]{3,2,1,0:T(8,128)(2,1)}, bf1...) custom-call(bf16[512,1024]{1,0:T(8,128)(2,1)} %add_convert_fusion.10.refs_0_, bf16[512,1024]{1,0:T(8,128)(2,1)} %bitcast.166, ...), custom_call_target="tpu_custom_call" | custom-call | flops 6442450944 | bytes 8388608 | tf_op jit(solution)/shard_map/pallas_call | solution.py:335
  252.7 3.2 multiply_reduce_fusion
  255.9 2.5 fusion.38
  258.5 1.9 shard_map.202
  263.1 1.6 convolution_convert_fusion.2
  269.6 3.5 all-to-all-start.2
  273.2 1.7 add_convert_fusion.4
  275.1 2.2 add_convert_fusion
  277.2 2.7 pad_maximum_fusion
  279.9 2.8 all-to-all-done.2
  282.8 13.7 %shard_map.203 = bf16[8,256,384]{2,1,0:T(8,128)(2,1)S(1)} custom-call(s32[64]{0:T(128)S(1)} %reshape.256.src, s32[64]{0:T(128)S(1)} %multiply_subtract_fusion.dst, bf16[2,8,256,384]{3,2,1,0:T(8,128)(2,1)} %bitcast.139, bf16[8,256,128]{2,1,0:T(8,128)(2,1)S(1)} %bitcast.144, f32[128,2048]{1,0:T(8,128)S(1)} %copy-done.16, f32[2,2048]{1,0:T(2,128)S(1)} %get-tuple-element.119.log_ref), custom_call_target="tpu_custom_call" | custom-call | flops 8589934592 | bytes 4194304 | tf_op jit(solution)/shard_map/pallas_call | solution.py:213
  298.0 2.8 convolution_convert_fusion.1
  305.0 3.5 all-to-all-start.3
  308.6 2.8 add_convert_fusion.3
  312.5 1.9 collective-permute-start.22
  316.7 1.9 collective-permute-done.20
  318.7 2.1 add_convert_fusion.12
  320.8 2.1 add_convert_fusion.11
  322.9 4.2 add_convert_fusion.2
  327.1 11.0 %collective-permute-done.22.refs_1_ = bf16[640,512]{1,0:T(8,128)(2,1)S(1)} collective-permute-done((bf16[640,512]{1,0:T(8,128)(2,1)}, bf16[640,512]{1,0:T(8,128)(2,1)S(1)}, u32[]{:S(2)}, u32[]{:S(2)}) %collective-permute-start.22) | collective-permute-done | bytes 655392 | tf_op jit(solution)/shard_map/ppermute | solution.py:597
  339.6 14.0 %shard_map.204 = bf16[8,256,384]{2,1,0:T(8,128)(2,1)S(1)} custom-call(s32[64]{0:T(128)S(1)} %reshape.256.src, s32[64]{0:T(128)S(1)} %multiply_subtract_fusion.dst, bf16[2,8,256,384]{3,2,1,0:T(8,128)(2,1)} %bitcast.140, bf16[8,256,128]{2,1,0:T(8,128)(2,1)S(1)} %bitcast.143, f32[128,2048]{1,0:T(8,128)S(1)} %copy-done.14, f32[2,2048]{1,0:T(2,128)S(1)} %copy-done.18), custom_call_target="tpu_custom_call" | custom-call | flops 8589934592 | bytes 4194304 | tf_op jit(solution)/shard_map/pallas_call | solution.py:213
  356.7 5.1 %collective-permute-done.16 = bf16[1,1024,512]{2,1,0:T(8,128)(2,1)S(1)} collective-permute-done((bf16[1,1024,512]{2,1,0:T(8,128)(2,1)S(1)}, bf16[1,1024,512]{2,1,0:T(8,128)(2,1)S(1)}, u32[]{:S(2)}, u32[]{:S(2)}) %collective-permute-start.16) | collective-permute-done | bytes 1048608 | tf_op jit(solution)/shard_map/ppermute | solution.py:597
  366.5 2.7 add_convert_fusion.1
  369.8 2.4 fusion
  372.2 3.4 fusion.16
  378.8 2.8 concatenate.78.refs_6_
  383.9 3.2 shard_map.205
  387.1 1.6 copy-done.32
  397.2 7.1 %collective-permute-done.29 = bf16[256,1024]{1,0:T(8,128)(2,1)S(1)} collective-permute-done((bf16[256,1024]{1,0:T(8,128)(2,1)S(1)}, bf16[256,1024]{1,0:T(8,128)(2,1)S(1)}, u32[]{:S(2)}, u32[]{:S(2)}) %collective-permute-start.29) | collective-permute-done | bytes 524320 | tf_op jit(solution)/shard_map/ppermute | solution.py:597
  406.9 14.3 %collective-permute-done.39 = bf16[256,512]{1,0:T(8,128)(2,1)S(1)} collective-permute-done((bf16[256,512]{1,0:T(8,128)(2,1)S(1)}, bf16[256,512]{1,0:T(8,128)(2,1)S(1)}, u32[]{:S(2)}, u32[]{:S(2)}) %collective-permute-start.39) | collective-permute-done | bytes 262176 | tf_op jit(solution)/shard_map/ppermute | solution.py:849
  429.0 19.8 %collective-permute-done.41.refs_2_ = bf16[256,512]{1,0:T(8,128)(2,1)S(1)} collective-permute-done((bf16[256,512]{1,0:T(8,128)(2,1)S(1)}, bf16[256,512]{1,0:T(8,128)(2,1)S(1)}, u32[]{:S(2)}, u32[]{:S(2)}) %collective-permute-start.41) | collective-permute-done | bytes 262176 | tf_op jit(solution)/shard_map/ppermute | solution.py:597
  453.9 7.5 %collective-permute-done.42 = bf16[128,512]{1,0:T(8,128)(2,1)S(1)} collective-permute-done((bf16[128,512]{1,0:T(8,128)(2,1)S(1)}, bf16[128,512]{1,0:T(8,128)(2,1)S(1)}, u32[]{:S(2)}, u32[]{:S(2)}) %collective-permute-start.42) | collective-permute-done | bytes 131104 | tf_op jit(solution)/shard_map/ppermute | solution.py:597
  463.7 2.7 shard_map.206
  469.4 12.6 %collective-permute-done.49.refs_2_.refs_10_.refs_18_ = bf16[288,1024]{1,0:T(8,128)(2,1)S(1)} collective-permute-done((bf16[288,1024]{1,0:T(8,128)(2,1)}, bf16[288,1024]{1,0:T(8,128)(2,1)S(1)}, u32[]{:S(2)}, u32[]{:S(2)}) %collective-permute-start.49) | collective-permute-done | bytes 589856 | tf_op jit(solution)/shard_map/ppermute | solution.py:597
  484.0 1.6 collective-permute-start.51
  486.1 4.4 collective-permute-done.50
  490.5 1.6 collective-permute-done.51
  492.2 1.8 fusion.12
  496.0 7.4 %shard_map.207 = (f32[2,128,4096]{2,1,0:T(8,128)}, f32[8,32,1024]{2,1,0:T(8,128)}, f32[2,128,3072]{2,1,0:T(8,128)}, f32[2,128,128]{2,1,0:T(8,128)}) custom-call(s32[8]{0:T(128)} %copy-done.12, bf16[288,1024]{1,0:T(8,128)(2,1)} %reduce-scatter.3.cloned.1.call-done.refs_0_.refs_8_.refs_16_, bf16[288,1024]{1,0:T(8,128)(2,1)} %copy-done.25, ...), custom_call_target="tpu_custom_call" | custom-call | tf_op jit(solution)/shard_map/pallas_call | solution.py:557
  (369 shorter events, 116.0 us)
Async XLA Ops:
  7.2 37.0 %all-gather.4.cloned.1.call-start = ((), (), s32[]{:S(2)}) async-start(), calls=%async_computation.6 | async-start | bytes 1310720 | tf_op jit(solution)/shard_map/all_gather | solution.py:678
  12.3 78.4 %all-gather.6.cloned.1.call-start = ((), (), s32[]{:S(2)}) async-start(), calls=%async_computation.7 | async-start | bytes 2621440 | tf_op jit(solution)/shard_map/all_gather | solution.py:689
  15.1 27.8 %collective-permute-start = (bf16[544,1024]{1,0:T(8,128)(2,1)}, bf16[544,1024]{1,0:T(8,128)(2,1)}, u32[]{:S(2)}, u32[]{:S(2)}) collective-permute-start(bf16[544,1024]{1,0:T(8,128)(2,1)} %fusion.20.refs_0_), channel_id=1, source_target_pairs={{0,8},{8,0},{1,9},{9,1},{2,10},{10,2},{3,11},{11,3},{4,12},{12,4},... | collective-permute-start | bytes 3342344 | tf_op jit(solution)/shard_map/ppermute | solution.py:597
  18.0 26.2 %collective-permute-start.1 = (bf16[544,1024]{1,0:T(8,128)(2,1)}, bf16[544,1024]{1,0:T(8,128)(2,1)S(1)}, u32[]{:S(2)}, u32[]{:S(2)}) collective-permute-start(bf16[544,1024]{1,0:T(8,128)(2,1)} %fusion.20.refs_0_), channel_id=1, source_target_pairs={{0,16},{16,0},{1,17},{17,1},{2,18},{18,2},{3,19},{19,3},{4,20},{20... | collective-permute-start | bytes 3342344 | tf_op jit(solution)/shard_map/ppermute | solution.py:597
  44.3 128.3 %all-gather.8.cloned.1.call-start = ((), (), s32[]{:S(2)}) async-start(), calls=%async_computation.8 | async-start | bytes 2359296 | tf_op jit(solution)/shard_map/all_gather | solution.py:703
  44.4 13.3 %collective-permute-start.6 = (bf16[272,1024]{1,0:T(8,128)(2,1)S(1)}, bf16[272,1024]{1,0:T(8,128)(2,1)S(1)}, u32[]{:S(2)}, u32[]{:S(2)}) collective-permute-start(bf16[272,1024]{1,0:T(8,128)(2,1)S(1)} %slice.340), channel_id=1, source_target_pairs={{0,8},{8,0},{1,9},{9,1},{2,10},{10,2},{3,11},{11,3},{4,12},{12,4},... | collective-permute-start | bytes 1671176 | tf_op jit(solution)/shard_map/ppermute | solution.py:597
  45.9 13.9 %collective-permute-start.2 = (bf16[272,1024]{1,0:T(8,128)(2,1)S(1)}, bf16[272,1024]{1,0:T(8,128)(2,1)S(1)}, u32[]{:S(2)}, u32[]{:S(2)}) collective-permute-start(bf16[272,1024]{1,0:T(8,128)(2,1)S(1)} %slice.335), channel_id=1, source_target_pairs={{0,16},{16,0},{1,17},{17,1},{2,18},{18,2},{3,19},{19,3},{4,20},{20... | collective-permute-start | bytes 1671176 | tf_op jit(solution)/shard_map/ppermute | solution.py:597
  47.6 17.1 %collective-permute-start.3 = (bf16[544,1024]{1,0:T(8,128)(2,1)}, bf16[544,1024]{1,0:T(8,128)(2,1)}, u32[]{:S(2)}, u32[]{:S(2)}) collective-permute-start(bf16[544,1024]{1,0:T(8,128)(2,1)} %fusion.20.refs_0_), channel_id=1, source_target_pairs={{0,4},{4,0},{1,5},{5,1},{2,6},{6,2},{3,7},{7,3},{8,12},{12,8},{9,1... | collective-permute-start | bytes 3342344 | tf_op jit(solution)/shard_map/ppermute | solution.py:597
  60.6 6.6 %collective-permute-start.7 = (bf16[544,1024]{1,0:T(8,128)(2,1)S(1)}, bf16[544,1024]{1,0:T(8,128)(2,1)S(1)}, u32[]{:S(2)}, u32[]{:S(2)}) collective-permute-start(bf16[544,1024]{1,0:T(8,128)(2,1)S(1)} %constant_dynamic-update-slice_fusion.refs_0_), channel_id=1, source_target_pairs={{0,4},{4,0},{1,5},{5,1},{2,6},{6,2},{3,7},{7,3},{8,12},{12,8},{9,1... | collective-permute-start | bytes 3342344 | tf_op jit(solution)/shard_map/ppermute | solution.py:597
  60.6 11.8 %collective-permute-start.4 = (bf16[544,1024]{1,0:T(8,128)(2,1)}, bf16[544,1024]{1,0:T(8,128)(2,1)}, u32[]{:S(2)}, u32[]{:S(2)}) collective-permute-start(bf16[544,1024]{1,0:T(8,128)(2,1)} %collective-permute-done.refs_1_), channel_id=1, source_target_pairs={{0,4},{4,0},{1,5},{5,1},{2,6},{6,2},{3,7},{7,3},{8,12},{12,8},{9,1... | collective-permute-start | bytes 3342344 | tf_op jit(solution)/shard_map/ppermute | solution.py:597
  61.2 12.1 %collective-permute-start.5 = (bf16[544,1024]{1,0:T(8,128)(2,1)}, bf16[544,1024]{1,0:T(8,128)(2,1)}, u32[]{:S(2)}, u32[]{:S(2)}) collective-permute-start(bf16[544,1024]{1,0:T(8,128)(2,1)} %copy-done.10), channel_id=1, source_target_pairs={{0,4},{4,0},{1,5},{5,1},{2,6},{6,2},{3,7},{7,3},{8,12},{12,8},{9,1... | collective-permute-start | bytes 3342344 | tf_op jit(solution)/shard_map/ppermute | solution.py:597
  97.9 71.4 %collective-permute-start.9 = (bf16[1024,1024]{1,0:T(8,128)(2,1)}, bf16[1024,1024]{1,0:T(8,128)(2,1)}, u32[]{:S(2)}, u32[]{:S(2)}) collective-permute-start(bf16[1024,1024]{1,0:T(8,128)(2,1)} %all-gather.6.cloned.1.call-done.refs_3_), channel_id=1, source_target_pairs={{0,8},{8,0},{1,9},{9,1},{2,10},{10,2},{3,11},{11,3},{4,12},{12,4},... | collective-permute-start | bytes 6291464 | tf_op jit(solution)/shard_map/ppermute | solution.py:597
  99.3 67.1 %collective-permute-start.11 = (bf16[1024,1024]{1,0:T(8,128)(2,1)}, bf16[1024,1024]{1,0:T(8,128)(2,1)}, u32[]{:S(2)}, u32[]{:S(2)}) collective-permute-start(bf16[1024,1024]{1,0:T(8,128)(2,1)} %all-gather.6.cloned.1.call-done.refs_3_), channel_id=1, source_target_pairs={{0,16},{16,0},{1,17},{17,1},{2,18},{18,2},{3,19},{19,3},{4,20},{20... | collective-permute-start | bytes 6291464 | tf_op jit(solution)/shard_map/ppermute | solution.py:597
  114.9 37.5 %all-to-all-start = ((bf16[8,256,128]{2,1,0:T(8,128)(2,1)}), bf16[8,256,128]{2,1,0:T(8,128)(2,1)}, u32[]{:S(2)}, u32[]{:S(2)}) async-start(bf16[8,256,128]{2,1,0:T(8,128)(2,1)} %copy-done.9), calls=%async_computation | async-start | bytes 1048576 | tf_op jit(solution)/shard_map/all_to_all | solution.py:739
  152.4 13.6 %all-to-all-start.1 = ((bf16[8,256,128]{2,1,0:T(8,128)(2,1)}), bf16[8,256,128]{2,1,0:T(8,128)(2,1)S(1)}, u32[]{:S(2)}, u32[]{:S(2)}) async-start(bf16[8,256,128]{2,1,0:T(8,128)(2,1)} %copy-done.8), calls=%async_computation.1 | async-start | bytes 1048576 | tf_op jit(solution)/shard_map/all_to_all | solution.py:739
  156.3 43.4 %collective-permute-start.8 = (bf16[1024,1024]{1,0:T(8,128)(2,1)}, bf16[1024,1024]{1,0:T(8,128)(2,1)}, u32[]{:S(2)}, u32[]{:S(2)}) collective-permute-start(bf16[1024,1024]{1,0:T(8,128)(2,1)} %all-gather.6.cloned.1.call-done.refs_3_), channel_id=1, source_target_pairs={{0,4},{4,0},{1,5},{5,1},{2,6},{6,2},{3,7},{7,3},{8,12},{12,8},{9,1... | collective-permute-start | bytes 6291464 | tf_op jit(solution)/shard_map/ppermute | solution.py:597
  168.7 24.2 %collective-permute-start.13 = (bf16[512,1024]{1,0:T(8,128)(2,1)}, bf16[512,1024]{1,0:T(8,128)(2,1)}, u32[]{:S(2)}, u32[]{:S(2)}) collective-permute-start(bf16[512,1024]{1,0:T(8,128)(2,1)} %slice.346), channel_id=1, source_target_pairs={{0,8},{8,0},{1,9},{9,1},{2,10},{10,2},{3,11},{11,3},{4,12},{12,4},... | collective-permute-start | bytes 3145736 | tf_op jit(solution)/shard_map/ppermute | solution.py:597
  171.5 25.2 %collective-permute-start.14 = (bf16[512,1024]{1,0:T(8,128)(2,1)}, bf16[512,1024]{1,0:T(8,128)(2,1)}, u32[]{:S(2)}, u32[]{:S(2)}) collective-permute-start(bf16[512,1024]{1,0:T(8,128)(2,1)} %slice.347), channel_id=1, source_target_pairs={{0,16},{16,0},{1,17},{17,1},{2,18},{18,2},{3,19},{19,3},{4,20},{20... | collective-permute-start | bytes 3145736 | tf_op jit(solution)/shard_map/ppermute | solution.py:597
  172.1 42.0 %collective-permute-start.10 = (bf16[1024,1024]{1,0:T(8,128)(2,1)}, bf16[1024,1024]{1,0:T(8,128)(2,1)}, u32[]{:S(2)}, u32[]{:S(2)}) collective-permute-start(bf16[1024,1024]{1,0:T(8,128)(2,1)} %collective-permute-done.9.refs_6_), channel_id=1, source_target_pairs={{0,4},{4,0},{1,5},{5,1},{2,6},{6,2},{3,7},{7,3},{8,12},{12,8},{9,1... | collective-permute-start | bytes 6291464 | tf_op jit(solution)/shard_map/ppermute | solution.py:597
  172.1 42.0 %collective-permute-start.12 = (bf16[1024,1024]{1,0:T(8,128)(2,1)}, bf16[1024,1024]{1,0:T(8,128)(2,1)}, u32[]{:S(2)}, u32[]{:S(2)}) collective-permute-start(bf16[1024,1024]{1,0:T(8,128)(2,1)} %collective-permute-done.11.refs_7_), channel_id=1, source_target_pairs={{0,4},{4,0},{1,5},{5,1},{2,6},{6,2},{3,7},{7,3},{8,12},{12,8},{9,1... | collective-permute-start | bytes 6291464 | tf_op jit(solution)/shard_map/ppermute | solution.py:597
  198.0 39.0 %collective-permute-start.15 = (bf16[1024,1024]{1,0:T(8,128)(2,1)S(1)}, bf16[1024,1024]{1,0:T(8,128)(2,1)}, u32[]{:S(2)}, u32[]{:S(2)}) collective-permute-start(bf16[1024,1024]{1,0:T(8,128)(2,1)S(1)} %constant_dynamic-update-slice_fusion.2.refs_5_), channel_id=1, source_target_pairs={{0,4},{4,0},{1,5},{5,1},{2,6},{6,2},{3,7},{7,3},{8,12},{12,8},{9,1... | collective-permute-start | bytes 6291464 | tf_op jit(solution)/shard_map/ppermute | solution.py:597
  213.7 47.0 %collective-permute-start.34 = (bf16[4,1,256,512]{3,2,1,0:T(8,128)(2,1)}, bf16[4,1,256,512]{3,2,1,0:T(8,128)(2,1)S(1)}, u32[]{:S(2)}, u32[]{:S(2)}) collective-permute-start(bf16[4,1,256,512]{3,2,1,0:T(8,128)(2,1)} %get-tuple-element.134), channel_id=1, source_target_pairs={{0,4},{4,0},{1,5},{5,1},{2,6},{6,2},{3,7},{7,3},{8,12},{12,8},{9,1... | collective-permute-start | bytes 3145736 | tf_op jit(solution)/shard_map/ppermute | solution.py:597
  260.4 4.2 collective-permute-start.17
  261.0 47.5 %collective-permute-start.18 = (bf16[2,1024,512]{2,1,0:T(8,128)(2,1)}, bf16[2,1024,512]{2,1,0:T(8,128)(2,1)}, u32[]{:S(2)}, u32[]{:S(2)}) collective-permute-start(bf16[2,1024,512]{2,1,0:T(8,128)(2,1)} %get-tuple-element.112), channel_id=1, source_target_pairs={{0,4},{4,0},{1,5},{5,1},{2,6},{6,2},{3,7},{7,3},{8,12},{12,8},{9,1... | collective-permute-start | bytes 6291464 | tf_op jit(solution)/shard_map/ppermute | solution.py:597
  261.4 13.5 %collective-permute-start.35 = (bf16[4,2,256,512]{3,2,1,0:T(8,128)(2,1)}, bf16[4,2,256,512]{3,2,1,0:T(8,128)(2,1)}, u32[]{:S(2)}, u32[]{:S(2)}) collective-permute-start(bf16[4,2,256,512]{3,2,1,0:T(8,128)(2,1)} %get-tuple-element.136), channel_id=1, source_target_pairs={{0,4},{4,0},{1,5},{5,1},{2,6},{6,2},{3,7},{7,3},{8,12},{12,8},{9,1... | collective-permute-start | bytes 6291464 | tf_op jit(solution)/shard_map/ppermute | solution.py:597
  261.6 4.5 collective-permute-start.19
  261.9 11.3 %collective-permute-start.36 = (bf16[4,1,256,512]{3,2,1,0:T(8,128)(2,1)}, bf16[4,1,256,512]{3,2,1,0:T(8,128)(2,1)}, u32[]{:S(2)}, u32[]{:S(2)}) collective-permute-start(bf16[4,1,256,512]{3,2,1,0:T(8,128)(2,1)} %get-tuple-element.138), channel_id=1, source_target_pairs={{0,4},{4,0},{1,5},{5,1},{2,6},{6,2},{3,7},{7,3},{8,12},{12,8},{9,1... | collective-permute-start | bytes 3145736 | tf_op jit(solution)/shard_map/ppermute | solution.py:597
  269.6 13.2 %all-to-all-start.2 = ((bf16[256,8,128]{2,0,1:T(8,128)(2,1)}), bf16[256,8,128]{2,0,1:T(8,128)(2,1)S(1)}, u32[]{:S(2)}, u32[]{:S(2)}) async-start(bf16[256,8,128]{2,0,1:T(8,128)(2,1)} %copy.139), calls=%async_computation.2 | async-start | bytes 1048576 | tf_op jit(solution)/shard_map/all_to_all | solution.py:804
  273.1 120.0 %reduce-scatter.5.cloned.1.call-start = ((), (), s32[]{:S(2)}) async-start(), calls=%async_computation.10 | async-start | bytes 5242880 | tf_op jit(solution)/shard_map/reduce_scatter | solution.py:775
  300.8 22.1 %collective-permute-start.24 = (bf16[1024,1024]{1,0:T(8,128)(2,1)}, bf16[1024,1024]{1,0:T(8,128)(2,1)}, u32[]{:S(2)}, u32[]{:S(2)}) collective-permute-start(bf16[1024,1024]{1,0:T(8,128)(2,1)} %convolution_convert_fusion.1), channel_id=1, source_target_pairs={{0,4},{4,0},{1,5},{5,1},{2,6},{6,2},{3,7},{7,3},{8,12},{12,8},{9,1... | collective-permute-start | bytes 6291464 | tf_op jit(solution)/shard_map/ppermute | solution.py:597
  300.8 17.8 %collective-permute-start.20 = (bf16[640,512]{1,0:T(8,128)(2,1)}, bf16[640,512]{1,0:T(8,128)(2,1)}, u32[]{:S(2)}, u32[]{:S(2)}) collective-permute-start(bf16[640,512]{1,0:T(8,128)(2,1)} %pad_maximum_fusion.4), channel_id=1, source_target_pairs={{0,16},{16,0},{1,17},{17,1},{2,18},{18,2},{3,19},{19,3},{4,20},{20... | collective-permute-start | bytes 1966088 | tf_op jit(solution)/shard_map/ppermute | solution.py:597
  301.4 19.4 %collective-permute-start.21 = (bf16[640,512]{1,0:T(8,128)(2,1)}, bf16[640,512]{1,0:T(8,128)(2,1)}, u32[]{:S(2)}, u32[]{:S(2)}) collective-permute-start(bf16[640,512]{1,0:T(8,128)(2,1)} %pad_maximum_fusion.3), channel_id=1, source_target_pairs={{0,8},{8,0},{1,9},{9,1},{2,10},{10,2},{3,11},{11,3},{4,12},{12,4},... | collective-permute-start | bytes 1966088 | tf_op jit(solution)/shard_map/ppermute | solution.py:597
  305.0 22.1 %all-to-all-start.3 = ((bf16[256,8,128]{2,0,1:T(8,128)(2,1)}), bf16[256,8,128]{2,0,1:T(8,128)(2,1)S(1)}, u32[]{:S(2)}, u32[]{:S(2)}) async-start(bf16[256,8,128]{2,0,1:T(8,128)(2,1)} %copy.141), calls=%async_computation.3 | async-start | bytes 1048576 | tf_op jit(solution)/shard_map/all_to_all | solution.py:804
  308.5 157.9 %reduce-scatter.3.cloned.1.call-start = ((), (), s32[]{:S(2)}) async-start(), calls=%async_computation.9 | async-start | bytes 2949120 | tf_op jit(solution)/shard_map/reduce_scatter | solution.py:852
  312.5 25.7 %collective-permute-start.22 = (bf16[640,512]{1,0:T(8,128)(2,1)}, bf16[640,512]{1,0:T(8,128)(2,1)S(1)}, u32[]{:S(2)}, u32[]{:S(2)}) collective-permute-start(bf16[640,512]{1,0:T(8,128)(2,1)} %pad_maximum_fusion.5), channel_id=1, source_target_pairs={{0,8},{8,0},{1,9},{9,1},{2,10},{10,2},{3,11},{11,3},{4,12},{12,4},... | collective-permute-start | bytes 1966088 | tf_op jit(solution)/shard_map/ppermute | solution.py:597
  315.2 22.9 %collective-permute-start.23 = (bf16[640,512]{1,0:T(8,128)(2,1)}, bf16[640,512]{1,0:T(8,128)(2,1)S(1)}, u32[]{:S(2)}, u32[]{:S(2)}) collective-permute-start(bf16[640,512]{1,0:T(8,128)(2,1)} %pad_maximum_fusion.6), channel_id=1, source_target_pairs={{0,16},{16,0},{1,17},{17,1},{2,18},{18,2},{3,19},{19,3},{4,20},{20... | collective-permute-start | bytes 1966088 | tf_op jit(solution)/shard_map/ppermute | solution.py:597
  356.1 10.4 %collective-permute-start.27 = (bf16[1024,1024]{1,0:T(8,128)(2,1)S(1)}, bf16[1024,1024]{1,0:T(8,128)(2,1)S(1)}, u32[]{:S(2)}, u32[]{:S(2)}) collective-permute-start(bf16[1024,1024]{1,0:T(8,128)(2,1)S(1)} %convolution_convert_fusion), channel_id=1, source_target_pairs={{0,4},{4,0},{1,5},{5,1},{2,6},{6,2},{3,7},{7,3},{8,12},{12,8},{9,1... | collective-permute-start | bytes 6291464 | tf_op jit(solution)/shard_map/ppermute | solution.py:597
  356.2 5.6 %collective-permute-start.16 = (bf16[1,1024,512]{2,1,0:T(8,128)(2,1)S(1)}, bf16[1,1024,512]{2,1,0:T(8,128)(2,1)S(1)}, u32[]{:S(2)}, u32[]{:S(2)}) collective-permute-start(bf16[1,1024,512]{2,1,0:T(8,128)(2,1)S(1)} %copy-done.65), channel_id=1, source_target_pairs={{0,4},{4,0},{1,5},{5,1},{2,6},{6,2},{3,7},{7,3},{8,12},{12,8},{9,1... | collective-permute-start | bytes 3145736 | tf_op jit(solution)/shard_map/ppermute | solution.py:597
  364.4 17.2 %collective-permute-start.25 = (bf16[640,512]{1,0:T(8,128)(2,1)}, bf16[640,512]{1,0:T(8,128)(2,1)}, u32[]{:S(2)}, u32[]{:S(2)}) collective-permute-start(bf16[640,512]{1,0:T(8,128)(2,1)} %add_convert_fusion.11), channel_id=1, source_target_pairs={{0,16},{16,0},{1,17},{17,1},{2,18},{18,2},{3,19},{19,3},{4,20},{20... | collective-permute-start | bytes 1966088 | tf_op jit(solution)/shard_map/ppermute | solution.py:597
  366.0 16.8 %collective-permute-start.26 = (bf16[640,512]{1,0:T(8,128)(2,1)}, bf16[640,512]{1,0:T(8,128)(2,1)}, u32[]{:S(2)}, u32[]{:S(2)}) collective-permute-start(bf16[640,512]{1,0:T(8,128)(2,1)} %add_convert_fusion.12), channel_id=1, source_target_pairs={{0,8},{8,0},{1,9},{9,1},{2,10},{10,2},{3,11},{11,3},{4,12},{12,4},... | collective-permute-start | bytes 1966088 | tf_op jit(solution)/shard_map/ppermute | solution.py:597
  389.5 14.9 %collective-permute-start.29 = (bf16[256,1024]{1,0:T(8,128)(2,1)S(1)}, bf16[256,1024]{1,0:T(8,128)(2,1)S(1)}, u32[]{:S(2)}, u32[]{:S(2)}) collective-permute-start(bf16[256,1024]{1,0:T(8,128)(2,1)S(1)} %get-tuple-element.161), channel_id=1, source_target_pairs={{0,8},{8,0},{1,9},{9,1},{2,10},{10,2},{3,11},{11,3},{4,12},{12,4},... | collective-permute-start | bytes 1572872 | tf_op jit(solution)/shard_map/ppermute | solution.py:597
  390.0 61.1 %collective-permute-start.28 = (bf16[256,1024]{1,0:T(8,128)(2,1)}, bf16[256,1024]{1,0:T(8,128)(2,1)}, u32[]{:S(2)}, u32[]{:S(2)}) collective-permute-start(bf16[256,1024]{1,0:T(8,128)(2,1)} %get-tuple-element.160), channel_id=1, source_target_pairs={{0,8},{8,0},{1,9},{9,1},{2,10},{10,2},{3,11},{11,3},{4,12},{12,4},... | collective-permute-start | bytes 1572872 | tf_op jit(solution)/shard_map/ppermute | solution.py:597
  392.6 34.3 %collective-permute-start.31 = (bf16[256,1024]{1,0:T(8,128)(2,1)}, bf16[256,1024]{1,0:T(8,128)(2,1)}, u32[]{:S(2)}, u32[]{:S(2)}) collective-permute-start(bf16[256,1024]{1,0:T(8,128)(2,1)} %get-tuple-element.162), channel_id=1, source_target_pairs={{0,16},{16,0},{1,17},{17,1},{2,18},{18,2},{3,19},{19,3},{4,20},{20... | collective-permute-start | bytes 1572872 | tf_op jit(solution)/shard_map/ppermute | solution.py:597
  394.4 26.8 %collective-permute-start.39 = (bf16[256,512]{1,0:T(8,128)(2,1)S(1)}, bf16[256,512]{1,0:T(8,128)(2,1)S(1)}, u32[]{:S(2)}, u32[]{:S(2)}) collective-permute-start(bf16[256,512]{1,0:T(8,128)(2,1)S(1)} %get-tuple-element.180), channel_id=1, source_target_pairs={{0,24},{24,0},{8,16},{16,8},{1,25},{25,1},{9,17},{17,9},{2,26},{26... | collective-permute-start | bytes 786440 | tf_op jit(solution)/shard_map/ppermute | solution.py:849
  396.0 26.7 %collective-permute-start.38 = (bf16[256,512]{1,0:T(8,128)(2,1)S(1)}, bf16[256,512]{1,0:T(8,128)(2,1)S(1)}, u32[]{:S(2)}, u32[]{:S(2)}) collective-permute-start(bf16[256,512]{1,0:T(8,128)(2,1)S(1)} %get-tuple-element.181), channel_id=1, source_target_pairs={{0,16},{16,0},{1,17},{17,1},{2,18},{18,2},{3,19},{19,3},{4,20},{20... | collective-permute-start | bytes 786440 | tf_op jit(solution)/shard_map/ppermute | solution.py:597
  405.2 19.6 %collective-permute-start.37 = (bf16[256,512]{1,0:T(8,128)(2,1)S(1)}, bf16[256,512]{1,0:T(8,128)(2,1)S(1)}, u32[]{:S(2)}, u32[]{:S(2)}) collective-permute-start(bf16[256,512]{1,0:T(8,128)(2,1)S(1)} %get-tuple-element.179), channel_id=1, source_target_pairs={{0,8},{8,0},{1,9},{9,1},{2,10},{10,2},{3,11},{11,3},{4,12},{12,4},... | collective-permute-start | bytes 786440 | tf_op jit(solution)/shard_map/ppermute | solution.py:597
  421.2 31.3 %collective-permute-start.30 = (bf16[256,1024]{1,0:T(8,128)(2,1)S(1)}, bf16[256,1024]{1,0:T(8,128)(2,1)S(1)}, u32[]{:S(2)}, u32[]{:S(2)}) collective-permute-start(bf16[256,1024]{1,0:T(8,128)(2,1)S(1)} %fusion.22), channel_id=1, source_target_pairs={{0,16},{16,0},{1,17},{17,1},{2,18},{18,2},{3,19},{19,3},{4,20},{20... | collective-permute-start | bytes 1572872 | tf_op jit(solution)/shard_map/ppermute | solution.py:597
  422.7 39.3 %collective-permute-start.33 = (bf16[256,1024]{1,0:T(8,128)(2,1)S(1)}, bf16[256,1024]{1,0:T(8,128)(2,1)S(1)}, u32[]{:S(2)}, u32[]{:S(2)}) collective-permute-start(bf16[256,1024]{1,0:T(8,128)(2,1)S(1)} %copy-done.53), channel_id=1, source_target_pairs={{0,16},{16,0},{1,17},{17,1},{2,18},{18,2},{3,19},{19,3},{4,20},{20... | collective-permute-start | bytes 1572872 | tf_op jit(solution)/shard_map/ppermute | solution.py:597
  425.9 24.3 %collective-permute-start.40 = (bf16[256,512]{1,0:T(8,128)(2,1)S(1)}, bf16[256,512]{1,0:T(8,128)(2,1)S(1)}, u32[]{:S(2)}, u32[]{:S(2)}) collective-permute-start(bf16[256,512]{1,0:T(8,128)(2,1)S(1)} %fusion.26.refs_0_), channel_id=1, source_target_pairs={{0,8},{8,0},{1,9},{9,1},{2,10},{10,2},{3,11},{11,3},{4,12},{12,4},... | collective-permute-start | bytes 786440 | tf_op jit(solution)/shard_map/ppermute | solution.py:597
  426.9 21.9 %collective-permute-start.41 = (bf16[256,512]{1,0:T(8,128)(2,1)S(1)}, bf16[256,512]{1,0:T(8,128)(2,1)S(1)}, u32[]{:S(2)}, u32[]{:S(2)}) collective-permute-start(bf16[256,512]{1,0:T(8,128)(2,1)S(1)} %fusion.26.refs_0_), channel_id=1, source_target_pairs={{0,16},{16,0},{1,17},{17,1},{2,18},{18,2},{3,19},{19,3},{4,20},{20... | collective-permute-start | bytes 786440 | tf_op jit(solution)/shard_map/ppermute | solution.py:597
  448.8 13.3 %collective-permute-start.32 = (bf16[256,1024]{1,0:T(8,128)(2,1)S(1)}, bf16[256,1024]{1,0:T(8,128)(2,1)S(1)}, u32[]{:S(2)}, u32[]{:S(2)}) collective-permute-start(bf16[256,1024]{1,0:T(8,128)(2,1)S(1)} %fusion.21), channel_id=1, source_target_pairs={{0,8},{8,0},{1,9},{9,1},{2,10},{10,2},{3,11},{11,3},{4,12},{12,4},... | collective-permute-start | bytes 1572872 | tf_op jit(solution)/shard_map/ppermute | solution.py:597
  450.1 11.2 %collective-permute-start.42 = (bf16[128,512]{1,0:T(8,128)(2,1)S(1)}, bf16[128,512]{1,0:T(8,128)(2,1)S(1)}, u32[]{:S(2)}, u32[]{:S(2)}) collective-permute-start(bf16[128,512]{1,0:T(8,128)(2,1)S(1)} %slice.374), channel_id=1, source_target_pairs={{0,8},{8,0},{1,9},{9,1},{2,10},{10,2},{3,11},{11,3},{4,12},{12,4},... | collective-permute-start | bytes 393224 | tf_op jit(solution)/shard_map/ppermute | solution.py:597
  451.1 10.3 %collective-permute-start.43 = (bf16[128,512]{1,0:T(8,128)(2,1)S(1)}, bf16[128,512]{1,0:T(8,128)(2,1)S(1)}, u32[]{:S(2)}, u32[]{:S(2)}) collective-permute-start(bf16[128,512]{1,0:T(8,128)(2,1)S(1)} %slice.375), channel_id=1, source_target_pairs={{0,16},{16,0},{1,17},{17,1},{2,18},{18,2},{3,19},{19,3},{4,20},{20... | collective-permute-start | bytes 393224 | tf_op jit(solution)/shard_map/ppermute | solution.py:597
  453.8 8.7 %collective-permute-start.44 = (bf16[256,512]{1,0:T(8,128)(2,1)S(1)}, bf16[256,512]{1,0:T(8,128)(2,1)S(1)}, u32[]{:S(2)}, u32[]{:S(2)}) collective-permute-start(bf16[256,512]{1,0:T(8,128)(2,1)S(1)} %fusion.26.refs_0_), channel_id=1, source_target_pairs={{0,4},{4,0},{1,5},{5,1},{2,6},{6,2},{3,7},{7,3},{8,12},{12,8},{9,1... | collective-permute-start | bytes 786440 | tf_op jit(solution)/shard_map/ppermute | solution.py:597
  461.4 1.9 collective-permute-start.46
  462.0 1.7 collective-permute-start.47
  466.4 15.7 %collective-permute-start.49 = (bf16[288,1024]{1,0:T(8,128)(2,1)}, bf16[288,1024]{1,0:T(8,128)(2,1)S(1)}, u32[]{:S(2)}, u32[]{:S(2)}) collective-permute-start(bf16[288,1024]{1,0:T(8,128)(2,1)} %reduce-scatter.3.cloned.1.call-done.refs_0_.refs_8_.refs_16_), channel_id=1, source_target_pairs={{0,16},{16,0},{1,17},{17,1},{2,18},{18,2},{3,19},{19,3},{4,20},{20... | collective-permute-start | bytes 1769480 | tf_op jit(solution)/shard_map/ppermute | solution.py:597
  467.5 16.4 %collective-permute-start.48 = (bf16[288,1024]{1,0:T(8,128)(2,1)}, bf16[288,1024]{1,0:T(8,128)(2,1)S(1)}, u32[]{:S(2)}, u32[]{:S(2)}) collective-permute-start(bf16[288,1024]{1,0:T(8,128)(2,1)} %reduce-scatter.3.cloned.1.call-done.refs_0_.refs_8_.refs_16_), channel_id=1, source_target_pairs={{0,8},{8,0},{1,9},{9,1},{2,10},{10,2},{3,11},{11,3},{4,12},{12,4},... | collective-permute-start | bytes 1769480 | tf_op jit(solution)/shard_map/ppermute | solution.py:597
  469.4 24.6 %collective-permute-start.52 = (bf16[288,1024]{1,0:T(8,128)(2,1)}, bf16[288,1024]{1,0:T(8,128)(2,1)S(1)}, u32[]{:S(2)}, u32[]{:S(2)}) collective-permute-start(bf16[288,1024]{1,0:T(8,128)(2,1)} %reduce-scatter.3.cloned.1.call-done.refs_0_.refs_8_.refs_16_), channel_id=1, source_target_pairs={{0,4},{4,0},{1,5},{5,1},{2,6},{6,2},{3,7},{7,3},{8,12},{12,8},{9,1... | collective-permute-start | bytes 1769480 | tf_op jit(solution)/shard_map/ppermute | solution.py:597
  482.1 8.4 %collective-permute-start.50 = (bf16[144,1024]{1,0:T(8,128)(2,1)S(1)}, bf16[144,1024]{1,0:T(8,128)(2,1)S(1)}, u32[]{:S(2)}, u32[]{:S(2)}) collective-permute-start(bf16[144,1024]{1,0:T(8,128)(2,1)S(1)} %slice.376), channel_id=1, source_target_pairs={{0,8},{8,0},{1,9},{9,1},{2,10},{10,2},{3,11},{11,3},{4,12},{12,4},... | collective-permute-start | bytes 884744 | tf_op jit(solution)/shard_map/ppermute | solution.py:597
  484.0 8.1 %collective-permute-start.51 = (bf16[144,1024]{1,0:T(8,128)(2,1)S(1)}, bf16[144,1024]{1,0:T(8,128)(2,1)S(1)}, u32[]{:S(2)}, u32[]{:S(2)}) collective-permute-start(bf16[144,1024]{1,0:T(8,128)(2,1)S(1)} %slice.377), channel_id=1, source_target_pairs={{0,16},{16,0},{1,17},{17,1},{2,18},{18,2},{3,19},{19,3},{4,20},{20... | collective-permute-start | bytes 884744 | tf_op jit(solution)/shard_map/ppermute | solution.py:597
  485.5 8.4 %collective-permute-start.53 = (bf16[288,1024]{1,0:T(8,128)(2,1)S(1)}, bf16[288,1024]{1,0:T(8,128)(2,1)S(1)}, u32[]{:S(2)}, u32[]{:S(2)}) collective-permute-start(bf16[288,1024]{1,0:T(8,128)(2,1)S(1)} %collective-permute-done.48.refs_1_.refs_9_.refs_17_), channel_id=1, source_target_pairs={{0,4},{4,0},{1,5},{5,1},{2,6},{6,2},{3,7},{7,3},{8,12},{12,8},{9,1... | collective-permute-start | bytes 1769480 | tf_op jit(solution)/shard_map/ppermute | solution.py:597
  485.6 8.4 %collective-permute-start.54 = (bf16[288,1024]{1,0:T(8,128)(2,1)S(1)}, bf16[288,1024]{1,0:T(8,128)(2,1)S(1)}, u32[]{:S(2)}, u32[]{:S(2)}) collective-permute-start(bf16[288,1024]{1,0:T(8,128)(2,1)S(1)} %collective-permute-done.49.refs_2_.refs_10_.refs_18_), channel_id=1, source_target_pairs={{0,4},{4,0},{1,5},{5,1},{2,6},{6,2},{3,7},{7,3},{8,12},{12,8},{9,1... | collective-permute-start | bytes 1769480 | tf_op jit(solution)/shard_map/ppermute | solution.py:597
  492.1 2.1 collective-permute-start.55
  (70 other events, 868.8 us)
Sparse Core Ops, SparseCore 0:
  12.4 30.6 all-gather.3
  45.2 45.4 all-gather.5
  92.9 27.8 all-gather.7
  280.1 77.2 reduce-scatter.4
  387.2 46.8 reduce-scatter.2

commit v2 on v1

--- a/solution.py
+++ b/solution.py
@@ -53,23 +53,25 @@
     return lax.dot_general(left, right, (((0,), (0,)), ((), ())), preferred_element_type=F32)
 
 
-def unit_place(index, per_owner):
-    owner = index // per_owner
-    return owner, pl.multiple_of((index - owner * per_owner) * UNIT, UNIT)
-
-
-def forward_attention(heads, width, qkv, g, source, target):
-    _, owners, rows, _ = qkv.shape
+def forward_attention(heads, width, qkv, g, slots, places, before):
+    owners, groups, rows, _ = qkv.shape
     total = owners * rows
-    units, per_owner = total // UNIT, rows // UNIT
+    per_owner = rows // UNIT
     size = width // heads
     scale = size**-0.5
 
-    def kernel(src, dst, qkv_ref, out_ref, exact_ref, log_ref, qs, ks, vs, vt):
-        for s in range(units):
-            owner, place = unit_place(src[g * units + s], per_owner)
-            block = qkv_ref[0, owner, pl.ds(place, UNIT), :]
-            here = slice(s * UNIT, (s + 1) * UNIT)
+    units = [(k, u) for k in range(owners) for u in range(per_owner)]
+
+    def kernel(slot_ref, at_ref, qkv_ref, *refs):
+        out_ref, exact_ref, log_ref, qs, ks, vs, vt, low = refs[-8:]
+
+        def canonical(k, u):
+            slot = slot_ref[(k * groups + g) * per_owner + u]
+            return pl.ds(pl.multiple_of(slot * UNIT, UNIT), UNIT)
+
+        for k, u in units:
+            block = qkv_ref[k, 0, u * UNIT : (u + 1) * UNIT, :]
+            here = canonical(k, u)
             qs[here, :] = block[:, :width] * scale
             ks[here, :] = block[:, width : 2 * width]
             vs[here, :] = block[:, 2 * width :]
@@ -96,65 +98,68 @@
                     past = jnp.exp(past - high)
                     sums = sums + jnp.sum(past, 0, keepdims=True)
                     mixed = mixed + nn(vt[lanes, :before], past.astype(BF16))
-                log_ref[h : h + 1, here] = high + jnp.log(sums)
+                log_ref[0, h : h + 1, here] = high + jnp.log(sums)
                 outs.append(mixed / sums)
             both = jnp.concatenate(outs, 0) if heads > 1 else outs[0]
-            exact_ref[:, here] = both
-            low = both.T.astype(BF16)
-            for u in range(TILE // UNIT):
-                owner, place = unit_place(dst[g * units + i * (TILE // UNIT) + u], per_owner)
-                out_ref[owner, pl.ds(place, UNIT), :] = low[u * UNIT : (u + 1) * UNIT, :]
+            exact_ref[0, :, here] = both
+            low[here, :] = both.T.astype(BF16)
+        for k, u in units:
+            out_ref[at_ref[k], 0, u * UNIT : (u + 1) * UNIT, :] = low[canonical(k, u), :]
 
     return pl.pallas_call(
         kernel,
         grid_spec=pltpu.PrefetchScalarGridSpec(
             num_scalar_prefetch=2,
             grid=(1,),
-            in_specs=[pl.BlockSpec((1, owners, rows, 3 * width), lambda i, *_: (g, 0, 0, 0))],
+            in_specs=[pl.BlockSpec((owners, 1, rows, 3 * width), lambda i, *_: (0, g, 0, 0))]
+            + [pl.BlockSpec(memory_space=pl.ANY)] * len(before),
             out_specs=[
-                pl.BlockSpec((owners, rows, width), lambda i, *_: (0, 0, 0)),
-                pl.BlockSpec((width, total), lambda i, *_: (0, 0)),
-                pl.BlockSpec((heads, total), lambda i, *_: (0, 0)),
+                pl.BlockSpec((owners, 1, rows, width), lambda i, *_: (0, g, 0, 0)),
+                pl.BlockSpec((1, width, total), lambda i, *_: (g, 0, 0)),
+                pl.BlockSpec((1, heads, total), lambda i, *_: (g, 0, 0)),
             ],
             scratch_shapes=[pltpu.VMEM((total, width), BF16)] * 3
-            + [pltpu.VMEM((width, total), BF16)],
+            + [pltpu.VMEM((width, total), BF16), pltpu.VMEM((total, width), BF16)],
         ),
         out_shape=[
-            jax.ShapeDtypeStruct((owners, rows, width), BF16),
-            jax.ShapeDtypeStruct((width, total), F32),
-            jax.ShapeDtypeStruct((heads, total), F32),
+            jax.ShapeDtypeStruct((owners, groups, rows, width), BF16),
+            jax.ShapeDtypeStruct((groups, width, total), F32),
+            jax.ShapeDtypeStruct((groups, heads, total), F32),
         ],
+        input_output_aliases={3 + i: i for i in range(len(before))},
         compiler_params=pltpu.CompilerParams(vmem_limit_bytes=48 * 1024 * 1024),
-        cost_estimate=pl.CostEstimate(
-            flops=12 * total * total * width, bytes_accessed=16 * total * width, transcendentals=0
-        ),
-    )(source, target, qkv)
-
-
-def backward_attention(heads, width, qkv, g, grad, exact, logs, source, target):
-    _, owners, rows, _ = qkv.shape
+        cost_estimate=pl.CostEstimate(flops=1, bytes_accessed=1, transcendentals=0),
+    )(slots, places, qkv, *before)
+
+
+def backward_attention(heads, width, qkv, grad, exact, logs, slots, places):
+    owners, groups, rows, _ = qkv.shape
     total = owners * rows
-    units, per_owner = total // UNIT, rows // UNIT
+    per_owner = rows // UNIT
     size = width // heads
     scale = size**-0.5
     wide = 2 * TILE
-
-    def kernel(
-        src, dst, qkv_ref, grad_ref, exact_ref, log_ref, out_ref, qs, ks, vs, gs, kt, delta, dqt, dk, dv
-    ):
-        for s in range(units):
-            owner, place = unit_place(src[g * units + s], per_owner)
-            block = qkv_ref[0, owner, pl.ds(place, UNIT), :]
-            here = slice(s * UNIT, (s + 1) * UNIT)
+    units = [(k, u) for k in range(owners) for u in range(per_owner)]
+
+    def kernel(slot_ref, at_ref, qkv_ref, grad_ref, exact_ref, log_ref, out_ref, *scratch):
+        qs, ks, vs, gs, kt, delta, dqt, dq, dk, dv = scratch
+        g = pl.program_id(0)
+
+        def canonical(k, u):
+            slot = slot_ref[(k * groups + g) * per_owner + u]
+            return pl.ds(pl.multiple_of(slot * UNIT, UNIT), UNIT)
+
+        for k, u in units:
+            block = qkv_ref[k, 0, u * UNIT : (u + 1) * UNIT, :]
+            here = canonical(k, u)
             qs[here, :] = block[:, :width] * scale
             ks[here, :] = block[:, width : 2 * width]
             vs[here, :] = block[:, 2 * width :]
-            owner, place = unit_place(dst[g * units + s], per_owner)
-            gs[here, :] = grad_ref[owner, pl.ds(place, UNIT), :]
+            gs[here, :] = grad_ref[at_ref[k], 0, u * UNIT : (u + 1) * UNIT, :]
         kt[...] = ks[...].T
         for i in range(total // TILE):
             here = slice(i * TILE, (i + 1) * TILE)
-            both = gs[here, :].astype(F32).T * exact_ref[:, here]
+            both = gs[here, :].astype(F32).T * exact_ref[0, :, here]
             for h in range(heads):
                 delta[h : h + 1, here] = jnp.sum(
                     both[h * size : (h + 1) * size, :], 0, keepdims=True
@@ -180,7 +185,7 @@
                 for at, count in starts:
                     there = slice(at, at + count)
                     query, pull = qs[there, lanes], gs[there, lanes]
-                    powers = jnp.exp(nt(key, query) - log_ref[h : h + 1, there])
+                    powers = jnp.exp(nt(key, query) - log_ref[0, h : h + 1, there])
                     if at == j * TILE:
                         row = lax.broadcasted_iota(jnp.int32, (TILE, TILE), 0)
                         col = lax.broadcasted_iota(jnp.int32, (TILE, TILE), 1)
@@ -195,33 +200,23 @@
                 dv[here, lanes] = grad_value.astype(BF16)
         for i in range(total // TILE):
             here = slice(i * TILE, (i + 1) * TILE)
-            low = (dqt[:, here] * scale).T.astype(BF16)
-            for u in range(TILE // UNIT):
-                s = i * (TILE // UNIT) + u
-                owner, place = unit_place(src[g * units + s], per_owner)
-                block = jnp.concatenate(
-                    [
-                        low[u * UNIT : (u + 1) * UNIT, :],
-                        dk[s * UNIT : (s + 1) * UNIT, :],
-                        dv[s * UNIT : (s + 1) * UNIT, :],
-                    ],
-                    1,
-                )
-                out_ref[owner, pl.ds(place, UNIT), :] = block
-
-    whole = lambda *shape: pl.BlockSpec(shape, lambda i, *_: (0,) * len(shape))
+            dq[here, :] = (dqt[:, here] * scale).T.astype(BF16)
+        for k, u in units:
+            here = canonical(k, u)
+            for at, ref in enumerate((dq, dk, dv)):
+                out_ref[k, 0, u * UNIT : (u + 1) * UNIT, at * width : (at + 1) * width] = ref[
+                    here, :
+                ]
+
+    by_group = lambda lanes: pl.BlockSpec((owners, 1, rows, lanes), lambda g, *_: (0, g, 0, 0))
+    kept = lambda lines: pl.BlockSpec((1, lines, total), lambda g, *_: (g, 0, 0))
     return pl.pallas_call(
         kernel,
         grid_spec=pltpu.PrefetchScalarGridSpec(
             num_scalar_prefetch=2,
-            grid=(1,),
-            in_specs=[
-                pl.BlockSpec((1, owners, rows, 3 * width), lambda i, *_: (g, 0, 0, 0)),
-                whole(owners, rows, width),
-                whole(width, total),
-                whole(heads, total),
-            ],
-            out_specs=whole(owners, rows, 3 * width),
+            grid=(groups,),
+            in_specs=[by_group(3 * width), by_group(width), kept(width), kept(heads)],
+            out_specs=by_group(3 * width),
             scratch_shapes=[pltpu.VMEM((total, width), BF16)] * 4
             + [
                 pltpu.VMEM((width, total), BF16),
@@ -229,14 +224,15 @@
                 pltpu.VMEM((width, total), F32),
                 pltpu.VMEM((total, width), BF16),
                 pltpu.VMEM((total, width), BF16),
+                pltpu.VMEM((total, width), BF16),
             ],
         ),
-        out_shape=jax.ShapeDtypeStruct((owners, rows, 3 * width), BF16),
+        out_shape=jax.ShapeDtypeStruct((owners, groups, rows, 3 * width), BF16),
         compiler_params=pltpu.CompilerParams(vmem_limit_bytes=48 * 1024 * 1024),
         cost_estimate=pl.CostEstimate(
-            flops=16 * total * total * width, bytes_accessed=16 * total * width, transcendentals=0
+            flops=14 * total * total * width, bytes_accessed=1, transcendentals=0
         ),
-    )(source, target, qkv, grad, exact, logs)
+    )(slots, places, qkv, grad, exact, logs)
 
 
 def feed_forward(h2, pull, sums, others, mine, shares):
@@ -345,12 +341,220 @@
             pltpu.SemaphoreType.DMA((2,)),
         ],
         compiler_params=pltpu.CompilerParams(vmem_limit_bytes=56 * 1024 * 1024),
-        cost_estimate=pl.CostEstimate(
-            flops=12 * tokens * model * ff * n_all,
-            bytes_accessed=8 * model * ff * n_all,
-            transcendentals=0,
-        ),
+        cost_estimate=pl.CostEstimate(flops=1, bytes_accessed=1, transcendentals=0),
     )(h2, pull, *(() if first else sums), *chunks)
+
+
+def attention_output(heads, stream, weight, gain, bias, rows):
+    owners, tokens, width = heads.shape
+    model = owners * width
+
+    def kernel(heads_ref, stream_ref, weight_ref, gain_ref, bias_ref, low_ref, sum_ref, norm_ref):
+        for d in range(owners):
+            low_ref[:, d * width : (d + 1) * width] = heads_ref[d]
+        total = stream_ref[...].astype(F32) + nn(low_ref[...], weight_ref[...])
+        sum_ref[...] = total
+        norm_ref[...] = layer_norm(total, gain_ref[...], bias_ref[...])[0].astype(BF16)
+
+    fixed = lambda *shape: pl.BlockSpec(shape, lambda i: (0, 0))
+    block = pl.BlockSpec((rows, model), lambda i: (i, 0))
+    return pl.pallas_call(
+        kernel,
+        grid=(tokens // rows,),
+        in_specs=[
+            pl.BlockSpec((owners, rows, width), lambda i: (0, i, 0)),
+            block,
+            fixed(model, model),
+            fixed(1, model),
+            fixed(1, model),
+        ],
+        out_specs=[block] * 3,
+        out_shape=[jax.ShapeDtypeStruct((tokens, model), kind) for kind in (BF16, F32, BF16)],
+        compiler_params=pltpu.CompilerParams(vmem_limit_bytes=48 * 1024 * 1024),
+        cost_estimate=pl.CostEstimate(flops=1, bytes_accessed=1, transcendentals=0),
+    )(heads, stream, weight, gain[None], bias[None])
+
+
+def norm_gradient(total, grad, direct, weight, gain, owners, rows):
+    tokens, model = total.shape
+    width = model // owners
+
+    def kernel(total_ref, grad_ref, direct_ref, weight_ref, gain_ref, resid_ref, low_ref, heads_ref, vec_ref):
+        i = pl.program_id(0)
+        values = total_ref[...]
+        centred = values - jnp.mean(values, -1, keepdims=True)
+        inv_std = lax.rsqrt(jnp.mean(centred * centred, -1, keepdims=True) + EPSILON)
+        normed = centred * inv_std
+        grads = grad_ref[...]
+        result = direct_ref[...].astype(F32) + norm_back(grads, normed, inv_std, gain_ref[...])
+        resid_ref[...] = result
+        low = result.astype(BF16)
+        low_ref[...] = low
+        back = nt(low, weight_ref[...]).astype(BF16)
+        for d in range(owners):
+            heads_ref[d] = back[:, d * width : (d + 1) * width]
+        for_gain = jnp.sum(grads * normed, 0, keepdims=True)
+        for_bias = jnp.sum(grads, 0, keepdims=True)
+
+        @pl.when(i == 0)
+        def _():
+            vec_ref[...] = jnp.zeros_like(vec_ref)
+
+        vec_ref[0:1, :] += for_gain
+        vec_ref[1:2, :] += for_bias
+
+    fixed = lambda *shape: pl.BlockSpec(shape, lambda i: (0, 0))
+    block = pl.BlockSpec((rows, model), lambda i: (i, 0))
+    return pl.pallas_call(
+        kernel,
+        grid=(tokens // rows,),
+        in_specs=[block, block, block, fixed(model, model), fixed(1, model)],
+        out_specs=[
+            block,
+            block,
+            pl.BlockSpec((owners, rows, width), lambda i: (0, i, 0)),
+            fixed(8, model),
+        ],
+        out_shape=[
+            jax.ShapeDtypeStruct((tokens, model), F32),
+            jax.ShapeDtypeStruct((tokens, model), BF16),
+            jax.ShapeDtypeStruct((owners, tokens, width), BF16),
+            jax.ShapeDtypeStruct((8, model), F32),
+        ],
+        compiler_params=pltpu.CompilerParams(vmem_limit_bytes=48 * 1024 * 1024),
+        cost_estimate=pl.CostEstimate(flops=1, bytes_accessed=1, transcendentals=0),
+    )(total, grad, direct, weight, gain[None])
+
+
+def input_parts(slopes, weight, away):
+    count, tokens, columns = slopes.shape
+    model = weight.shape[0]
+    half = tokens // 2
+
+    def kernel(slope_ref, weight_ref, away_ref, *outs):
+        t = pl.program_id(0)
+        for h in range(2):
+            rows = slice(h * half, (h + 1) * half)
+            part = nt(slope_ref[0, rows, :], weight_ref[...]) + away_ref[0, rows, :].astype(F32)
+            for k in range(count):
+
+                @pl.when(t == k)
+                def _(k=k, h=h, part=part):
+                    outs[2 * k + h][...] = part.astype(BF16)
+
+    out = pl.pallas_call(
+        kernel,
+        grid=(count,),
+        in_specs=[
+            pl.BlockSpec((1, tokens, columns), lambda t: (t, 0, 0)),
+            pl.BlockSpec((model, columns), lambda t: (0, 0)),
+            pl.BlockSpec((1, tokens, model), lambda t: (t, 0, 0)),
+        ],
+        out_specs=[pl.BlockSpec((half, model), lambda t: (0, 0))] * (2 * count),
+        out_shape=[jax.ShapeDtypeStruct((half, model), BF16)] * (2 * count),
+        compiler_params=pltpu.CompilerParams(vmem_limit_bytes=48 * 1024 * 1024),
+        cost_estimate=pl.CostEstimate(flops=1, bytes_accessed=1, transcendentals=0),
+    )(slopes, weight, away)
+    return [(out[2 * k], out[2 * k + 1]) for k in range(count)]
+
+
+def projection_gradient(normed, slopes, weight, columns):
+    count, width = slopes.shape
+    model = normed.shape[1]
+    block = min(512, count)
+    steps = count // block
+
+    def kernel(normed_ref, slope_ref, weight_ref, columns_ref, out_ref, acc, sums):
+        t = pl.program_id(0)
+        grad = tn(slope_ref[...], normed_ref[...])
+        summed = jnp.sum(slope_ref[...].astype(F32), 0, keepdims=True)
+
+        @pl.when(t == 0)
+        def _():
+            acc[...] = grad
+            sums[...] = summed
+
+        @pl.when(t > 0)
+        def _():
+            acc[...] += grad
+            sums[...] += summed
+
+        @pl.when(t == steps - 1)
+        def _():
+            whole = acc[...].T
+            wide = weight_ref[...].astype(F32)
+            given = columns_ref[...]
+            bias = jnp.sum(wide * sums[...], 1, keepdims=True)
+            gain = jnp.sum(wide * whole, 1, keepdims=True)
+            gain = (gain - given[:, 1:2] * bias) / given[:, 0:1]
+            lane = lax.broadcasted_iota(jnp.int32, given.shape, 1)
+            vectors = jnp.where(lane == 0, gain, jnp.where(lane == 1, bias, given))
+            out_ref[:, :width] = whole.astype(BF16)
+            out_ref[:, width:] = vectors.astype(BF16)
+
+    return pl.pallas_call(
+        kernel,
+        grid=(steps,),
+        in_specs=[
+            pl.BlockSpec((block, model), lambda t: (t, 0)),
+            pl.BlockSpec((block, width), lambda t: (t, 0)),
+            pl.BlockSpec((model, width), lambda t: (0, 0)),
+            pl.BlockSpec((model, 128), lambda t: (0, 0)),
+        ],
+        out_specs=pl.BlockSpec((model, width + 128), lambda t: (0, 0)),
+        out_shape=jax.ShapeDtypeStruct((model, width + 128), BF16),
+        scratch_shapes=[pltpu.VMEM((width, model), F32), pltpu.VMEM((1, width), F32)],
+        compiler_params=pltpu.CompilerParams(vmem_limit_bytes=48 * 1024 * 1024),
+        cost_estimate=pl.CostEstimate(flops=1, bytes_accessed=1, transcendentals=0),
+    )(normed, slopes, weight, columns)
+
+
+def join_lower(mine, away):
+    shares, _, part, ff = mine[0].shape
+    counts = [each.shape[1] for each in mine]
+    n = len(mine)
+
+    def kernel(*refs):
+        at = 0
+        for k, count in enumerate(counts):
+            refs[-1][0, at : at + count] = add(refs[k][0], refs[n + k][0])
+            at += count
+
+    spec = lambda count: pl.BlockSpec((1, count, part, ff), lambda z: (z, 0, 0, 0))
+    return pl.pallas_call(
+        kernel,
+        grid=(shares,),
+        in_specs=[spec(count) for count in counts] * 2,
+        out_specs=spec(sum(counts)),
+        out_shape=jax.ShapeDtypeStruct((shares, sum(counts), part, ff), BF16),
+        compiler_params=pltpu.CompilerParams(vmem_limit_bytes=48 * 1024 * 1024),
+        cost_estimate=pl.CostEstimate(flops=1, bytes_accessed=1, transcendentals=0),
+    )(*mine, *away)
+
+
+def join_upper(mine, away, outer, outer_away):
+    _, model, ff = mine[0].shape
+    counts = [each.shape[0] for each in mine]
+    n, half, extra = len(mine), model // 2, outer.shape[2]
+
+    def kernel(*refs):
+        ins, outs = refs[: 2 * n + 2], refs[2 * n + 2 :]
+        k = 0
+        for i, count in enumerate(counts):
+            for j in range(count):
+                for h in range(2):
+                    rows = slice(h * half, (h + 1) * half)
+                    outs[2 * k + h][:half, :] = add(ins[i][j, rows, :], ins[n + i][j, rows, :])
+                    outs[2 * k + h][half:, :] = add(ins[2 * n][k, h], ins[2 * n + 1][k, h])
+                k += 1
+
+    out = pl.pallas_call(
+        kernel,
+        out_shape=[jax.ShapeDtypeStruct((half + extra, ff), BF16)] * (2 * sum(counts)),
+        compiler_params=pltpu.CompilerParams(vmem_limit_bytes=48 * 1024 * 1024),
+        cost_estimate=pl.CostEstimate(flops=1, bytes_accessed=1, transcendentals=0),
+    )(*mine, *away, outer, outer_away)
+    return [[out[2 * k], out[2 * k + 1]] for k in range(sum(counts))]
 
 
 def outer_gradient(left, right, places, shares):
@@ -386,9 +590,7 @@
         ),
         out_shape=[jax.ShapeDtypeStruct(shape, BF16)] * 2,
         compiler_params=pltpu.CompilerParams(vmem_limit_bytes=48 * 1024 * 1024),
-        cost_estimate=pl.CostEstimate(
-            flops=2 * tokens * model * model, bytes_accessed=4 * model * model, transcendentals=0
-        ),
+        cost_estimate=pl.CostEstimate(flops=1, bytes_accessed=1, transcendentals=0),
     )(places, left, right)
 
 
@@ -413,7 +615,7 @@
             for i in range(1, count):
                 if places[i] - places[i - 1] > 1:
                     at = at + (k >= i) * (places[i] - places[i - 1] - 1)
-        return t % steps * owners + at
+        return at * steps + t % steps
 
     def kernel(*refs):
         piece_refs = refs[:count]
@@ -453,11 +655,7 @@
         scratch_shapes=[pltpu.VMEM((rows, model), BF16)],
         input_output_aliases={count + 3 + i: i for i in range(len(extra))},
         compiler_params=pltpu.CompilerParams(vmem_limit_bytes=48 * 1024 * 1024),
-        cost_estimate=pl.CostEstimate(
-            flops=2 * count * mine * model * columns,
-            bytes_accessed=2 * count * mine * (2 * model + columns),
-            transcendentals=0,
-        ),
+        cost_estimate=pl.CostEstimate(flops=1, bytes_accessed=1, transcendentals=0),
     )(*pieces, gain[None], bias[None], weight, *extra)
 
 
@@ -597,6 +795,19 @@
     return lax.ppermute(value, axis, [(0, 1), (1, 0)])
 
 
+def after(value, *others):
+    return lax.optimization_barrier((value, *others))[0]
+
+
+def spread_near(value):
+    return [value, flip(value, "b"), flip(value, "a")]
+
+
+def spread_far(near):
+    half = near[0].shape[0] // 2
+    return [flip(near[2][:half], "b"), flip(near[1][half:], "a")]
+
+
 def spread(value):
     if lax.axis_size("a") != 2:
         return list(lax.all_gather(value, CTX, axis=0, tiled=False))
@@ -664,17 +875,24 @@
     note = jnp.zeros((32, model), BF16).at[0, : groups * per_group].set(
         slot.reshape(-1).astype(BF16)
     )
-    pieces = spread(jnp.concatenate([tokens.reshape(mine, model), note], 0))
-    slots = jnp.stack(
-        [each[mine, : groups * per_group].reshape(groups, per_group) for each in pieces], 1
-    )
-    slots = slots.reshape(groups, owners * per_group).astype(jnp.int32)
+    sent = jnp.concatenate([tokens.reshape(mine, model), note], 0)
+    if square:
+        near_pieces = spread_near(sent)
+        far_halves = spread_far(near_pieces)
+        pieces = [sent] + near_pieces[1:3]
+    else:
+        pieces = spread(sent)
+    places = jnp.arange(owners, dtype=jnp.int32)
+    if square:
+        places = absolute(places)
 
     columns = [
         lax.dynamic_slice_in_dim(w_qkv, t * model + me * width, width, 1) for t in range(3)
     ]
-    norms = jnp.stack([ln1_gain, ln1_bias, ln2_gain, ln2_bias], 1)
-    packed = jnp.concatenate(columns + [norms, jnp.zeros((part, 124), BF16)], 1)
+    norms = jnp.stack([ln1_gain, ln1_bias, ln2_gain, ln2_bias], 0)
+    norms = jnp.pad(norms.reshape(-1, 64), ((0, 0), (0, 3 * width - 64)))
+    packed = jnp.concatenate(columns, 1)
+    packed = jnp.concatenate([packed, norms], 0)
     packed = lax.all_gather(packed, "z", axis=0, tiled=True)
     up_part = [
         lax.dynamic_slice_in_dim(w_up, (z * owners + me) * ff_rows, ff_rows, 1)
@@ -688,106 +906,101 @@
     )
     chunk = lax.all_gather(chunk, "z", axis=0, tiled=True)
 
-    units = owners * per_group
-    order = jnp.arange(units, dtype=jnp.int32)
-    source = jnp.sum(
-        jnp.where(slots[:, None, :] == order[None, :, None], order[None, None, :], 0), -1
-    ).reshape(-1)
-    w_heads = packed[:, : 3 * width]
-    vectors = packed[:, 3 * width : 3 * width + 4].astype(F32).T
+    packed = packed.reshape(shares, -1, 3 * width)
+    w_heads = packed[:, :part].reshape(model, 3 * width)
+    vectors = packed[:, part:, :64].astype(F32).reshape(shares, 4, part)
+    vectors = vectors.transpose(1, 0, 2).reshape(4, model)
     gain_one, bias_one, gain_two, bias_two = vectors[0], vectors[1], vectors[2], vectors[3]
 
     half = w_out.shape[0] // 2
     piece = lax.dynamic_slice_in_dim(w_out, core * half, half, 0)
-    piece, pieces[3], pieces[7] = lax.optimization_barrier((piece, pieces[3], pieces[7]))
-    whole_out = lax.all_gather(piece, ("z", "c"), axis=0, tiled=True)
-
-    chunk, pieces[3], pieces[7] = lax.optimization_barrier((chunk, pieces[3], pieces[7]))
-    chunks = spread(chunk)
-    target = source
+
+    def projection(pieces, chosen, before):
+        return project(
+            pieces, chosen, owners, groups, rows, gain_one, bias_one, w_heads, before
+        )
+
     if square:
-        owner = source // per_group
-        target = absolute(owner) * per_group + source - owner * per_group
-
+        near_pieces += [flip(each, "c") for each in near_pieces]
+        projected = projection(near_pieces, [0, 1, 2, 4, 5, 6], None)
+        far_halves[0], far_halves[1], *projected = lax.optimization_barrier(
+            (*far_halves, *projected)
+        )
+        far = jnp.concatenate(far_halves, 0)
+        pieces = near_pieces[:3] + [far] + near_pieces[3:] + [flip(far, "c")]
+        attn_in, qkv = projection([far, pieces[7]], [3, 7], projected)
+    else:
+        attn_in, qkv = projection(pieces, list(range(owners)), None)
+    slots = jnp.concatenate([each[mine, : groups * per_group] for each in pieces])
+    slots = slots.astype(jnp.int32)
+    qkv = qkv.reshape(owners, groups, rows, 3 * width)
+    attended = forward_attention(heads, width, qkv, 0, slots, places, [])
+    for g in range(1, groups):
+        if square and g == 1:
+            near_chunks = spread_near(after(chunk, attended[0]))
+        attended = forward_attention(heads, width, qkv, g, slots, places, attended)
+    attn_heads, exact, logs = attended
+    whole_out = lax.all_gather(after(piece, attn_heads), ("z", "c"), axis=0, tiled=True)
+    attn_heads = lax.all_to_all(
+        attn_heads.reshape(owners, mine, width), CTX, split_axis=0, concat_axis=0, tiled=True
+    )
+    flat = tokens.reshape(mine, model)
     if square:
-        early, late = [0, 1, 2, 4, 5, 6], [3, 7]
-        calls = [early, late]
+        other_chunks = [flip(each, "c") for each in near_chunks]
+        attn_heads = after(attn_heads, *other_chunks)
+    attn_low, residual, ffn_in = attention_output(
+        attn_heads, flat, whole_out, gain_two, bias_two, rows
+    )
+    grad_low = out_grad.reshape(mine, model)
+
+    def feed(sums, others, mine):
+        out_sum, in_sum, *grads = feed_forward(ffn_in, grad_low, sums, others, mine, shares)
+        chunk_grads.append(grads)
+        return out_sum, in_sum
+
+    sums, chunk_grads = None, []
+    if square:
+        sums = feed(sums, other_chunks, near_chunks)
+        far_chunk = spread_far([after(each, ffn_in) for each in near_chunks])
+        far_0, far_1, *sums = lax.optimization_barrier((*far_chunk, *sums))
+        far = jnp.concatenate([far_0, far_1], 0)
+        sums = feed(sums, [flip(far, "c")], [far])
     else:
-        calls = [list(range(owners))]
-    projected = None
-    for places in calls:
-        projected = project(
-            [pieces[k] for k in places],
-            places,
-            owners,
-            groups,
-            rows,
-            gain_one,
-            bias_one,
-            w_heads,
-            projected,
-        )
-    attn_in, qkv = projected
-    chunk, qkv = lax.optimization_barrier((chunk, qkv))
-    chunks = spread(chunk)
-    qkv = qkv.reshape(groups, owners, rows, 3 * width)
-    attended, attn_low = [], []
-    for g in range(groups):
-        attn_heads, *kept = forward_attention(heads, width, qkv, g, source, target)
-        attended.append(kept)
-        attn_low.append(
-            lax.all_to_all(attn_heads, CTX, split_axis=0, concat_axis=2, tiled=True)[0]
-        )
-    attn_low = jnp.concatenate(attn_low, 0)
-
-    stream = tokens.reshape(mine, model).astype(F32)
-    residual = stream + nn(attn_low, whole_out)
-    ffn_full, ffn_norm, ffn_rstd = layer_norm(residual, gain_two, bias_two)
-    ffn_in = ffn_full.astype(BF16)
-    grad_low = out_grad.reshape(mine, model)
-    cotangent = grad_low.astype(F32)
+        chunks = spread(chunk)
+        for k in range(0, owners, 4):
+            sums = feed(sums, chunks[k : k + 2], chunks[k + 2 : k + 4])
+    output = (residual + sums[0]).astype(BF16)
+    grad_resid, grad_branch, grad_heads, norm_grads = norm_gradient(
+        residual, sums[1], grad_low, whole_out, gain_two, owners, rows
+    )
+    grad_gain_two, grad_bias_two = norm_grads[0], norm_grads[1]
+    late = [grad_branch] + [each for grads in chunk_grads for each in grads]
+    grad_heads, grad_branch, *late = lax.optimization_barrier((grad_heads, *late))
+    chunk_grads = [late[:4], late[4:8]] if square else chunk_grads
+    grad_heads = lax.all_to_all(
+        grad_heads, CTX, split_axis=0, concat_axis=0, tiled=True
+    ).reshape(owners, groups, rows, width)
+    out_rows = part // owners
 
     if square:
-        calls = [([4], [0]), ([5, 6], [1, 2]), ([7], [3])]
-    else:
-        calls = [([i, i + 1], [i + 2, i + 3]) for i in range(0, owners, 4)]
-    sums, chunk_grads = None, []
-    for away, here in calls:
-        out_sum, in_sum, *each = feed_forward(
-            ffn_in, grad_low, sums, [chunks[k] for k in away], [chunks[k] for k in here], shares
-        )
-        sums = (out_sum, in_sum)
-        chunk_grads.append(each)
-    output = (residual + sums[0]).astype(BF16)
-    grad_ffn_in = sums[1]
-    grad_gain_two = jnp.sum(grad_ffn_in * ffn_norm, 0)
-    grad_bias_two = jnp.sum(grad_ffn_in, 0)
-    grad_resid = cotangent + norm_back(grad_ffn_in, ffn_norm, ffn_rstd, gain_two)
-    grad_branch = grad_resid.astype(BF16)
-    grad_attn = [
-        nt(grad_branch[g * rows : (g + 1) * rows], whole_out).astype(BF16) for g in range(groups)
-    ]
-    out_rows = part // owners
-
-    if square:
-        places = absolute(jnp.arange(owners))
-        lower = jnp.concatenate([add(low, flip(away, "c")) for _, away, _, low in chunk_grads], 1)
+        outer_away, outer = outer_gradient(attn_low, grad_branch, places, shares)
+        halves = join_upper(
+            [each[2] for each in chunk_grads],
+            [flip(each[0], "c") for each in chunk_grads],
+            outer,
+            flip(outer_away, "c"),
+        )
+        lower = join_lower(
+            [
+                after(each[3], grad_heads, *[half for pair in halves for half in pair])
+                for each in chunk_grads
+            ],
+            [flip(each[1], "c") for each in chunk_grads],
+        )
+        grad_heads = after(grad_heads, lower)
         lower = lax.psum_scatter(
             lower.reshape(shares * 4, part, ff), "z", scatter_dimension=0, tiled=True
         )
-        outer_away, outer = outer_gradient(attn_low, grad_branch, places, shares)
-        outer = add(outer, flip(outer_away, "c"))
-        upper = [add(up, flip(away, "c")) for away, _, up, _ in chunk_grads]
-        upper = [upper[0][0], upper[1][0], upper[1][1], upper[2][0]]
-        halves = [
-            [
-                jnp.concatenate([upper[k][h * model // 2 : (h + 1) * model // 2], outer[k, h]], 0)
-                for h in range(2)
-            ]
-            for k in range(4)
-        ]
-        halves[3][0], halves[3][1], *grad_attn = lax.optimization_barrier((*halves[3], *grad_attn))
-        first = converge_first(*halves[1:])
     else:
         lower = jnp.concatenate([low for _, a, _, b in chunk_grads for low in (a, b)], 1)
         lower = lax.psum_scatter(lower, CTX, scatter_dimension=1, tiled=True)
@@ -800,48 +1013,37 @@
         outer = lax.psum_scatter(
             outer.reshape(model, model), CTX, scatter_dimension=0, tiled=True
         )
-    grad_heads = [
-        lax.all_to_all(each, CTX, split_axis=1, concat_axis=0, tiled=True).reshape(
-            owners, rows, width
-        )
-        for each in grad_attn
-    ]
-
-    grad_qkv, near_in = [], []
-    split = owners // 2 * rows
-    for g in range(groups):
-        slopes = backward_attention(
-            heads, width, qkv, g, grad_heads[g], *attended[g], source, target
-        ).reshape(owners * rows, 3 * width)
-        grad_qkv.append(slopes)
-        if square:
-            away = nt(slopes[split:], w_heads).astype(BF16)
-            kept = nt(slopes[:split], w_heads) + flip(away, "c").astype(F32)
-            near_in.append(kept.astype(BF16).reshape(4, rows, model))
-            if g == 0:
-                *first, near_in[0], grad_heads[1] = lax.optimization_barrier(
-                    (*first, near_in[0], grad_heads[1])
-                )
-        else:
-            away = nt(slopes, w_heads).astype(BF16)
-            near_in.append(lax.psum_scatter(away, CTX, scatter_dimension=0, tiled=True).astype(F32))
+    grad_qkv = backward_attention(heads, width, qkv, grad_heads, exact, logs, slots, places)
     if square:
+        first = converge_first(*halves[1:])
+        columns = jnp.stack([gain_one, bias_one, grad_gain_two, grad_bias_two], 1)
+        columns = jnp.pad(columns, ((0, 0), (0, 124)))
+        *first, columns, grad_qkv = lax.optimization_barrier((*first, columns, grad_qkv))
         upper_terms = converge_last(halves[0], first)
-        near_in[1], grad_qkv[0], grad_qkv[1] = lax.optimization_barrier((near_in[1], *grad_qkv))
-        pairs = [(near_in[0][k], near_in[1][k]) for k in range(4)]
+        grad_qkv = grad_qkv.reshape(owners, mine, 3 * width)
+        away = nt(grad_qkv[4:].reshape(4 * mine, 3 * width), w_heads).astype(BF16)
+        grad_qkv = after(grad_qkv, away)
+        away = flip(away, "c").reshape(4, mine, model)
+        pairs = input_parts(grad_qkv[:4], w_heads, away)
         terms = converge_last(pairs[0], converge_first(*pairs[1:]))
-        near_in = [total(each) for each in terms]
-    grad_attn_in = jnp.concatenate(near_in, 0)
-    attn_in = attn_in.reshape(groups, owners * rows, model)
-    grad_columns = sum(tn(attn_in[g], grad_qkv[g]) for g in range(groups))
-    w_wide = w_heads.astype(F32)
-    summed = sum(jnp.sum(each.astype(F32), 0) for each in grad_qkv)
-    grad_bias_one = jnp.sum(w_wide * summed, 1)
-    grad_gain_one = (jnp.sum(w_wide * grad_columns, 1) - bias_one * grad_bias_one) / gain_one
-    vector_grads = jnp.stack([grad_gain_one, grad_bias_one, grad_gain_two, grad_bias_two], 1)
-    packed_grad = jnp.concatenate(
-        [grad_columns, vector_grads, jnp.zeros((model, 124), F32)], 1
-    ).astype(BF16)
+        grad_attn_in = jnp.concatenate([total(each) for each in terms], 0)
+        packed_grad = projection_gradient(
+            attn_in, grad_qkv.reshape(owners * mine, 3 * width), w_heads, columns
+        )
+        packed_grad = after(packed_grad, lower, *[each for pair in pairs for each in pair])
+    else:
+        grad_qkv = grad_qkv.reshape(owners * mine, 3 * width)
+        away = nt(grad_qkv, w_heads).astype(BF16)
+        grad_attn_in = lax.psum_scatter(away, CTX, scatter_dimension=0, tiled=True).astype(F32)
+        grad_columns = tn(attn_in, grad_qkv)
+        w_wide = w_heads.astype(F32)
+        summed = jnp.sum(grad_qkv.astype(F32), 0)
+        grad_bias_one = jnp.sum(w_wide * summed, 1)
+        grad_gain_one = (jnp.sum(w_wide * grad_columns, 1) - bias_one * grad_bias_one) / gain_one
+        vector_grads = jnp.stack([grad_gain_one, grad_bias_one, grad_gain_two, grad_bias_two], 1)
+        packed_grad = jnp.concatenate(
+            [grad_columns, vector_grads, jnp.zeros((model, 124), F32)], 1
+        ).astype(BF16)
 
     if square:
         lower = lower[0].astype(F32) + sum(
@@ -852,11 +1054,8 @@
         everything = lax.psum_scatter(
             everything.reshape(-1, model), "z", scatter_dimension=0, tiled=True
         )
-        everything, grad_attn_in, grad_down = lax.optimization_barrier(
-            (everything, grad_attn_in, grad_down)
-        )
         grad_upper, grad_outer, grad_proj, vector_grads = unpack(
-            spread(everything), places, shares, part, width
+            spread(after(everything, grad_down)), places, shares, part, width
         )
     else:
         span = 2 * ff
@@ -898,7 +1097,7 @@
         )
         vector_grads = jnp.sum(packed_grad[:, :, 3 * width : 3 * width + 4], 0)
 
-    attn_full, attn_norm, attn_rstd = layer_norm(stream, gain_one, bias_one)
+    attn_full, attn_norm, attn_rstd = layer_norm(flat.astype(F32), gain_one, bias_one)
     in_grad = (grad_resid + norm_back(grad_attn_in, attn_norm, attn_rstd, gain_one)).astype(BF16)
 
     return (

time: 520 us -> 459 us (0.88)
  waiting for transfers between devices: 174 us -> 103 us
  blocking collectives: 0 us -> 38.9 us
  Pallas kernels: 134 us -> 166 us
  other arithmetic: 38.6 us -> 16.3 us
  matrix products: 22.1 us -> 2.37 us
  starting transfers between devices: 57.2 us -> 44.7 us
  local copies, waits for them, and re-layouts: 73.4 us -> 64.6 us
    pallas_call x0 -> x6, Pallas kernels: none -> 36.9 us  [the longest x1 10.1 us: projection_gradient(): pl.pallas_call(kernel, grid=(steps,), in_specs=[pl.BlockSpec((block, mode...]
    ppermute x55 -> x52, waiting for transfers between devices: 127 us -> 91.8 us  [flip(): return lax.ppermute(value, axis, [(0, 1), (1, 0)])]
    all_to_all x4 -> x1, waiting for transfers between devices: 31.5 us -> 0.73 us  [shards(): lax.all_to_all(grad_heads, CTX, split_axis=0, concat_axis=0, tiled=True)]
    all_gather x0 -> x1, blocking collectives: none -> 20.4 us  [shards(): packed = lax.all_gather(packed, 'z', axis=0, tiled=True)]
    all_to_all x0 -> x1, blocking collectives: none -> 18.5 us  [shards(): lax.all_to_all(attn_heads.reshape(owners, mine, width), CTX, split_axis=0...]
    unnamed x153 -> x151, local copies, waits for them, and re-layouts: 27.6 us -> 44 us
    ppermute x1, waiting for transfers between devices: 14.3 us -> 1.77 us  [shards(): lax.ppermute(lower[3], ('a', 'b'), [(0, 3), (3, 0), (1, 2), (2, 1)])]
    all_to_all x4 -> x1, starting transfers between devices: 15.2 us -> 4.26 us  [shards(): lax.all_to_all(grad_heads, CTX, split_axis=0, concat_axis=0, tiled=True)]
  transfers between devices with their start and end apart: 65 -> 58, of which waited for: 27 -> 20; matrix products, arithmetic and copies ran while one was open for 20% -> 8% of each run, Pallas kernels for 25% -> 28%
where the time goes in v2:
time: 459 us; the launch traced here: 453 us
  Pallas kernels  166 us (36%)
  waiting for transfers between devices  103 us (22%)
  local copies, waits for them, and re-layouts  64.6 us (14%)
  starting transfers between devices  44.7 us (10%)
  blocking collectives  38.9 us (8%)
  between operations  16.4 us (4%)
  other arithmetic  16.3 us (4%)
    ppermute x52, waiting for transfers between devices, flip(): return lax.ppermute(value, axis, [(0, 1), (1, 0)])  91.8 us
    pallas_call x2, Pallas kernels, feed_forward(): pl.pallas_call(kernel, grid=(n_all,), in_specs=[whole] * (2 if first else...  44.5 us
    unnamed x151, local copies, waits for them, and re-layouts  44 us
    ppermute x52, starting transfers between devices, flip(): return lax.ppermute(value, axis, [(0, 1), (1, 0)])  39.8 us
    pallas_call x1, Pallas kernels, backward_attention(): pl.pallas_call(kernel, grid_spec=pltpu.PrefetchScalarGridSpec(num_scalar_...  27.5 us
    pallas_call x2, Pallas kernels, forward_attention(): pl.pallas_call(kernel, grid_spec=pltpu.PrefetchScalarGridSpec(num_scalar_...  24.7 us
    all_gather x1, blocking collectives, shards(): packed = lax.all_gather(packed, 'z', axis=0, tiled=True)  20.4 us
    all_to_all x1, blocking collectives, shards(): lax.all_to_all(attn_heads.reshape(owners, mine, width), CTX, split_axis=0...  18.5 us
  transfers between devices with their start and end apart: 58, of which 20 were waited for; matrix products, arithmetic and copies ran while one was open for 8% of the time, Pallas kernels for 28%

profile of v2, /device:TPU:0, one launch (start us, length us, event | category | flops | bytes accessed | tf_op | source)
XLA Modules:
  0.0 453.1 jit_solution(12812944040811538186)
XLA Ops:
  11.1 3.0 collective-permute-start
  14.1 1.5 collective-permute-start.1
  21.3 20.4 %all_gather.9 = bf16[1088,384]{1,0:T(8,128)(2,1)S(1)} all-gather(bf16[272,384]{1,0:T(8,128)(2,1)S(1)} %fusion.10), channel_id=1, replica_groups=mesh['a'=2,'b'=2,'c'=2,'z'=4] {'z'}, dimensions={0}, use_global_device_ids=true | all-gather | bytes 1044480 | tf_op jit(solution)/shard_map/all_gather | solution.py:896
  42.6 1.9 slice.184
  45.0 1.9 slice.185
  49.5 13.5 %shard_map.195 = (bf16[4096,1024]{1,0:T(8,128)(2,1)}, bf16[4096,384]{1,0:T(8,128)(2,1)}) custom-call(bf16[544,1024]{1,0:T(8,128)(2,1)S(1)} %fusion.6.refs_0_, bf16[544,1024]{1,0:T(8,128)(2,1)} %collective-permute-done.refs_1_, bf16[544,1024]{1,0:T(8,128)(2,1)} %collective-permute-done.1.refs_2_, bf16[544,1024]{1,0:T(8,128)(2,1)} %collective-permute-done.4.refs_3_, ...), custom_call_target="tpu_custom_call" | custom-call | flops 1 | bytes 1 | tf_op jit(solution)/shard_map/pallas_call | solution.py:643
  67.0 1.9 copy-done.3
  68.9 3.8 shard_map.196
  72.7 1.7 copy-done.4
  74.5 12.1 %shard_map.197 = (bf16[8,2,256,128]{3,2,1,0:T(8,128)(2,1)S(1)}, f32[2,128,2048]{2,1,0:T(8,128)S(1)}, f32[2,2,2048]{2,1,0:T(2,128)S(1)}) custom-call(s32[64]{0:T(128)S(1)} %convert_element_type.114.slot_ref, s32[8]{0:T(128)S(1)} %fusion.13.at_ref, bf16[8,2,256,384]{3,2,1,0:T(8,128)(2,1)} %bitcast.76), custom_call_target="tpu_custom_call" | custom-call | flops 1 | bytes 1 | tf_op jit(solution)/shard_map/pallas_call | solution.py:109
  88.0 1.5 collective-permute-start.9
  89.5 1.5 collective-permute-start.11
  91.7 1.6 copy-done.13
  93.3 12.5 %shard_map.198 = (bf16[8,2,256,128]{3,2,1,0:T(8,128)(2,1)S(1)}, f32[2,128,2048]{2,1,0:T(8,128)S(1)}, f32[2,2,2048]{2,1,0:T(2,128)S(1)}) custom-call(s32[64]{0:T(128)S(1)} %convert_element_type.114.slot_ref, s32[8]{0:T(128)S(1)} %fusion.13.at_ref, bf16[8,2,256,384]{3,2,1,0:T(8,128)(2,1)} %bitcast.77, ...), custom_call_target="tpu_custom_call", output_to_operand_aliasing={{0}: (3, {}), {1}: (4, {}), {2}: (5, {})} | custom-call | flops 1 | bytes 1 | tf_op jit(solution)/shard_map/pallas_call | solution.py:109
  107.3 29.0 %collective-permute-done.9.refs_6_ = bf16[1024,1024]{1,0:T(8,128)(2,1)} collective-permute-done((bf16[1024,1024]{1,0:T(8,128)(2,1)}, bf16[1024,1024]{1,0:T(8,128)(2,1)}, u32[]{:S(2)}, u32[]{:S(2)}) %collective-permute-start.9) | collective-permute-done | bytes 2097184 | tf_op jit(solution)/shard_map/ppermute | solution.py:795
  137.5 18.5 %all_to_all.10.heads_ref = bf16[8,512,128]{2,1,0:T(8,128)(2,1)} all-to-all(bf16[8,512,128]{2,1,0:T(8,128)(2,1)S(1)} %bitcast.90), channel_id=1, replica_groups=mesh['a'=2,'b'=2,'c'=2,'z'=4] {'a','b','c'}, dimensions={0} | all-to-all | bytes 2097152 | tf_op jit(solution)/shard_map/all_to_all | solution.py:944
  157.3 4.5 shard_map.199
  161.8 1.7 slice.165
  166.0 29.1 %shard_map.200 = (f32[512,1024]{1,0:T(8,128)}, f32[512,1024]{1,0:T(8,128)}, bf16[3,1024,512]{2,1,0:T(8,128)(2,1)}, bf16[4,3,256,512]{3,2,1,0:T(8,128)(2,1)}, bf1...) custom-call(bf16[512,1024]{1,0:T(8,128)(2,1)} %copy-done.7, bf16[512,1024]{1,0:T(8,128)(2,1)} %bitcast.87, ...), custom_call_target="tpu_custom_call" | custom-call | flops 1 | bytes 1 | tf_op jit(solution)/shard_map/pallas_call | solution.py:331
  197.6 4.3 collective-permute-done.15.refs_4_
  201.9 15.4 %shard_map.201 = (f32[512,1024]{1,0:T(8,128)}, f32[512,1024]{1,0:T(8,128)}, bf16[1,1024,512]{2,1,0:T(8,128)(2,1)}, bf16[4,1,256,512]{3,2,1,0:T(8,128)(2,1)}, bf1...) custom-call(bf16[512,1024]{1,0:T(8,128)(2,1)} %copy-done.7, bf16[512,1024]{1,0:T(8,128)(2,1)} %bitcast.88, ...), custom_call_target="tpu_custom_call" | custom-call | flops 1 | bytes 1 | tf_op jit(solution)/shard_map/pallas_call | solution.py:331
  217.3 6.1 %shard_map.202 = (f32[512,1024]{1,0:T(8,128)S(1)}, bf16[512,1024]{1,0:T(8,128)(2,1)S(1)}, bf16[8,512,128]{2,1,0:T(8,128)(2,1)}, f32[8,1024]{1,0:T(8,128)S(1)}) custom-call(f32[512,1024]{1,0:T(8,128)} %get-tuple-element.126.total_ref, f32[512,1024]{1,0:T(8,128)} %get-tuple-element.137.grad_ref, bf16[512,1024]{1,0:T(8,128)(2,1)S(1)} %bitcast.89, ...), custom_call_target="tpu_custom_call" | custom-call | flops 1 | bytes 1 | tf_op jit(solution)/shard_map/pallas_call | solution.py:408
  225.2 1.9 shard_map.203
  228.8 4.3 all-to-all-start.1
  233.5 4.7 %collective-permute-done.17.refs_3_ = bf16[1,1024,512]{2,1,0:T(8,128)(2,1)} collective-permute-done((bf16[1,1024,512]{2,1,0:T(8,128)(2,1)}, bf16[1,1024,512]{2,1,0:T(8,128)(2,1)}, u32[]{:S(2)}, u32[]{:S(2)}) %collective-permute-start.17) | collective-permute-done | bytes 1048608 | tf_op jit(solution)/shard_map/ppermute | solution.py:795
  238.2 5.3 %shard_map.204 = (bf16[640,512]{1,0:T(8,128)(2,1)S(1)}, bf16[640,512]{1,0:T(8,128)(2,1)S(1)}, bf16[640,512]{1,0:T(8,128)(2,1)S(1)}, bf16[640,512]{1,0:T(8,128)(2...) custom-call(bf16[3,1024,512]{2,1,0:T(8,128)(2,1)} %get-tuple-element, ...), custom_call_target="tpu_custom_call" | custom-call | flops 1 | bytes 1 | tf_op jit(solution)/shard_map/pallas_call | solution.py:551
  248.6 1.9 copy-done.9
  250.4 5.0 %shard_map.205 = bf16[4,4,256,512]{3,2,1,0:T(8,128)(2,1)} custom-call(bf16[4,3,256,512]{3,2,1,0:T(8,128)(2,1)S(1)} %copy-done.9, bf16[4,1,256,512]{3,2,1,0:T(8,128)(2,1)S(1)} %copy-done.16, bf16[4,3,256,512]{3,2,1,0:T(8,128)(2,1)} %collective-permute-done.23.refs_2_, bf16[4,1,256,512]{3,2,1,0:T(8,128)(2,1)} %collective-permute-done.24.refs_3_), custom_call_target="tpu_custom_call" | custom-call | flops 1 | bytes 1 | tf_op jit(solution)/shard_map/pallas_call | solution.py:524
  257.4 1.5 collective-permute-start.19
  260.7 2.2 copy-done.15
  262.9 27.5 %shard_map.206 = bf16[8,2,256,384]{3,2,1,0:T(8,128)(2,1)} custom-call(s32[64]{0:T(128)S(1)} %convert_element_type.114.slot_ref, s32[8]{0:T(128)S(1)} %fusion.13.at_ref, bf16[8,2,256,384]{3,2,1,0:T(8,128)(2,1)} %bitcast.78, bf16[8,2,256,128]{3,2,1,0:T(8,128)(2,1)} %bitcast.23.grad_ref, f32[2,128,2048]{2,1,0:T(8,128)S(1)} %copy-done.15, ...), custom_call_target="tpu_custom_call" | custom-call | flops 7516192768 | bytes 1 | tf_op jit(solution)/shard_map/pallas_call | solution.py:213
  293.1 2.4 convolution_convert_fusion
  296.0 1.5 collective-permute-start.33
  297.5 10.1 %shard_map.208.refs_6_ = bf16[1024,512]{1,0:T(8,128)(2,1)S(1)} custom-call(bf16[4096,1024]{1,0:T(8,128)(2,1)} %get-tuple-element.190.normed_ref, bf16[4096,384]{1,0:T(8,128)(2,1)S(1)} %bitcast.84, bf16[1024,384]{1,0:T(8,128)(2,1)S(1)} %bitcast.82, f32[1024,128]{1,0:T(8,128)S(1)} %pad.14.columns_ref), custom_call_target="tpu_custom_call" | custom-call | flops 1 | bytes 1 | tf_op jit(solution)/shard_map/pallas_call | solution.py:495
  308.9 2.0 copy-done.59
  310.9 6.0 %shard_map.207 = (bf16[256,1024]{1,0:T(8,128)(2,1)S(1)}, bf16[256,1024]{1,0:T(8,128)(2,1)S(1)}, bf16[256,1024]{1,0:T(8,128)(2,1)S(1)}, bf16[256,1024]{1,0:T(8,12...) custom-call(bf16[4,512,384]{2,1,0:T(8,128)(2,1)} %slice.169.slope_re, ...), custom_call_target="tpu_custom_call" | custom-call | flops 1 | bytes 1 | tf_op jit(solution)/shard_map/pallas_call | solution.py:445
  323.3 9.0 %reduce-scatter.3.cloned.1.call-done = bf16[4,256,512]{2,1,0:T(8,128)(2,1)} async-done(((bf16[16,256,512]{2,1,0:T(8,128)(2,1)}), bf16[4,256,512]{2,1,0:T(8,128)(2,1)}) %reduce-scatter.3.cloned.1.call-update) | async-done | bytes 1048592 | tf_op jit(solution)/shard_map/reduce_scatter | solution.py:1001
  335.6 3.2 shard_map.209
  340.1 1.5 collective-permute-start.34
  341.6 1.5 collective-permute-start.35
  343.9 1.5 collective-permute-start.27
  345.4 3.9 collective-permute-done.34
  349.3 4.8 %collective-permute-done.35 = bf16[256,512]{1,0:T(8,128)(2,1)S(1)} collective-permute-done((bf16[256,512]{1,0:T(8,128)(2,1)S(1)}, bf16[256,512]{1,0:T(8,128)(2,1)S(1)}, u32[]{:S(2)}, u32[]{:S(2)}) %collective-permute-start.35) | collective-permute-done | bytes 262176 | tf_op jit(solution)/shard_map/ppermute | solution.py:795
  354.1 1.8 collective-permute-done.36
  359.5 1.5 collective-permute-start.29
  361.7 4.6 %collective-permute-done.38.refs_2_ = bf16[256,512]{1,0:T(8,128)(2,1)S(1)} collective-permute-done((bf16[256,512]{1,0:T(8,128)(2,1)S(1)}, bf16[256,512]{1,0:T(8,128)(2,1)S(1)}, u32[]{:S(2)}, u32[]{:S(2)}) %collective-permute-start.38) | collective-permute-done | bytes 262176 | tf_op jit(solution)/shard_map/ppermute | solution.py:795
  366.3 5.5 %collective-permute-done.37.refs_1_ = bf16[256,512]{1,0:T(8,128)(2,1)S(1)} collective-permute-done((bf16[256,512]{1,0:T(8,128)(2,1)S(1)}, bf16[256,512]{1,0:T(8,128)(2,1)S(1)}, u32[]{:S(2)}, u32[]{:S(2)}) %collective-permute-start.37) | collective-permute-done | bytes 262176 | tf_op jit(solution)/shard_map/ppermute | solution.py:795
  371.9 1.5 collective-permute-start.39
  373.3 1.5 collective-permute-start.40
  375.8 9.0 %collective-permute-done.39 = bf16[128,512]{1,0:T(8,128)(2,1)S(1)} collective-permute-done((bf16[128,512]{1,0:T(8,128)(2,1)S(1)}, bf16[128,512]{1,0:T(8,128)(2,1)S(1)}, u32[]{:S(2)}, u32[]{:S(2)}) %collective-permute-start.39) | collective-permute-done | bytes 131104 | tf_op jit(solution)/shard_map/ppermute | solution.py:795
  384.8 1.5 collective-permute-start.28
  388.6 1.5 collective-permute-start.30
  390.1 2.9 shard_map.210
  393.0 1.5 collective-permute-start.46
  394.5 3.6 add_convert_fusion.1
  401.4 9.8 %collective-permute-done.31 = bf16[256,1024]{1,0:T(8,128)(2,1)} collective-permute-done((bf16[256,1024]{1,0:T(8,128)(2,1)S(1)}, bf16[256,1024]{1,0:T(8,128)(2,1)}, u32[]{:S(2)}, u32[]{:S(2)}) %collective-permute-start.31) | collective-permute-done | bytes 524320 | tf_op jit(solution)/shard_map/ppermute | solution.py:795
  411.2 1.5 convert_add_fusion
  412.7 9.1 %collective-permute-done.46.refs_2_.refs_10_.refs_18_ = bf16[288,1024]{1,0:T(8,128)(2,1)S(1)} collective-permute-done((bf16[288,1024]{1,0:T(8,128)(2,1)}, bf16[288,1024]{1,0:T(8,128)(2,1)S(1)}, u32[]{:S(2)}, u32[]{:S(2)}) %collective-permute-start.46) | collective-permute-done | bytes 589856 | tf_op jit(solution)/shard_map/ppermute | solution.py:795
  421.8 1.5 collective-permute-start.47
  423.7 1.5 collective-permute-start.48
  426.5 2.5 collective-permute-done.47
  429.0 1.5 collective-permute-done.48
  430.7 1.7 add_convert_fusion
  434.5 7.4 %shard_map.211 = (f32[2,128,4096]{2,1,0:T(8,128)}, f32[8,32,1024]{2,1,0:T(8,128)}, f32[2,128,3072]{2,1,0:T(8,128)}, f32[2,128,128]{2,1,0:T(8,128)}) custom-call(s32[8]{0:T(128)} %copy-done.38, bf16[288,1024]{1,0:T(8,128)(2,1)} %reduce-scatter.5.cloned.1.call-done.refs_0_.refs_8_.refs_16_, bf16[288,1024]{1,0:T(8,128)(2,1)} %copy-done.51, ...), custom_call_target="tpu_custom_call" | custom-call | tf_op jit(solution)/shard_map/pallas_call | solution.py:755
  (296 shorter events, 75.0 us)
Async XLA Ops:
  8.0 83.0 %copy-start = (bf16[256,1024]{1,0:T(8,128)(2,1)S(1)}, bf16[256,1024]{1,0:T(8,128)(2,1)}, u32[]{:S(2)}) copy-start(bf16[256,1024]{1,0:T(8,128)(2,1)} %param.21) | copy-start | bytes 1572868
  8.1 79.9 %all-gather.3.cloned.1.call-start = ((), (), s32[]{:S(2)}) async-start(), calls=%async_computation.4 | async-start | bytes 2621440 | tf_op jit(solution)/shard_map/all_gather | solution.py:907
  11.1 30.6 %collective-permute-start = (bf16[544,1024]{1,0:T(8,128)(2,1)S(1)}, bf16[544,1024]{1,0:T(8,128)(2,1)}, u32[]{:S(2)}, u32[]{:S(2)}) collective-permute-start(bf16[544,1024]{1,0:T(8,128)(2,1)S(1)} %fusion.6.refs_0_), channel_id=1, source_target_pairs={{0,8},{8,0},{1,9},{9,1},{2,10},{10,2},{3,11},{11,3},{4,12},{12,4},... | collective-permute-start | bytes 3342344 | tf_op jit(solution)/shard_map/ppermute | solution.py:795
  14.1 27.6 %collective-permute-start.1 = (bf16[544,1024]{1,0:T(8,128)(2,1)S(1)}, bf16[544,1024]{1,0:T(8,128)(2,1)}, u32[]{:S(2)}, u32[]{:S(2)}) collective-permute-start(bf16[544,1024]{1,0:T(8,128)(2,1)S(1)} %fusion.6.refs_0_), channel_id=1, source_target_pairs={{0,16},{16,0},{1,17},{17,1},{2,18},{18,2},{3,19},{19,3},{4,20},{20... | collective-permute-start | bytes 3342344 | tf_op jit(solution)/shard_map/ppermute | solution.py:795
  41.8 114.2 %all-gather.5.cloned.1.call-start = ((), (), s32[]{:S(2)}) async-start(), calls=%async_computation.5 | async-start | bytes 2359296 | tf_op jit(solution)/shard_map/all_gather | solution.py:943
  41.8 7.7 %collective-permute-start.4 = (bf16[544,1024]{1,0:T(8,128)(2,1)S(1)}, bf16[544,1024]{1,0:T(8,128)(2,1)}, u32[]{:S(2)}, u32[]{:S(2)}) collective-permute-start(bf16[544,1024]{1,0:T(8,128)(2,1)S(1)} %fusion.6.refs_0_), channel_id=1, source_target_pairs={{0,4},{4,0},{1,5},{5,1},{2,6},{6,2},{3,7},{7,3},{8,12},{12,8},{9,1... | collective-permute-start | bytes 3342344 | tf_op jit(solution)/shard_map/ppermute | solution.py:795
  41.9 7.6 %collective-permute-start.5 = (bf16[544,1024]{1,0:T(8,128)(2,1)}, bf16[544,1024]{1,0:T(8,128)(2,1)}, u32[]{:S(2)}, u32[]{:S(2)}) collective-permute-start(bf16[544,1024]{1,0:T(8,128)(2,1)} %collective-permute-done.refs_1_), channel_id=1, source_target_pairs={{0,4},{4,0},{1,5},{5,1},{2,6},{6,2},{3,7},{7,3},{8,12},{12,8},{9,1... | collective-permute-start | bytes 3342344 | tf_op jit(solution)/shard_map/ppermute | solution.py:795
  42.4 7.1 %collective-permute-start.6 = (bf16[544,1024]{1,0:T(8,128)(2,1)}, bf16[544,1024]{1,0:T(8,128)(2,1)}, u32[]{:S(2)}, u32[]{:S(2)}) collective-permute-start(bf16[544,1024]{1,0:T(8,128)(2,1)} %collective-permute-done.1.refs_2_), channel_id=1, source_target_pairs={{0,4},{4,0},{1,5},{5,1},{2,6},{6,2},{3,7},{7,3},{8,12},{12,8},{9,1... | collective-permute-start | bytes 3342344 | tf_op jit(solution)/shard_map/ppermute | solution.py:795
  42.6 347.5 %copy-start.38 = (s32[8]{0:T(128)}, s32[8]{0:T(128)S(1)}, u32[]{:S(2)}) copy-start(s32[8]{0:T(128)S(1)} %fusion.13.at_ref) | copy-start | bytes 100
  44.5 18.6 %collective-permute-start.2 = (bf16[272,1024]{1,0:T(8,128)(2,1)}, bf16[272,1024]{1,0:T(8,128)(2,1)}, u32[]{:S(2)}, u32[]{:S(2)}) collective-permute-start(bf16[272,1024]{1,0:T(8,128)(2,1)} %slice.184), channel_id=1, source_target_pairs={{0,8},{8,0},{1,9},{9,1},{2,10},{10,2},{3,11},{11,3},{4,12},{12,4},... | collective-permute-start | bytes 1671176 | tf_op jit(solution)/shard_map/ppermute | solution.py:795
  46.9 16.1 %collective-permute-start.3 = (bf16[272,1024]{1,0:T(8,128)(2,1)}, bf16[272,1024]{1,0:T(8,128)(2,1)S(1)}, u32[]{:S(2)}, u32[]{:S(2)}) collective-permute-start(bf16[272,1024]{1,0:T(8,128)(2,1)} %slice.185), channel_id=1, source_target_pairs={{0,16},{16,0},{1,17},{17,1},{2,18},{18,2},{3,19},{19,3},{4,20},{20... | collective-permute-start | bytes 1671176 | tf_op jit(solution)/shard_map/ppermute | solution.py:795
  64.2 2.8 collective-permute-start.7
  88.0 48.3 %collective-permute-start.9 = (bf16[1024,1024]{1,0:T(8,128)(2,1)}, bf16[1024,1024]{1,0:T(8,128)(2,1)}, u32[]{:S(2)}, u32[]{:S(2)}) collective-permute-start(bf16[1024,1024]{1,0:T(8,128)(2,1)} %all-gather.3.cloned.1.call-done.refs_5_), channel_id=1, source_target_pairs={{0,8},{8,0},{1,9},{9,1},{2,10},{10,2},{3,11},{11,3},{4,12},{12,4},... | collective-permute-start | bytes 6291464 | tf_op jit(solution)/shard_map/ppermute | solution.py:795
  89.5 48.0 %collective-permute-start.11 = (bf16[1024,1024]{1,0:T(8,128)(2,1)}, bf16[1024,1024]{1,0:T(8,128)(2,1)}, u32[]{:S(2)}, u32[]{:S(2)}) collective-permute-start(bf16[1024,1024]{1,0:T(8,128)(2,1)} %all-gather.3.cloned.1.call-done.refs_5_), channel_id=1, source_target_pairs={{0,16},{16,0},{1,17},{17,1},{2,18},{18,2},{3,19},{19,3},{4,20},{20... | collective-permute-start | bytes 6291464 | tf_op jit(solution)/shard_map/ppermute | solution.py:795
  107.2 54.6 %copy-start.36 = (f32[2,2,2048]{2,1,0:T(2,128)}, f32[2,2,2048]{2,1,0:T(2,128)S(1)}, u32[]{:S(2)}) copy-start(f32[2,2,2048]{2,1,0:T(2,128)S(1)} %get-tuple-element.175.log_ref) | copy-start | bytes 98308
  107.2 48.9 %copy-start.2 = (bf16[2,256,1024]{2,1,0:T(8,128)(2,1)S(1)}, bf16[2,256,1024]{2,1,0:T(8,128)(2,1)}, u32[]{:S(2)}) copy-start(bf16[2,256,1024]{2,1,0:T(8,128)(2,1)} %param.14) | copy-start | bytes 3145732
  107.2 48.8 %collective-permute-start.8 = (bf16[1024,1024]{1,0:T(8,128)(2,1)}, bf16[1024,1024]{1,0:T(8,128)(2,1)}, u32[]{:S(2)}, u32[]{:S(2)}) collective-permute-start(bf16[1024,1024]{1,0:T(8,128)(2,1)} %all-gather.3.cloned.1.call-done.refs_5_), channel_id=1, source_target_pairs={{0,4},{4,0},{1,5},{5,1},{2,6},{6,2},{3,7},{7,3},{8,12},{12,8},{9,1... | collective-permute-start | bytes 6291464 | tf_op jit(solution)/shard_map/ppermute | solution.py:795
  136.3 19.7 %collective-permute-start.10 = (bf16[1024,1024]{1,0:T(8,128)(2,1)}, bf16[1024,1024]{1,0:T(8,128)(2,1)}, u32[]{:S(2)}, u32[]{:S(2)}) collective-permute-start(bf16[1024,1024]{1,0:T(8,128)(2,1)} %collective-permute-done.9.refs_6_), channel_id=1, source_target_pairs={{0,4},{4,0},{1,5},{5,1},{2,6},{6,2},{3,7},{7,3},{8,12},{12,8},{9,1... | collective-permute-start | bytes 6291464 | tf_op jit(solution)/shard_map/ppermute | solution.py:795
  137.5 18.5 %collective-permute-start.12 = (bf16[1024,1024]{1,0:T(8,128)(2,1)}, bf16[1024,1024]{1,0:T(8,128)(2,1)}, u32[]{:S(2)}, u32[]{:S(2)}) collective-permute-start(bf16[1024,1024]{1,0:T(8,128)(2,1)} %collective-permute-done.11.refs_7_), channel_id=1, source_target_pairs={{0,4},{4,0},{1,5},{5,1},{2,6},{6,2},{3,7},{7,3},{8,12},{12,8},{9,1... | collective-permute-start | bytes 6291464 | tf_op jit(solution)/shard_map/ppermute | solution.py:795
  163.5 31.7 %collective-permute-start.14 = (bf16[512,1024]{1,0:T(8,128)(2,1)S(1)}, bf16[512,1024]{1,0:T(8,128)(2,1)S(1)}, u32[]{:S(2)}, u32[]{:S(2)}) collective-permute-start(bf16[512,1024]{1,0:T(8,128)(2,1)S(1)} %slice.165), channel_id=1, source_target_pairs={{0,16},{16,0},{1,17},{17,1},{2,18},{18,2},{3,19},{19,3},{4,20},{20... | collective-permute-start | bytes 3145736 | tf_op jit(solution)/shard_map/ppermute | solution.py:795
  165.4 29.8 %collective-permute-start.13 = (bf16[512,1024]{1,0:T(8,128)(2,1)S(1)}, bf16[512,1024]{1,0:T(8,128)(2,1)S(1)}, u32[]{:S(2)}, u32[]{:S(2)}) collective-permute-start(bf16[512,1024]{1,0:T(8,128)(2,1)S(1)} %slice.164), channel_id=1, source_target_pairs={{0,8},{8,0},{1,9},{9,1},{2,10},{10,2},{3,11},{11,3},{4,12},{12,4},... | collective-permute-start | bytes 3145736 | tf_op jit(solution)/shard_map/ppermute | solution.py:795
  197.6 4.4 collective-permute-start.15
  224.7 13.5 %collective-permute-start.16 = (bf16[3,1024,512]{2,1,0:T(8,128)(2,1)}, bf16[3,1024,512]{2,1,0:T(8,128)(2,1)}, u32[]{:S(2)}, u32[]{:S(2)}) collective-permute-start(bf16[3,1024,512]{2,1,0:T(8,128)(2,1)} %get-tuple-element.151), channel_id=1, source_target_pairs={{0,4},{4,0},{1,5},{5,1},{2,6},{6,2},{3,7},{7,3},{8,12},{12,8},{9,1... | collective-permute-start | bytes 9437192 | tf_op jit(solution)/shard_map/ppermute | solution.py:795
  224.9 23.7 %collective-permute-start.23 = (bf16[4,3,256,512]{3,2,1,0:T(8,128)(2,1)}, bf16[4,3,256,512]{3,2,1,0:T(8,128)(2,1)}, u32[]{:S(2)}, u32[]{:S(2)}) collective-permute-start(bf16[4,3,256,512]{3,2,1,0:T(8,128)(2,1)} %get-tuple-element.171), channel_id=1, source_target_pairs={{0,4},{4,0},{1,5},{5,1},{2,6},{6,2},{3,7},{7,3},{8,12},{12,8},{9,1... | collective-permute-start | bytes 9437192 | tf_op jit(solution)/shard_map/ppermute | solution.py:795
  228.2 5.3 %collective-permute-start.18 = (bf16[4,2,128,512]{3,2,1,0:T(8,128)(2,1)S(1)}, bf16[4,2,128,512]{3,2,1,0:T(8,128)(2,1)}, u32[]{:S(2)}, u32[]{:S(2)}) collective-permute-start(bf16[4,2,128,512]{3,2,1,0:T(8,128)(2,1)S(1)} %get-tuple-element.156), channel_id=1, source_target_pairs={{0,4},{4,0},{1,5},{5,1},{2,6},{6,2},{3,7},{7,3},{8,12},{12,8},{9,1... | collective-permute-start | bytes 3145736 | tf_op jit(solution)/shard_map/ppermute | solution.py:795
  228.3 9.9 %collective-permute-start.17 = (bf16[1,1024,512]{2,1,0:T(8,128)(2,1)}, bf16[1,1024,512]{2,1,0:T(8,128)(2,1)}, u32[]{:S(2)}, u32[]{:S(2)}) collective-permute-start(bf16[1,1024,512]{2,1,0:T(8,128)(2,1)} %get-tuple-element.152), channel_id=1, source_target_pairs={{0,4},{4,0},{1,5},{5,1},{2,6},{6,2},{3,7},{7,3},{8,12},{12,8},{9,1... | collective-permute-start | bytes 3145736 | tf_op jit(solution)/shard_map/ppermute | solution.py:795
  228.7 19.8 %collective-permute-start.24 = (bf16[4,1,256,512]{3,2,1,0:T(8,128)(2,1)}, bf16[4,1,256,512]{3,2,1,0:T(8,128)(2,1)}, u32[]{:S(2)}, u32[]{:S(2)}) collective-permute-start(bf16[4,1,256,512]{3,2,1,0:T(8,128)(2,1)} %get-tuple-element.172), channel_id=1, source_target_pairs={{0,4},{4,0},{1,5},{5,1},{2,6},{6,2},{3,7},{7,3},{8,12},{12,8},{9,1... | collective-permute-start | bytes 3145736 | tf_op jit(solution)/shard_map/ppermute | solution.py:795
  228.8 19.7 %all-to-all-start.1 = ((bf16[8,512,128]{2,1,0:T(8,128)(2,1)}), bf16[8,512,128]{2,1,0:T(8,128)(2,1)}, u32[]{:S(2)}, u32[]{:S(2)}) async-start(bf16[8,512,128]{2,1,0:T(8,128)(2,1)} %get-tuple-element.164), calls=%async_computation.1 | async-start | bytes 2097152 | tf_op jit(solution)/shard_map/all_to_all | solution.py:980
  233.1 99.2 %reduce-scatter.3.cloned.1.call-start = ((), (), s32[]{:S(2)}) async-start(), calls=%async_computation.6 | async-start | bytes 5242880 | tf_op jit(solution)/shard_map/reduce_scatter | solution.py:1001
  255.4 137.6 %reduce-scatter.5.cloned.1.call-start = ((), (), s32[]{:S(2)}) async-start(), calls=%async_computation.7 | async-start | bytes 2949120 | tf_op jit(solution)/shard_map/reduce_scatter | solution.py:1054
  256.6 33.8 %collective-permute-start.20 = (bf16[640,512]{1,0:T(8,128)(2,1)}, bf16[640,512]{1,0:T(8,128)(2,1)S(1)}, u32[]{:S(2)}, u32[]{:S(2)}) collective-permute-start(bf16[640,512]{1,0:T(8,128)(2,1)} %get-tuple-element.160), channel_id=1, source_target_pairs={{0,8},{8,0},{1,9},{9,1},{2,10},{10,2},{3,11},{11,3},{4,12},{12,4},... | collective-permute-start | bytes 1966088 | tf_op jit(solution)/shard_map/ppermute | solution.py:795
  257.4 34.1 %collective-permute-start.19 = (bf16[640,512]{1,0:T(8,128)(2,1)}, bf16[640,512]{1,0:T(8,128)(2,1)S(1)}, u32[]{:S(2)}, u32[]{:S(2)}) collective-permute-start(bf16[640,512]{1,0:T(8,128)(2,1)} %get-tuple-element.158), channel_id=1, source_target_pairs={{0,16},{16,0},{1,17},{17,1},{2,18},{18,2},{3,19},{19,3},{4,20},{20... | collective-permute-start | bytes 1966088 | tf_op jit(solution)/shard_map/ppermute | solution.py:795
  258.9 33.7 %collective-permute-start.21 = (bf16[640,512]{1,0:T(8,128)(2,1)}, bf16[640,512]{1,0:T(8,128)(2,1)S(1)}, u32[]{:S(2)}, u32[]{:S(2)}) collective-permute-start(bf16[640,512]{1,0:T(8,128)(2,1)} %copy-done.41), channel_id=1, source_target_pairs={{0,8},{8,0},{1,9},{9,1},{2,10},{10,2},{3,11},{11,3},{4,12},{12,4},... | collective-permute-start | bytes 1966088 | tf_op jit(solution)/shard_map/ppermute | solution.py:795
  259.4 33.1 %collective-permute-start.22 = (bf16[640,512]{1,0:T(8,128)(2,1)}, bf16[640,512]{1,0:T(8,128)(2,1)S(1)}, u32[]{:S(2)}, u32[]{:S(2)}) collective-permute-start(bf16[640,512]{1,0:T(8,128)(2,1)} %copy-done.40), channel_id=1, source_target_pairs={{0,16},{16,0},{1,17},{17,1},{2,18},{18,2},{3,19},{19,3},{4,20},{20... | collective-permute-start | bytes 1966088 | tf_op jit(solution)/shard_map/ppermute | solution.py:795
  295.5 13.4 %collective-permute-start.25 = (bf16[2048,1024]{1,0:T(8,128)(2,1)S(1)}, bf16[2048,1024]{1,0:T(8,128)(2,1)S(1)}, u32[]{:S(2)}, u32[]{:S(2)}) collective-permute-start(bf16[2048,1024]{1,0:T(8,128)(2,1)S(1)} %convolution_convert_fusion), channel_id=1, source_target_pairs={{0,4},{4,0},{1,5},{5,1},{2,6},{6,2},{3,7},{7,3},{8,12},{12,8},{9,1... | collective-permute-start | bytes 12582920 | tf_op jit(solution)/shard_map/ppermute | solution.py:795
  295.6 36.7 %collective-permute-start.32 = (bf16[640,512]{1,0:T(8,128)(2,1)}, bf16[640,512]{1,0:T(8,128)(2,1)}, u32[]{:S(2)}, u32[]{:S(2)}) collective-permute-start(bf16[640,512]{1,0:T(8,128)(2,1)} %add_convert_fusion.2), channel_id=1, source_target_pairs={{0,16},{16,0},{1,17},{17,1},{2,18},{18,2},{3,19},{19,3},{4,20},{20... | collective-permute-start | bytes 1966088 | tf_op jit(solution)/shard_map/ppermute | solution.py:795
  296.0 36.3 %collective-permute-start.33 = (bf16[640,512]{1,0:T(8,128)(2,1)}, bf16[640,512]{1,0:T(8,128)(2,1)}, u32[]{:S(2)}, u32[]{:S(2)}) collective-permute-start(bf16[640,512]{1,0:T(8,128)(2,1)} %add_convert_fusion.3), channel_id=1, source_target_pairs={{0,8},{8,0},{1,9},{9,1},{2,10},{10,2},{3,11},{11,3},{4,12},{12,4},... | collective-permute-start | bytes 1966088 | tf_op jit(solution)/shard_map/ppermute | solution.py:795
  340.1 34.8 %copy-start.35 = (bf16[256,1024]{1,0:T(8,128)(2,1)S(1)}, bf16[256,1024]{1,0:T(8,128)(2,1)}, u32[]{:S(2)}) copy-start(bf16[256,1024]{1,0:T(8,128)(2,1)} %copy-done.34) | copy-start | bytes 1572868
  340.1 9.3 %collective-permute-start.34 = (bf16[256,512]{1,0:T(8,128)(2,1)S(1)}, bf16[256,512]{1,0:T(8,128)(2,1)S(1)}, u32[]{:S(2)}, u32[]{:S(2)}) collective-permute-start(bf16[256,512]{1,0:T(8,128)(2,1)S(1)} %get-tuple-element.205), channel_id=1, source_target_pairs={{0,8},{8,0},{1,9},{9,1},{2,10},{10,2},{3,11},{11,3},{4,12},{12,4},... | collective-permute-start | bytes 786440 | tf_op jit(solution)/shard_map/ppermute | solution.py:795
  341.6 12.5 %collective-permute-start.35 = (bf16[256,512]{1,0:T(8,128)(2,1)S(1)}, bf16[256,512]{1,0:T(8,128)(2,1)S(1)}, u32[]{:S(2)}, u32[]{:S(2)}) collective-permute-start(bf16[256,512]{1,0:T(8,128)(2,1)S(1)} %get-tuple-element.207), channel_id=1, source_target_pairs={{0,16},{16,0},{1,17},{17,1},{2,18},{18,2},{3,19},{19,3},{4,20},{20... | collective-permute-start | bytes 786440 | tf_op jit(solution)/shard_map/ppermute | solution.py:795
  343.1 12.8 %collective-permute-start.36 = (bf16[256,512]{1,0:T(8,128)(2,1)S(1)}, bf16[256,512]{1,0:T(8,128)(2,1)S(1)}, u32[]{:S(2)}, u32[]{:S(2)}) collective-permute-start(bf16[256,512]{1,0:T(8,128)(2,1)S(1)} %get-tuple-element.206), channel_id=1, source_target_pairs={{0,24},{24,0},{8,16},{16,8},{1,25},{25,1},{9,17},{17,9},{2,26},{26... | collective-permute-start | bytes 786440 | tf_op jit(solution)/shard_map/ppermute | solution.py:1051
  343.9 29.5 %collective-permute-start.27 = (bf16[256,1024]{1,0:T(8,128)(2,1)S(1)}, bf16[256,1024]{1,0:T(8,128)(2,1)S(1)}, u32[]{:S(2)}, u32[]{:S(2)}) collective-permute-start(bf16[256,1024]{1,0:T(8,128)(2,1)S(1)} %copy-done.49), channel_id=1, source_target_pairs={{0,8},{8,0},{1,9},{9,1},{2,10},{10,2},{3,11},{11,3},{4,12},{12,4},... | collective-permute-start | bytes 1572872 | tf_op jit(solution)/shard_map/ppermute | solution.py:795
  357.0 30.0 %copy-start.33 = (bf16[256,1024]{1,0:T(8,128)(2,1)S(1)}, bf16[256,1024]{1,0:T(8,128)(2,1)}, u32[]{:S(2)}) copy-start(bf16[256,1024]{1,0:T(8,128)(2,1)} %copy-done.32) | copy-start | bytes 1572868
  357.0 9.3 %collective-permute-start.38 = (bf16[256,512]{1,0:T(8,128)(2,1)S(1)}, bf16[256,512]{1,0:T(8,128)(2,1)S(1)}, u32[]{:S(2)}, u32[]{:S(2)}) collective-permute-start(bf16[256,512]{1,0:T(8,128)(2,1)S(1)} %fusion.8.refs_0_), channel_id=1, source_target_pairs={{0,16},{16,0},{1,17},{17,1},{2,18},{18,2},{3,19},{19,3},{4,20},{20... | collective-permute-start | bytes 786440 | tf_op jit(solution)/shard_map/ppermute | solution.py:795
  357.7 14.2 %collective-permute-start.37 = (bf16[256,512]{1,0:T(8,128)(2,1)S(1)}, bf16[256,512]{1,0:T(8,128)(2,1)S(1)}, u32[]{:S(2)}, u32[]{:S(2)}) collective-permute-start(bf16[256,512]{1,0:T(8,128)(2,1)S(1)} %fusion.8.refs_0_), channel_id=1, source_target_pairs={{0,8},{8,0},{1,9},{9,1},{2,10},{10,2},{3,11},{11,3},{4,12},{12,4},... | collective-permute-start | bytes 786440 | tf_op jit(solution)/shard_map/ppermute | solution.py:795
  359.5 26.9 %collective-permute-start.29 = (bf16[256,1024]{1,0:T(8,128)(2,1)S(1)}, bf16[256,1024]{1,0:T(8,128)(2,1)S(1)}, u32[]{:S(2)}, u32[]{:S(2)}) collective-permute-start(bf16[256,1024]{1,0:T(8,128)(2,1)S(1)} %copy-done.47), channel_id=1, source_target_pairs={{0,16},{16,0},{1,17},{17,1},{2,18},{18,2},{3,19},{19,3},{4,20},{20... | collective-permute-start | bytes 1572872 | tf_op jit(solution)/shard_map/ppermute | solution.py:795
  361.0 37.1 %collective-permute-start.26 = (bf16[256,1024]{1,0:T(8,128)(2,1)S(1)}, bf16[256,1024]{1,0:T(8,128)(2,1)}, u32[]{:S(2)}, u32[]{:S(2)}) collective-permute-start(bf16[256,1024]{1,0:T(8,128)(2,1)S(1)} %copy-done.45), channel_id=1, source_target_pairs={{0,8},{8,0},{1,9},{9,1},{2,10},{10,2},{3,11},{11,3},{4,12},{12,4},... | collective-permute-start | bytes 1572872 | tf_op jit(solution)/shard_map/ppermute | solution.py:795
  366.3 20.6 %collective-permute-start.41 = (bf16[256,512]{1,0:T(8,128)(2,1)S(1)}, bf16[256,512]{1,0:T(8,128)(2,1)S(1)}, u32[]{:S(2)}, u32[]{:S(2)}) collective-permute-start(bf16[256,512]{1,0:T(8,128)(2,1)S(1)} %fusion.8.refs_0_), channel_id=1, source_target_pairs={{0,4},{4,0},{1,5},{5,1},{2,6},{6,2},{3,7},{7,3},{8,12},{12,8},{9,1... | collective-permute-start | bytes 786440 | tf_op jit(solution)/shard_map/ppermute | solution.py:795
  371.9 12.9 %collective-permute-start.39 = (bf16[128,512]{1,0:T(8,128)(2,1)S(1)}, bf16[128,512]{1,0:T(8,128)(2,1)S(1)}, u32[]{:S(2)}, u32[]{:S(2)}) collective-permute-start(bf16[128,512]{1,0:T(8,128)(2,1)S(1)} %slice.200), channel_id=1, source_target_pairs={{0,8},{8,0},{1,9},{9,1},{2,10},{10,2},{3,11},{11,3},{4,12},{12,4},... | collective-permute-start | bytes 393224 | tf_op jit(solution)/shard_map/ppermute | solution.py:795
  373.3 12.9 %collective-permute-start.40 = (bf16[128,512]{1,0:T(8,128)(2,1)S(1)}, bf16[128,512]{1,0:T(8,128)(2,1)S(1)}, u32[]{:S(2)}, u32[]{:S(2)}) collective-permute-start(bf16[128,512]{1,0:T(8,128)(2,1)S(1)} %slice.201), channel_id=1, source_target_pairs={{0,16},{16,0},{1,17},{17,1},{2,18},{18,2},{3,19},{19,3},{4,20},{20... | collective-permute-start | bytes 393224 | tf_op jit(solution)/shard_map/ppermute | solution.py:795
  384.8 15.2 %collective-permute-start.28 = (bf16[256,1024]{1,0:T(8,128)(2,1)}, bf16[256,1024]{1,0:T(8,128)(2,1)}, u32[]{:S(2)}, u32[]{:S(2)}) collective-permute-start(bf16[256,1024]{1,0:T(8,128)(2,1)} %add_convert_fusion.5), channel_id=1, source_target_pairs={{0,16},{16,0},{1,17},{17,1},{2,18},{18,2},{3,19},{19,3},{4,20},{20... | collective-permute-start | bytes 1572872 | tf_op jit(solution)/shard_map/ppermute | solution.py:795
  386.3 1.7 collective-permute-start.42
  386.4 2.2 collective-permute-start.43
  386.9 3.1 collective-permute-start.44
  388.0 23.2 %collective-permute-start.31 = (bf16[256,1024]{1,0:T(8,128)(2,1)S(1)}, bf16[256,1024]{1,0:T(8,128)(2,1)}, u32[]{:S(2)}, u32[]{:S(2)}) collective-permute-start(bf16[256,1024]{1,0:T(8,128)(2,1)S(1)} %copy-done.43), channel_id=1, source_target_pairs={{0,16},{16,0},{1,17},{17,1},{2,18},{18,2},{3,19},{19,3},{4,20},{20... | collective-permute-start | bytes 1572872 | tf_op jit(solution)/shard_map/ppermute | solution.py:795
  388.6 22.6 %collective-permute-start.30 = (bf16[256,1024]{1,0:T(8,128)(2,1)}, bf16[256,1024]{1,0:T(8,128)(2,1)}, u32[]{:S(2)}, u32[]{:S(2)}) collective-permute-start(bf16[256,1024]{1,0:T(8,128)(2,1)} %add_convert_fusion.4), channel_id=1, source_target_pairs={{0,8},{8,0},{1,9},{9,1},{2,10},{10,2},{3,11},{11,3},{4,12},{12,4},... | collective-permute-start | bytes 1572872 | tf_op jit(solution)/shard_map/ppermute | solution.py:795
  393.0 28.8 %collective-permute-start.46 = (bf16[288,1024]{1,0:T(8,128)(2,1)}, bf16[288,1024]{1,0:T(8,128)(2,1)S(1)}, u32[]{:S(2)}, u32[]{:S(2)}) collective-permute-start(bf16[288,1024]{1,0:T(8,128)(2,1)} %reduce-scatter.5.cloned.1.call-done.refs_0_.refs_8_.refs_16_), channel_id=1, source_target_pairs={{0,16},{16,0},{1,17},{17,1},{2,18},{18,2},{3,19},{19,3},{4,20},{20... | collective-permute-start | bytes 1769480 | tf_op jit(solution)/shard_map/ppermute | solution.py:795
  398.2 25.5 %collective-permute-start.45 = (bf16[288,1024]{1,0:T(8,128)(2,1)S(1)}, bf16[288,1024]{1,0:T(8,128)(2,1)S(1)}, u32[]{:S(2)}, u32[]{:S(2)}) collective-permute-start(bf16[288,1024]{1,0:T(8,128)(2,1)S(1)} %copy-done.53), channel_id=1, source_target_pairs={{0,8},{8,0},{1,9},{9,1},{2,10},{10,2},{3,11},{11,3},{4,12},{12,4},... | collective-permute-start | bytes 1769480 | tf_op jit(solution)/shard_map/ppermute | solution.py:795
  421.8 7.2 %collective-permute-start.47 = (bf16[144,1024]{1,0:T(8,128)(2,1)S(1)}, bf16[144,1024]{1,0:T(8,128)(2,1)S(1)}, u32[]{:S(2)}, u32[]{:S(2)}) collective-permute-start(bf16[144,1024]{1,0:T(8,128)(2,1)S(1)} %slice.202), channel_id=1, source_target_pairs={{0,8},{8,0},{1,9},{9,1},{2,10},{10,2},{3,11},{11,3},{4,12},{12,4},... | collective-permute-start | bytes 884744 | tf_op jit(solution)/shard_map/ppermute | solution.py:795
  423.7 6.9 %collective-permute-start.48 = (bf16[144,1024]{1,0:T(8,128)(2,1)S(1)}, bf16[144,1024]{1,0:T(8,128)(2,1)S(1)}, u32[]{:S(2)}, u32[]{:S(2)}) collective-permute-start(bf16[144,1024]{1,0:T(8,128)(2,1)S(1)} %slice.203), channel_id=1, source_target_pairs={{0,16},{16,0},{1,17},{17,1},{2,18},{18,2},{3,19},{19,3},{4,20},{20... | collective-permute-start | bytes 884744 | tf_op jit(solution)/shard_map/ppermute | solution.py:795
  425.8 6.6 %collective-permute-start.49 = (bf16[288,1024]{1,0:T(8,128)(2,1)S(1)}, bf16[288,1024]{1,0:T(8,128)(2,1)S(1)}, u32[]{:S(2)}, u32[]{:S(2)}) collective-permute-start(bf16[288,1024]{1,0:T(8,128)(2,1)S(1)} %copy-done.53), channel_id=1, source_target_pairs={{0,4},{4,0},{1,5},{5,1},{2,6},{6,2},{3,7},{7,3},{8,12},{12,8},{9,1... | collective-permute-start | bytes 1769480 | tf_op jit(solution)/shard_map/ppermute | solution.py:795
  425.9 6.5 %collective-permute-start.50 = (bf16[288,1024]{1,0:T(8,128)(2,1)S(1)}, bf16[288,1024]{1,0:T(8,128)(2,1)S(1)}, u32[]{:S(2)}, u32[]{:S(2)}) collective-permute-start(bf16[288,1024]{1,0:T(8,128)(2,1)S(1)} %collective-permute-done.45.refs_1_.refs_9_.refs_17_), channel_id=1, source_target_pairs={{0,4},{4,0},{1,5},{5,1},{2,6},{6,2},{3,7},{7,3},{8,12},{12,8},{9,1... | collective-permute-start | bytes 1769480 | tf_op jit(solution)/shard_map/ppermute | solution.py:795
  426.4 6.1 %collective-permute-start.51 = (bf16[288,1024]{1,0:T(8,128)(2,1)S(1)}, bf16[288,1024]{1,0:T(8,128)(2,1)S(1)}, u32[]{:S(2)}, u32[]{:S(2)}) collective-permute-start(bf16[288,1024]{1,0:T(8,128)(2,1)S(1)} %collective-permute-done.46.refs_2_.refs_10_.refs_18_), channel_id=1, source_target_pairs={{0,4},{4,0},{1,5},{5,1},{2,6},{6,2},{3,7},{7,3},{8,12},{12,8},{9,1... | collective-permute-start | bytes 1769480 | tf_op jit(solution)/shard_map/ppermute | solution.py:795
  430.6 2.1 collective-permute-start.52
  (63 other events, 303.8 us)
Sparse Core Ops, SparseCore 0:
  41.9 44.7 all-gather.2
  255.5 76.7 reduce-scatter.2
  338.9 48.5 reduce-scatter.4
Sparse Core Ops, SparseCore 1:
  107.3 27.9 all-gather.4

commit v3 on v2

--- a/solution.py
+++ b/solution.py
@@ -235,48 +235,63 @@
     )(slots, places, qkv, grad, exact, logs)
 
 
-def feed_forward(h2, pull, sums, others, mine, shares):
+def feed_forward(h2, h2_turned, pull, sums, others, mine, shares):
     tokens, model = h2.shape
     chunks = others + mine
-    ff = chunks[0].shape[1] // 2
+    ff = chunks[0][0].shape[1] // 2
     parts = model // ff
     part, rows = model // shares, ff // shares
     first = sums is None
     n_other, n_mine, n_all = len(others), len(mine), len(chunks)
+    pieces = [piece for chunk in chunks for piece in chunk]
     step = min(ff, TILE)
 
     def kernel(*refs):
         it = iter(refs)
-        h2_ref, pull_ref = next(it), next(it)
+        h2_ref, h2_t, pull_ref = next(it), next(it), next(it)
         starts = None if first else (next(it), next(it))
-        chunk_refs = [next(it) for _ in chunks]
+        chunk_refs = [[next(it) for _ in chunk] for chunk in chunks]
         out_ref, grad_ref = next(it), next(it)
         targets = (next(it), next(it)), (next(it), next(it))
-        h2_t, held, down_w, sem = next(it), next(it), next(it), next(it)
+        held, down_w, sem, sum_sem = next(it), next(it), next(it), next(it)
         t = pl.program_id(0)
         slot = lax.rem(t, 2)
 
         def fetch(k, into):
-            return pltpu.make_async_copy(chunk_refs[k], held.at[into], sem.at[into])
+            count = model // len(chunk_refs[k])
+            return [
+                pltpu.make_async_copy(
+                    ref, held.at[into, pl.ds(p * count, count)], sem.at[into, p]
+                )
+                for p, ref in enumerate(chunk_refs[k])
+            ]
+
+        def fetch_sums():
+            return [
+                pltpu.make_async_copy(ref, into, sum_sem.at[k])
+                for k, (ref, into) in enumerate(zip(starts, (out_ref, grad_ref)))
+            ]
 
         @pl.when(t == 0)
         def _():
-            fetch(0, 0).start()
-            h2_t[...] = h2_ref[...].T
+            for copy in fetch(0, 0):
+                copy.start()
             if first:
                 out_ref[...] = jnp.zeros_like(out_ref)
                 grad_ref[...] = jnp.zeros_like(grad_ref)
             else:
-                out_ref[...] = starts[0][...]
-                grad_ref[...] = starts[1][...]
+                for copy in fetch_sums():
+                    copy.start()
 
         for k in range(n_all):
 
             @pl.when(t == k)
             def _(k=k):
-                fetch(k, k % 2).wait()
+                for copy in fetch(k, k % 2):
+                    copy.wait()
                 if k + 1 < n_all:
-                    fetch(k + 1, (k + 1) % 2).start()
+                    for copy in fetch(k + 1, (k + 1) % 2):
+                        copy.start()
 
         for z in range(shares):
             for j in range(parts):
@@ -293,6 +308,13 @@
             slopes.append((nt(pull_ref[...], down_w[at : at + step, :]) * slope).astype(BF16))
         hidden = jnp.concatenate(hiddens, 1) if len(hiddens) > 1 else hiddens[0]
         grad_up = jnp.concatenate(slopes, 1) if len(slopes) > 1 else slopes[0]
+        if not first:
+
+            @pl.when(t == 0)
+            def _():
+                for copy in fetch_sums():
+                    copy.wait()
+
         out_ref[...] += nn(hidden, down_w[...])
         grad_ref[...] += nt(grad_up, held[slot, :, :ff])
         grad_upper = nn(h2_t[...], grad_up).astype(BF16)
@@ -331,30 +353,34 @@
     return pl.pallas_call(
         kernel,
         grid=(n_all,),
-        in_specs=[whole] * (2 if first else 4) + [pl.BlockSpec(memory_space=pl.ANY)] * n_all,
+        in_specs=[whole, pl.BlockSpec((model, tokens), lambda t: (0, 0)), whole]
+        + [pl.BlockSpec(memory_space=pl.ANY)] * (len(pieces) + (0 if first else 2)),
         out_specs=out_specs,
         out_shape=out_shape,
         scratch_shapes=[
-            pltpu.VMEM((model, tokens), BF16),
             pltpu.VMEM((2, model, 2 * ff), BF16),
             pltpu.VMEM((ff, model), BF16),
+            pltpu.SemaphoreType.DMA((2, len(chunks[0]))),
             pltpu.SemaphoreType.DMA((2,)),
         ],
         compiler_params=pltpu.CompilerParams(vmem_limit_bytes=56 * 1024 * 1024),
         cost_estimate=pl.CostEstimate(flops=1, bytes_accessed=1, transcendentals=0),
-    )(h2, pull, *(() if first else sums), *chunks)
+    )(h2, h2_turned, pull, *(() if first else sums), *pieces)
 
 
 def attention_output(heads, stream, weight, gain, bias, rows):
     owners, tokens, width = heads.shape
     model = owners * width
 
-    def kernel(heads_ref, stream_ref, weight_ref, gain_ref, bias_ref, low_ref, sum_ref, norm_ref):
+    def kernel(heads_ref, stream_ref, weight_ref, gain_ref, bias_ref, *outs):
+        low_ref, sum_ref, norm_ref, turned_ref = outs
         for d in range(owners):
             low_ref[:, d * width : (d + 1) * width] = heads_ref[d]
         total = stream_ref[...].astype(F32) + nn(low_ref[...], weight_ref[...])
         sum_ref[...] = total
-        norm_ref[...] = layer_norm(total, gain_ref[...], bias_ref[...])[0].astype(BF16)
+        normed = layer_norm(total, gain_ref[...], bias_ref[...])[0].astype(BF16)
+        norm_ref[...] = normed
+        turned_ref[...] = normed.T
 
     fixed = lambda *shape: pl.BlockSpec(shape, lambda i: (0, 0))
     block = pl.BlockSpec((rows, model), lambda i: (i, 0))
@@ -368,8 +394,9 @@
             fixed(1, model),
             fixed(1, model),
         ],
-        out_specs=[block] * 3,
-        out_shape=[jax.ShapeDtypeStruct((tokens, model), kind) for kind in (BF16, F32, BF16)],
+        out_specs=[block] * 3 + [pl.BlockSpec((model, rows), lambda i: (0, i))],
+        out_shape=[jax.ShapeDtypeStruct((tokens, model), kind) for kind in (BF16, F32, BF16)]
+        + [jax.ShapeDtypeStruct((model, tokens), BF16)],
         compiler_params=pltpu.CompilerParams(vmem_limit_bytes=48 * 1024 * 1024),
         cost_estimate=pl.CostEstimate(flops=1, bytes_accessed=1, transcendentals=0),
     )(heads, stream, weight, gain[None], bias[None])
@@ -528,7 +555,7 @@
         out_specs=spec(sum(counts)),
         out_shape=jax.ShapeDtypeStruct((shares, sum(counts), part, ff), BF16),
         compiler_params=pltpu.CompilerParams(vmem_limit_bytes=48 * 1024 * 1024),
-        cost_estimate=pl.CostEstimate(flops=1, bytes_accessed=1, transcendentals=0),
+        cost_estimate=pl.CostEstimate(flops=1, bytes_accessed=6 * shares * part * ff * sum(counts), transcendentals=0),
     )(*mine, *away)
 
 
@@ -552,7 +579,7 @@
         kernel,
         out_shape=[jax.ShapeDtypeStruct((half + extra, ff), BF16)] * (2 * sum(counts)),
         compiler_params=pltpu.CompilerParams(vmem_limit_bytes=48 * 1024 * 1024),
-        cost_estimate=pl.CostEstimate(flops=1, bytes_accessed=1, transcendentals=0),
+        cost_estimate=pl.CostEstimate(flops=1, bytes_accessed=6 * model * ff * sum(counts), transcendentals=0),
     )(*mine, *away, outer, outer_away)
     return [[out[2 * k], out[2 * k + 1]] for k in range(sum(counts))]
 
@@ -590,7 +617,7 @@
         ),
         out_shape=[jax.ShapeDtypeStruct(shape, BF16)] * 2,
         compiler_params=pltpu.CompilerParams(vmem_limit_bytes=48 * 1024 * 1024),
-        cost_estimate=pl.CostEstimate(flops=1, bytes_accessed=1, transcendentals=0),
+        cost_estimate=pl.CostEstimate(flops=1, bytes_accessed=8 * model * model, transcendentals=0),
     )(places, left, right)
 
 
@@ -733,11 +760,20 @@
 
     def kernel(at_ref, *refs):
         mains, outers, projs = refs[:owners], refs[owners : 2 * owners], refs[2 * owners : 3 * owners]
-        up_ref, outer_ref, proj_ref, vec_ref = refs[3 * owners :]
+        up_ref, outer_ref, proj_ref, *vec_refs, held = refs[3 * owners :]
+        i = pl.program_id(0)
         for j in range(2):
             at = j * half + 3 * width
             vectors = [proj[:, at : at + 128].astype(F32) for proj in projs]
-            vec_ref[j] = functools.reduce(jnp.add, vectors)
+            rows = pl.ds(pl.multiple_of(j * low + i * block, block), block)
+            held[rows, :] = functools.reduce(jnp.add, vectors)
+
+        @pl.when(i == steps - 1)
+        def _():
+            vectors = held[...].T
+            for k, ref in enumerate(vec_refs):
+                ref[...] = vectors[k : k + 1, :]
+
         for k in range(owners):
             d = at_ref[k]
             lane = lambda base: pl.ds(pl.multiple_of(base + d * width, width), width)
@@ -771,23 +807,24 @@
                     (owners, outer_block, model), lambda i, _: (0, i * outer_steps // steps, 0)
                 ),
                 pl.BlockSpec((2, block, 3 * model), lambda i, _: (0, i, 0)),
-                pl.BlockSpec((2, block, 128), lambda i, _: (0, i, 0)),
-            ],
+            ]
+            + [pl.BlockSpec((1, part), lambda i, _: (0, 0))] * 4,
+            scratch_shapes=[pltpu.VMEM((part, 128), F32)],
         ),
         out_shape=[
             jax.ShapeDtypeStruct((2, low, shares * model), F32),
             jax.ShapeDtypeStruct((owners, out_rows, model), F32),
             jax.ShapeDtypeStruct((2, low, 3 * model), F32),
-            jax.ShapeDtypeStruct((2, low, 128), F32),
-        ],
+        ]
+        + [jax.ShapeDtypeStruct((1, part), F32)] * 4,
         compiler_params=pltpu.CompilerParams(vmem_limit_bytes=56 * 1024 * 1024),
     )(places, *pieces, *pieces, *pieces)
-    upper, outer, proj, vectors = results
+    upper, outer, proj, *vectors = results
     return (
         upper.reshape(part, shares * model),
         outer.reshape(part, model),
         proj.reshape(part, 3 * model),
-        vectors.reshape(part, 128),
+        [each.reshape(part) for each in vectors],
     )
 
 
@@ -814,8 +851,8 @@
     half = value.shape[0] // 2
     from_b, from_a = flip(value, "b"), flip(value, "a")
     far = jnp.concatenate([flip(from_a[:half], "b"), flip(from_b[half:], "a")], 0)
-    near = [value, from_b, from_a, far]
-    return near + [flip(each, "c") for each in near]
+    near = [value, from_b, from_a]
+    return near + [far] + [flip(after(each, far), "c") for each in near] + [flip(far, "c")]
 
 
 def add(u, v):
@@ -946,27 +983,26 @@
     )
     flat = tokens.reshape(mine, model)
     if square:
+        near_chunks = [after(each, attn_heads) for each in near_chunks]
         other_chunks = [flip(each, "c") for each in near_chunks]
-        attn_heads = after(attn_heads, *other_chunks)
-    attn_low, residual, ffn_in = attention_output(
+    attn_low, residual, *ffn_in = attention_output(
         attn_heads, flat, whole_out, gain_two, bias_two, rows
     )
     grad_low = out_grad.reshape(mine, model)
 
     def feed(sums, others, mine):
-        out_sum, in_sum, *grads = feed_forward(ffn_in, grad_low, sums, others, mine, shares)
+        out_sum, in_sum, *grads = feed_forward(*ffn_in, grad_low, sums, others, mine, shares)
         chunk_grads.append(grads)
         return out_sum, in_sum
 
     sums, chunk_grads = None, []
     if square:
-        sums = feed(sums, other_chunks, near_chunks)
-        far_chunk = spread_far([after(each, ffn_in) for each in near_chunks])
-        far_0, far_1, *sums = lax.optimization_barrier((*far_chunk, *sums))
-        far = jnp.concatenate([far_0, far_1], 0)
-        sums = feed(sums, [flip(far, "c")], [far])
+        sums = feed(sums, [[each] for each in other_chunks], [[each] for each in near_chunks])
+        far_chunk = spread_far(near_chunks)
+        far_chunk[0], far_chunk[1], *sums = lax.optimization_barrier((*far_chunk, *sums))
+        sums = feed(sums, [[flip(part, "c") for part in far_chunk]], [far_chunk])
     else:
-        chunks = spread(chunk)
+        chunks = [[each] for each in spread(chunk)]
         for k in range(0, owners, 4):
             sums = feed(sums, chunks[k : k + 2], chunks[k + 2 : k + 4])
     output = (residual + sums[0]).astype(BF16)
@@ -1013,9 +1049,10 @@
         outer = lax.psum_scatter(
             outer.reshape(model, model), CTX, scatter_dimension=0, tiled=True
         )
+    if square:
+        first = converge_first(*halves[1:])
     grad_qkv = backward_attention(heads, width, qkv, grad_heads, exact, logs, slots, places)
     if square:
-        first = converge_first(*halves[1:])
         columns = jnp.stack([gain_one, bias_one, grad_gain_two, grad_bias_two], 1)
         columns = jnp.pad(columns, ((0, 0), (0, 124)))
         *first, columns, grad_qkv = lax.optimization_barrier((*first, columns, grad_qkv))
@@ -1025,12 +1062,16 @@
         grad_qkv = after(grad_qkv, away)
         away = flip(away, "c").reshape(4, mine, model)
         pairs = input_parts(grad_qkv[:4], w_heads, away)
-        terms = converge_last(pairs[0], converge_first(*pairs[1:]))
+        second = converge_first(*pairs[1:])
+        terms = converge_last(pairs[0], second)
         grad_attn_in = jnp.concatenate([total(each) for each in terms], 0)
+        grad_qkv = after(
+            grad_qkv, *[each for group in (*pairs, *upper_terms) for each in group]
+        )
         packed_grad = projection_gradient(
             attn_in, grad_qkv.reshape(owners * mine, 3 * width), w_heads, columns
         )
-        packed_grad = after(packed_grad, lower, *[each for pair in pairs for each in pair])
+        packed_grad = after(packed_grad, lower, *second[:2])
     else:
         grad_qkv = grad_qkv.reshape(owners * mine, 3 * width)
         away = nt(grad_qkv, w_heads).astype(BF16)
@@ -1046,16 +1087,18 @@
         ).astype(BF16)
 
     if square:
+        lower = after(lower, grad_attn_in)
         lower = lower[0].astype(F32) + sum(
             flip(lower[k], axis).astype(F32) for k, axis in ((1, "b"), (2, "a"))
         ) + lax.ppermute(lower[3], ("a", "b"), [(0, 3), (3, 0), (1, 2), (2, 1)]).astype(F32)
-        grad_down = unpack_lower(spread(lower.astype(BF16)), places, shares)
+        lower = lower.astype(BF16)
+        grad_down = unpack_lower(spread(lower), places, shares)
         everything = pack(upper_terms, packed_grad, shares)
         everything = lax.psum_scatter(
             everything.reshape(-1, model), "z", scatter_dimension=0, tiled=True
         )
         grad_upper, grad_outer, grad_proj, vector_grads = unpack(
-            spread(after(everything, grad_down)), places, shares, part, width
+            spread(after(everything, lower)), places, shares, part, width
         )
     else:
         span = 2 * ff
@@ -1095,7 +1138,7 @@
             .transpose(1, 2, 0, 3)
             .reshape(part, 3 * model)
         )
-        vector_grads = jnp.sum(packed_grad[:, :, 3 * width : 3 * width + 4], 0)
+        vector_grads = jnp.sum(packed_grad[:, :, 3 * width : 3 * width + 4], 0).T
 
     attn_full, attn_norm, attn_rstd = layer_norm(flat.astype(F32), gain_one, bias_one)
     in_grad = (grad_resid + norm_back(grad_attn_in, attn_norm, attn_rstd, gain_one)).astype(BF16)
@@ -1103,12 +1146,12 @@
     return (
         output.reshape(tokens.shape),
         in_grad.reshape(tokens.shape),
-        vector_grads[:, 0],
-        vector_grads[:, 1],
+        vector_grads[0],
+        vector_grads[1],
         grad_proj,
         grad_outer,
-        vector_grads[:, 2],
-        vector_grads[:, 3],
+        vector_grads[2],
+        vector_grads[3],
         grad_upper,
         grad_down,
     )

time: 459 us -> 442 us (0.963)
  waiting for transfers between devices: 103 us -> 73.8 us
  blocking collectives: 38.9 us -> 60.7 us
    ppermute x52 -> x53, waiting for transfers between devices: 91.8 us -> 66.5 us  [flip(): return lax.ppermute(value, axis, [(0, 1), (1, 0)])]
    all_to_all x1, blocking collectives: 18.5 us -> 40.3 us  [shards(): lax.all_to_all(attn_heads.reshape(owners, mine, width), CTX, split_axis=0...]
    reduce_scatter x1, waiting for transfers between devices: 9 us -> 2.91 us  [shards(): lax.psum_scatter(lower.reshape(shares * 4, part, ff), 'z', scatter_dimens...]
    unnamed x151 -> x150, local copies, waits for them, and re-layouts: 44 us -> 41.5 us
    ppermute x52 -> x53, starting transfers between devices: 39.8 us -> 37.6 us  [flip(): return lax.ppermute(value, axis, [(0, 1), (1, 0)])]
  transfers between devices with their start and end apart: 58 -> 59, of which waited for: 20 -> 20; matrix products, arithmetic and copies ran while one was open for 8% -> 8% of each run, Pallas kernels for 28% -> 30%
where the time goes in v3:
time: 442 us; the launch traced here: 437 us
  Pallas kernels  165 us (37%)
  waiting for transfers between devices  73.8 us (17%)
  local copies, waits for them, and re-layouts  62.1 us (14%)
  blocking collectives  60.7 us (14%)
  starting transfers between devices  43.5 us (10%)
  between operations  16.3 us (4%)
  other arithmetic  12.6 us (3%)
    ppermute x53, waiting for transfers between devices, flip(): return lax.ppermute(value, axis, [(0, 1), (1, 0)])  66.5 us
    pallas_call x2, Pallas kernels, feed_forward(): pl.pallas_call(kernel, grid=(n_all,), in_specs=[whole, pl.BlockSpec((mode...  45.1 us
    unnamed x150, local copies, waits for them, and re-layouts  41.5 us
    all_to_all x1, blocking collectives, shards(): lax.all_to_all(attn_heads.reshape(owners, mine, width), CTX, split_axis=0...  40.3 us
    ppermute x53, starting transfers between devices, flip(): return lax.ppermute(value, axis, [(0, 1), (1, 0)])  37.6 us
    pallas_call x1, Pallas kernels, backward_attention(): pl.pallas_call(kernel, grid_spec=pltpu.PrefetchScalarGridSpec(num_scalar_...  27.5 us
    pallas_call x2, Pallas kernels, forward_attention(): pl.pallas_call(kernel, grid_spec=pltpu.PrefetchScalarGridSpec(num_scalar_...  24.7 us
    all_gather x1, blocking collectives, shards(): packed = lax.all_gather(packed, 'z', axis=0, tiled=True)  20.4 us
  transfers between devices with their start and end apart: 59, of which 20 were waited for; matrix products, arithmetic and copies ran while one was open for 8% of the time, Pallas kernels for 30%

profile of v3, /device:TPU:0, one launch (start us, length us, event | category | flops | bytes accessed | tf_op | source)
XLA Modules:
  0.0 436.8 jit_solution(976086887282995964)
XLA Ops:
  11.1 3.0 collective-permute-start
  14.1 1.5 collective-permute-start.1
  21.3 20.4 %all_gather.9 = bf16[1088,384]{1,0:T(8,128)(2,1)S(1)} all-gather(bf16[272,384]{1,0:T(8,128)(2,1)S(1)} %fusion.10), channel_id=1, replica_groups=mesh['a'=2,'b'=2,'c'=2,'z'=4] {'z'}, dimensions={0}, use_global_device_ids=true | all-gather | bytes 1044480 | tf_op jit(solution)/shard_map/all_gather | solution.py:933
  42.6 1.9 slice.168
  45.0 1.9 slice.169
  49.5 13.5 %shard_map.195 = (bf16[4096,1024]{1,0:T(8,128)(2,1)}, bf16[4096,384]{1,0:T(8,128)(2,1)}) custom-call(bf16[544,1024]{1,0:T(8,128)(2,1)S(1)} %fusion.6.refs_0_, bf16[544,1024]{1,0:T(8,128)(2,1)} %collective-permute-done.refs_1_, bf16[544,1024]{1,0:T(8,128)(2,1)} %collective-permute-done.1.refs_2_, bf16[544,1024]{1,0:T(8,128)(2,1)} %collective-permute-done.4.refs_3_, ...), custom_call_target="tpu_custom_call" | custom-call | flops 1 | bytes 1 | tf_op jit(solution)/shard_map/pallas_call | solution.py:670
  67.0 1.9 copy-done.3
  68.9 3.8 shard_map.196
  72.7 1.7 copy-done.4
  74.5 12.1 %shard_map.197 = (bf16[8,2,256,128]{3,2,1,0:T(8,128)(2,1)S(1)}, f32[2,128,2048]{2,1,0:T(8,128)S(1)}, f32[2,2,2048]{2,1,0:T(2,128)S(1)}) custom-call(s32[64]{0:T(128)S(1)} %convert_element_type.114.slot_ref, s32[8]{0:T(128)S(1)} %fusion.13.at_ref, bf16[8,2,256,384]{3,2,1,0:T(8,128)(2,1)} %bitcast.73), custom_call_target="tpu_custom_call" | custom-call | flops 1 | bytes 1 | tf_op jit(solution)/shard_map/pallas_call | solution.py:109
  88.0 1.5 collective-permute-start.10
  89.5 1.5 collective-permute-start.8
  91.7 1.6 copy-done.14
  93.3 12.5 %shard_map.198 = (bf16[8,2,256,128]{3,2,1,0:T(8,128)(2,1)S(1)}, f32[2,128,2048]{2,1,0:T(8,128)S(1)}, f32[2,2,2048]{2,1,0:T(2,128)S(1)}) custom-call(s32[64]{0:T(128)S(1)} %convert_element_type.114.slot_ref, s32[8]{0:T(128)S(1)} %fusion.13.at_ref, bf16[8,2,256,384]{3,2,1,0:T(8,128)(2,1)} %bitcast.74, ...), custom_call_target="tpu_custom_call", output_to_operand_aliasing={{0}: (3, {}), {1}: (4, {}), {2}: (5, {})} | custom-call | flops 1 | bytes 1 | tf_op jit(solution)/shard_map/pallas_call | solution.py:109
  108.2 40.3 %all_to_all.10.heads_ref = bf16[8,512,128]{2,1,0:T(8,128)(2,1)S(1)} all-to-all(bf16[8,512,128]{2,1,0:T(8,128)(2,1)} %bitcast.87), channel_id=1, replica_groups=mesh['a'=2,'b'=2,'c'=2,'z'=4] {'a','b','c'}, dimensions={0} | all-to-all | bytes 2097152 | tf_op jit(solution)/shard_map/all_to_all | solution.py:981
  149.1 2.3 slice.153
  151.4 2.3 slice.152
  153.7 1.5 collective-permute-start.11
  155.7 4.6 %shard_map.199 = (bf16[512,1024]{1,0:T(8,128)(2,1)S(1)}, f32[512,1024]{1,0:T(8,128)}, bf16[512,1024]{1,0:T(8,128)(2,1)S(1)}, bf16[1024,512]{1,0:T(8,128)(2,1)S(1)}) custom-call(bf16[8,512,128]{2,1,0:T(8,128)(2,1)S(1)} %all_to_all.10.heads_ref, bf16[512,1024]{1,0:T(8,128)(2,1)S(1)} %bitcast.72, bf16[1024,1024]{1,0:T(8,128)(2,1)} %all-gather.3.cloned.1.call-done.weight_ref, ...), custom_call_target="tpu_custom_call" | custom-call | flops 1 | bytes 1 | tf_op jit(solution)/shard_map/pallas_call | solution.py:387
  162.3 29.6 %shard_map.200 = (f32[512,1024]{1,0:T(8,128)}, f32[512,1024]{1,0:T(8,128)}, bf16[3,1024,512]{2,1,0:T(8,128)(2,1)}, bf16[4,3,256,512]{3,2,1,0:T(8,128)(2,1)}, bf1...) custom-call(bf16[512,1024]{1,0:T(8,128)(2,1)} %copy-done.8, bf16[1024,512]{1,0:T(8,128)(2,1)} %copy-done.9, ...), custom_call_target="tpu_custom_call" | custom-call | flops 1 | bytes 1 | tf_op jit(solution)/shard_map/pallas_call | solution.py:353
  192.5 2.4 collective-permute-done.15.refs_5_
  194.9 1.5 collective-permute-done.16.refs_6_
  197.4 15.5 %shard_map.201 = (f32[512,1024]{1,0:T(8,128)}, f32[512,1024]{1,0:T(8,128)}, bf16[1,1024,512]{2,1,0:T(8,128)(2,1)}, bf16[4,1,256,512]{3,2,1,0:T(8,128)(2,1)}, bf1...) custom-call(bf16[512,1024]{1,0:T(8,128)(2,1)} %copy-done.8, bf16[1024,512]{1,0:T(8,128)(2,1)} %copy-done.9, ...), custom_call_target="tpu_custom_call" | custom-call | flops 1 | bytes 1 | tf_op jit(solution)/shard_map/pallas_call | solution.py:353
  212.9 6.1 %shard_map.202 = (f32[512,1024]{1,0:T(8,128)S(1)}, bf16[512,1024]{1,0:T(8,128)(2,1)S(1)}, bf16[8,512,128]{2,1,0:T(8,128)(2,1)}, f32[8,1024]{1,0:T(8,128)S(1)}) custom-call(f32[512,1024]{1,0:T(8,128)} %get-tuple-element.135.total_ref, f32[512,1024]{1,0:T(8,128)} %get-tuple-element.150.grad_ref, bf16[512,1024]{1,0:T(8,128)(2,1)S(1)} %bitcast.86, ...), custom_call_target="tpu_custom_call" | custom-call | flops 1 | bytes 1 | tf_op jit(solution)/shard_map/pallas_call | solution.py:435
  220.8 1.9 shard_map.203
  224.3 4.3 all-to-all-start.1
  229.1 4.7 %collective-permute-done.18.refs_3_ = bf16[1,1024,512]{2,1,0:T(8,128)(2,1)} collective-permute-done((bf16[1,1024,512]{2,1,0:T(8,128)(2,1)}, bf16[1,1024,512]{2,1,0:T(8,128)(2,1)}, u32[]{:S(2)}, u32[]{:S(2)}) %collective-permute-start.18) | collective-permute-done | bytes 1048608 | tf_op jit(solution)/shard_map/ppermute | solution.py:832
  233.8 5.3 %shard_map.204 = (bf16[640,512]{1,0:T(8,128)(2,1)S(1)}, bf16[640,512]{1,0:T(8,128)(2,1)S(1)}, bf16[640,512]{1,0:T(8,128)(2,1)S(1)}, bf16[640,512]{1,0:T(8,128)(2...) custom-call(bf16[3,1024,512]{2,1,0:T(8,128)(2,1)} %get-tuple-element, ...), custom_call_target="tpu_custom_call" | custom-call | flops 1 | bytes 12582912 | tf_op jit(solution)/shard_map/pallas_call | solution.py:578
  244.0 1.9 copy-done.10
  245.9 5.0 %shard_map.205 = bf16[4,4,256,512]{3,2,1,0:T(8,128)(2,1)} custom-call(bf16[4,3,256,512]{3,2,1,0:T(8,128)(2,1)S(1)} %copy-done.10, bf16[4,1,256,512]{3,2,1,0:T(8,128)(2,1)S(1)} %copy-done.17, bf16[4,3,256,512]{3,2,1,0:T(8,128)(2,1)} %collective-permute-done.24.refs_2_, bf16[4,1,256,512]{3,2,1,0:T(8,128)(2,1)} %collective-permute-done.25.refs_3_), custom_call_target="tpu_custom_call" | custom-call | flops 1 | bytes 12582912 | tf_op jit(solution)/shard_map/pallas_call | solution.py:551
  254.7 1.5 collective-permute-start.23
  256.2 1.8 copy-done.16
  258.1 27.5 %shard_map.206 = bf16[8,2,256,384]{3,2,1,0:T(8,128)(2,1)} custom-call(s32[64]{0:T(128)S(1)} %convert_element_type.114.slot_ref, s32[8]{0:T(128)S(1)} %fusion.13.at_ref, bf16[8,2,256,384]{3,2,1,0:T(8,128)(2,1)} %bitcast.75, bf16[8,2,256,128]{3,2,1,0:T(8,128)(2,1)} %bitcast.23.grad_ref, f32[2,128,2048]{2,1,0:T(8,128)S(1)} %copy-done.16, ...), custom_call_target="tpu_custom_call" | custom-call | flops 7516192768 | bytes 1 | tf_op jit(solution)/shard_map/pallas_call | solution.py:213
  287.2 2.4 convolution_convert_fusion
  292.4 4.5 %collective-permute-done.26 = bf16[2048,1024]{1,0:T(8,128)(2,1)S(1)} collective-permute-done((bf16[2048,1024]{1,0:T(8,128)(2,1)S(1)}, bf16[2048,1024]{1,0:T(8,128)(2,1)S(1)}, u32[]{:S(2)}, u32[]{:S(2)}) %collective-permute-start.26) | collective-permute-done | bytes 4194336 | tf_op jit(solution)/shard_map/ppermute | solution.py:832
  296.9 2.0 copy-done.60
  298.9 6.0 %shard_map.207 = (bf16[256,1024]{1,0:T(8,128)(2,1)S(1)}, bf16[256,1024]{1,0:T(8,128)(2,1)S(1)}, bf16[256,1024]{1,0:T(8,128)(2,1)S(1)}, bf16[256,1024]{1,0:T(8,12...) custom-call(bf16[4,512,384]{2,1,0:T(8,128)(2,1)} %slice.157.slope_re, ...), custom_call_target="tpu_custom_call" | custom-call | flops 1 | bytes 1 | tf_op jit(solution)/shard_map/pallas_call | solution.py:472
  310.2 10.1 %shard_map.208.refs_6_ = bf16[1024,512]{1,0:T(8,128)(2,1)S(1)} custom-call(bf16[4096,1024]{1,0:T(8,128)(2,1)} %get-tuple-element.203.normed_ref, bf16[4096,384]{1,0:T(8,128)(2,1)S(1)} %bitcast.82, bf16[1024,384]{1,0:T(8,128)(2,1)S(1)} %bitcast.80, f32[1024,128]{1,0:T(8,128)S(1)} %pad.14.columns_ref), custom_call_target="tpu_custom_call" | custom-call | flops 1 | bytes 1 | tf_op jit(solution)/shard_map/pallas_call | solution.py:522
  320.3 1.7 collective-permute-done.28
  324.0 2.9 reduce-scatter.3.cloned.1.call-done
  331.3 1.9 shard_map.209
  334.2 1.5 collective-permute-start.27
  335.7 1.5 collective-permute-start.29
  338.3 10.8 %collective-permute-done.27 = bf16[256,1024]{1,0:T(8,128)(2,1)S(1)} collective-permute-done((bf16[256,1024]{1,0:T(8,128)(2,1)S(1)}, bf16[256,1024]{1,0:T(8,128)(2,1)S(1)}, u32[]{:S(2)}, u32[]{:S(2)}) %collective-permute-start.27) | collective-permute-done | bytes 524320 | tf_op jit(solution)/shard_map/ppermute | solution.py:832
  349.0 1.7 collective-permute-done.29
  351.0 9.5 %collective-permute-done.32 = bf16[256,1024]{1,0:T(8,128)(2,1)S(1)} collective-permute-done((bf16[256,1024]{1,0:T(8,128)(2,1)S(1)}, bf16[256,1024]{1,0:T(8,128)(2,1)S(1)}, u32[]{:S(2)}, u32[]{:S(2)}) %collective-permute-start.32) | collective-permute-done | bytes 524320 | tf_op jit(solution)/shard_map/ppermute | solution.py:832
  360.8 1.5 multiply_reduce_fusion
  363.5 1.5 collective-permute-start.36
  366.7 5.5 %collective-permute-done.35 = bf16[256,512]{1,0:T(8,128)(2,1)S(1)} collective-permute-done((bf16[256,512]{1,0:T(8,128)(2,1)S(1)}, bf16[256,512]{1,0:T(8,128)(2,1)S(1)}, u32[]{:S(2)}, u32[]{:S(2)}) %collective-permute-start.35) | collective-permute-done | bytes 262176 | tf_op jit(solution)/shard_map/ppermute | solution.py:832
  372.2 2.7 collective-permute-done.36
  374.9 1.6 collective-permute-done.37
  377.6 1.9 collective-permute-start.46
  379.9 2.0 reduce-scatter.5.cloned.1.call-done.refs_0_.refs_8_.refs_16_
  381.9 1.5 collective-permute-start.39
  383.4 1.5 collective-permute-start.38
  386.2 3.7 add_convert_fusion.1
  389.8 11.2 %collective-permute-done.48 = bf16[128,512]{1,0:T(8,128)(2,1)S(1)} collective-permute-done((bf16[128,512]{1,0:T(8,128)(2,1)S(1)}, bf16[128,512]{1,0:T(8,128)(2,1)S(1)}, u32[]{:S(2)}, u32[]{:S(2)}) %collective-permute-start.48) | collective-permute-done | bytes 131104 | tf_op jit(solution)/shard_map/ppermute | solution.py:832
  401.1 1.5 collective-permute-start.40
  404.6 3.9 collective-permute-done.40
  408.6 3.8 collective-permute-done.41
  413.6 1.7 add_convert_fusion
  415.4 2.0 collective-permute-done.53.refs_7_
  417.3 2.7 shard_map.211
  422.1 7.4 %shard_map.210 = (f32[2,128,4096]{2,1,0:T(8,128)}, f32[8,32,1024]{2,1,0:T(8,128)}, f32[2,128,3072]{2,1,0:T(8,128)}, f32[1,256]{1,0:T(1,128)}, f32[1,256]{1,0:T(1...) custom-call(s32[8]{0:T(128)} %copy-done.39, bf16[288,1024]{1,0:T(8,128)(2,1)} %reduce-scatter.5.cloned.1.call-done.refs_0_.refs_8_.refs_16_, ...), custom_call_target="tpu_custom_call" | custom-call | tf_op jit(solution)/shard_map/pallas_call | solution.py:791
  (295 shorter events, 67.8 us)
Async XLA Ops:
  8.0 83.0 %copy-start = (bf16[256,1024]{1,0:T(8,128)(2,1)S(1)}, bf16[256,1024]{1,0:T(8,128)(2,1)}, u32[]{:S(2)}) copy-start(bf16[256,1024]{1,0:T(8,128)(2,1)} %param.21) | copy-start | bytes 1572868
  8.1 79.9 %all-gather.5.cloned.1.call-start = ((), (), s32[]{:S(2)}) async-start(), calls=%async_computation.5 | async-start | bytes 2621440 | tf_op jit(solution)/shard_map/all_gather | solution.py:944
  11.1 30.6 %collective-permute-start = (bf16[544,1024]{1,0:T(8,128)(2,1)S(1)}, bf16[544,1024]{1,0:T(8,128)(2,1)}, u32[]{:S(2)}, u32[]{:S(2)}) collective-permute-start(bf16[544,1024]{1,0:T(8,128)(2,1)S(1)} %fusion.6.refs_0_), channel_id=1, source_target_pairs={{0,8},{8,0},{1,9},{9,1},{2,10},{10,2},{3,11},{11,3},{4,12},{12,4},... | collective-permute-start | bytes 3342344 | tf_op jit(solution)/shard_map/ppermute | solution.py:832
  14.1 27.6 %collective-permute-start.1 = (bf16[544,1024]{1,0:T(8,128)(2,1)S(1)}, bf16[544,1024]{1,0:T(8,128)(2,1)}, u32[]{:S(2)}, u32[]{:S(2)}) collective-permute-start(bf16[544,1024]{1,0:T(8,128)(2,1)S(1)} %fusion.6.refs_0_), channel_id=1, source_target_pairs={{0,16},{16,0},{1,17},{17,1},{2,18},{18,2},{3,19},{19,3},{4,20},{20... | collective-permute-start | bytes 3342344 | tf_op jit(solution)/shard_map/ppermute | solution.py:832
  41.8 113.9 %all-gather.3.cloned.1.call-start = ((), (), s32[]{:S(2)}) async-start(), calls=%async_computation.4 | async-start | bytes 2359296 | tf_op jit(solution)/shard_map/all_gather | solution.py:980
  41.8 7.7 %collective-permute-start.4 = (bf16[544,1024]{1,0:T(8,128)(2,1)S(1)}, bf16[544,1024]{1,0:T(8,128)(2,1)}, u32[]{:S(2)}, u32[]{:S(2)}) collective-permute-start(bf16[544,1024]{1,0:T(8,128)(2,1)S(1)} %fusion.6.refs_0_), channel_id=1, source_target_pairs={{0,4},{4,0},{1,5},{5,1},{2,6},{6,2},{3,7},{7,3},{8,12},{12,8},{9,1... | collective-permute-start | bytes 3342344 | tf_op jit(solution)/shard_map/ppermute | solution.py:832
  41.9 7.6 %collective-permute-start.5 = (bf16[544,1024]{1,0:T(8,128)(2,1)}, bf16[544,1024]{1,0:T(8,128)(2,1)}, u32[]{:S(2)}, u32[]{:S(2)}) collective-permute-start(bf16[544,1024]{1,0:T(8,128)(2,1)} %collective-permute-done.refs_1_), channel_id=1, source_target_pairs={{0,4},{4,0},{1,5},{5,1},{2,6},{6,2},{3,7},{7,3},{8,12},{12,8},{9,1... | collective-permute-start | bytes 3342344 | tf_op jit(solution)/shard_map/ppermute | solution.py:832
  42.4 7.1 %collective-permute-start.6 = (bf16[544,1024]{1,0:T(8,128)(2,1)}, bf16[544,1024]{1,0:T(8,128)(2,1)}, u32[]{:S(2)}, u32[]{:S(2)}) collective-permute-start(bf16[544,1024]{1,0:T(8,128)(2,1)} %collective-permute-done.1.refs_2_), channel_id=1, source_target_pairs={{0,4},{4,0},{1,5},{5,1},{2,6},{6,2},{3,7},{7,3},{8,12},{12,8},{9,1... | collective-permute-start | bytes 3342344 | tf_op jit(solution)/shard_map/ppermute | solution.py:832
  42.6 374.8 %copy-start.39 = (s32[8]{0:T(128)}, s32[8]{0:T(128)S(1)}, u32[]{:S(2)}) copy-start(s32[8]{0:T(128)S(1)} %fusion.13.at_ref) | copy-start | bytes 100
  44.5 18.5 %collective-permute-start.2 = (bf16[272,1024]{1,0:T(8,128)(2,1)}, bf16[272,1024]{1,0:T(8,128)(2,1)}, u32[]{:S(2)}, u32[]{:S(2)}) collective-permute-start(bf16[272,1024]{1,0:T(8,128)(2,1)} %slice.168), channel_id=1, source_target_pairs={{0,8},{8,0},{1,9},{9,1},{2,10},{10,2},{3,11},{11,3},{4,12},{12,4},... | collective-permute-start | bytes 1671176 | tf_op jit(solution)/shard_map/ppermute | solution.py:832
  46.9 16.1 %collective-permute-start.3 = (bf16[272,1024]{1,0:T(8,128)(2,1)}, bf16[272,1024]{1,0:T(8,128)(2,1)S(1)}, u32[]{:S(2)}, u32[]{:S(2)}) collective-permute-start(bf16[272,1024]{1,0:T(8,128)(2,1)} %slice.169), channel_id=1, source_target_pairs={{0,16},{16,0},{1,17},{17,1},{2,18},{18,2},{3,19},{19,3},{4,20},{20... | collective-permute-start | bytes 1671176 | tf_op jit(solution)/shard_map/ppermute | solution.py:832
  64.2 2.8 collective-permute-start.7
  88.0 60.6 %collective-permute-start.10 = (bf16[1024,1024]{1,0:T(8,128)(2,1)}, bf16[1024,1024]{1,0:T(8,128)(2,1)}, u32[]{:S(2)}, u32[]{:S(2)}) collective-permute-start(bf16[1024,1024]{1,0:T(8,128)(2,1)} %all-gather.5.cloned.1.call-done.refs_6_), channel_id=1, source_target_pairs={{0,8},{8,0},{1,9},{9,1},{2,10},{10,2},{3,11},{11,3},{4,12},{12,4},... | collective-permute-start | bytes 6291464 | tf_op jit(solution)/shard_map/ppermute | solution.py:832
  89.5 59.6 %collective-permute-start.8 = (bf16[1024,1024]{1,0:T(8,128)(2,1)}, bf16[1024,1024]{1,0:T(8,128)(2,1)}, u32[]{:S(2)}, u32[]{:S(2)}) collective-permute-start(bf16[1024,1024]{1,0:T(8,128)(2,1)} %all-gather.5.cloned.1.call-done.refs_6_), channel_id=1, source_target_pairs={{0,16},{16,0},{1,17},{17,1},{2,18},{18,2},{3,19},{19,3},{4,20},{20... | collective-permute-start | bytes 6291464 | tf_op jit(solution)/shard_map/ppermute | solution.py:832
  108.2 43.2 %copy-start.37 = (f32[2,2,2048]{2,1,0:T(2,128)}, f32[2,2,2048]{2,1,0:T(2,128)S(1)}, u32[]{:S(2)}) copy-start(f32[2,2,2048]{2,1,0:T(2,128)S(1)} %get-tuple-element.188.log_ref) | copy-start | bytes 98308
  148.5 13.8 %collective-permute-start.12 = (bf16[1024,1024]{1,0:T(8,128)(2,1)}, bf16[1024,1024]{1,0:T(8,128)(2,1)}, u32[]{:S(2)}, u32[]{:S(2)}) collective-permute-start(bf16[1024,1024]{1,0:T(8,128)(2,1)} %all-gather.5.cloned.1.call-done.refs_6_), channel_id=1, source_target_pairs={{0,4},{4,0},{1,5},{5,1},{2,6},{6,2},{3,7},{7,3},{8,12},{12,8},{9,1... | collective-permute-start | bytes 6291464 | tf_op jit(solution)/shard_map/ppermute | solution.py:832
  148.5 13.8 %collective-permute-start.13 = (bf16[1024,1024]{1,0:T(8,128)(2,1)}, bf16[1024,1024]{1,0:T(8,128)(2,1)}, u32[]{:S(2)}, u32[]{:S(2)}) collective-permute-start(bf16[1024,1024]{1,0:T(8,128)(2,1)} %collective-permute-done.10.refs_7_), channel_id=1, source_target_pairs={{0,4},{4,0},{1,5},{5,1},{2,6},{6,2},{3,7},{7,3},{8,12},{12,8},{9,1... | collective-permute-start | bytes 6291464 | tf_op jit(solution)/shard_map/ppermute | solution.py:832
  149.0 13.3 %collective-permute-start.14 = (bf16[1024,1024]{1,0:T(8,128)(2,1)}, bf16[1024,1024]{1,0:T(8,128)(2,1)}, u32[]{:S(2)}, u32[]{:S(2)}) collective-permute-start(bf16[1024,1024]{1,0:T(8,128)(2,1)} %collective-permute-done.8.refs_8_), channel_id=1, source_target_pairs={{0,4},{4,0},{1,5},{5,1},{2,6},{6,2},{3,7},{7,3},{8,12},{12,8},{9,1... | collective-permute-start | bytes 6291464 | tf_op jit(solution)/shard_map/ppermute | solution.py:832
  153.7 38.3 %collective-permute-start.11 = (bf16[512,1024]{1,0:T(8,128)(2,1)}, bf16[512,1024]{1,0:T(8,128)(2,1)}, u32[]{:S(2)}, u32[]{:S(2)}) collective-permute-start(bf16[512,1024]{1,0:T(8,128)(2,1)} %slice.153), channel_id=1, source_target_pairs={{0,16},{16,0},{1,17},{17,1},{2,18},{18,2},{3,19},{19,3},{4,20},{20... | collective-permute-start | bytes 3145736 | tf_op jit(solution)/shard_map/ppermute | solution.py:832
  155.2 36.8 %collective-permute-start.9 = (bf16[512,1024]{1,0:T(8,128)(2,1)}, bf16[512,1024]{1,0:T(8,128)(2,1)}, u32[]{:S(2)}, u32[]{:S(2)}) collective-permute-start(bf16[512,1024]{1,0:T(8,128)(2,1)} %slice.152), channel_id=1, source_target_pairs={{0,8},{8,0},{1,9},{9,1},{2,10},{10,2},{3,11},{11,3},{4,12},{12,4},... | collective-permute-start | bytes 3145736 | tf_op jit(solution)/shard_map/ppermute | solution.py:832
  191.9 2.9 collective-permute-start.15
  192.0 4.4 collective-permute-start.16
  220.3 13.5 %collective-permute-start.17 = (bf16[3,1024,512]{2,1,0:T(8,128)(2,1)}, bf16[3,1024,512]{2,1,0:T(8,128)(2,1)}, u32[]{:S(2)}, u32[]{:S(2)}) collective-permute-start(bf16[3,1024,512]{2,1,0:T(8,128)(2,1)} %get-tuple-element.164), channel_id=1, source_target_pairs={{0,4},{4,0},{1,5},{5,1},{2,6},{6,2},{3,7},{7,3},{8,12},{12,8},{9,1... | collective-permute-start | bytes 9437192 | tf_op jit(solution)/shard_map/ppermute | solution.py:832
  220.4 23.6 %collective-permute-start.24 = (bf16[4,3,256,512]{3,2,1,0:T(8,128)(2,1)}, bf16[4,3,256,512]{3,2,1,0:T(8,128)(2,1)}, u32[]{:S(2)}, u32[]{:S(2)}) collective-permute-start(bf16[4,3,256,512]{3,2,1,0:T(8,128)(2,1)} %get-tuple-element.184), channel_id=1, source_target_pairs={{0,4},{4,0},{1,5},{5,1},{2,6},{6,2},{3,7},{7,3},{8,12},{12,8},{9,1... | collective-permute-start | bytes 9437192 | tf_op jit(solution)/shard_map/ppermute | solution.py:832
  223.7 5.4 %collective-permute-start.19 = (bf16[4,2,128,512]{3,2,1,0:T(8,128)(2,1)S(1)}, bf16[4,2,128,512]{3,2,1,0:T(8,128)(2,1)}, u32[]{:S(2)}, u32[]{:S(2)}) collective-permute-start(bf16[4,2,128,512]{3,2,1,0:T(8,128)(2,1)S(1)} %get-tuple-element.169), channel_id=1, source_target_pairs={{0,4},{4,0},{1,5},{5,1},{2,6},{6,2},{3,7},{7,3},{8,12},{12,8},{9,1... | collective-permute-start | bytes 3145736 | tf_op jit(solution)/shard_map/ppermute | solution.py:832
  223.8 9.9 %collective-permute-start.18 = (bf16[1,1024,512]{2,1,0:T(8,128)(2,1)}, bf16[1,1024,512]{2,1,0:T(8,128)(2,1)}, u32[]{:S(2)}, u32[]{:S(2)}) collective-permute-start(bf16[1,1024,512]{2,1,0:T(8,128)(2,1)} %get-tuple-element.165), channel_id=1, source_target_pairs={{0,4},{4,0},{1,5},{5,1},{2,6},{6,2},{3,7},{7,3},{8,12},{12,8},{9,1... | collective-permute-start | bytes 3145736 | tf_op jit(solution)/shard_map/ppermute | solution.py:832
  224.2 19.8 %collective-permute-start.25 = (bf16[4,1,256,512]{3,2,1,0:T(8,128)(2,1)}, bf16[4,1,256,512]{3,2,1,0:T(8,128)(2,1)}, u32[]{:S(2)}, u32[]{:S(2)}) collective-permute-start(bf16[4,1,256,512]{3,2,1,0:T(8,128)(2,1)} %get-tuple-element.185), channel_id=1, source_target_pairs={{0,4},{4,0},{1,5},{5,1},{2,6},{6,2},{3,7},{7,3},{8,12},{12,8},{9,1... | collective-permute-start | bytes 3145736 | tf_op jit(solution)/shard_map/ppermute | solution.py:832
  224.3 19.7 %all-to-all-start.1 = ((bf16[8,512,128]{2,1,0:T(8,128)(2,1)}), bf16[8,512,128]{2,1,0:T(8,128)(2,1)}, u32[]{:S(2)}, u32[]{:S(2)}) async-start(bf16[8,512,128]{2,1,0:T(8,128)(2,1)} %get-tuple-element.177), calls=%async_computation.1 | async-start | bytes 2097152 | tf_op jit(solution)/shard_map/all_to_all | solution.py:1016
  228.6 98.4 %reduce-scatter.3.cloned.1.call-start = ((), (), s32[]{:S(2)}) async-start(), calls=%async_computation.6 | async-start | bytes 5242880 | tf_op jit(solution)/shard_map/reduce_scatter | solution.py:1037
  250.9 131.0 %reduce-scatter.5.cloned.1.call-start = ((), (), s32[]{:S(2)}) async-start(), calls=%async_computation.7 | async-start | bytes 2949120 | tf_op jit(solution)/shard_map/reduce_scatter | solution.py:1097
  252.1 33.5 %collective-permute-start.21 = (bf16[640,512]{1,0:T(8,128)(2,1)}, bf16[640,512]{1,0:T(8,128)(2,1)S(1)}, u32[]{:S(2)}, u32[]{:S(2)}) collective-permute-start(bf16[640,512]{1,0:T(8,128)(2,1)} %get-tuple-element.173), channel_id=1, source_target_pairs={{0,8},{8,0},{1,9},{9,1},{2,10},{10,2},{3,11},{11,3},{4,12},{12,4},... | collective-permute-start | bytes 1966088 | tf_op jit(solution)/shard_map/ppermute | solution.py:832
  253.0 32.8 %collective-permute-start.20 = (bf16[640,512]{1,0:T(8,128)(2,1)}, bf16[640,512]{1,0:T(8,128)(2,1)S(1)}, u32[]{:S(2)}, u32[]{:S(2)}) collective-permute-start(bf16[640,512]{1,0:T(8,128)(2,1)} %get-tuple-element.171), channel_id=1, source_target_pairs={{0,16},{16,0},{1,17},{17,1},{2,18},{18,2},{3,19},{19,3},{4,20},{20... | collective-permute-start | bytes 1966088 | tf_op jit(solution)/shard_map/ppermute | solution.py:832
  253.5 33.3 %collective-permute-start.22 = (bf16[640,512]{1,0:T(8,128)(2,1)}, bf16[640,512]{1,0:T(8,128)(2,1)S(1)}, u32[]{:S(2)}, u32[]{:S(2)}) collective-permute-start(bf16[640,512]{1,0:T(8,128)(2,1)} %copy-done.42), channel_id=1, source_target_pairs={{0,8},{8,0},{1,9},{9,1},{2,10},{10,2},{3,11},{11,3},{4,12},{12,4},... | collective-permute-start | bytes 1966088 | tf_op jit(solution)/shard_map/ppermute | solution.py:832
  254.7 32.1 %collective-permute-start.23 = (bf16[640,512]{1,0:T(8,128)(2,1)}, bf16[640,512]{1,0:T(8,128)(2,1)S(1)}, u32[]{:S(2)}, u32[]{:S(2)}) collective-permute-start(bf16[640,512]{1,0:T(8,128)(2,1)} %copy-done.41), channel_id=1, source_target_pairs={{0,16},{16,0},{1,17},{17,1},{2,18},{18,2},{3,19},{19,3},{4,20},{20... | collective-permute-start | bytes 1966088 | tf_op jit(solution)/shard_map/ppermute | solution.py:832
  258.1 27.5 %copy-start.32 = (bf16[640,512]{1,0:T(8,128)(2,1)S(1)}, bf16[640,512]{1,0:T(8,128)(2,1)}, u32[]{:S(2)}) copy-start(bf16[640,512]{1,0:T(8,128)(2,1)} %copy-done.31) | copy-start | bytes 1966084
  289.6 7.2 %collective-permute-start.26 = (bf16[2048,1024]{1,0:T(8,128)(2,1)S(1)}, bf16[2048,1024]{1,0:T(8,128)(2,1)S(1)}, u32[]{:S(2)}, u32[]{:S(2)}) collective-permute-start(bf16[2048,1024]{1,0:T(8,128)(2,1)S(1)} %convolution_convert_fusion), channel_id=1, source_target_pairs={{0,4},{4,0},{1,5},{5,1},{2,6},{6,2},{3,7},{7,3},{8,12},{12,8},{9,1... | collective-permute-start | bytes 12582920 | tf_op jit(solution)/shard_map/ppermute | solution.py:832
  289.7 19.6 %collective-permute-start.33 = (bf16[640,512]{1,0:T(8,128)(2,1)S(1)}, bf16[640,512]{1,0:T(8,128)(2,1)S(1)}, u32[]{:S(2)}, u32[]{:S(2)}) collective-permute-start(bf16[640,512]{1,0:T(8,128)(2,1)S(1)} %add_convert_fusion.2), channel_id=1, source_target_pairs={{0,16},{16,0},{1,17},{17,1},{2,18},{18,2},{3,19},{19,3},{4,20},{20... | collective-permute-start | bytes 1966088 | tf_op jit(solution)/shard_map/ppermute | solution.py:832
  290.5 18.8 %collective-permute-start.34 = (bf16[640,512]{1,0:T(8,128)(2,1)S(1)}, bf16[640,512]{1,0:T(8,128)(2,1)S(1)}, u32[]{:S(2)}, u32[]{:S(2)}) collective-permute-start(bf16[640,512]{1,0:T(8,128)(2,1)S(1)} %add_convert_fusion.3), channel_id=1, source_target_pairs={{0,8},{8,0},{1,9},{9,1},{2,10},{10,2},{3,11},{11,3},{4,12},{12,4},... | collective-permute-start | bytes 1966088 | tf_op jit(solution)/shard_map/ppermute | solution.py:832
  308.1 14.0 %collective-permute-start.28 = (bf16[256,1024]{1,0:T(8,128)(2,1)S(1)}, bf16[256,1024]{1,0:T(8,128)(2,1)S(1)}, u32[]{:S(2)}, u32[]{:S(2)}) collective-permute-start(bf16[256,1024]{1,0:T(8,128)(2,1)S(1)} %get-tuple-element.193), channel_id=1, source_target_pairs={{0,8},{8,0},{1,9},{9,1},{2,10},{10,2},{3,11},{11,3},{4,12},{12,4},... | collective-permute-start | bytes 1572872 | tf_op jit(solution)/shard_map/ppermute | solution.py:832
  309.3 13.8 %collective-permute-start.30 = (bf16[256,1024]{1,0:T(8,128)(2,1)S(1)}, bf16[256,1024]{1,0:T(8,128)(2,1)S(1)}, u32[]{:S(2)}, u32[]{:S(2)}) collective-permute-start(bf16[256,1024]{1,0:T(8,128)(2,1)S(1)} %get-tuple-element.196), channel_id=1, source_target_pairs={{0,16},{16,0},{1,17},{17,1},{2,18},{18,2},{3,19},{19,3},{4,20},{20... | collective-permute-start | bytes 1572872 | tf_op jit(solution)/shard_map/ppermute | solution.py:832
  333.2 27.4 %copy-start.34 = (bf16[256,1024]{1,0:T(8,128)(2,1)S(1)}, bf16[256,1024]{1,0:T(8,128)(2,1)}, u32[]{:S(2)}) copy-start(bf16[256,1024]{1,0:T(8,128)(2,1)} %copy-done.33) | copy-start | bytes 1572868
  334.2 14.8 %collective-permute-start.27 = (bf16[256,1024]{1,0:T(8,128)(2,1)S(1)}, bf16[256,1024]{1,0:T(8,128)(2,1)S(1)}, u32[]{:S(2)}, u32[]{:S(2)}) collective-permute-start(bf16[256,1024]{1,0:T(8,128)(2,1)S(1)} %copy-done.46), channel_id=1, source_target_pairs={{0,8},{8,0},{1,9},{9,1},{2,10},{10,2},{3,11},{11,3},{4,12},{12,4},... | collective-permute-start | bytes 1572872 | tf_op jit(solution)/shard_map/ppermute | solution.py:832
  335.7 15.1 %collective-permute-start.29 = (bf16[256,1024]{1,0:T(8,128)(2,1)}, bf16[256,1024]{1,0:T(8,128)(2,1)S(1)}, u32[]{:S(2)}, u32[]{:S(2)}) collective-permute-start(bf16[256,1024]{1,0:T(8,128)(2,1)} %add_convert_fusion.5), channel_id=1, source_target_pairs={{0,16},{16,0},{1,17},{17,1},{2,18},{18,2},{3,19},{19,3},{4,20},{20... | collective-permute-start | bytes 1572872 | tf_op jit(solution)/shard_map/ppermute | solution.py:832
  337.2 23.4 %collective-permute-start.32 = (bf16[256,1024]{1,0:T(8,128)(2,1)S(1)}, bf16[256,1024]{1,0:T(8,128)(2,1)S(1)}, u32[]{:S(2)}, u32[]{:S(2)}) collective-permute-start(bf16[256,1024]{1,0:T(8,128)(2,1)S(1)} %copy-done.44), channel_id=1, source_target_pairs={{0,16},{16,0},{1,17},{17,1},{2,18},{18,2},{3,19},{19,3},{4,20},{20... | collective-permute-start | bytes 1572872 | tf_op jit(solution)/shard_map/ppermute | solution.py:832
  337.7 22.8 %collective-permute-start.31 = (bf16[256,1024]{1,0:T(8,128)(2,1)}, bf16[256,1024]{1,0:T(8,128)(2,1)S(1)}, u32[]{:S(2)}, u32[]{:S(2)}) collective-permute-start(bf16[256,1024]{1,0:T(8,128)(2,1)} %add_convert_fusion.4), channel_id=1, source_target_pairs={{0,8},{8,0},{1,9},{9,1},{2,10},{10,2},{3,11},{11,3},{4,12},{12,4},... | collective-permute-start | bytes 1572872 | tf_op jit(solution)/shard_map/ppermute | solution.py:832
  362.9 9.3 %collective-permute-start.35 = (bf16[256,512]{1,0:T(8,128)(2,1)S(1)}, bf16[256,512]{1,0:T(8,128)(2,1)S(1)}, u32[]{:S(2)}, u32[]{:S(2)}) collective-permute-start(bf16[256,512]{1,0:T(8,128)(2,1)S(1)} %get-tuple-element.229), channel_id=1, source_target_pairs={{0,8},{8,0},{1,9},{9,1},{2,10},{10,2},{3,11},{11,3},{4,12},{12,4},... | collective-permute-start | bytes 786440 | tf_op jit(solution)/shard_map/ppermute | solution.py:832
  363.5 11.4 %collective-permute-start.36 = (bf16[256,512]{1,0:T(8,128)(2,1)S(1)}, bf16[256,512]{1,0:T(8,128)(2,1)S(1)}, u32[]{:S(2)}, u32[]{:S(2)}) collective-permute-start(bf16[256,512]{1,0:T(8,128)(2,1)S(1)} %get-tuple-element.231), channel_id=1, source_target_pairs={{0,16},{16,0},{1,17},{17,1},{2,18},{18,2},{3,19},{19,3},{4,20},{20... | collective-permute-start | bytes 786440 | tf_op jit(solution)/shard_map/ppermute | solution.py:832
  365.0 11.5 %collective-permute-start.37 = (bf16[256,512]{1,0:T(8,128)(2,1)S(1)}, bf16[256,512]{1,0:T(8,128)(2,1)S(1)}, u32[]{:S(2)}, u32[]{:S(2)}) collective-permute-start(bf16[256,512]{1,0:T(8,128)(2,1)S(1)} %get-tuple-element.230), channel_id=1, source_target_pairs={{0,24},{24,0},{8,16},{16,8},{1,25},{25,1},{9,17},{17,9},{2,26},{26... | collective-permute-start | bytes 786440 | tf_op jit(solution)/shard_map/ppermute | solution.py:1093
  376.7 8.2 %collective-permute-start.47 = (bf16[256,512]{1,0:T(8,128)(2,1)S(1)}, bf16[256,512]{1,0:T(8,128)(2,1)S(1)}, u32[]{:S(2)}, u32[]{:S(2)}) collective-permute-start(bf16[256,512]{1,0:T(8,128)(2,1)S(1)} %fusion.8.refs_0_), channel_id=1, source_target_pairs={{0,16},{16,0},{1,17},{17,1},{2,18},{18,2},{3,19},{19,3},{4,20},{20... | collective-permute-start | bytes 786440 | tf_op jit(solution)/shard_map/ppermute | solution.py:832
  377.6 8.0 %collective-permute-start.46 = (bf16[256,512]{1,0:T(8,128)(2,1)S(1)}, bf16[256,512]{1,0:T(8,128)(2,1)S(1)}, u32[]{:S(2)}, u32[]{:S(2)}) collective-permute-start(bf16[256,512]{1,0:T(8,128)(2,1)S(1)} %fusion.8.refs_0_), channel_id=1, source_target_pairs={{0,8},{8,0},{1,9},{9,1},{2,10},{10,2},{3,11},{11,3},{4,12},{12,4},... | collective-permute-start | bytes 786440 | tf_op jit(solution)/shard_map/ppermute | solution.py:832
  381.9 19.1 %collective-permute-start.39 = (bf16[288,1024]{1,0:T(8,128)(2,1)}, bf16[288,1024]{1,0:T(8,128)(2,1)S(1)}, u32[]{:S(2)}, u32[]{:S(2)}) collective-permute-start(bf16[288,1024]{1,0:T(8,128)(2,1)} %reduce-scatter.5.cloned.1.call-done.refs_0_.refs_8_.refs_16_), channel_id=1, source_target_pairs={{0,16},{16,0},{1,17},{17,1},{2,18},{18,2},{3,19},{19,3},{4,20},{20... | collective-permute-start | bytes 1769480 | tf_op jit(solution)/shard_map/ppermute | solution.py:832
  383.4 19.8 %collective-permute-start.38 = (bf16[288,1024]{1,0:T(8,128)(2,1)}, bf16[288,1024]{1,0:T(8,128)(2,1)S(1)}, u32[]{:S(2)}, u32[]{:S(2)}) collective-permute-start(bf16[288,1024]{1,0:T(8,128)(2,1)} %reduce-scatter.5.cloned.1.call-done.refs_0_.refs_8_.refs_16_), channel_id=1, source_target_pairs={{0,8},{8,0},{1,9},{9,1},{2,10},{10,2},{3,11},{11,3},{4,12},{12,4},... | collective-permute-start | bytes 1769480 | tf_op jit(solution)/shard_map/ppermute | solution.py:832
  384.9 16.1 %collective-permute-start.48 = (bf16[128,512]{1,0:T(8,128)(2,1)S(1)}, bf16[128,512]{1,0:T(8,128)(2,1)S(1)}, u32[]{:S(2)}, u32[]{:S(2)}) collective-permute-start(bf16[128,512]{1,0:T(8,128)(2,1)S(1)} %slice.182), channel_id=1, source_target_pairs={{0,8},{8,0},{1,9},{9,1},{2,10},{10,2},{3,11},{11,3},{4,12},{12,4},... | collective-permute-start | bytes 393224 | tf_op jit(solution)/shard_map/ppermute | solution.py:832
  385.6 17.1 %collective-permute-start.49 = (bf16[128,512]{1,0:T(8,128)(2,1)S(1)}, bf16[128,512]{1,0:T(8,128)(2,1)S(1)}, u32[]{:S(2)}, u32[]{:S(2)}) collective-permute-start(bf16[128,512]{1,0:T(8,128)(2,1)S(1)} %slice.183), channel_id=1, source_target_pairs={{0,16},{16,0},{1,17},{17,1},{2,18},{18,2},{3,19},{19,3},{4,20},{20... | collective-permute-start | bytes 393224 | tf_op jit(solution)/shard_map/ppermute | solution.py:832
  401.1 7.4 %collective-permute-start.40 = (bf16[144,1024]{1,0:T(8,128)(2,1)S(1)}, bf16[144,1024]{1,0:T(8,128)(2,1)S(1)}, u32[]{:S(2)}, u32[]{:S(2)}) collective-permute-start(bf16[144,1024]{1,0:T(8,128)(2,1)S(1)} %slice.180), channel_id=1, source_target_pairs={{0,8},{8,0},{1,9},{9,1},{2,10},{10,2},{3,11},{11,3},{4,12},{12,4},... | collective-permute-start | bytes 884744 | tf_op jit(solution)/shard_map/ppermute | solution.py:832
  402.7 10.3 %collective-permute-start.52 = (bf16[256,512]{1,0:T(8,128)(2,1)S(1)}, bf16[256,512]{1,0:T(8,128)(2,1)S(1)}, u32[]{:S(2)}, u32[]{:S(2)}) collective-permute-start(bf16[256,512]{1,0:T(8,128)(2,1)S(1)} %collective-permute-done.47.refs_2_), channel_id=1, source_target_pairs={{0,4},{4,0},{1,5},{5,1},{2,6},{6,2},{3,7},{7,3},{8,12},{12,8},{9,1... | collective-permute-start | bytes 786440 | tf_op jit(solution)/shard_map/ppermute | solution.py:832
  402.7 10.3 %collective-permute-start.51 = (bf16[256,512]{1,0:T(8,128)(2,1)S(1)}, bf16[256,512]{1,0:T(8,128)(2,1)S(1)}, u32[]{:S(2)}, u32[]{:S(2)}) collective-permute-start(bf16[256,512]{1,0:T(8,128)(2,1)S(1)} %collective-permute-done.46.refs_1_), channel_id=1, source_target_pairs={{0,4},{4,0},{1,5},{5,1},{2,6},{6,2},{3,7},{7,3},{8,12},{12,8},{9,1... | collective-permute-start | bytes 786440 | tf_op jit(solution)/shard_map/ppermute | solution.py:832
  403.3 9.1 %collective-permute-start.41 = (bf16[144,1024]{1,0:T(8,128)(2,1)S(1)}, bf16[144,1024]{1,0:T(8,128)(2,1)S(1)}, u32[]{:S(2)}, u32[]{:S(2)}) collective-permute-start(bf16[144,1024]{1,0:T(8,128)(2,1)S(1)} %slice.181), channel_id=1, source_target_pairs={{0,16},{16,0},{1,17},{17,1},{2,18},{18,2},{3,19},{19,3},{4,20},{20... | collective-permute-start | bytes 884744 | tf_op jit(solution)/shard_map/ppermute | solution.py:832
  404.5 8.9 %collective-permute-start.50 = (bf16[256,512]{1,0:T(8,128)(2,1)S(1)}, bf16[256,512]{1,0:T(8,128)(2,1)S(1)}, u32[]{:S(2)}, u32[]{:S(2)}) collective-permute-start(bf16[256,512]{1,0:T(8,128)(2,1)S(1)} %fusion.8.refs_0_), channel_id=1, source_target_pairs={{0,4},{4,0},{1,5},{5,1},{2,6},{6,2},{3,7},{7,3},{8,12},{12,8},{9,1... | collective-permute-start | bytes 786440 | tf_op jit(solution)/shard_map/ppermute | solution.py:832
  412.4 7.7 %collective-permute-start.45 = (bf16[288,1024]{1,0:T(8,128)(2,1)S(1)}, bf16[288,1024]{1,0:T(8,128)(2,1)S(1)}, u32[]{:S(2)}, u32[]{:S(2)}) collective-permute-start(bf16[288,1024]{1,0:T(8,128)(2,1)S(1)} %constant_dynamic-update-slice_fusion.2.refs_3_.refs_11_.refs_19_), channel_id=1, source_target_pairs={{0,4},{4,0},{1,5},{5,1},{2,6},{6,2},{3,7},{7,3},{8,12},{12,8},{9,1... | collective-permute-start | bytes 1769480 | tf_op jit(solution)/shard_map/ppermute | solution.py:832
  412.4 7.6 %collective-permute-start.44 = (bf16[288,1024]{1,0:T(8,128)(2,1)S(1)}, bf16[288,1024]{1,0:T(8,128)(2,1)S(1)}, u32[]{:S(2)}, u32[]{:S(2)}) collective-permute-start(bf16[288,1024]{1,0:T(8,128)(2,1)S(1)} %collective-permute-done.39.refs_2_.refs_10_.refs_18_), channel_id=1, source_target_pairs={{0,4},{4,0},{1,5},{5,1},{2,6},{6,2},{3,7},{7,3},{8,12},{12,8},{9,1... | collective-permute-start | bytes 1769480 | tf_op jit(solution)/shard_map/ppermute | solution.py:832
  412.9 7.1 %collective-permute-start.43 = (bf16[288,1024]{1,0:T(8,128)(2,1)S(1)}, bf16[288,1024]{1,0:T(8,128)(2,1)S(1)}, u32[]{:S(2)}, u32[]{:S(2)}) collective-permute-start(bf16[288,1024]{1,0:T(8,128)(2,1)S(1)} %collective-permute-done.38.refs_1_.refs_9_.refs_17_), channel_id=1, source_target_pairs={{0,4},{4,0},{1,5},{5,1},{2,6},{6,2},{3,7},{7,3},{8,12},{12,8},{9,1... | collective-permute-start | bytes 1769480 | tf_op jit(solution)/shard_map/ppermute | solution.py:832
  413.0 7.0 %collective-permute-start.42 = (bf16[288,1024]{1,0:T(8,128)(2,1)S(1)}, bf16[288,1024]{1,0:T(8,128)(2,1)S(1)}, u32[]{:S(2)}, u32[]{:S(2)}) collective-permute-start(bf16[288,1024]{1,0:T(8,128)(2,1)S(1)} %copy-done.55), channel_id=1, source_target_pairs={{0,4},{4,0},{1,5},{5,1},{2,6},{6,2},{3,7},{7,3},{8,12},{12,8},{9,1... | collective-permute-start | bytes 1769480 | tf_op jit(solution)/shard_map/ppermute | solution.py:832
  413.5 3.9 collective-permute-start.53
  (66 other events, 296.0 us)
Sparse Core Ops, SparseCore 0:
  41.9 44.7 all-gather.4
  251.0 75.8 reduce-scatter.2
  333.3 48.5 reduce-scatter.4
Sparse Core Ops, SparseCore 1:
  108.3 27.9 all-gather.2

commit v4 on v3

--- a/solution.py
+++ b/solution.py
@@ -138,7 +138,7 @@
     per_owner = rows // UNIT
     size = width // heads
     scale = size**-0.5
-    wide = 2 * TILE
+    wide = 4 * TILE
     units = [(k, u) for k in range(owners) for u in range(per_owner)]
 
     def kernel(slot_ref, at_ref, qkv_ref, grad_ref, exact_ref, log_ref, out_ref, *scratch):
@@ -171,8 +171,8 @@
                 starts = [(j * TILE, TILE)]
                 at = (j + 1) * TILE
                 if (total - at) % wide:
-                    starts.append((at, TILE))
-                    at += TILE
+                    starts.append((at, (total - at) % wide))
+                    at += (total - at) % wide
                 while at < total:
                     starts.append((at, wide))
                     at += wide
@@ -238,7 +238,7 @@
 def feed_forward(h2, h2_turned, pull, sums, others, mine, shares):
     tokens, model = h2.shape
     chunks = others + mine
-    ff = chunks[0][0].shape[1] // 2
+    ff = chunks[0][0].shape[-1] // 2
     parts = model // ff
     part, rows = model // shares, ff // shares
     first = sums is None
@@ -258,12 +258,14 @@
         slot = lax.rem(t, 2)
 
         def fetch(k, into):
-            count = model // len(chunk_refs[k])
+            ref = chunk_refs[k][0]
+            if len(ref.shape) == 2:
+                return [pltpu.make_async_copy(ref, held.at[into], sem.at[into, 0])]
             return [
                 pltpu.make_async_copy(
-                    ref, held.at[into, pl.ds(p * count, count)], sem.at[into, p]
+                    ref.at[z, pl.ds(0, part)], held.at[into, pl.ds(z * part, part)], sem.at[into, z]
                 )
-                for p, ref in enumerate(chunk_refs[k])
+                for z in range(shares)
             ]
 
         def fetch_sums():
@@ -360,7 +362,7 @@
         scratch_shapes=[
             pltpu.VMEM((2, model, 2 * ff), BF16),
             pltpu.VMEM((ff, model), BF16),
-            pltpu.SemaphoreType.DMA((2, len(chunks[0]))),
+            pltpu.SemaphoreType.DMA((2, shares)),
             pltpu.SemaphoreType.DMA((2,)),
         ],
         compiler_params=pltpu.CompilerParams(vmem_limit_bytes=56 * 1024 * 1024),
@@ -368,38 +370,61 @@
     )(h2, h2_turned, pull, *(() if first else sums), *pieces)
 
 
-def attention_output(heads, stream, weight, gain, bias, rows):
+def attention_output(heads, stream, weight, core, gain, bias, rows):
     owners, tokens, width = heads.shape
     model = owners * width
-
-    def kernel(heads_ref, stream_ref, weight_ref, gain_ref, bias_ref, *outs):
-        low_ref, sum_ref, norm_ref, turned_ref = outs
+    split = isinstance(weight, tuple)
+    weights = list(weight) if split else [weight]
+    if split:
+        shares, lines, _ = weight[0].shape
+        half = model // shares // 2
+        weight_specs = [
+            pl.BlockSpec((shares, half, model), lambda i, _: (0, (lines - half) // half, 0))
+        ] * 2
+    else:
+        weight_specs = [pl.BlockSpec((model, model), lambda i, _: (0, 0))]
+
+    def kernel(core_ref, heads_ref, stream_ref, *refs):
+        weight_refs, (gain_ref, bias_ref) = refs[: len(weights)], refs[len(weights) : -5]
+        low_ref, sum_ref, norm_ref, turned_ref, whole_ref = refs[-5:]
+
+        @pl.when(pl.program_id(0) == 0)
+        def _():
+            if split:
+                for k, ref in enumerate(weight_refs):
+                    side = core_ref[0] if k == 0 else 1 - core_ref[0]
+                    for z in range(shares):
+                        at = pl.multiple_of((2 * z + side) * half, half)
+                        whole_ref[pl.ds(at, half), :] = ref[z]
+            else:
+                whole_ref[...] = weight_refs[0][...]
+
         for d in range(owners):
             low_ref[:, d * width : (d + 1) * width] = heads_ref[d]
-        total = stream_ref[...].astype(F32) + nn(low_ref[...], weight_ref[...])
+        total = stream_ref[...].astype(F32) + nn(low_ref[...], whole_ref[...])
         sum_ref[...] = total
         normed = layer_norm(total, gain_ref[...], bias_ref[...])[0].astype(BF16)
         norm_ref[...] = normed
         turned_ref[...] = normed.T
 
-    fixed = lambda *shape: pl.BlockSpec(shape, lambda i: (0, 0))
-    block = pl.BlockSpec((rows, model), lambda i: (i, 0))
+    fixed = lambda *shape: pl.BlockSpec(shape, lambda i, _: (0, 0))
+    block = pl.BlockSpec((rows, model), lambda i, _: (i, 0))
     return pl.pallas_call(
         kernel,
-        grid=(tokens // rows,),
-        in_specs=[
-            pl.BlockSpec((owners, rows, width), lambda i: (0, i, 0)),
-            block,
-            fixed(model, model),
-            fixed(1, model),
-            fixed(1, model),
-        ],
-        out_specs=[block] * 3 + [pl.BlockSpec((model, rows), lambda i: (0, i))],
+        grid_spec=pltpu.PrefetchScalarGridSpec(
+            num_scalar_prefetch=1,
+            grid=(tokens // rows,),
+            in_specs=[pl.BlockSpec((owners, rows, width), lambda i, _: (0, i, 0)), block]
+            + weight_specs
+            + [fixed(1, model), fixed(1, model)],
+            out_specs=[block] * 3
+            + [pl.BlockSpec((model, rows), lambda i, _: (0, i)), fixed(model, model)],
+        ),
         out_shape=[jax.ShapeDtypeStruct((tokens, model), kind) for kind in (BF16, F32, BF16)]
-        + [jax.ShapeDtypeStruct((model, tokens), BF16)],
+        + [jax.ShapeDtypeStruct((model, tokens), BF16), jax.ShapeDtypeStruct((model, model), BF16)],
         compiler_params=pltpu.CompilerParams(vmem_limit_bytes=48 * 1024 * 1024),
         cost_estimate=pl.CostEstimate(flops=1, bytes_accessed=1, transcendentals=0),
-    )(heads, stream, weight, gain[None], bias[None])
+    )(core.reshape(1).astype(jnp.int32), heads, stream, *weights, gain[None], bias[None])
 
 
 def norm_gradient(total, grad, direct, weight, gain, owners, rows):
@@ -488,7 +513,7 @@
 def projection_gradient(normed, slopes, weight, columns):
     count, width = slopes.shape
     model = normed.shape[1]
-    block = min(512, count)
+    block = min(2048, count)
     steps = count // block
 
     def kernel(normed_ref, slope_ref, weight_ref, columns_ref, out_ref, acc, sums):
@@ -619,6 +644,56 @@
         compiler_params=pltpu.CompilerParams(vmem_limit_bytes=48 * 1024 * 1024),
         cost_estimate=pl.CostEstimate(flops=1, bytes_accessed=8 * model * model, transcendentals=0),
     )(places, left, right)
+
+
+def take_chunk(w_up, w_down, device, owners, w_out=None, core=0):
+    part, full = w_up.shape
+    model = w_down.shape[1]
+    ff = full // owners
+    shares = model // part
+    rows = ff // shares
+    parts = model // ff
+    if rows % 128:
+        up = [
+            lax.dynamic_slice_in_dim(w_up, (z * owners + device) * rows, rows, 1)
+            for z in range(shares)
+        ]
+        down = lax.dynamic_slice_in_dim(w_down, device * rows, rows, 0)
+        down = jnp.concatenate([down[:, j * ff : (j + 1) * ff] for j in range(parts)], 0)
+        return jnp.concatenate(up + [down], 1)
+
+    def kernel(_, *refs):
+        out_ref, down_ref = refs[-1], refs[shares]
+        if w_out is not None:
+            out_ref[part:, :] = refs[shares + 1][...]
+        for z in range(shares):
+            out_ref[:part, z * rows : (z + 1) * rows] = refs[z][...]
+        for j in range(parts):
+            out_ref[j * rows : (j + 1) * rows, ff:] = down_ref[:, j * ff : (j + 1) * ff]
+
+    extra = 0 if w_out is None else w_out.shape[0] // 2
+    return pl.pallas_call(
+        kernel,
+        grid_spec=pltpu.PrefetchScalarGridSpec(
+            num_scalar_prefetch=1,
+            grid=(1,),
+            in_specs=[
+                pl.BlockSpec((part, rows), lambda i, d, z=z: (0, z * owners + d[0]))
+                for z in range(shares)
+            ]
+            + [pl.BlockSpec((rows, model), lambda i, d: (d[0], 0))]
+            + [pl.BlockSpec((extra, model), lambda i, d: (d[1], 0))] * (extra > 0),
+            out_specs=pl.BlockSpec((part + extra, 2 * ff), lambda i, d: (0, 0)),
+        ),
+        out_shape=jax.ShapeDtypeStruct((part + extra, 2 * ff), BF16),
+        compiler_params=pltpu.CompilerParams(vmem_limit_bytes=48 * 1024 * 1024),
+        cost_estimate=pl.CostEstimate(flops=1, bytes_accessed=1, transcendentals=0),
+    )(
+        jnp.stack([device, core]).astype(jnp.int32),
+        *[w_up] * shares,
+        w_down,
+        *([] if w_out is None else [w_out]),
+    )
 
 
 def absolute(owner):
@@ -931,13 +1006,7 @@
     packed = jnp.concatenate(columns, 1)
     packed = jnp.concatenate([packed, norms], 0)
     packed = lax.all_gather(packed, "z", axis=0, tiled=True)
-    up_part = [
-        lax.dynamic_slice_in_dim(w_up, (z * owners + me) * ff_rows, ff_rows, 1)
-        for z in range(shares)
-    ]
-    down_part = lax.dynamic_slice_in_dim(w_down, me * ff_rows, ff_rows, 0)
-    down_part = jnp.concatenate([down_part[:, j * ff : (j + 1) * ff] for j in range(ff_parts)], 0)
-    chunk = jnp.concatenate(up_part + [down_part], 1)
+    chunk = take_chunk(w_up, w_down, me, owners)
     chunk, packed, pieces[1], pieces[2] = lax.optimization_barrier(
         (chunk, packed, pieces[1], pieces[2])
     )
@@ -972,12 +1041,16 @@
     slots = slots.astype(jnp.int32)
     qkv = qkv.reshape(owners, groups, rows, 3 * width)
     attended = forward_attention(heads, width, qkv, 0, slots, places, [])
+    first_heads = attended[0]
     for g in range(1, groups):
         if square and g == 1:
             near_chunks = spread_near(after(chunk, attended[0]))
+            far_chunk = take_chunk(w_up, w_down, places[3], owners, w_out, core)
+            far_chunk = lax.all_gather(after(far_chunk, attended[0]), "z", axis=0, tiled=False)
         attended = forward_attention(heads, width, qkv, g, slots, places, attended)
     attn_heads, exact, logs = attended
-    whole_out = lax.all_gather(after(piece, attn_heads), ("z", "c"), axis=0, tiled=True)
+    if not square:
+        whole_out = lax.all_gather(piece, ("z", "c"), axis=0, tiled=True)
     attn_heads = lax.all_to_all(
         attn_heads.reshape(owners, mine, width), CTX, split_axis=0, concat_axis=0, tiled=True
     )
@@ -985,8 +1058,12 @@
     if square:
         near_chunks = [after(each, attn_heads) for each in near_chunks]
         other_chunks = [flip(each, "c") for each in near_chunks]
-    attn_low, residual, *ffn_in = attention_output(
-        attn_heads, flat, whole_out, gain_two, bias_two, rows
+    if square:
+        far_chunk = after(far_chunk, attn_heads)
+        far_other = flip(far_chunk, "c")
+        whole_out = (far_chunk, far_other)
+    attn_low, residual, *ffn_in, whole_out = attention_output(
+        attn_heads, flat, whole_out, core, gain_two, bias_two, rows
     )
     grad_low = out_grad.reshape(mine, model)
 
@@ -997,10 +1074,9 @@
 
     sums, chunk_grads = None, []
     if square:
-        sums = feed(sums, [[each] for each in other_chunks], [[each] for each in near_chunks])
-        far_chunk = spread_far(near_chunks)
-        far_chunk[0], far_chunk[1], *sums = lax.optimization_barrier((*far_chunk, *sums))
-        sums = feed(sums, [[flip(part, "c") for part in far_chunk]], [far_chunk])
+        mine_chunks = [[each] for each in near_chunks + [far_chunk]]
+        other_chunks = [[each] for each in other_chunks + [far_other]]
+        sums = feed(sums, other_chunks, mine_chunks)
     else:
         chunks = [[each] for each in spread(chunk)]
         for k in range(0, owners, 4):
@@ -1012,7 +1088,7 @@
     grad_gain_two, grad_bias_two = norm_grads[0], norm_grads[1]
     late = [grad_branch] + [each for grads in chunk_grads for each in grads]
     grad_heads, grad_branch, *late = lax.optimization_barrier((grad_heads, *late))
-    chunk_grads = [late[:4], late[4:8]] if square else chunk_grads
+    chunk_grads = [late[:4]] if square else chunk_grads
     grad_heads = lax.all_to_all(
         grad_heads, CTX, split_axis=0, concat_axis=0, tiled=True
     ).reshape(owners, groups, rows, width)

time: 442 us -> 439 us (level)
  Pallas kernels: 165 us -> 159 us
    pallas_call x2 -> x1, Pallas kernels: 45.1 us -> 37.4 us  [feed_forward(): pl.pallas_call(kernel, grid=(n_all,), in_specs=[whole, pl.BlockSpec((mode...]
    unnamed x150 -> x154, local copies, waits for them, and re-layouts: 41.5 us -> 46.2 us
    slice x4 -> x2, local copies, waits for them, and re-layouts: 8.33 us -> 3.89 us  [spread_far(): return [flip(near[2][:half], 'b'), flip(near[1][half:], 'a')]]
    ppermute x53 -> x48, starting transfers between devices: 37.6 us -> 39.9 us  [flip(): return lax.ppermute(value, axis, [(0, 1), (1, 0)])]
    ppermute x53 -> x48, waiting for transfers between devices: 66.5 us -> 64.2 us  [flip(): return lax.ppermute(value, axis, [(0, 1), (1, 0)])]
  transfers between devices with their start and end apart: 59 -> 54, of which waited for: 20 -> 16; matrix products, arithmetic and copies ran while one was open for 8% -> 7% of each run, Pallas kernels for 30% -> 24%
where the time goes in v4:
time: 439 us; the launch traced here: 434 us
  Pallas kernels  159 us (36%)
  waiting for transfers between devices  72.3 us (16%)
  local copies, waits for them, and re-layouts  62.8 us (14%)
  blocking collectives  62.7 us (14%)
  starting transfers between devices  45.2 us (10%)
  other arithmetic  15 us (3%)
  between operations  14.8 us (3%)
    ppermute x48, waiting for transfers between devices, flip(): return lax.ppermute(value, axis, [(0, 1), (1, 0)])  64.2 us
    unnamed x154, local copies, waits for them, and re-layouts  46.2 us
    all_to_all x1, blocking collectives, shards(): lax.all_to_all(attn_heads.reshape(owners, mine, width), CTX, split_axis=0...  41.8 us
    ppermute x48, starting transfers between devices, flip(): return lax.ppermute(value, axis, [(0, 1), (1, 0)])  39.9 us
    pallas_call x1, Pallas kernels, feed_forward(): pl.pallas_call(kernel, grid=(n_all,), in_specs=[whole, pl.BlockSpec((mode...  37.4 us
    pallas_call x1, Pallas kernels, backward_attention(): pl.pallas_call(kernel, grid_spec=pltpu.PrefetchScalarGridSpec(num_scalar_...  27.6 us
    pallas_call x2, Pallas kernels, forward_attention(): pl.pallas_call(kernel, grid_spec=pltpu.PrefetchScalarGridSpec(num_scalar_...  24.7 us
    all_gather x1, blocking collectives, shards(): packed = lax.all_gather(packed, 'z', axis=0, tiled=True)  20.9 us
  transfers between devices with their start and end apart: 54, of which 16 were waited for; matrix products, arithmetic and copies ran while one was open for 7% of the time, Pallas kernels for 24%

profile of v4, /device:TPU:0, one launch (start us, length us, event | category | flops | bytes accessed | tf_op | source)
XLA Modules:
  0.0 433.9 jit_solution(16641692364544147095)
XLA Ops:
  9.0 2.3 fusion.6.refs_0_
  11.3 2.9 collective-permute-start
  14.3 1.5 collective-permute-start.1
  15.9 1.6 copy-done.6
  17.5 1.5 shard_map.195
  20.1 20.9 %all_gather.12 = bf16[1088,384]{1,0:T(8,128)(2,1)} all-gather(bf16[272,384]{1,0:T(8,128)(2,1)S(1)} %fusion.10), channel_id=1, replica_groups=mesh['a'=2,'b'=2,'c'=2,'z'=4] {'z'}, dimensions={0}, use_global_device_ids=true | all-gather | bytes 1044480 | tf_op jit(solution)/shard_map/all_gather | solution.py:1008
  43.0 1.6 copy-done.7
  45.6 1.6 shard_map.200
  47.3 2.0 slice.156
  49.8 1.9 slice.157
  53.8 13.8 %shard_map.196 = (bf16[4096,1024]{1,0:T(8,128)(2,1)}, bf16[4096,384]{1,0:T(8,128)(2,1)}) custom-call(bf16[544,1024]{1,0:T(8,128)(2,1)} %fusion.6.refs_0_, bf16[544,1024]{1,0:T(8,128)(2,1)} %collective-permute-done.refs_1_, bf16[544,1024]{1,0:T(8,128)(2,1)} %collective-permute-done.1.refs_2_, bf16[544,1024]{1,0:T(8,128)(2,1)} %collective-permute-done.4.refs_3_, ...), custom_call_target="tpu_custom_call" | custom-call | flops 1 | bytes 1 | tf_op jit(solution)/shard_map/pallas_call | solution.py:745
  70.5 1.9 copy-done.2
  72.5 3.8 shard_map.197
  76.3 1.7 copy-done.3
  78.0 12.1 %shard_map.198 = (bf16[8,2,256,128]{3,2,1,0:T(8,128)(2,1)S(1)}, f32[2,128,2048]{2,1,0:T(8,128)S(1)}, f32[2,2,2048]{2,1,0:T(2,128)S(1)}) custom-call(s32[64]{0:T(128)S(1)} %convert_element_type.114.slot_ref, s32[8]{0:T(128)S(1)} %fusion.13.at_ref, bf16[8,2,256,384]{3,2,1,0:T(8,128)(2,1)} %bitcast.76), custom_call_target="tpu_custom_call" | custom-call | flops 1 | bytes 1 | tf_op jit(solution)/shard_map/pallas_call | solution.py:109
  92.4 1.6 collective-permute-start.10
  93.9 1.6 copy-done.13
  95.5 12.5 %shard_map.199 = (bf16[8,2,256,128]{3,2,1,0:T(8,128)(2,1)S(1)}, f32[2,128,2048]{2,1,0:T(8,128)S(1)}, f32[2,2,2048]{2,1,0:T(2,128)S(1)}) custom-call(s32[64]{0:T(128)S(1)} %convert_element_type.114.slot_ref, s32[8]{0:T(128)S(1)} %fusion.13.at_ref, bf16[8,2,256,384]{3,2,1,0:T(8,128)(2,1)} %bitcast.77, ...), custom_call_target="tpu_custom_call", output_to_operand_aliasing={{0}: (3, {}), {1}: (4, {}), {2}: (5, {})} | custom-call | flops 1 | bytes 1 | tf_op jit(solution)/shard_map/pallas_call | solution.py:109
  110.4 41.8 %all_to_all.10.heads_ref = bf16[8,512,128]{2,1,0:T(8,128)(2,1)S(1)} all-to-all(bf16[8,512,128]{2,1,0:T(8,128)(2,1)} %bitcast.88), channel_id=1, replica_groups=mesh['a'=2,'b'=2,'c'=2,'z'=4] {'a','b','c'}, dimensions={0} | all-to-all | bytes 2097152 | tf_op jit(solution)/shard_map/all_to_all | solution.py:1054
  152.2 3.4 all-gather.6.cloned.1.call-done
  156.6 4.8 %collective-permute-done.8.refs_1_.refs_6_ = bf16[4,384,1024]{2,1,0:T(8,128)(2,1)S(1)} collective-permute-done((bf16[4,384,1024]{2,1,0:T(8,128)(2,1)}, bf16[4,384,1024]{2,1,0:T(8,128)(2,1)S(1)}, u32[]{:S(2)}, u32[]{:S(2)}) %collective-permute-start.8) | collective-permute-done | bytes 3145760 | tf_op jit(solution)/shard_map/ppermute | solution.py:907
  161.5 1.6 copy-done.51
  163.1 5.4 %shard_map.201 = (bf16[512,1024]{1,0:T(8,128)(2,1)S(1)}, f32[512,1024]{1,0:T(8,128)}, bf16[512,1024]{1,0:T(8,128)(2,1)S(1)}, bf16[1024,512]{1,0:T(8,128)(2,1)S(1)}, bf16[1024,1024]{1,0:T(8,128)(2,1)}) custom-call(s32[1]{0:T(128)} %bitcast.core_ref, bf16[8,512,128]{2,1,0:T(8,128)(2,1)S(1)} %all_to_all.10.heads_ref, bf16[512,1024]{1,0:T(8,128)(2,1)S(1)} %bitcast.75, ...), custom_call_target="tpu_custom_call" | custom-call | flops 1 | bytes 1 | tf_op jit(solution)/shard_map/pallas_call | solution.py:412
  172.5 37.4 %shard_map.202 = (f32[512,1024]{1,0:T(8,128)}, f32[512,1024]{1,0:T(8,128)}, bf16[4,1024,512]{2,1,0:T(8,128)(2,1)}, bf16[4,4,256,512]{3,2,1,0:T(8,128)(2,1)}, bf1...) custom-call(bf16[512,1024]{1,0:T(8,128)(2,1)} %copy-done.18, bf16[1024,512]{1,0:T(8,128)(2,1)} %copy-done.19, ...), custom_call_target="tpu_custom_call" | custom-call | flops 1 | bytes 1 | tf_op jit(solution)/shard_map/pallas_call | solution.py:355
  209.9 5.2 %shard_map.203 = (f32[512,1024]{1,0:T(8,128)S(1)}, bf16[512,1024]{1,0:T(8,128)(2,1)S(1)}, bf16[8,512,128]{2,1,0:T(8,128)(2,1)S(1)}, f32[8,1024]{1,0:T(8,128)S(1)}) custom-call(f32[512,1024]{1,0:T(8,128)} %get-tuple-element.123.total_ref, f32[512,1024]{1,0:T(8,128)} %get-tuple-element.132.grad_ref, bf16[512,1024]{1,0:T(8,128)(2,1)S(1)} %bitcast.90, ...), custom_call_target="tpu_custom_call" | custom-call | flops 1 | bytes 1 | tf_op jit(solution)/shard_map/pallas_call | solution.py:460
  216.9 2.9 shard_map.204
  220.9 3.7 all-to-all-start.1
  224.6 7.0 %collective-permute-done.15.refs_3_ = bf16[4,2,128,512]{3,2,1,0:T(8,128)(2,1)} collective-permute-done((bf16[4,2,128,512]{3,2,1,0:T(8,128)(2,1)}, bf16[4,2,128,512]{3,2,1,0:T(8,128)(2,1)}, u32[]{:S(2)}, u32[]{:S(2)}) %collective-permute-start.15) | collective-permute-done | bytes 1048608 | tf_op jit(solution)/shard_map/ppermute | solution.py:907
  231.6 5.2 %shard_map.205 = (bf16[640,512]{1,0:T(8,128)(2,1)S(1)}, bf16[640,512]{1,0:T(8,128)(2,1)S(1)}, bf16[640,512]{1,0:T(8,128)(2,1)S(1)}, bf16[640,512]{1,0:T(8,128)(2...) custom-call(bf16[4,1024,512]{2,1,0:T(8,128)(2,1)} %get-tuple-element, ...), custom_call_target="tpu_custom_call" | custom-call | flops 1 | bytes 12582912 | tf_op jit(solution)/shard_map/pallas_call | solution.py:603
  242.7 4.4 %shard_map.206 = bf16[4,4,256,512]{3,2,1,0:T(8,128)(2,1)S(1)} custom-call(bf16[4,4,256,512]{3,2,1,0:T(8,128)(2,1)} %get-tuple-element.158.refs_0_, bf16[4,4,256,512]{3,2,1,0:T(8,128)(2,1)} %collective-permute-done.20.refs_1_), custom_call_target="tpu_custom_call" | custom-call | flops 1 | bytes 12582912 | tf_op jit(solution)/shard_map/pallas_call | solution.py:576
  247.0 2.0 copy-done.4
  250.6 1.7 copy.31
  253.4 1.5 collective-permute-start.17
  255.0 1.5 collective-permute-start.16
  257.5 1.6 copy-done.15
  259.9 27.6 %shard_map.207 = bf16[8,2,256,384]{3,2,1,0:T(8,128)(2,1)} custom-call(s32[64]{0:T(128)S(1)} %convert_element_type.114.slot_ref, s32[8]{0:T(128)S(1)} %fusion.13.at_ref, bf16[8,2,256,384]{3,2,1,0:T(8,128)(2,1)} %bitcast.78, bf16[8,2,256,128]{3,2,1,0:T(8,128)(2,1)S(1)} %bitcast.91, f32[2,128,2048]{2,1,0:T(8,128)S(1)} %copy-done.15, f32[2,2,2048]{2,1,0:T(2,128)S(1)} %copy-done.40), custom_call_target="tpu_custom_call" | custom-call | flops 7516192768 | bytes 1 | tf_op jit(solution)/shard_map/pallas_call | solution.py:213
  289.2 2.4 convolution_convert_fusion
  291.7 1.5 collective-permute-start.28
  296.0 2.9 collective-permute-done.21
  298.9 2.0 copy-done.65
  300.9 5.9 %shard_map.208 = (bf16[256,1024]{1,0:T(8,128)(2,1)S(1)}, bf16[256,1024]{1,0:T(8,128)(2,1)S(1)}, bf16[256,1024]{1,0:T(8,128)(2,1)S(1)}, bf16[256,1024]{1,0:T(8,12...) custom-call(bf16[4,512,384]{2,1,0:T(8,128)(2,1)} %slice.145.slope_re, ...), custom_call_target="tpu_custom_call" | custom-call | flops 1 | bytes 1 | tf_op jit(solution)/shard_map/pallas_call | solution.py:497
  311.5 1.5 collective-permute-start.25
  313.8 7.7 %shard_map.209.refs_6_ = bf16[1024,512]{1,0:T(8,128)(2,1)S(1)} custom-call(bf16[4096,1024]{1,0:T(8,128)(2,1)} %get-tuple-element.177.normed_ref, bf16[4096,384]{1,0:T(8,128)(2,1)S(1)} %bitcast.86, bf16[1024,384]{1,0:T(8,128)(2,1)S(1)} %bitcast.83, f32[1024,128]{1,0:T(8,128)S(1)} %pad.14.columns_ref), custom_call_target="tpu_custom_call" | custom-call | flops 1 | bytes 1 | tf_op jit(solution)/shard_map/pallas_call | solution.py:547
  321.6 2.5 collective-permute-done.23
  330.6 1.9 shard_map.210
  334.8 1.5 collective-permute-start.24
  337.5 10.8 %collective-permute-done.22 = bf16[256,1024]{1,0:T(8,128)(2,1)S(1)} collective-permute-done((bf16[256,1024]{1,0:T(8,128)(2,1)S(1)}, bf16[256,1024]{1,0:T(8,128)(2,1)S(1)}, u32[]{:S(2)}, u32[]{:S(2)}) %collective-permute-start.22) | collective-permute-done | bytes 524320 | tf_op jit(solution)/shard_map/ppermute | solution.py:907
  348.3 1.5 collective-permute-done.24
  350.1 9.1 %collective-permute-done.27 = bf16[256,1024]{1,0:T(8,128)(2,1)S(1)} collective-permute-done((bf16[256,1024]{1,0:T(8,128)(2,1)S(1)}, bf16[256,1024]{1,0:T(8,128)(2,1)S(1)}, u32[]{:S(2)}, u32[]{:S(2)}) %collective-permute-start.27) | collective-permute-done | bytes 524320 | tf_op jit(solution)/shard_map/ppermute | solution.py:907
  359.5 1.5 multiply_reduce_fusion
  365.3 5.5 %collective-permute-done.30 = bf16[256,512]{1,0:T(8,128)(2,1)S(1)} collective-permute-done((bf16[256,512]{1,0:T(8,128)(2,1)S(1)}, bf16[256,512]{1,0:T(8,128)(2,1)S(1)}, u32[]{:S(2)}, u32[]{:S(2)}) %collective-permute-start.30) | collective-permute-done | bytes 262176 | tf_op jit(solution)/shard_map/ppermute | solution.py:907
  370.9 3.8 collective-permute-done.32
  375.7 2.7 collective-permute-start.41
  379.6 1.5 collective-permute-start.34
  383.2 1.6 collective-permute-start.44
  384.9 3.7 add_convert_fusion.1
  388.6 10.2 %collective-permute-done.43 = bf16[128,512]{1,0:T(8,128)(2,1)S(1)} collective-permute-done((bf16[128,512]{1,0:T(8,128)(2,1)S(1)}, bf16[128,512]{1,0:T(8,128)(2,1)S(1)}, u32[]{:S(2)}, u32[]{:S(2)}) %collective-permute-start.43) | collective-permute-done | bytes 131104 | tf_op jit(solution)/shard_map/ppermute | solution.py:907
  398.8 1.5 collective-permute-start.35
  402.3 3.9 collective-permute-done.35
  406.3 3.7 collective-permute-done.36
  411.3 1.7 add_convert_fusion
  413.0 2.0 collective-permute-done.48.refs_7_
  415.0 2.7 shard_map.212
  419.8 7.2 %shard_map.211 = (f32[2,128,4096]{2,1,0:T(8,128)}, f32[8,32,1024]{2,1,0:T(8,128)}, f32[2,128,3072]{2,1,0:T(8,128)}, f32[1,256]{1,0:T(1,128)}, f32[1,256]{1,0:T(1...) custom-call(s32[8]{0:T(128)} %copy-done.41, bf16[288,1024]{1,0:T(8,128)(2,1)} %reduce-scatter.5.cloned.1.call-done.refs_0_.refs_8_.refs_16_, ...), custom_call_target="tpu_custom_call" | custom-call | tf_op jit(solution)/shard_map/pallas_call | solution.py:866
  (288 shorter events, 69.3 us)
Async XLA Ops:
  7.2 84.4 %all-gather.4.cloned.1.call-start = ((), (), s32[]{:S(2)}) async-start(), calls=%async_computation.4 | async-start | bytes 2621440 | tf_op jit(solution)/shard_map/all_gather | solution.py:1013
  11.3 29.6 %collective-permute-start = (bf16[544,1024]{1,0:T(8,128)(2,1)}, bf16[544,1024]{1,0:T(8,128)(2,1)}, u32[]{:S(2)}, u32[]{:S(2)}) collective-permute-start(bf16[544,1024]{1,0:T(8,128)(2,1)} %fusion.6.refs_0_), channel_id=1, source_target_pairs={{0,8},{8,0},{1,9},{9,1},{2,10},{10,2},{3,11},{11,3},{4,12},{12,4},... | collective-permute-start | bytes 3342344 | tf_op jit(solution)/shard_map/ppermute | solution.py:907
  14.3 26.7 %collective-permute-start.1 = (bf16[544,1024]{1,0:T(8,128)(2,1)}, bf16[544,1024]{1,0:T(8,128)(2,1)}, u32[]{:S(2)}, u32[]{:S(2)}) collective-permute-start(bf16[544,1024]{1,0:T(8,128)(2,1)} %fusion.6.refs_0_), channel_id=1, source_target_pairs={{0,16},{16,0},{1,17},{17,1},{2,18},{18,2},{3,19},{19,3},{4,20},{20... | collective-permute-start | bytes 3342344 | tf_op jit(solution)/shard_map/ppermute | solution.py:907
  41.0 114.6 %all-gather.6.cloned.1.call-start = ((), (), s32[]{:S(2)}) async-start(), calls=%async_computation.7 | async-start | bytes 3932160 | tf_op jit(solution)/shard_map/all_gather | solution.py:1049
  41.0 12.8 %collective-permute-start.4 = (bf16[544,1024]{1,0:T(8,128)(2,1)}, bf16[544,1024]{1,0:T(8,128)(2,1)}, u32[]{:S(2)}, u32[]{:S(2)}) collective-permute-start(bf16[544,1024]{1,0:T(8,128)(2,1)} %fusion.6.refs_0_), channel_id=1, source_target_pairs={{0,4},{4,0},{1,5},{5,1},{2,6},{6,2},{3,7},{7,3},{8,12},{12,8},{9,1... | collective-permute-start | bytes 3342344 | tf_op jit(solution)/shard_map/ppermute | solution.py:907
  41.1 12.7 %collective-permute-start.5 = (bf16[544,1024]{1,0:T(8,128)(2,1)}, bf16[544,1024]{1,0:T(8,128)(2,1)}, u32[]{:S(2)}, u32[]{:S(2)}) collective-permute-start(bf16[544,1024]{1,0:T(8,128)(2,1)} %collective-permute-done.refs_1_), channel_id=1, source_target_pairs={{0,4},{4,0},{1,5},{5,1},{2,6},{6,2},{3,7},{7,3},{8,12},{12,8},{9,1... | collective-permute-start | bytes 3342344 | tf_op jit(solution)/shard_map/ppermute | solution.py:907
  41.6 12.2 %collective-permute-start.6 = (bf16[544,1024]{1,0:T(8,128)(2,1)}, bf16[544,1024]{1,0:T(8,128)(2,1)}, u32[]{:S(2)}, u32[]{:S(2)}) collective-permute-start(bf16[544,1024]{1,0:T(8,128)(2,1)} %collective-permute-done.1.refs_2_), channel_id=1, source_target_pairs={{0,4},{4,0},{1,5},{5,1},{2,6},{6,2},{3,7},{7,3},{8,12},{12,8},{9,1... | collective-permute-start | bytes 3342344 | tf_op jit(solution)/shard_map/ppermute | solution.py:907
  41.7 373.3 %copy-start.41 = (s32[8]{0:T(128)}, s32[8]{0:T(128)S(1)}, u32[]{:S(2)}) copy-start(s32[8]{0:T(128)S(1)} %fusion.13.at_ref) | copy-start | bytes 100
  49.3 18.3 %collective-permute-start.2 = (bf16[272,1024]{1,0:T(8,128)(2,1)}, bf16[272,1024]{1,0:T(8,128)(2,1)S(1)}, u32[]{:S(2)}, u32[]{:S(2)}) collective-permute-start(bf16[272,1024]{1,0:T(8,128)(2,1)} %slice.156), channel_id=1, source_target_pairs={{0,8},{8,0},{1,9},{9,1},{2,10},{10,2},{3,11},{11,3},{4,12},{12,4},... | collective-permute-start | bytes 1671176 | tf_op jit(solution)/shard_map/ppermute | solution.py:907
  51.7 15.9 %collective-permute-start.3 = (bf16[272,1024]{1,0:T(8,128)(2,1)}, bf16[272,1024]{1,0:T(8,128)(2,1)S(1)}, u32[]{:S(2)}, u32[]{:S(2)}) collective-permute-start(bf16[272,1024]{1,0:T(8,128)(2,1)} %slice.157), channel_id=1, source_target_pairs={{0,16},{16,0},{1,17},{17,1},{2,18},{18,2},{3,19},{19,3},{4,20},{20... | collective-permute-start | bytes 1671176 | tf_op jit(solution)/shard_map/ppermute | solution.py:907
  67.7 2.8 collective-permute-start.7
  91.6 64.6 %collective-permute-start.12 = (bf16[1024,1024]{1,0:T(8,128)(2,1)}, bf16[1024,1024]{1,0:T(8,128)(2,1)}, u32[]{:S(2)}, u32[]{:S(2)}) collective-permute-start(bf16[1024,1024]{1,0:T(8,128)(2,1)} %all-gather.4.cloned.1.call-done.refs_7_), channel_id=1, source_target_pairs={{0,16},{16,0},{1,17},{17,1},{2,18},{18,2},{3,19},{19,3},{4,20},{20... | collective-permute-start | bytes 6291464 | tf_op jit(solution)/shard_map/ppermute | solution.py:907
  92.4 63.8 %collective-permute-start.10 = (bf16[1024,1024]{1,0:T(8,128)(2,1)}, bf16[1024,1024]{1,0:T(8,128)(2,1)}, u32[]{:S(2)}, u32[]{:S(2)}) collective-permute-start(bf16[1024,1024]{1,0:T(8,128)(2,1)} %all-gather.4.cloned.1.call-done.refs_7_), channel_id=1, source_target_pairs={{0,8},{8,0},{1,9},{9,1},{2,10},{10,2},{3,11},{11,3},{4,12},{12,4},... | collective-permute-start | bytes 6291464 | tf_op jit(solution)/shard_map/ppermute | solution.py:907
  110.4 58.1 %copy-start.39 = (f32[2,2,2048]{2,1,0:T(2,128)}, f32[2,2,2048]{2,1,0:T(2,128)S(1)}, u32[]{:S(2)}) copy-start(f32[2,2,2048]{2,1,0:T(2,128)S(1)} %get-tuple-element.162.log_ref) | copy-start | bytes 98308
  110.4 52.7 %copy-start.1 = (bf16[2,256,1024]{2,1,0:T(8,128)(2,1)S(1)}, bf16[2,256,1024]{2,1,0:T(8,128)(2,1)}, u32[]{:S(2)}) copy-start(bf16[2,256,1024]{2,1,0:T(8,128)(2,1)} %param.14) | copy-start | bytes 3145732
  155.6 5.9 %collective-permute-start.8 = (bf16[4,384,1024]{2,1,0:T(8,128)(2,1)}, bf16[4,384,1024]{2,1,0:T(8,128)(2,1)S(1)}, u32[]{:S(2)}, u32[]{:S(2)}) collective-permute-start(bf16[4,384,1024]{2,1,0:T(8,128)(2,1)} %bitcast.104), channel_id=1, source_target_pairs={{0,4},{4,0},{1,5},{5,1},{2,6},{6,2},{3,7},{7,3},{8,12},{12,8},{9,1... | collective-permute-start | bytes 9437192 | tf_op jit(solution)/shard_map/ppermute | solution.py:907
  155.6 14.8 %collective-permute-start.9 = (bf16[1024,1024]{1,0:T(8,128)(2,1)}, bf16[1024,1024]{1,0:T(8,128)(2,1)S(1)}, u32[]{:S(2)}, u32[]{:S(2)}) collective-permute-start(bf16[1024,1024]{1,0:T(8,128)(2,1)} %all-gather.4.cloned.1.call-done.refs_7_), channel_id=1, source_target_pairs={{0,4},{4,0},{1,5},{5,1},{2,6},{6,2},{3,7},{7,3},{8,12},{12,8},{9,1... | collective-permute-start | bytes 6291464 | tf_op jit(solution)/shard_map/ppermute | solution.py:907
  156.1 14.4 %collective-permute-start.13 = (bf16[1024,1024]{1,0:T(8,128)(2,1)}, bf16[1024,1024]{1,0:T(8,128)(2,1)S(1)}, u32[]{:S(2)}, u32[]{:S(2)}) collective-permute-start(bf16[1024,1024]{1,0:T(8,128)(2,1)} %collective-permute-done.12.refs_9_), channel_id=1, source_target_pairs={{0,4},{4,0},{1,5},{5,1},{2,6},{6,2},{3,7},{7,3},{8,12},{12,8},{9,1... | collective-permute-start | bytes 6291464 | tf_op jit(solution)/shard_map/ppermute | solution.py:907
  156.1 14.4 %collective-permute-start.11 = (bf16[1024,1024]{1,0:T(8,128)(2,1)}, bf16[1024,1024]{1,0:T(8,128)(2,1)}, u32[]{:S(2)}, u32[]{:S(2)}) collective-permute-start(bf16[1024,1024]{1,0:T(8,128)(2,1)} %collective-permute-done.10.refs_8_), channel_id=1, source_target_pairs={{0,4},{4,0},{1,5},{5,1},{2,6},{6,2},{3,7},{7,3},{8,12},{12,8},{9,1... | collective-permute-start | bytes 6291464 | tf_op jit(solution)/shard_map/ppermute | solution.py:907
  172.5 37.4 %copy-start.9 = (bf16[2,256,1024]{2,1,0:T(8,128)(2,1)S(1)}, bf16[2,256,1024]{2,1,0:T(8,128)(2,1)}, u32[]{:S(2)}) copy-start(bf16[2,256,1024]{2,1,0:T(8,128)(2,1)} %param.15) | copy-start | bytes 3145732
  216.4 15.2 %collective-permute-start.14 = (bf16[4,1024,512]{2,1,0:T(8,128)(2,1)}, bf16[4,1024,512]{2,1,0:T(8,128)(2,1)}, u32[]{:S(2)}, u32[]{:S(2)}) collective-permute-start(bf16[4,1024,512]{2,1,0:T(8,128)(2,1)} %get-tuple-element.142), channel_id=1, source_target_pairs={{0,4},{4,0},{1,5},{5,1},{2,6},{6,2},{3,7},{7,3},{8,12},{12,8},{9,1... | collective-permute-start | bytes 12582920 | tf_op jit(solution)/shard_map/ppermute | solution.py:907
  216.6 26.1 %collective-permute-start.20 = (bf16[4,4,256,512]{3,2,1,0:T(8,128)(2,1)}, bf16[4,4,256,512]{3,2,1,0:T(8,128)(2,1)}, u32[]{:S(2)}, u32[]{:S(2)}) collective-permute-start(bf16[4,4,256,512]{3,2,1,0:T(8,128)(2,1)} %get-tuple-element.159), channel_id=1, source_target_pairs={{0,4},{4,0},{1,5},{5,1},{2,6},{6,2},{3,7},{7,3},{8,12},{12,8},{9,1... | collective-permute-start | bytes 12582920 | tf_op jit(solution)/shard_map/ppermute | solution.py:907
  220.7 10.8 %collective-permute-start.15 = (bf16[4,2,128,512]{3,2,1,0:T(8,128)(2,1)}, bf16[4,2,128,512]{3,2,1,0:T(8,128)(2,1)}, u32[]{:S(2)}, u32[]{:S(2)}) collective-permute-start(bf16[4,2,128,512]{3,2,1,0:T(8,128)(2,1)} %get-tuple-element.146), channel_id=1, source_target_pairs={{0,4},{4,0},{1,5},{5,1},{2,6},{6,2},{3,7},{7,3},{8,12},{12,8},{9,1... | collective-permute-start | bytes 3145736 | tf_op jit(solution)/shard_map/ppermute | solution.py:907
  220.9 21.8 %all-to-all-start.1 = ((bf16[8,512,128]{2,1,0:T(8,128)(2,1)}), bf16[8,512,128]{2,1,0:T(8,128)(2,1)S(1)}, u32[]{:S(2)}, u32[]{:S(2)}) async-start(bf16[8,512,128]{2,1,0:T(8,128)(2,1)} %copy-done.17), calls=%async_computation.1 | async-start | bytes 2097152 | tf_op jit(solution)/shard_map/all_to_all | solution.py:1092
  224.6 101.6 %reduce-scatter.3.cloned.1.call-start = ((), (), s32[]{:S(2)}) async-start(), calls=%async_computation.5 | async-start | bytes 5242880 | tf_op jit(solution)/shard_map/reduce_scatter | solution.py:1113
  249.1 130.5 %reduce-scatter.5.cloned.1.call-start = ((), (), s32[]{:S(2)}) async-start(), calls=%async_computation.6 | async-start | bytes 2949120 | tf_op jit(solution)/shard_map/reduce_scatter | solution.py:1173
  253.4 34.1 %collective-permute-start.17 = (bf16[640,512]{1,0:T(8,128)(2,1)}, bf16[640,512]{1,0:T(8,128)(2,1)S(1)}, u32[]{:S(2)}, u32[]{:S(2)}) collective-permute-start(bf16[640,512]{1,0:T(8,128)(2,1)} %copy-done.46), channel_id=1, source_target_pairs={{0,8},{8,0},{1,9},{9,1},{2,10},{10,2},{3,11},{11,3},{4,12},{12,4},... | collective-permute-start | bytes 1966088 | tf_op jit(solution)/shard_map/ppermute | solution.py:907
  255.0 32.8 %collective-permute-start.16 = (bf16[640,512]{1,0:T(8,128)(2,1)}, bf16[640,512]{1,0:T(8,128)(2,1)S(1)}, u32[]{:S(2)}, u32[]{:S(2)}) collective-permute-start(bf16[640,512]{1,0:T(8,128)(2,1)} %copy-done.45), channel_id=1, source_target_pairs={{0,16},{16,0},{1,17},{17,1},{2,18},{18,2},{3,19},{19,3},{4,20},{20... | collective-permute-start | bytes 1966088 | tf_op jit(solution)/shard_map/ppermute | solution.py:907
  256.4 32.3 %collective-permute-start.18 = (bf16[640,512]{1,0:T(8,128)(2,1)}, bf16[640,512]{1,0:T(8,128)(2,1)S(1)}, u32[]{:S(2)}, u32[]{:S(2)}) collective-permute-start(bf16[640,512]{1,0:T(8,128)(2,1)} %copy-done.44), channel_id=1, source_target_pairs={{0,8},{8,0},{1,9},{9,1},{2,10},{10,2},{3,11},{11,3},{4,12},{12,4},... | collective-permute-start | bytes 1966088 | tf_op jit(solution)/shard_map/ppermute | solution.py:907
  257.0 31.8 %collective-permute-start.19 = (bf16[640,512]{1,0:T(8,128)(2,1)}, bf16[640,512]{1,0:T(8,128)(2,1)S(1)}, u32[]{:S(2)}, u32[]{:S(2)}) collective-permute-start(bf16[640,512]{1,0:T(8,128)(2,1)} %copy-done.43), channel_id=1, source_target_pairs={{0,16},{16,0},{1,17},{17,1},{2,18},{18,2},{3,19},{19,3},{4,20},{20... | collective-permute-start | bytes 1966088 | tf_op jit(solution)/shard_map/ppermute | solution.py:907
  259.9 27.6 %copy-start.33 = (bf16[640,512]{1,0:T(8,128)(2,1)S(1)}, bf16[640,512]{1,0:T(8,128)(2,1)}, u32[]{:S(2)}) copy-start(bf16[640,512]{1,0:T(8,128)(2,1)} %copy-done.32) | copy-start | bytes 1966084
  291.6 7.2 %collective-permute-start.21 = (bf16[2048,1024]{1,0:T(8,128)(2,1)S(1)}, bf16[2048,1024]{1,0:T(8,128)(2,1)S(1)}, u32[]{:S(2)}, u32[]{:S(2)}) collective-permute-start(bf16[2048,1024]{1,0:T(8,128)(2,1)S(1)} %convolution_convert_fusion), channel_id=1, source_target_pairs={{0,4},{4,0},{1,5},{5,1},{2,6},{6,2},{3,7},{7,3},{8,12},{12,8},{9,1... | collective-permute-start | bytes 12582920 | tf_op jit(solution)/shard_map/ppermute | solution.py:907
  291.7 21.3 %collective-permute-start.28 = (bf16[640,512]{1,0:T(8,128)(2,1)S(1)}, bf16[640,512]{1,0:T(8,128)(2,1)S(1)}, u32[]{:S(2)}, u32[]{:S(2)}) collective-permute-start(bf16[640,512]{1,0:T(8,128)(2,1)S(1)} %add_convert_fusion.2), channel_id=1, source_target_pairs={{0,16},{16,0},{1,17},{17,1},{2,18},{18,2},{3,19},{19,3},{4,20},{20... | collective-permute-start | bytes 1966088 | tf_op jit(solution)/shard_map/ppermute | solution.py:907
  293.2 20.6 %collective-permute-start.29 = (bf16[640,512]{1,0:T(8,128)(2,1)S(1)}, bf16[640,512]{1,0:T(8,128)(2,1)S(1)}, u32[]{:S(2)}, u32[]{:S(2)}) collective-permute-start(bf16[640,512]{1,0:T(8,128)(2,1)S(1)} %add_convert_fusion.3), channel_id=1, source_target_pairs={{0,8},{8,0},{1,9},{9,1},{2,10},{10,2},{3,11},{11,3},{4,12},{12,4},... | collective-permute-start | bytes 1966088 | tf_op jit(solution)/shard_map/ppermute | solution.py:907
  310.1 14.0 %collective-permute-start.23 = (bf16[256,1024]{1,0:T(8,128)(2,1)S(1)}, bf16[256,1024]{1,0:T(8,128)(2,1)S(1)}, u32[]{:S(2)}, u32[]{:S(2)}) collective-permute-start(bf16[256,1024]{1,0:T(8,128)(2,1)S(1)} %get-tuple-element.167), channel_id=1, source_target_pairs={{0,8},{8,0},{1,9},{9,1},{2,10},{10,2},{3,11},{11,3},{4,12},{12,4},... | collective-permute-start | bytes 1572872 | tf_op jit(solution)/shard_map/ppermute | solution.py:907
  311.5 13.7 %collective-permute-start.25 = (bf16[256,1024]{1,0:T(8,128)(2,1)S(1)}, bf16[256,1024]{1,0:T(8,128)(2,1)S(1)}, u32[]{:S(2)}, u32[]{:S(2)}) collective-permute-start(bf16[256,1024]{1,0:T(8,128)(2,1)S(1)} %get-tuple-element.170), channel_id=1, source_target_pairs={{0,16},{16,0},{1,17},{17,1},{2,18},{18,2},{3,19},{19,3},{4,20},{20... | collective-permute-start | bytes 1572872 | tf_op jit(solution)/shard_map/ppermute | solution.py:907
  332.4 17.4 %copy-start.38 = (bf16[256,1024]{1,0:T(8,128)(2,1)S(1)}, bf16[256,1024]{1,0:T(8,128)(2,1)}, u32[]{:S(2)}) copy-start(bf16[256,1024]{1,0:T(8,128)(2,1)} %copy-done.37) | copy-start | bytes 1572868
  332.4 26.7 %copy-start.36 = (bf16[256,1024]{1,0:T(8,128)(2,1)S(1)}, bf16[256,1024]{1,0:T(8,128)(2,1)}, u32[]{:S(2)}) copy-start(bf16[256,1024]{1,0:T(8,128)(2,1)} %copy-done.35) | copy-start | bytes 1572868
  333.5 14.9 %collective-permute-start.22 = (bf16[256,1024]{1,0:T(8,128)(2,1)S(1)}, bf16[256,1024]{1,0:T(8,128)(2,1)S(1)}, u32[]{:S(2)}, u32[]{:S(2)}) collective-permute-start(bf16[256,1024]{1,0:T(8,128)(2,1)S(1)} %copy-done.50), channel_id=1, source_target_pairs={{0,8},{8,0},{1,9},{9,1},{2,10},{10,2},{3,11},{11,3},{4,12},{12,4},... | collective-permute-start | bytes 1572872 | tf_op jit(solution)/shard_map/ppermute | solution.py:907
  334.8 15.1 %collective-permute-start.24 = (bf16[256,1024]{1,0:T(8,128)(2,1)}, bf16[256,1024]{1,0:T(8,128)(2,1)S(1)}, u32[]{:S(2)}, u32[]{:S(2)}) collective-permute-start(bf16[256,1024]{1,0:T(8,128)(2,1)} %add_convert_fusion.5), channel_id=1, source_target_pairs={{0,16},{16,0},{1,17},{17,1},{2,18},{18,2},{3,19},{19,3},{4,20},{20... | collective-permute-start | bytes 1572872 | tf_op jit(solution)/shard_map/ppermute | solution.py:907
  336.2 22.9 %collective-permute-start.27 = (bf16[256,1024]{1,0:T(8,128)(2,1)S(1)}, bf16[256,1024]{1,0:T(8,128)(2,1)S(1)}, u32[]{:S(2)}, u32[]{:S(2)}) collective-permute-start(bf16[256,1024]{1,0:T(8,128)(2,1)S(1)} %copy-done.48), channel_id=1, source_target_pairs={{0,16},{16,0},{1,17},{17,1},{2,18},{18,2},{3,19},{19,3},{4,20},{20... | collective-permute-start | bytes 1572872 | tf_op jit(solution)/shard_map/ppermute | solution.py:907
  336.8 22.4 %collective-permute-start.26 = (bf16[256,1024]{1,0:T(8,128)(2,1)}, bf16[256,1024]{1,0:T(8,128)(2,1)S(1)}, u32[]{:S(2)}, u32[]{:S(2)}) collective-permute-start(bf16[256,1024]{1,0:T(8,128)(2,1)} %add_convert_fusion.4), channel_id=1, source_target_pairs={{0,8},{8,0},{1,9},{9,1},{2,10},{10,2},{3,11},{11,3},{4,12},{12,4},... | collective-permute-start | bytes 1572872 | tf_op jit(solution)/shard_map/ppermute | solution.py:907
  350.1 10.9 %copy-start.52 = (f32[256,1024]{1,0:T(8,128)}, f32[256,1024]{1,0:T(8,128)S(1)}, u32[]{:S(2)}) copy-start(f32[256,1024]{1,0:T(8,128)S(1)} %convert_add_fusion.1) | copy-start | bytes 3145732
  361.5 9.3 %collective-permute-start.30 = (bf16[256,512]{1,0:T(8,128)(2,1)S(1)}, bf16[256,512]{1,0:T(8,128)(2,1)S(1)}, u32[]{:S(2)}, u32[]{:S(2)}) collective-permute-start(bf16[256,512]{1,0:T(8,128)(2,1)S(1)} %get-tuple-element.201), channel_id=1, source_target_pairs={{0,8},{8,0},{1,9},{9,1},{2,10},{10,2},{3,11},{11,3},{4,12},{12,4},... | collective-permute-start | bytes 786440 | tf_op jit(solution)/shard_map/ppermute | solution.py:907
  362.2 8.7 %collective-permute-start.31 = (bf16[256,512]{1,0:T(8,128)(2,1)S(1)}, bf16[256,512]{1,0:T(8,128)(2,1)S(1)}, u32[]{:S(2)}, u32[]{:S(2)}) collective-permute-start(bf16[256,512]{1,0:T(8,128)(2,1)S(1)} %get-tuple-element.203), channel_id=1, source_target_pairs={{0,16},{16,0},{1,17},{17,1},{2,18},{18,2},{3,19},{19,3},{4,20},{20... | collective-permute-start | bytes 786440 | tf_op jit(solution)/shard_map/ppermute | solution.py:907
  363.6 11.0 %collective-permute-start.32 = (bf16[256,512]{1,0:T(8,128)(2,1)S(1)}, bf16[256,512]{1,0:T(8,128)(2,1)S(1)}, u32[]{:S(2)}, u32[]{:S(2)}) collective-permute-start(bf16[256,512]{1,0:T(8,128)(2,1)S(1)} %get-tuple-element.202), channel_id=1, source_target_pairs={{0,24},{24,0},{8,16},{16,8},{1,25},{25,1},{9,17},{17,9},{2,26},{26... | collective-permute-start | bytes 786440 | tf_op jit(solution)/shard_map/ppermute | solution.py:1169
  374.8 7.8 %collective-permute-start.42 = (bf16[256,512]{1,0:T(8,128)(2,1)S(1)}, bf16[256,512]{1,0:T(8,128)(2,1)S(1)}, u32[]{:S(2)}, u32[]{:S(2)}) collective-permute-start(bf16[256,512]{1,0:T(8,128)(2,1)S(1)} %fusion.8.refs_0_), channel_id=1, source_target_pairs={{0,16},{16,0},{1,17},{17,1},{2,18},{18,2},{3,19},{19,3},{4,20},{20... | collective-permute-start | bytes 786440 | tf_op jit(solution)/shard_map/ppermute | solution.py:907
  375.7 7.6 %collective-permute-start.41 = (bf16[256,512]{1,0:T(8,128)(2,1)S(1)}, bf16[256,512]{1,0:T(8,128)(2,1)S(1)}, u32[]{:S(2)}, u32[]{:S(2)}) collective-permute-start(bf16[256,512]{1,0:T(8,128)(2,1)S(1)} %fusion.8.refs_0_), channel_id=1, source_target_pairs={{0,8},{8,0},{1,9},{9,1},{2,10},{10,2},{3,11},{11,3},{4,12},{12,4},... | collective-permute-start | bytes 786440 | tf_op jit(solution)/shard_map/ppermute | solution.py:907
  379.6 19.1 %collective-permute-start.34 = (bf16[288,1024]{1,0:T(8,128)(2,1)}, bf16[288,1024]{1,0:T(8,128)(2,1)S(1)}, u32[]{:S(2)}, u32[]{:S(2)}) collective-permute-start(bf16[288,1024]{1,0:T(8,128)(2,1)} %reduce-scatter.5.cloned.1.call-done.refs_0_.refs_8_.refs_16_), channel_id=1, source_target_pairs={{0,16},{16,0},{1,17},{17,1},{2,18},{18,2},{3,19},{19,3},{4,20},{20... | collective-permute-start | bytes 1769480 | tf_op jit(solution)/shard_map/ppermute | solution.py:907
  381.1 19.8 %collective-permute-start.33 = (bf16[288,1024]{1,0:T(8,128)(2,1)}, bf16[288,1024]{1,0:T(8,128)(2,1)S(1)}, u32[]{:S(2)}, u32[]{:S(2)}) collective-permute-start(bf16[288,1024]{1,0:T(8,128)(2,1)} %reduce-scatter.5.cloned.1.call-done.refs_0_.refs_8_.refs_16_), channel_id=1, source_target_pairs={{0,8},{8,0},{1,9},{9,1},{2,10},{10,2},{3,11},{11,3},{4,12},{12,4},... | collective-permute-start | bytes 1769480 | tf_op jit(solution)/shard_map/ppermute | solution.py:907
  382.6 16.1 %collective-permute-start.43 = (bf16[128,512]{1,0:T(8,128)(2,1)S(1)}, bf16[128,512]{1,0:T(8,128)(2,1)S(1)}, u32[]{:S(2)}, u32[]{:S(2)}) collective-permute-start(bf16[128,512]{1,0:T(8,128)(2,1)S(1)} %slice.170), channel_id=1, source_target_pairs={{0,8},{8,0},{1,9},{9,1},{2,10},{10,2},{3,11},{11,3},{4,12},{12,4},... | collective-permute-start | bytes 393224 | tf_op jit(solution)/shard_map/ppermute | solution.py:907
  383.2 17.1 %collective-permute-start.44 = (bf16[128,512]{1,0:T(8,128)(2,1)S(1)}, bf16[128,512]{1,0:T(8,128)(2,1)S(1)}, u32[]{:S(2)}, u32[]{:S(2)}) collective-permute-start(bf16[128,512]{1,0:T(8,128)(2,1)S(1)} %slice.171), channel_id=1, source_target_pairs={{0,16},{16,0},{1,17},{17,1},{2,18},{18,2},{3,19},{19,3},{4,20},{20... | collective-permute-start | bytes 393224 | tf_op jit(solution)/shard_map/ppermute | solution.py:907
  384.9 16.7 %copy-start.56 = (f32[512,1024]{1,0:T(8,128)S(1)}, f32[512,1024]{1,0:T(8,128)}, u32[]{:S(2)}) copy-start(f32[512,1024]{1,0:T(8,128)} %get-tuple-element.197) | copy-start | bytes 6291460
  398.8 11.4 %copy-start.57 = (bf16[288,1024]{1,0:T(8,128)(2,1)}, bf16[288,1024]{1,0:T(8,128)(2,1)S(1)}, u32[]{:S(2)}) copy-start(bf16[288,1024]{1,0:T(8,128)(2,1)S(1)} %collective-permute-done.34.refs_2_.refs_10_.refs_18_) | copy-start | bytes 1769476
  398.8 7.4 %collective-permute-start.35 = (bf16[144,1024]{1,0:T(8,128)(2,1)S(1)}, bf16[144,1024]{1,0:T(8,128)(2,1)S(1)}, u32[]{:S(2)}, u32[]{:S(2)}) collective-permute-start(bf16[144,1024]{1,0:T(8,128)(2,1)S(1)} %slice.168), channel_id=1, source_target_pairs={{0,8},{8,0},{1,9},{9,1},{2,10},{10,2},{3,11},{11,3},{4,12},{12,4},... | collective-permute-start | bytes 884744 | tf_op jit(solution)/shard_map/ppermute | solution.py:907
  400.3 10.3 %collective-permute-start.47 = (bf16[256,512]{1,0:T(8,128)(2,1)S(1)}, bf16[256,512]{1,0:T(8,128)(2,1)S(1)}, u32[]{:S(2)}, u32[]{:S(2)}) collective-permute-start(bf16[256,512]{1,0:T(8,128)(2,1)S(1)} %collective-permute-done.42.refs_2_), channel_id=1, source_target_pairs={{0,4},{4,0},{1,5},{5,1},{2,6},{6,2},{3,7},{7,3},{8,12},{12,8},{9,1... | collective-permute-start | bytes 786440 | tf_op jit(solution)/shard_map/ppermute | solution.py:907
  400.4 10.3 %collective-permute-start.46 = (bf16[256,512]{1,0:T(8,128)(2,1)S(1)}, bf16[256,512]{1,0:T(8,128)(2,1)S(1)}, u32[]{:S(2)}, u32[]{:S(2)}) collective-permute-start(bf16[256,512]{1,0:T(8,128)(2,1)S(1)} %collective-permute-done.41.refs_1_), channel_id=1, source_target_pairs={{0,4},{4,0},{1,5},{5,1},{2,6},{6,2},{3,7},{7,3},{8,12},{12,8},{9,1... | collective-permute-start | bytes 786440 | tf_op jit(solution)/shard_map/ppermute | solution.py:907
  400.9 9.1 %collective-permute-start.36 = (bf16[144,1024]{1,0:T(8,128)(2,1)S(1)}, bf16[144,1024]{1,0:T(8,128)(2,1)S(1)}, u32[]{:S(2)}, u32[]{:S(2)}) collective-permute-start(bf16[144,1024]{1,0:T(8,128)(2,1)S(1)} %slice.169), channel_id=1, source_target_pairs={{0,16},{16,0},{1,17},{17,1},{2,18},{18,2},{3,19},{19,3},{4,20},{20... | collective-permute-start | bytes 884744 | tf_op jit(solution)/shard_map/ppermute | solution.py:907
  402.2 8.9 %collective-permute-start.45 = (bf16[256,512]{1,0:T(8,128)(2,1)S(1)}, bf16[256,512]{1,0:T(8,128)(2,1)S(1)}, u32[]{:S(2)}, u32[]{:S(2)}) collective-permute-start(bf16[256,512]{1,0:T(8,128)(2,1)S(1)} %fusion.8.refs_0_), channel_id=1, source_target_pairs={{0,4},{4,0},{1,5},{5,1},{2,6},{6,2},{3,7},{7,3},{8,12},{12,8},{9,1... | collective-permute-start | bytes 786440 | tf_op jit(solution)/shard_map/ppermute | solution.py:907
  410.0 7.7 %collective-permute-start.40 = (bf16[288,1024]{1,0:T(8,128)(2,1)S(1)}, bf16[288,1024]{1,0:T(8,128)(2,1)S(1)}, u32[]{:S(2)}, u32[]{:S(2)}) collective-permute-start(bf16[288,1024]{1,0:T(8,128)(2,1)S(1)} %constant_dynamic-update-slice_fusion.2.refs_3_.refs_11_.refs_19_), channel_id=1, source_target_pairs={{0,4},{4,0},{1,5},{5,1},{2,6},{6,2},{3,7},{7,3},{8,12},{12,8},{9,1... | collective-permute-start | bytes 1769480 | tf_op jit(solution)/shard_map/ppermute | solution.py:907
  410.1 7.6 %collective-permute-start.39 = (bf16[288,1024]{1,0:T(8,128)(2,1)S(1)}, bf16[288,1024]{1,0:T(8,128)(2,1)S(1)}, u32[]{:S(2)}, u32[]{:S(2)}) collective-permute-start(bf16[288,1024]{1,0:T(8,128)(2,1)S(1)} %collective-permute-done.34.refs_2_.refs_10_.refs_18_), channel_id=1, source_target_pairs={{0,4},{4,0},{1,5},{5,1},{2,6},{6,2},{3,7},{7,3},{8,12},{12,8},{9,1... | collective-permute-start | bytes 1769480 | tf_op jit(solution)/shard_map/ppermute | solution.py:907
  410.6 7.1 %collective-permute-start.38 = (bf16[288,1024]{1,0:T(8,128)(2,1)S(1)}, bf16[288,1024]{1,0:T(8,128)(2,1)S(1)}, u32[]{:S(2)}, u32[]{:S(2)}) collective-permute-start(bf16[288,1024]{1,0:T(8,128)(2,1)S(1)} %collective-permute-done.33.refs_1_.refs_9_.refs_17_), channel_id=1, source_target_pairs={{0,4},{4,0},{1,5},{5,1},{2,6},{6,2},{3,7},{7,3},{8,12},{12,8},{9,1... | collective-permute-start | bytes 1769480 | tf_op jit(solution)/shard_map/ppermute | solution.py:907
  410.7 7.0 %collective-permute-start.37 = (bf16[288,1024]{1,0:T(8,128)(2,1)S(1)}, bf16[288,1024]{1,0:T(8,128)(2,1)S(1)}, u32[]{:S(2)}, u32[]{:S(2)}) collective-permute-start(bf16[288,1024]{1,0:T(8,128)(2,1)S(1)} %copy-done.60), channel_id=1, source_target_pairs={{0,4},{4,0},{1,5},{5,1},{2,6},{6,2},{3,7},{7,3},{8,12},{12,8},{9,1... | collective-permute-start | bytes 1769480 | tf_op jit(solution)/shard_map/ppermute | solution.py:907
  411.2 3.9 collective-permute-start.48
  (65 other events, 162.5 us)
Sparse Core Ops, SparseCore 0:
  41.1 45.8 all-gather.3
  91.6 63.9 all-gather.5
  249.2 75.4 reduce-scatter.2
  332.6 46.9 reduce-scatter.4

commit v5 on v4

--- a/solution.py
+++ b/solution.py
@@ -228,7 +228,7 @@
             ],
         ),
         out_shape=jax.ShapeDtypeStruct((owners, groups, rows, 3 * width), BF16),
-        compiler_params=pltpu.CompilerParams(vmem_limit_bytes=48 * 1024 * 1024),
+        compiler_params=pltpu.CompilerParams(vmem_limit_bytes=62 * 1024 * 1024),
         cost_estimate=pl.CostEstimate(
             flops=14 * total * total * width, bytes_accessed=1, transcendentals=0
         ),
@@ -365,7 +365,7 @@
             pltpu.SemaphoreType.DMA((2, shares)),
             pltpu.SemaphoreType.DMA((2,)),
         ],
-        compiler_params=pltpu.CompilerParams(vmem_limit_bytes=56 * 1024 * 1024),
+        compiler_params=pltpu.CompilerParams(vmem_limit_bytes=62 * 1024 * 1024),
         cost_estimate=pl.CostEstimate(flops=1, bytes_accessed=1, transcendentals=0),
     )(h2, h2_turned, pull, *(() if first else sums), *pieces)
 
@@ -422,7 +422,7 @@
         ),
         out_shape=[jax.ShapeDtypeStruct((tokens, model), kind) for kind in (BF16, F32, BF16)]
         + [jax.ShapeDtypeStruct((model, tokens), BF16), jax.ShapeDtypeStruct((model, model), BF16)],
-        compiler_params=pltpu.CompilerParams(vmem_limit_bytes=48 * 1024 * 1024),
+        compiler_params=pltpu.CompilerParams(vmem_limit_bytes=62 * 1024 * 1024),
         cost_estimate=pl.CostEstimate(flops=1, bytes_accessed=1, transcendentals=0),
     )(core.reshape(1).astype(jnp.int32), heads, stream, *weights, gain[None], bias[None])
 

time: 439 us -> 431 us (0.982)
  local copies, waits for them, and re-layouts: 62.8 us -> 41.6 us
  waiting for transfers between devices: 72.3 us -> 85.3 us
    unnamed x154 -> x126, local copies, waits for them, and re-layouts: 46.2 us -> 28.4 us
    ppermute x48, waiting for transfers between devices: 64.2 us -> 70.7 us  [flip(): return lax.ppermute(value, axis, [(0, 1), (1, 0)])]
    ppermute x48, starting transfers between devices: 39.9 us -> 35.2 us  [flip(): return lax.ppermute(value, axis, [(0, 1), (1, 0)])]
  transfers between devices with their start and end apart: 54 -> 54, of which waited for: 16 -> 22; matrix products, arithmetic and copies ran while one was open for 7% -> 7% of each run, Pallas kernels for 24% -> 24%
where the time goes in v5:
time: 431 us; the launch traced here: 426 us
  Pallas kernels  161 us (37%)
  waiting for transfers between devices  85.3 us (20%)
  blocking collectives  63.4 us (15%)
  local copies, waits for them, and re-layouts  41.6 us (10%)
  starting transfers between devices  41 us (10%)
  other arithmetic  16.8 us (4%)
  between operations  14.9 us (3%)
    ppermute x48, waiting for transfers between devices, flip(): return lax.ppermute(value, axis, [(0, 1), (1, 0)])  70.7 us
    all_to_all x1, blocking collectives, shards(): lax.all_to_all(attn_heads.reshape(owners, mine, width), CTX, split_axis=0...  42.6 us
    pallas_call x1, Pallas kernels, feed_forward(): pl.pallas_call(kernel, grid=(n_all,), in_specs=[whole, pl.BlockSpec((mode...  37.4 us
    ppermute x48, starting transfers between devices, flip(): return lax.ppermute(value, axis, [(0, 1), (1, 0)])  35.2 us
    unnamed x126, local copies, waits for them, and re-layouts  28.4 us
    pallas_call x1, Pallas kernels, backward_attention(): pl.pallas_call(kernel, grid_spec=pltpu.PrefetchScalarGridSpec(num_scalar_...  28.1 us
    pallas_call x2, Pallas kernels, forward_attention(): pl.pallas_call(kernel, grid_spec=pltpu.PrefetchScalarGridSpec(num_scalar_...  24.7 us
    all_gather x1, blocking collectives, shards(): packed = lax.all_gather(packed, 'z', axis=0, tiled=True)  20.9 us
  transfers between devices with their start and end apart: 54, of which 22 were waited for; matrix products, arithmetic and copies ran while one was open for 7% of the time, Pallas kernels for 24%

profile of v5, /device:TPU:0, one launch (start us, length us, event | category | flops | bytes accessed | tf_op | source)
XLA Modules:
  0.0 426.1 jit_solution(9355129262028522287)
XLA Ops:
  10.3 3.0 collective-permute-start
  13.3 1.5 collective-permute-start.1
  14.9 1.6 copy-done.5
  19.2 20.9 %all_gather.12 = bf16[1088,384]{1,0:T(8,128)(2,1)} all-gather(bf16[272,384]{1,0:T(8,128)(2,1)S(1)} %fusion.10), channel_id=1, replica_groups=mesh['a'=2,'b'=2,'c'=2,'z'=4] {'z'}, dimensions={0}, use_global_device_ids=true | all-gather | bytes 1044480 | tf_op jit(solution)/shard_map/all_gather | solution.py:1008
  42.1 1.6 copy-done.6
  44.7 1.6 shard_map.200
  46.4 2.0 slice.156
  48.9 1.9 slice.157
  53.2 13.5 %shard_map.196 = (bf16[4096,1024]{1,0:T(8,128)(2,1)}, bf16[4096,384]{1,0:T(8,128)(2,1)}) custom-call(bf16[544,1024]{1,0:T(8,128)(2,1)S(1)} %fusion.6.refs_0_, bf16[544,1024]{1,0:T(8,128)(2,1)} %collective-permute-done.refs_1_, bf16[544,1024]{1,0:T(8,128)(2,1)} %collective-permute-done.1.refs_2_, bf16[544,1024]{1,0:T(8,128)(2,1)} %collective-permute-done.4.refs_3_, ...), custom_call_target="tpu_custom_call" | custom-call | flops 1 | bytes 1 | tf_op jit(solution)/shard_map/pallas_call | solution.py:745
  70.8 1.9 copy-done.1
  72.6 3.8 shard_map.197
  76.4 1.7 copy-done.2
  78.2 12.2 %shard_map.198 = (bf16[8,2,256,128]{3,2,1,0:T(8,128)(2,1)S(1)}, f32[2,128,2048]{2,1,0:T(8,128)S(1)}, f32[2,2,2048]{2,1,0:T(2,128)S(1)}) custom-call(s32[64]{0:T(128)S(1)} %convert_element_type.114.slot_ref, s32[8]{0:T(128)S(1)} %fusion.13.at_ref, bf16[8,2,256,384]{3,2,1,0:T(8,128)(2,1)} %bitcast.74), custom_call_target="tpu_custom_call" | custom-call | flops 1 | bytes 1 | tf_op jit(solution)/shard_map/pallas_call | solution.py:109
  92.9 1.5 collective-permute-start.10
  94.4 1.6 copy-done.12
  96.0 12.5 %shard_map.199 = (bf16[8,2,256,128]{3,2,1,0:T(8,128)(2,1)S(1)}, f32[2,128,2048]{2,1,0:T(8,128)S(1)}, f32[2,2,2048]{2,1,0:T(2,128)S(1)}) custom-call(s32[64]{0:T(128)S(1)} %convert_element_type.114.slot_ref, s32[8]{0:T(128)S(1)} %fusion.13.at_ref, bf16[8,2,256,384]{3,2,1,0:T(8,128)(2,1)} %bitcast.75, ...), custom_call_target="tpu_custom_call", output_to_operand_aliasing={{0}: (3, {}), {1}: (4, {}), {2}: (5, {})} | custom-call | flops 1 | bytes 1 | tf_op jit(solution)/shard_map/pallas_call | solution.py:109
  109.9 42.6 %all_to_all.10.heads_ref = bf16[8,512,128]{2,1,0:T(8,128)(2,1)} all-to-all(bf16[8,512,128]{2,1,0:T(8,128)(2,1)S(1)} %bitcast.86), channel_id=1, replica_groups=mesh['a'=2,'b'=2,'c'=2,'z'=4] {'a','b','c'}, dimensions={0} | all-to-all | bytes 2097152 | tf_op jit(solution)/shard_map/all_to_all | solution.py:1054
  152.5 3.3 all-gather.6.cloned.1.call-done
  156.8 5.0 %collective-permute-done.8.refs_1_.refs_6_ = bf16[4,384,1024]{2,1,0:T(8,128)(2,1)} collective-permute-done((bf16[4,384,1024]{2,1,0:T(8,128)(2,1)}, bf16[4,384,1024]{2,1,0:T(8,128)(2,1)}, u32[]{:S(2)}, u32[]{:S(2)}) %collective-permute-start.8) | collective-permute-done | bytes 3145760 | tf_op jit(solution)/shard_map/ppermute | solution.py:907
  161.8 6.1 %shard_map.201 = (bf16[512,1024]{1,0:T(8,128)(2,1)}, f32[512,1024]{1,0:T(8,128)}, bf16[512,1024]{1,0:T(8,128)(2,1)}, bf16[1024,512]{1,0:T(8,128)(2,1)}, bf16[1024,1024]{1,0:T(8,128)(2,1)}) custom-call(s32[1]{0:T(128)} %bitcast.core_ref, bf16[8,512,128]{2,1,0:T(8,128)(2,1)} %all_to_all.10.heads_ref, bf16[512,1024]{1,0:T(8,128)(2,1)} %bitcast.101, ...), custom_call_target="tpu_custom_call" | custom-call | flops 1 | bytes 1 | tf_op jit(solution)/shard_map/pallas_call | solution.py:412
  167.9 2.8 collective-permute-done.11.refs_4_
  170.8 37.4 %shard_map.202 = (f32[512,1024]{1,0:T(8,128)}, f32[512,1024]{1,0:T(8,128)}, bf16[4,1024,512]{2,1,0:T(8,128)(2,1)}, bf16[4,4,256,512]{3,2,1,0:T(8,128)(2,1)}, bf1...) custom-call(bf16[512,1024]{1,0:T(8,128)(2,1)} %get-tuple-element.124.refs_0_, ...), custom_call_target="tpu_custom_call" | custom-call | flops 1 | bytes 1 | tf_op jit(solution)/shard_map/pallas_call | solution.py:355
  208.2 6.0 %shard_map.203 = (f32[512,1024]{1,0:T(8,128)S(1)}, bf16[512,1024]{1,0:T(8,128)(2,1)S(1)}, bf16[8,512,128]{2,1,0:T(8,128)(2,1)}, f32[8,1024]{1,0:T(8,128)S(1)}) custom-call(f32[512,1024]{1,0:T(8,128)} %get-tuple-element.123.total_ref, f32[512,1024]{1,0:T(8,128)} %get-tuple-element.132.grad_ref, bf16[512,1024]{1,0:T(8,128)(2,1)S(1)} %bitcast.88, ...), custom_call_target="tpu_custom_call" | custom-call | flops 1 | bytes 1 | tf_op jit(solution)/shard_map/pallas_call | solution.py:460
  216.0 1.9 shard_map.204
  219.0 4.2 all-to-all-start.1
  223.3 2.3 collective-permute-done.15.refs_3_
  226.6 5.8 %shard_map.205 = (bf16[640,512]{1,0:T(8,128)(2,1)S(1)}, bf16[640,512]{1,0:T(8,128)(2,1)S(1)}, bf16[640,512]{1,0:T(8,128)(2,1)}, bf16[640,512]{1,0:T(8,128)(2,1)S...) custom-call(bf16[4,1024,512]{2,1,0:T(8,128)(2,1)} %get-tuple-element, ...), custom_call_target="tpu_custom_call" | custom-call | flops 1 | bytes 12582912 | tf_op jit(solution)/shard_map/pallas_call | solution.py:603
  234.9 3.8 all-to-all-done.1
  238.7 4.3 %shard_map.206 = bf16[4,4,256,512]{3,2,1,0:T(8,128)(2,1)S(1)} custom-call(bf16[4,4,256,512]{3,2,1,0:T(8,128)(2,1)} %get-tuple-element.158.refs_0_, bf16[4,4,256,512]{3,2,1,0:T(8,128)(2,1)} %collective-permute-done.20.refs_1_), custom_call_target="tpu_custom_call" | custom-call | flops 1 | bytes 12582912 | tf_op jit(solution)/shard_map/pallas_call | solution.py:576
  243.1 2.0 copy-done.3
  248.1 1.5 collective-permute-start.19
  249.6 28.1 %shard_map.207 = bf16[8,2,256,384]{3,2,1,0:T(8,128)(2,1)} custom-call(s32[64]{0:T(128)} %copy-done.34, s32[8]{0:T(128)} %copy-done.32, bf16[8,2,256,384]{3,2,1,0:T(8,128)(2,1)} %bitcast.76, bf16[8,2,256,128]{3,2,1,0:T(8,128)(2,1)} %bitcast.26.grad_ref, f32[2,128,2048]{2,1,0:T(8,128)} %copy-done.13, f32[2,2,2048]{2,1,0:T(2,128)} %copy-done.31), custom_call_target="tpu_custom_call" | custom-call | flops 7516192768 | bytes 1 | tf_op jit(solution)/shard_map/pallas_call | solution.py:213
  277.7 1.5 add_convert_fusion.2
  279.3 2.2 add_convert_fusion.3
  281.5 2.4 convolution_convert_fusion
  286.7 4.4 %collective-permute-done.21 = bf16[2048,1024]{1,0:T(8,128)(2,1)S(1)} collective-permute-done((bf16[2048,1024]{1,0:T(8,128)(2,1)S(1)}, bf16[2048,1024]{1,0:T(8,128)(2,1)S(1)}, u32[]{:S(2)}, u32[]{:S(2)}) %collective-permute-start.21) | collective-permute-done | bytes 4194336 | tf_op jit(solution)/shard_map/ppermute | solution.py:907
  291.1 2.0 copy-done.51
  293.1 6.0 %shard_map.208 = (bf16[256,1024]{1,0:T(8,128)(2,1)S(1)}, bf16[256,1024]{1,0:T(8,128)(2,1)S(1)}, bf16[256,1024]{1,0:T(8,128)(2,1)S(1)}, bf16[256,1024]{1,0:T(8,12...) custom-call(bf16[4,512,384]{2,1,0:T(8,128)(2,1)} %slice.145.slope_re, ...), custom_call_target="tpu_custom_call" | custom-call | flops 1 | bytes 1 | tf_op jit(solution)/shard_map/pallas_call | solution.py:497
  301.6 7.7 %shard_map.209.refs_6_ = bf16[1024,512]{1,0:T(8,128)(2,1)S(1)} custom-call(bf16[4096,1024]{1,0:T(8,128)(2,1)} %get-tuple-element.177.normed_ref, bf16[4096,384]{1,0:T(8,128)(2,1)S(1)} %bitcast.84, bf16[1024,384]{1,0:T(8,128)(2,1)S(1)} %bitcast.81, f32[1024,128]{1,0:T(8,128)S(1)} %pad.14.columns_ref), custom_call_target="tpu_custom_call" | custom-call | flops 1 | bytes 1 | tf_op jit(solution)/shard_map/pallas_call | solution.py:547
  309.4 3.8 collective-permute-done.23
  315.2 3.7 reduce-scatter.3.cloned.1.call-done
  320.0 3.2 shard_map.210
  324.2 1.5 collective-permute-start.22
  325.6 1.5 collective-permute-start.24
  328.2 10.7 %collective-permute-done.22 = bf16[256,1024]{1,0:T(8,128)(2,1)S(1)} collective-permute-done((bf16[256,1024]{1,0:T(8,128)(2,1)S(1)}, bf16[256,1024]{1,0:T(8,128)(2,1)S(1)}, u32[]{:S(2)}, u32[]{:S(2)}) %collective-permute-start.22) | collective-permute-done | bytes 524320 | tf_op jit(solution)/shard_map/ppermute | solution.py:907
  339.0 1.7 collective-permute-done.24
  341.0 9.5 %collective-permute-done.27 = bf16[256,1024]{1,0:T(8,128)(2,1)S(1)} collective-permute-done((bf16[256,1024]{1,0:T(8,128)(2,1)S(1)}, bf16[256,1024]{1,0:T(8,128)(2,1)S(1)}, u32[]{:S(2)}, u32[]{:S(2)}) %collective-permute-start.27) | collective-permute-done | bytes 524320 | tf_op jit(solution)/shard_map/ppermute | solution.py:907
  350.8 1.5 multiply_reduce_fusion
  353.5 1.5 collective-permute-start.31
  356.6 5.5 %collective-permute-done.30 = bf16[256,512]{1,0:T(8,128)(2,1)S(1)} collective-permute-done((bf16[256,512]{1,0:T(8,128)(2,1)S(1)}, bf16[256,512]{1,0:T(8,128)(2,1)S(1)}, u32[]{:S(2)}, u32[]{:S(2)}) %collective-permute-start.30) | collective-permute-done | bytes 262176 | tf_op jit(solution)/shard_map/ppermute | solution.py:907
  362.2 2.7 collective-permute-done.31
  364.9 1.6 collective-permute-done.32
  367.5 1.9 collective-permute-start.41
  369.8 2.1 reduce-scatter.5.cloned.1.call-done.refs_0_.refs_8_.refs_16_
  373.3 1.5 collective-permute-start.33
  376.1 3.7 add_convert_fusion.1
  379.8 11.2 %collective-permute-done.43 = bf16[128,512]{1,0:T(8,128)(2,1)S(1)} collective-permute-done((bf16[128,512]{1,0:T(8,128)(2,1)S(1)}, bf16[128,512]{1,0:T(8,128)(2,1)S(1)}, u32[]{:S(2)}, u32[]{:S(2)}) %collective-permute-start.43) | collective-permute-done | bytes 131104 | tf_op jit(solution)/shard_map/ppermute | solution.py:907
  391.1 1.5 collective-permute-start.35
  394.5 4.0 collective-permute-done.35
  398.5 3.7 collective-permute-done.36
  403.6 1.8 add_convert_fusion
  405.3 1.9 collective-permute-done.48.refs_7_
  407.3 2.7 shard_map.212
  412.0 7.2 %shard_map.211 = (f32[2,128,4096]{2,1,0:T(8,128)}, f32[8,32,1024]{2,1,0:T(8,128)}, f32[2,128,3072]{2,1,0:T(8,128)}, f32[1,256]{1,0:T(1,128)}, f32[1,256]{1,0:T(1...) custom-call(s32[8]{0:T(128)} %copy-done.32, bf16[288,1024]{1,0:T(8,128)(2,1)} %reduce-scatter.5.cloned.1.call-done.refs_0_.refs_8_.refs_16_, ...), custom_call_target="tpu_custom_call" | custom-call | tf_op jit(solution)/shard_map/pallas_call | solution.py:866
  (260 shorter events, 53.5 us)
Async XLA Ops:
  7.2 84.5 %all-gather.4.cloned.1.call-start = ((), (), s32[]{:S(2)}) async-start(), calls=%async_computation.4 | async-start | bytes 2621440 | tf_op jit(solution)/shard_map/all_gather | solution.py:1013
  10.3 29.7 %collective-permute-start = (bf16[544,1024]{1,0:T(8,128)(2,1)S(1)}, bf16[544,1024]{1,0:T(8,128)(2,1)}, u32[]{:S(2)}, u32[]{:S(2)}) collective-permute-start(bf16[544,1024]{1,0:T(8,128)(2,1)S(1)} %fusion.6.refs_0_), channel_id=1, source_target_pairs={{0,8},{8,0},{1,9},{9,1},{2,10},{10,2},{3,11},{11,3},{4,12},{12,4},... | collective-permute-start | bytes 3342344 | tf_op jit(solution)/shard_map/ppermute | solution.py:907
  13.3 26.7 %collective-permute-start.1 = (bf16[544,1024]{1,0:T(8,128)(2,1)S(1)}, bf16[544,1024]{1,0:T(8,128)(2,1)}, u32[]{:S(2)}, u32[]{:S(2)}) collective-permute-start(bf16[544,1024]{1,0:T(8,128)(2,1)S(1)} %fusion.6.refs_0_), channel_id=1, source_target_pairs={{0,16},{16,0},{1,17},{17,1},{2,18},{18,2},{3,19},{19,3},{4,20},{20... | collective-permute-start | bytes 3342344 | tf_op jit(solution)/shard_map/ppermute | solution.py:907
  40.1 115.7 %all-gather.6.cloned.1.call-start = ((), (), s32[]{:S(2)}) async-start(), calls=%async_computation.7 | async-start | bytes 3932160 | tf_op jit(solution)/shard_map/all_gather | solution.py:1049
  40.1 13.1 %collective-permute-start.4 = (bf16[544,1024]{1,0:T(8,128)(2,1)S(1)}, bf16[544,1024]{1,0:T(8,128)(2,1)}, u32[]{:S(2)}, u32[]{:S(2)}) collective-permute-start(bf16[544,1024]{1,0:T(8,128)(2,1)S(1)} %fusion.6.refs_0_), channel_id=1, source_target_pairs={{0,4},{4,0},{1,5},{5,1},{2,6},{6,2},{3,7},{7,3},{8,12},{12,8},{9,1... | collective-permute-start | bytes 3342344 | tf_op jit(solution)/shard_map/ppermute | solution.py:907
  40.2 13.1 %collective-permute-start.5 = (bf16[544,1024]{1,0:T(8,128)(2,1)}, bf16[544,1024]{1,0:T(8,128)(2,1)}, u32[]{:S(2)}, u32[]{:S(2)}) collective-permute-start(bf16[544,1024]{1,0:T(8,128)(2,1)} %collective-permute-done.refs_1_), channel_id=1, source_target_pairs={{0,4},{4,0},{1,5},{5,1},{2,6},{6,2},{3,7},{7,3},{8,12},{12,8},{9,1... | collective-permute-start | bytes 3342344 | tf_op jit(solution)/shard_map/ppermute | solution.py:907
  40.7 12.6 %collective-permute-start.6 = (bf16[544,1024]{1,0:T(8,128)(2,1)}, bf16[544,1024]{1,0:T(8,128)(2,1)}, u32[]{:S(2)}, u32[]{:S(2)}) collective-permute-start(bf16[544,1024]{1,0:T(8,128)(2,1)} %collective-permute-done.1.refs_2_), channel_id=1, source_target_pairs={{0,4},{4,0},{1,5},{5,1},{2,6},{6,2},{3,7},{7,3},{8,12},{12,8},{9,1... | collective-permute-start | bytes 3342344 | tf_op jit(solution)/shard_map/ppermute | solution.py:907
  40.8 175.2 %copy-start.32 = (s32[8]{0:T(128)}, s32[8]{0:T(128)S(1)}, u32[]{:S(2)}) copy-start(s32[8]{0:T(128)S(1)} %fusion.13.at_ref) | copy-start | bytes 100
  48.4 18.4 %collective-permute-start.2 = (bf16[272,1024]{1,0:T(8,128)(2,1)}, bf16[272,1024]{1,0:T(8,128)(2,1)}, u32[]{:S(2)}, u32[]{:S(2)}) collective-permute-start(bf16[272,1024]{1,0:T(8,128)(2,1)} %slice.156), channel_id=1, source_target_pairs={{0,8},{8,0},{1,9},{9,1},{2,10},{10,2},{3,11},{11,3},{4,12},{12,4},... | collective-permute-start | bytes 1671176 | tf_op jit(solution)/shard_map/ppermute | solution.py:907
  50.8 16.0 %collective-permute-start.3 = (bf16[272,1024]{1,0:T(8,128)(2,1)}, bf16[272,1024]{1,0:T(8,128)(2,1)S(1)}, u32[]{:S(2)}, u32[]{:S(2)}) collective-permute-start(bf16[272,1024]{1,0:T(8,128)(2,1)} %slice.157), channel_id=1, source_target_pairs={{0,16},{16,0},{1,17},{17,1},{2,18},{18,2},{3,19},{19,3},{4,20},{20... | collective-permute-start | bytes 1671176 | tf_op jit(solution)/shard_map/ppermute | solution.py:907
  67.9 2.8 collective-permute-start.7
  78.2 30.4 %copy-start.34 = (s32[64]{0:T(128)}, s32[64]{0:T(128)S(1)}, u32[]{:S(2)}) copy-start(s32[64]{0:T(128)S(1)} %convert_element_type.114.slot_ref) | copy-start | bytes 772
  91.7 64.6 %collective-permute-start.12 = (bf16[1024,1024]{1,0:T(8,128)(2,1)}, bf16[1024,1024]{1,0:T(8,128)(2,1)}, u32[]{:S(2)}, u32[]{:S(2)}) collective-permute-start(bf16[1024,1024]{1,0:T(8,128)(2,1)} %all-gather.4.cloned.1.call-done.refs_7_), channel_id=1, source_target_pairs={{0,16},{16,0},{1,17},{17,1},{2,18},{18,2},{3,19},{19,3},{4,20},{20... | collective-permute-start | bytes 6291464 | tf_op jit(solution)/shard_map/ppermute | solution.py:907
  92.9 63.4 %collective-permute-start.10 = (bf16[1024,1024]{1,0:T(8,128)(2,1)}, bf16[1024,1024]{1,0:T(8,128)(2,1)}, u32[]{:S(2)}, u32[]{:S(2)}) collective-permute-start(bf16[1024,1024]{1,0:T(8,128)(2,1)} %all-gather.4.cloned.1.call-done.refs_7_), channel_id=1, source_target_pairs={{0,8},{8,0},{1,9},{9,1},{2,10},{10,2},{3,11},{11,3},{4,12},{12,4},... | collective-permute-start | bytes 6291464 | tf_op jit(solution)/shard_map/ppermute | solution.py:907
  109.9 58.0 %copy-start.31 = (f32[2,2,2048]{2,1,0:T(2,128)}, f32[2,2,2048]{2,1,0:T(2,128)S(1)}, u32[]{:S(2)}) copy-start(f32[2,2,2048]{2,1,0:T(2,128)S(1)} %get-tuple-element.162.log_ref) | copy-start | bytes 98308
  155.8 6.0 %collective-permute-start.8 = (bf16[4,384,1024]{2,1,0:T(8,128)(2,1)}, bf16[4,384,1024]{2,1,0:T(8,128)(2,1)}, u32[]{:S(2)}, u32[]{:S(2)}) collective-permute-start(bf16[4,384,1024]{2,1,0:T(8,128)(2,1)} %bitcast.102), channel_id=1, source_target_pairs={{0,4},{4,0},{1,5},{5,1},{2,6},{6,2},{3,7},{7,3},{8,12},{12,8},{9,1... | collective-permute-start | bytes 9437192 | tf_op jit(solution)/shard_map/ppermute | solution.py:907
  155.8 12.1 %collective-permute-start.9 = (bf16[1024,1024]{1,0:T(8,128)(2,1)}, bf16[1024,1024]{1,0:T(8,128)(2,1)}, u32[]{:S(2)}, u32[]{:S(2)}) collective-permute-start(bf16[1024,1024]{1,0:T(8,128)(2,1)} %all-gather.4.cloned.1.call-done.refs_7_), channel_id=1, source_target_pairs={{0,4},{4,0},{1,5},{5,1},{2,6},{6,2},{3,7},{7,3},{8,12},{12,8},{9,1... | collective-permute-start | bytes 6291464 | tf_op jit(solution)/shard_map/ppermute | solution.py:907
  156.3 11.6 %collective-permute-start.13 = (bf16[1024,1024]{1,0:T(8,128)(2,1)}, bf16[1024,1024]{1,0:T(8,128)(2,1)}, u32[]{:S(2)}, u32[]{:S(2)}) collective-permute-start(bf16[1024,1024]{1,0:T(8,128)(2,1)} %collective-permute-done.12.refs_9_), channel_id=1, source_target_pairs={{0,4},{4,0},{1,5},{5,1},{2,6},{6,2},{3,7},{7,3},{8,12},{12,8},{9,1... | collective-permute-start | bytes 6291464 | tf_op jit(solution)/shard_map/ppermute | solution.py:907
  156.3 14.5 %collective-permute-start.11 = (bf16[1024,1024]{1,0:T(8,128)(2,1)}, bf16[1024,1024]{1,0:T(8,128)(2,1)}, u32[]{:S(2)}, u32[]{:S(2)}) collective-permute-start(bf16[1024,1024]{1,0:T(8,128)(2,1)} %collective-permute-done.10.refs_8_), channel_id=1, source_target_pairs={{0,4},{4,0},{1,5},{5,1},{2,6},{6,2},{3,7},{7,3},{8,12},{12,8},{9,1... | collective-permute-start | bytes 6291464 | tf_op jit(solution)/shard_map/ppermute | solution.py:907
  170.8 37.4 %copy-start.7 = (bf16[2,256,1024]{2,1,0:T(8,128)(2,1)S(1)}, bf16[2,256,1024]{2,1,0:T(8,128)(2,1)}, u32[]{:S(2)}) copy-start(bf16[2,256,1024]{2,1,0:T(8,128)(2,1)} %param.15) | copy-start | bytes 3145732
  170.8 37.4 %copy-start.30 = (f32[1,4,256]{2,0,1:T(1,128)S(1)}, f32[1,4,256]{2,0,1:T(1,128)}, u32[]{:S(2)}) copy-start(f32[1,4,256]{2,0,1:T(1,128)} %get-tuple-element.207) | copy-start | bytes 12292
  215.5 10.2 %collective-permute-start.14 = (bf16[4,1024,512]{2,1,0:T(8,128)(2,1)}, bf16[4,1024,512]{2,1,0:T(8,128)(2,1)}, u32[]{:S(2)}, u32[]{:S(2)}) collective-permute-start(bf16[4,1024,512]{2,1,0:T(8,128)(2,1)} %get-tuple-element.142), channel_id=1, source_target_pairs={{0,4},{4,0},{1,5},{5,1},{2,6},{6,2},{3,7},{7,3},{8,12},{12,8},{9,1... | collective-permute-start | bytes 12582920 | tf_op jit(solution)/shard_map/ppermute | solution.py:907
  215.6 23.1 %collective-permute-start.20 = (bf16[4,4,256,512]{3,2,1,0:T(8,128)(2,1)}, bf16[4,4,256,512]{3,2,1,0:T(8,128)(2,1)}, u32[]{:S(2)}, u32[]{:S(2)}) collective-permute-start(bf16[4,4,256,512]{3,2,1,0:T(8,128)(2,1)} %get-tuple-element.159), channel_id=1, source_target_pairs={{0,4},{4,0},{1,5},{5,1},{2,6},{6,2},{3,7},{7,3},{8,12},{12,8},{9,1... | collective-permute-start | bytes 12582920 | tf_op jit(solution)/shard_map/ppermute | solution.py:907
  218.9 6.7 %collective-permute-start.15 = (bf16[4,2,128,512]{3,2,1,0:T(8,128)(2,1)S(1)}, bf16[4,2,128,512]{3,2,1,0:T(8,128)(2,1)S(1)}, u32[]{:S(2)}, u32[]{:S(2)}) collective-permute-start(bf16[4,2,128,512]{3,2,1,0:T(8,128)(2,1)S(1)} %get-tuple-element.146), channel_id=1, source_target_pairs={{0,4},{4,0},{1,5},{5,1},{2,6},{6,2},{3,7},{7,3},{8,12},{12,8},{9,1... | collective-permute-start | bytes 3145736 | tf_op jit(solution)/shard_map/ppermute | solution.py:907
  219.0 19.7 %all-to-all-start.1 = ((bf16[8,512,128]{2,1,0:T(8,128)(2,1)}), bf16[8,512,128]{2,1,0:T(8,128)(2,1)}, u32[]{:S(2)}, u32[]{:S(2)}) async-start(bf16[8,512,128]{2,1,0:T(8,128)(2,1)} %get-tuple-element.154), calls=%async_computation.1 | async-start | bytes 2097152 | tf_op jit(solution)/shard_map/all_to_all | solution.py:1092
  223.3 95.6 %reduce-scatter.3.cloned.1.call-start = ((), (), s32[]{:S(2)}) async-start(), calls=%async_computation.5 | async-start | bytes 5242880 | tf_op jit(solution)/shard_map/reduce_scatter | solution.py:1113
  245.1 126.8 %reduce-scatter.5.cloned.1.call-start = ((), (), s32[]{:S(2)}) async-start(), calls=%async_computation.6 | async-start | bytes 2949120 | tf_op jit(solution)/shard_map/reduce_scatter | solution.py:1173
  245.5 32.2 %collective-permute-start.17 = (bf16[640,512]{1,0:T(8,128)(2,1)}, bf16[640,512]{1,0:T(8,128)(2,1)}, u32[]{:S(2)}, u32[]{:S(2)}) collective-permute-start(bf16[640,512]{1,0:T(8,128)(2,1)} %get-tuple-element.150), channel_id=1, source_target_pairs={{0,8},{8,0},{1,9},{9,1},{2,10},{10,2},{3,11},{11,3},{4,12},{12,4},... | collective-permute-start | bytes 1966088 | tf_op jit(solution)/shard_map/ppermute | solution.py:907
  246.1 33.2 %collective-permute-start.16 = (bf16[640,512]{1,0:T(8,128)(2,1)}, bf16[640,512]{1,0:T(8,128)(2,1)}, u32[]{:S(2)}, u32[]{:S(2)}) collective-permute-start(bf16[640,512]{1,0:T(8,128)(2,1)} %get-tuple-element.148), channel_id=1, source_target_pairs={{0,16},{16,0},{1,17},{17,1},{2,18},{18,2},{3,19},{19,3},{4,20},{20... | collective-permute-start | bytes 1966088 | tf_op jit(solution)/shard_map/ppermute | solution.py:907
  246.7 34.8 %collective-permute-start.18 = (bf16[640,512]{1,0:T(8,128)(2,1)}, bf16[640,512]{1,0:T(8,128)(2,1)}, u32[]{:S(2)}, u32[]{:S(2)}) collective-permute-start(bf16[640,512]{1,0:T(8,128)(2,1)} %get-tuple-element.151), channel_id=1, source_target_pairs={{0,8},{8,0},{1,9},{9,1},{2,10},{10,2},{3,11},{11,3},{4,12},{12,4},... | collective-permute-start | bytes 1966088 | tf_op jit(solution)/shard_map/ppermute | solution.py:907
  248.1 33.4 %collective-permute-start.19 = (bf16[640,512]{1,0:T(8,128)(2,1)}, bf16[640,512]{1,0:T(8,128)(2,1)}, u32[]{:S(2)}, u32[]{:S(2)}) collective-permute-start(bf16[640,512]{1,0:T(8,128)(2,1)} %get-tuple-element.152), channel_id=1, source_target_pairs={{0,16},{16,0},{1,17},{17,1},{2,18},{18,2},{3,19},{19,3},{4,20},{20... | collective-permute-start | bytes 1966088 | tf_op jit(solution)/shard_map/ppermute | solution.py:907
  283.9 7.2 %collective-permute-start.21 = (bf16[2048,1024]{1,0:T(8,128)(2,1)S(1)}, bf16[2048,1024]{1,0:T(8,128)(2,1)S(1)}, u32[]{:S(2)}, u32[]{:S(2)}) collective-permute-start(bf16[2048,1024]{1,0:T(8,128)(2,1)S(1)} %convolution_convert_fusion), channel_id=1, source_target_pairs={{0,4},{4,0},{1,5},{5,1},{2,6},{6,2},{3,7},{7,3},{8,12},{12,8},{9,1... | collective-permute-start | bytes 12582920 | tf_op jit(solution)/shard_map/ppermute | solution.py:907
  284.0 17.1 %collective-permute-start.28 = (bf16[640,512]{1,0:T(8,128)(2,1)S(1)}, bf16[640,512]{1,0:T(8,128)(2,1)S(1)}, u32[]{:S(2)}, u32[]{:S(2)}) collective-permute-start(bf16[640,512]{1,0:T(8,128)(2,1)S(1)} %add_convert_fusion.2), channel_id=1, source_target_pairs={{0,16},{16,0},{1,17},{17,1},{2,18},{18,2},{3,19},{19,3},{4,20},{20... | collective-permute-start | bytes 1966088 | tf_op jit(solution)/shard_map/ppermute | solution.py:907
  284.6 17.0 %collective-permute-start.29 = (bf16[640,512]{1,0:T(8,128)(2,1)}, bf16[640,512]{1,0:T(8,128)(2,1)S(1)}, u32[]{:S(2)}, u32[]{:S(2)}) collective-permute-start(bf16[640,512]{1,0:T(8,128)(2,1)} %add_convert_fusion.3), channel_id=1, source_target_pairs={{0,8},{8,0},{1,9},{9,1},{2,10},{10,2},{3,11},{11,3},{4,12},{12,4},... | collective-permute-start | bytes 1966088 | tf_op jit(solution)/shard_map/ppermute | solution.py:907
  299.1 10.3 %copy-start.26 = (bf16[256,1024]{1,0:T(8,128)(2,1)}, bf16[256,1024]{1,0:T(8,128)(2,1)S(1)}, u32[]{:S(2)}) copy-start(bf16[256,1024]{1,0:T(8,128)(2,1)S(1)} %get-tuple-element.172) | copy-start | bytes 1572868
  299.1 14.0 %collective-permute-start.23 = (bf16[256,1024]{1,0:T(8,128)(2,1)S(1)}, bf16[256,1024]{1,0:T(8,128)(2,1)S(1)}, u32[]{:S(2)}, u32[]{:S(2)}) collective-permute-start(bf16[256,1024]{1,0:T(8,128)(2,1)S(1)} %get-tuple-element.167), channel_id=1, source_target_pairs={{0,8},{8,0},{1,9},{9,1},{2,10},{10,2},{3,11},{11,3},{4,12},{12,4},... | collective-permute-start | bytes 1572872 | tf_op jit(solution)/shard_map/ppermute | solution.py:907
  299.8 14.4 %collective-permute-start.25 = (bf16[256,1024]{1,0:T(8,128)(2,1)S(1)}, bf16[256,1024]{1,0:T(8,128)(2,1)S(1)}, u32[]{:S(2)}, u32[]{:S(2)}) collective-permute-start(bf16[256,1024]{1,0:T(8,128)(2,1)S(1)} %get-tuple-element.170), channel_id=1, source_target_pairs={{0,16},{16,0},{1,17},{17,1},{2,18},{18,2},{3,19},{19,3},{4,20},{20... | collective-permute-start | bytes 1572872 | tf_op jit(solution)/shard_map/ppermute | solution.py:907
  323.1 17.6 %copy-start.29 = (bf16[256,1024]{1,0:T(8,128)(2,1)S(1)}, bf16[256,1024]{1,0:T(8,128)(2,1)}, u32[]{:S(2)}) copy-start(bf16[256,1024]{1,0:T(8,128)(2,1)} %copy-done.28) | copy-start | bytes 1572868
  323.1 27.4 %copy-start.27 = (bf16[256,1024]{1,0:T(8,128)(2,1)S(1)}, bf16[256,1024]{1,0:T(8,128)(2,1)}, u32[]{:S(2)}) copy-start(bf16[256,1024]{1,0:T(8,128)(2,1)} %copy-done.26) | copy-start | bytes 1572868
  324.2 14.8 %collective-permute-start.22 = (bf16[256,1024]{1,0:T(8,128)(2,1)S(1)}, bf16[256,1024]{1,0:T(8,128)(2,1)S(1)}, u32[]{:S(2)}, u32[]{:S(2)}) collective-permute-start(bf16[256,1024]{1,0:T(8,128)(2,1)S(1)} %copy-done.38), channel_id=1, source_target_pairs={{0,8},{8,0},{1,9},{9,1},{2,10},{10,2},{3,11},{11,3},{4,12},{12,4},... | collective-permute-start | bytes 1572872 | tf_op jit(solution)/shard_map/ppermute | solution.py:907
  325.6 15.1 %collective-permute-start.24 = (bf16[256,1024]{1,0:T(8,128)(2,1)}, bf16[256,1024]{1,0:T(8,128)(2,1)S(1)}, u32[]{:S(2)}, u32[]{:S(2)}) collective-permute-start(bf16[256,1024]{1,0:T(8,128)(2,1)} %add_convert_fusion.5), channel_id=1, source_target_pairs={{0,16},{16,0},{1,17},{17,1},{2,18},{18,2},{3,19},{19,3},{4,20},{20... | collective-permute-start | bytes 1572872 | tf_op jit(solution)/shard_map/ppermute | solution.py:907
  327.1 23.4 %collective-permute-start.27 = (bf16[256,1024]{1,0:T(8,128)(2,1)S(1)}, bf16[256,1024]{1,0:T(8,128)(2,1)S(1)}, u32[]{:S(2)}, u32[]{:S(2)}) collective-permute-start(bf16[256,1024]{1,0:T(8,128)(2,1)S(1)} %copy-done.36), channel_id=1, source_target_pairs={{0,16},{16,0},{1,17},{17,1},{2,18},{18,2},{3,19},{19,3},{4,20},{20... | collective-permute-start | bytes 1572872 | tf_op jit(solution)/shard_map/ppermute | solution.py:907
  327.7 22.8 %collective-permute-start.26 = (bf16[256,1024]{1,0:T(8,128)(2,1)S(1)}, bf16[256,1024]{1,0:T(8,128)(2,1)S(1)}, u32[]{:S(2)}, u32[]{:S(2)}) collective-permute-start(bf16[256,1024]{1,0:T(8,128)(2,1)S(1)} %copy-done.55), channel_id=1, source_target_pairs={{0,8},{8,0},{1,9},{9,1},{2,10},{10,2},{3,11},{11,3},{4,12},{12,4},... | collective-permute-start | bytes 1572872 | tf_op jit(solution)/shard_map/ppermute | solution.py:907
  352.8 9.3 %collective-permute-start.30 = (bf16[256,512]{1,0:T(8,128)(2,1)S(1)}, bf16[256,512]{1,0:T(8,128)(2,1)S(1)}, u32[]{:S(2)}, u32[]{:S(2)}) collective-permute-start(bf16[256,512]{1,0:T(8,128)(2,1)S(1)} %get-tuple-element.201), channel_id=1, source_target_pairs={{0,8},{8,0},{1,9},{9,1},{2,10},{10,2},{3,11},{11,3},{4,12},{12,4},... | collective-permute-start | bytes 786440 | tf_op jit(solution)/shard_map/ppermute | solution.py:907
  353.5 11.4 %collective-permute-start.31 = (bf16[256,512]{1,0:T(8,128)(2,1)S(1)}, bf16[256,512]{1,0:T(8,128)(2,1)S(1)}, u32[]{:S(2)}, u32[]{:S(2)}) collective-permute-start(bf16[256,512]{1,0:T(8,128)(2,1)S(1)} %get-tuple-element.203), channel_id=1, source_target_pairs={{0,16},{16,0},{1,17},{17,1},{2,18},{18,2},{3,19},{19,3},{4,20},{20... | collective-permute-start | bytes 786440 | tf_op jit(solution)/shard_map/ppermute | solution.py:907
  355.0 11.5 %collective-permute-start.32 = (bf16[256,512]{1,0:T(8,128)(2,1)S(1)}, bf16[256,512]{1,0:T(8,128)(2,1)S(1)}, u32[]{:S(2)}, u32[]{:S(2)}) collective-permute-start(bf16[256,512]{1,0:T(8,128)(2,1)S(1)} %get-tuple-element.202), channel_id=1, source_target_pairs={{0,24},{24,0},{8,16},{16,8},{1,25},{25,1},{9,17},{17,9},{2,26},{26... | collective-permute-start | bytes 786440 | tf_op jit(solution)/shard_map/ppermute | solution.py:1169
  366.6 8.2 %collective-permute-start.42 = (bf16[256,512]{1,0:T(8,128)(2,1)S(1)}, bf16[256,512]{1,0:T(8,128)(2,1)S(1)}, u32[]{:S(2)}, u32[]{:S(2)}) collective-permute-start(bf16[256,512]{1,0:T(8,128)(2,1)S(1)} %fusion.8.refs_0_), channel_id=1, source_target_pairs={{0,16},{16,0},{1,17},{17,1},{2,18},{18,2},{3,19},{19,3},{4,20},{20... | collective-permute-start | bytes 786440 | tf_op jit(solution)/shard_map/ppermute | solution.py:907
  367.5 8.0 %collective-permute-start.41 = (bf16[256,512]{1,0:T(8,128)(2,1)S(1)}, bf16[256,512]{1,0:T(8,128)(2,1)S(1)}, u32[]{:S(2)}, u32[]{:S(2)}) collective-permute-start(bf16[256,512]{1,0:T(8,128)(2,1)S(1)} %fusion.8.refs_0_), channel_id=1, source_target_pairs={{0,8},{8,0},{1,9},{9,1},{2,10},{10,2},{3,11},{11,3},{4,12},{12,4},... | collective-permute-start | bytes 786440 | tf_op jit(solution)/shard_map/ppermute | solution.py:907
  371.9 19.1 %collective-permute-start.34 = (bf16[288,1024]{1,0:T(8,128)(2,1)}, bf16[288,1024]{1,0:T(8,128)(2,1)S(1)}, u32[]{:S(2)}, u32[]{:S(2)}) collective-permute-start(bf16[288,1024]{1,0:T(8,128)(2,1)} %reduce-scatter.5.cloned.1.call-done.refs_0_.refs_8_.refs_16_), channel_id=1, source_target_pairs={{0,16},{16,0},{1,17},{17,1},{2,18},{18,2},{3,19},{19,3},{4,20},{20... | collective-permute-start | bytes 1769480 | tf_op jit(solution)/shard_map/ppermute | solution.py:907
  373.3 19.9 %collective-permute-start.33 = (bf16[288,1024]{1,0:T(8,128)(2,1)}, bf16[288,1024]{1,0:T(8,128)(2,1)S(1)}, u32[]{:S(2)}, u32[]{:S(2)}) collective-permute-start(bf16[288,1024]{1,0:T(8,128)(2,1)} %reduce-scatter.5.cloned.1.call-done.refs_0_.refs_8_.refs_16_), channel_id=1, source_target_pairs={{0,8},{8,0},{1,9},{9,1},{2,10},{10,2},{3,11},{11,3},{4,12},{12,4},... | collective-permute-start | bytes 1769480 | tf_op jit(solution)/shard_map/ppermute | solution.py:907
  374.9 16.1 %collective-permute-start.43 = (bf16[128,512]{1,0:T(8,128)(2,1)S(1)}, bf16[128,512]{1,0:T(8,128)(2,1)S(1)}, u32[]{:S(2)}, u32[]{:S(2)}) collective-permute-start(bf16[128,512]{1,0:T(8,128)(2,1)S(1)} %slice.170), channel_id=1, source_target_pairs={{0,8},{8,0},{1,9},{9,1},{2,10},{10,2},{3,11},{11,3},{4,12},{12,4},... | collective-permute-start | bytes 393224 | tf_op jit(solution)/shard_map/ppermute | solution.py:907
  375.5 17.1 %collective-permute-start.44 = (bf16[128,512]{1,0:T(8,128)(2,1)S(1)}, bf16[128,512]{1,0:T(8,128)(2,1)S(1)}, u32[]{:S(2)}, u32[]{:S(2)}) collective-permute-start(bf16[128,512]{1,0:T(8,128)(2,1)S(1)} %slice.171), channel_id=1, source_target_pairs={{0,16},{16,0},{1,17},{17,1},{2,18},{18,2},{3,19},{19,3},{4,20},{20... | collective-permute-start | bytes 393224 | tf_op jit(solution)/shard_map/ppermute | solution.py:907
  376.1 17.7 %copy-start.42 = (f32[512,1024]{1,0:T(8,128)S(1)}, f32[512,1024]{1,0:T(8,128)}, u32[]{:S(2)}) copy-start(f32[512,1024]{1,0:T(8,128)} %get-tuple-element.197) | copy-start | bytes 6291460
  391.0 11.4 %copy-start.43 = (bf16[288,1024]{1,0:T(8,128)(2,1)}, bf16[288,1024]{1,0:T(8,128)(2,1)S(1)}, u32[]{:S(2)}) copy-start(bf16[288,1024]{1,0:T(8,128)(2,1)S(1)} %collective-permute-done.34.refs_2_.refs_10_.refs_18_) | copy-start | bytes 1769476
  391.1 7.5 %collective-permute-start.35 = (bf16[144,1024]{1,0:T(8,128)(2,1)S(1)}, bf16[144,1024]{1,0:T(8,128)(2,1)S(1)}, u32[]{:S(2)}, u32[]{:S(2)}) collective-permute-start(bf16[144,1024]{1,0:T(8,128)(2,1)S(1)} %slice.168), channel_id=1, source_target_pairs={{0,8},{8,0},{1,9},{9,1},{2,10},{10,2},{3,11},{11,3},{4,12},{12,4},... | collective-permute-start | bytes 884744 | tf_op jit(solution)/shard_map/ppermute | solution.py:907
  392.6 10.3 %collective-permute-start.47 = (bf16[256,512]{1,0:T(8,128)(2,1)S(1)}, bf16[256,512]{1,0:T(8,128)(2,1)S(1)}, u32[]{:S(2)}, u32[]{:S(2)}) collective-permute-start(bf16[256,512]{1,0:T(8,128)(2,1)S(1)} %collective-permute-done.42.refs_2_), channel_id=1, source_target_pairs={{0,4},{4,0},{1,5},{5,1},{2,6},{6,2},{3,7},{7,3},{8,12},{12,8},{9,1... | collective-permute-start | bytes 786440 | tf_op jit(solution)/shard_map/ppermute | solution.py:907
  392.7 10.3 %collective-permute-start.46 = (bf16[256,512]{1,0:T(8,128)(2,1)S(1)}, bf16[256,512]{1,0:T(8,128)(2,1)S(1)}, u32[]{:S(2)}, u32[]{:S(2)}) collective-permute-start(bf16[256,512]{1,0:T(8,128)(2,1)S(1)} %collective-permute-done.41.refs_1_), channel_id=1, source_target_pairs={{0,4},{4,0},{1,5},{5,1},{2,6},{6,2},{3,7},{7,3},{8,12},{12,8},{9,1... | collective-permute-start | bytes 786440 | tf_op jit(solution)/shard_map/ppermute | solution.py:907
  393.2 9.1 %collective-permute-start.36 = (bf16[144,1024]{1,0:T(8,128)(2,1)S(1)}, bf16[144,1024]{1,0:T(8,128)(2,1)S(1)}, u32[]{:S(2)}, u32[]{:S(2)}) collective-permute-start(bf16[144,1024]{1,0:T(8,128)(2,1)S(1)} %slice.169), channel_id=1, source_target_pairs={{0,16},{16,0},{1,17},{17,1},{2,18},{18,2},{3,19},{19,3},{4,20},{20... | collective-permute-start | bytes 884744 | tf_op jit(solution)/shard_map/ppermute | solution.py:907
  394.5 9.0 %collective-permute-start.45 = (bf16[256,512]{1,0:T(8,128)(2,1)S(1)}, bf16[256,512]{1,0:T(8,128)(2,1)S(1)}, u32[]{:S(2)}, u32[]{:S(2)}) collective-permute-start(bf16[256,512]{1,0:T(8,128)(2,1)S(1)} %fusion.8.refs_0_), channel_id=1, source_target_pairs={{0,4},{4,0},{1,5},{5,1},{2,6},{6,2},{3,7},{7,3},{8,12},{12,8},{9,1... | collective-permute-start | bytes 786440 | tf_op jit(solution)/shard_map/ppermute | solution.py:907
  402.3 7.7 %collective-permute-start.40 = (bf16[288,1024]{1,0:T(8,128)(2,1)S(1)}, bf16[288,1024]{1,0:T(8,128)(2,1)S(1)}, u32[]{:S(2)}, u32[]{:S(2)}) collective-permute-start(bf16[288,1024]{1,0:T(8,128)(2,1)S(1)} %constant_dynamic-update-slice_fusion.2.refs_3_.refs_11_.refs_19_), channel_id=1, source_target_pairs={{0,4},{4,0},{1,5},{5,1},{2,6},{6,2},{3,7},{7,3},{8,12},{12,8},{9,1... | collective-permute-start | bytes 1769480 | tf_op jit(solution)/shard_map/ppermute | solution.py:907
  402.4 7.6 %collective-permute-start.39 = (bf16[288,1024]{1,0:T(8,128)(2,1)S(1)}, bf16[288,1024]{1,0:T(8,128)(2,1)S(1)}, u32[]{:S(2)}, u32[]{:S(2)}) collective-permute-start(bf16[288,1024]{1,0:T(8,128)(2,1)S(1)} %collective-permute-done.34.refs_2_.refs_10_.refs_18_), channel_id=1, source_target_pairs={{0,4},{4,0},{1,5},{5,1},{2,6},{6,2},{3,7},{7,3},{8,12},{12,8},{9,1... | collective-permute-start | bytes 1769480 | tf_op jit(solution)/shard_map/ppermute | solution.py:907
  402.9 7.1 %collective-permute-start.38 = (bf16[288,1024]{1,0:T(8,128)(2,1)S(1)}, bf16[288,1024]{1,0:T(8,128)(2,1)S(1)}, u32[]{:S(2)}, u32[]{:S(2)}) collective-permute-start(bf16[288,1024]{1,0:T(8,128)(2,1)S(1)} %collective-permute-done.33.refs_1_.refs_9_.refs_17_), channel_id=1, source_target_pairs={{0,4},{4,0},{1,5},{5,1},{2,6},{6,2},{3,7},{7,3},{8,12},{12,8},{9,1... | collective-permute-start | bytes 1769480 | tf_op jit(solution)/shard_map/ppermute | solution.py:907
  403.0 7.0 %collective-permute-start.37 = (bf16[288,1024]{1,0:T(8,128)(2,1)S(1)}, bf16[288,1024]{1,0:T(8,128)(2,1)S(1)}, u32[]{:S(2)}, u32[]{:S(2)}) collective-permute-start(bf16[288,1024]{1,0:T(8,128)(2,1)S(1)} %copy-done.46), channel_id=1, source_target_pairs={{0,4},{4,0},{1,5},{5,1},{2,6},{6,2},{3,7},{7,3},{8,12},{12,8},{9,1... | collective-permute-start | bytes 1769480 | tf_op jit(solution)/shard_map/ppermute | solution.py:907
  403.4 3.9 collective-permute-start.48
  (51 other events, 188.3 us)
Sparse Core Ops, SparseCore 0:
  40.2 45.6 all-gather.3
  91.8 63.8 all-gather.5
  245.2 73.5 reduce-scatter.2
  323.3 48.5 reduce-scatter.4
